TPU v7x, 512 devices: a whole 4x4x16 slice. The times are simulated.
512 devices in a mesh: ep: 32 (over z, x_lo), fsdp: 16 (over y, x_hi, core).
Axes of the slice: x: 4 (x_hi: 2, x_lo: 2; x = x_hi * 2 + x_lo), y: 4, z: 16, core: 2. Of those that a mesh axis runs over, the one named last changes fastest.
Arguments:
- tokens: bfloat16 [65536, 2048], P(('ep', 'fsdp')), may hold values from -6 to 6
- cotangent: bfloat16 [65536, 2048], P(('ep', 'fsdp')), may hold values from -1.1953125 to 1.1953125
- bucket: int32 [65536, 1], P(('ep', 'fsdp')), may hold values from 0 to 31; in each aligned block of 128 rows (0 to 127, 128 to 255, ...) at most 5 rows name the same one
- w_gate: bfloat16 [32, 2048, 512], P('ep', 'fsdp'), may hold values from -0.125 to 0.125
- w_up: bfloat16 [32, 2048, 512], P('ep', 'fsdp'), may hold values from -0.125 to 0.125
- w_down: bfloat16 [32, 2048, 512], P('ep', 'fsdp'), may hold values from -0.25 to 0.25
Outputs:
- outputs: bfloat16 [65536, 2048], P(('ep', 'fsdp'))
- input_grad: bfloat16 [65536, 2048], P(('ep', 'fsdp'))
- grad_gate: bfloat16 [32, 2048, 512], P('ep', 'fsdp')
- grad_up: bfloat16 [32, 2048, 512], P('ep', 'fsdp')
- grad_down: bfloat16 [32, 2048, 512], P('ep', 'fsdp')
Inputs may be any that keep to these rules, and one draw needn't show every extreme that they name: `bucket`: among the 128 rows of one device no expert is named more than 5 times, and in every draw some device names some expert exactly 5 times.
All inputs are finite; a program needn't handle non-finite values.
Results may differ from a plain program's by a relative error of at most 0.019.
Values may be sent and summed in bfloat16 or wider, within the bound.
No kernel may reach another device: no remote copies, remote signals or barrier semaphores. Data moves between devices by JAX's collectives and lax.ppermute only.
A program may use at most 64 MiB of HBM per device.

v0:
```python
import jax
import jax.numpy as jnp
from jax import lax
from jax.sharding import PartitionSpec as P


def slot_matrix(bucket, expert_count, capacity):
    token_count = bucket.shape[0]
    labels = lax.broadcasted_iota(jnp.int32, (token_count, expert_count), 1)
    chosen = (bucket == labels).astype(jnp.int32)
    earlier = jnp.cumsum(chosen, axis=0) - chosen
    slot_index = jnp.sum(earlier * chosen, axis=1)
    position = bucket[:, 0] * capacity + slot_index
    targets = lax.broadcasted_iota(jnp.int32, (expert_count * capacity, token_count), 0)
    return (targets == position[None, :]).astype(jnp.bfloat16)


def contract_rows(left_rows, right_rows):
    return lax.dot_general(
        left_rows, right_rows, (((0,), (0,)), ((), ())), preferred_element_type=jnp.float32
    )


def contract_cols(left_rows, right_rows):
    return lax.dot_general(
        left_rows, right_rows, (((1,), (1,)), ((), ())), preferred_element_type=jnp.float32
    )


def shard_partials(left_rows, right_rows, shard_rows):
    block_count = left_rows.shape[0] // shard_rows
    left_operand_blocks = left_rows.reshape(block_count, shard_rows, left_rows.shape[1])
    right_operand_blocks = right_rows.reshape(block_count, shard_rows, right_rows.shape[1])
    partial_terms = jnp.einsum(
        "ohy,ohs->oys",
        left_operand_blocks,
        right_operand_blocks,
        preferred_element_type=jnp.float32,
    )
    rounded = lax.optimization_barrier(partial_terms.astype(jnp.bfloat16))
    return jnp.sum(rounded.astype(jnp.float32), axis=0)


def local(tokens, cotangent, bucket, w_gate, w_up, w_down):
    token_count = tokens.shape[0]
    model_width = tokens.shape[1]
    expert_count = lax.axis_size("ep")
    capacity = max(2, 5 * token_count // (4 * expert_count))
    slot_rows = expert_count * capacity
    per_shard_width = w_gate.shape[1]
    hidden_width = w_gate.shape[2]
    selector = slot_matrix(bucket, expert_count, capacity)
    joined = jnp.concatenate([tokens, cotangent], axis=1)
    packed = jnp.dot(selector, joined, preferred_element_type=jnp.float32).astype(jnp.bfloat16)
    arrived = lax.all_to_all(
        packed.reshape(expert_count, capacity, 2 * model_width),
        "ep",
        split_axis=0,
        concat_axis=0,
        tiled=True,
    )
    arrived = arrived.reshape(slot_rows, 2 * model_width)
    rows_x = arrived[:, :model_width]
    rows_dy = arrived[:, model_width:]
    full_gate, full_up, full_down = (
        lax.all_gather(w_gate, "fsdp", axis=1, tiled=True),
        lax.all_gather(w_up, "fsdp", axis=1, tiled=True),
        lax.all_gather(w_down, "fsdp", axis=1, tiled=True),
    )
    full_gate = full_gate[0]
    full_up = full_up[0]
    full_down = full_down[0]
    gate_pre = jnp.dot(rows_x, full_gate, preferred_element_type=jnp.float32)
    up_projection_weight = jnp.dot(rows_x, full_up, preferred_element_type=jnp.float32)
    sigmoid_gate = jax.nn.sigmoid(gate_pre)
    activated = gate_pre * sigmoid_gate
    hidden = (activated * up_projection_weight).astype(jnp.bfloat16)
    rows_y = contract_cols(hidden, full_down).astype(jnp.bfloat16)
    back_y = lax.all_to_all(
        rows_y.reshape(expert_count, capacity, model_width),
        "ep",
        split_axis=0,
        concat_axis=0,
        tiled=True,
    )
    grad_hidden = jnp.dot(rows_dy, full_down, preferred_element_type=jnp.float32)
    grad_pre_gate = (
        grad_hidden * up_projection_weight * sigmoid_gate * (1.0 + gate_pre * (1.0 - sigmoid_gate))
    ).astype(jnp.bfloat16)
    grad_pre_up = (grad_hidden * activated).astype(jnp.bfloat16)
    rows_dx = (
        contract_cols(grad_pre_gate, full_gate) + contract_cols(grad_pre_up, full_up)
    ).astype(jnp.bfloat16)
    back_dx = lax.all_to_all(
        rows_dx.reshape(expert_count, capacity, model_width),
        "ep",
        split_axis=0,
        concat_axis=0,
        tiled=True,
    )
    outputs = contract_rows(selector, back_y.reshape(slot_rows, model_width)).astype(jnp.bfloat16)
    input_grad = contract_rows(selector, back_dx.reshape(slot_rows, model_width)).astype(
        jnp.bfloat16
    )
    both_grads = jnp.concatenate([grad_pre_gate, grad_pre_up], axis=1)
    summed = lax.psum_scatter(
        contract_rows(rows_x, both_grads).astype(jnp.bfloat16),
        "fsdp",
        scatter_dimension=0,
        tiled=True,
    ).astype(jnp.float32)
    grad_wg = summed[:, :hidden_width]
    grad_wu = summed[:, hidden_width:]
    dy_columns = lax.all_to_all(rows_dy, "fsdp", split_axis=1, concat_axis=0, tiled=True)
    grad_wd = shard_partials(
        dy_columns, lax.all_gather(hidden, "fsdp", axis=0, tiled=True), slot_rows
    )
    grad_wg = grad_wg.astype(jnp.bfloat16).reshape(1, per_shard_width, hidden_width)
    grad_wu = grad_wu.astype(jnp.bfloat16).reshape(1, per_shard_width, hidden_width)
    grad_wd = grad_wd.astype(jnp.bfloat16).reshape(1, per_shard_width, hidden_width)
    return (outputs, input_grad, grad_wg, grad_wu, grad_wd)


def solution(mesh):
    in_specs = (
        P(("ep", "fsdp"), None),
        P(("ep", "fsdp"), None),
        P(("ep", "fsdp"), None),
        P("ep", "fsdp", None),
        P("ep", "fsdp", None),
        P("ep", "fsdp", None),
    )
    out_specs = (
        P(("ep", "fsdp"), None),
        P(("ep", "fsdp"), None),
        P("ep", "fsdp", None),
        P("ep", "fsdp", None),
        P("ep", "fsdp", None),
    )
    return jax.shard_map(local, mesh=mesh, in_specs=in_specs, out_specs=out_specs, check_vma=False)
```

profile of v0, /device:TPU:6, one launch (start us, length us, event | category | flops | bytes accessed | tf_op | source)
XLA Modules:
  0.0 399.5 jit_solution(14891024153024725717)
XLA Ops:
  11.1 1.7 convolution_convert_fusion
  12.8 1.6 reshape.53
  14.4 16.7 %all-to-all-start = ((bf16[32,5,4096]{2,1,0:T(8,128)(2,1)}), bf16[32,5,4096]{2,1,0:T(8,128)(2,1)S(1)}, u32[]{:S(2)}, u32[]{:S(2)}) async-start(bf16[32,5,4096]{2,1,0:T(8,128)(2,1)} %reshape.53), calls=%async_computation | async-start | bytes 4194304 | tf_op jit(solution)/shard_map/all_to_all | solution.py:55
  31.9 98.5 %all-to-all-done = bf16[32,5,4096]{2,1,0:T(8,128)(2,1)S(1)} async-done(((bf16[32,5,4096]{2,1,0:T(8,128)(2,1)}), bf16[32,5,4096]{2,1,0:T(8,128)(2,1)S(1)}, u32[]{:S(2)}, u32[]{:S(2)}) %all-to-all-start) | async-done | bytes 1310752 | tf_op jit(solution)/shard_map/all_to_all | solution.py:55
  131.0 2.1 fusion.9
  133.1 11.4 %all-gather.7.cloned.1.call-done = bf16[1,2048,512]{2,1,0:T(8,128)(2,1)} async-done(((bf16[1,128,512]{2,1,0:T(8,128)(2,1)}), bf16[1,2048,512]{2,1,0:T(8,128)(2,1)}) %all-gather.7.cloned.1.call-update) | async-done | bytes 2097168 | tf_op jit(solution)/shard_map/all_gather | solution.py:67
  144.5 2.1 fusion.5
  146.6 63.1 %all-gather.9.cloned.1.call-done = bf16[1,2048,512]{2,1,0:T(8,128)(2,1)} async-done(((bf16[1,128,512]{2,1,0:T(8,128)(2,1)}), bf16[1,2048,512]{2,1,0:T(8,128)(2,1)}) %all-gather.9.cloned.1.call-update) | async-done | bytes 2097168 | tf_op jit(solution)/shard_map/all_gather | solution.py:68
  209.6 2.8 multiply_convert_fusion
  212.5 3.3 convolution_convert_fusion.1
  215.8 1.6 copy-done.2
  217.4 2.6 convolution_convert_fusion.2
  220.0 2.4 reshape.55
  222.4 13.9 %all-to-all-start.1 = ((bf16[32,5,2048]{2,1,0:T(8,128)(2,1)}), bf16[32,5,2048]{2,1,0:T(8,128)(2,1)}, u32[]{:S(2)}, u32[]{:S(2)}) async-start(bf16[32,5,2048]{2,1,0:T(8,128)(2,1)} %reshape.55), calls=%async_computation.1 | async-start | bytes 2097152 | tf_op jit(solution)/shard_map/all_to_all | solution.py:79
  236.3 1.9 fusion.7
  240.3 50.0 %all-to-all-done.1 = bf16[32,5,2048]{2,1,0:T(8,128)(2,1)} async-done(((bf16[32,5,2048]{2,1,0:T(8,128)(2,1)}), bf16[32,5,2048]{2,1,0:T(8,128)(2,1)}, u32[]{:S(2)}, u32[]{:S(2)}) %all-to-all-start.1) | async-done | bytes 655392 | tf_op jit(solution)/shard_map/all_to_all | solution.py:79
  290.2 5.4 %all-to-all-start.2 = ((bf16[32,5,2048]{2,1,0:T(8,128)(2,1)}), bf16[32,5,2048]{2,1,0:T(8,128)(2,1)S(1)}, u32[]{:S(2)}, u32[]{:S(2)}) async-start(bf16[32,5,2048]{2,1,0:T(8,128)(2,1)} %reshape.57), calls=%async_computation.2 | async-start | bytes 2097152 | tf_op jit(solution)/shard_map/all_to_all | solution.py:94
  296.6 52.4 %all-to-all-done.2 = bf16[32,5,2048]{2,1,0:T(8,128)(2,1)S(1)} async-done(((bf16[32,5,2048]{2,1,0:T(8,128)(2,1)}), bf16[32,5,2048]{2,1,0:T(8,128)(2,1)S(1)}, u32[]{:S(2)}, u32[]{:S(2)}) %all-to-all-start.2) | async-done | bytes 655392 | tf_op jit(solution)/shard_map/all_to_all | solution.py:94
  349.0 6.7 %all-to-all-start.3 = ((bf16[160,16,128]{2,0,1:T(8,128)(2,1)}), bf16[160,16,128]{2,0,1:T(8,128)(2,1)S(1)}, u32[]{:S(2)}, u32[]{:S(2)}) async-start(bf16[160,16,128]{2,0,1:T(8,128)(2,1)} %copy_bitcast_fusion), calls=%async_computation.4 | async-start | bytes 1310720 | tf_op jit(solution)/shard_map/all_to_all | solution.py:114
  355.7 1.5 reshape.56
  359.7 7.1 %all-to-all-done.3 = bf16[160,16,128]{2,0,1:T(8,128)(2,1)S(1)} async-done(((bf16[160,16,128]{2,0,1:T(8,128)(2,1)}), bf16[160,16,128]{2,0,1:T(8,128)(2,1)S(1)}, u32[]{:S(2)}, u32[]{:S(2)}) %all-to-all-start.3) | async-done | bytes 655392 | tf_op jit(solution)/shard_map/all_to_all | solution.py:114
  366.8 2.6 convolution_convert_fusion.5
  370.4 20.9 %reduce-scatter.2.cloned.1.call-done = bf16[128,1024]{1,0:T(8,128)(2,1)} async-done(((bf16[2048,1024]{1,0:T(8,128)(2,1)}), bf16[128,1024]{1,0:T(8,128)(2,1)}) %reduce-scatter.2.cloned.1.call-update) | async-done | bytes 262160 | tf_op jit(solution)/shard_map/reduce_scatter | solution.py:106
  391.3 1.7 slice_bitcast_fusion.1
  (35 shorter events, 11.9 us)
Async XLA Ops:
  7.2 123.8 %all-gather.5.cloned.1.call-start = ((), (), s32[]{:S(2)}) async-start(), calls=%async_computation.5 | async-start | bytes 2228224 | tf_op jit(solution)/shard_map/all_gather | solution.py:66
  7.9 136.6 %all-gather.7.cloned.1.call-start = ((), (), s32[]{:S(2)}) async-start(), calls=%async_computation.6 | async-start | bytes 2228224 | tf_op jit(solution)/shard_map/all_gather | solution.py:67
  14.4 116.0 %all-to-all-start = ((bf16[32,5,4096]{2,1,0:T(8,128)(2,1)}), bf16[32,5,4096]{2,1,0:T(8,128)(2,1)S(1)}, u32[]{:S(2)}, u32[]{:S(2)}) async-start(bf16[32,5,4096]{2,1,0:T(8,128)(2,1)} %reshape.53), calls=%async_computation | async-start | bytes 4194304 | tf_op jit(solution)/shard_map/all_to_all | solution.py:55
  31.1 178.5 %all-gather.9.cloned.1.call-start = ((), (), s32[]{:S(2)}) async-start(), calls=%async_computation.7 | async-start | bytes 2228224 | tf_op jit(solution)/shard_map/all_gather | solution.py:68
  31.8 335.0 %all-gather.11.cloned.1.call-start = ((), (), s32[]{:S(2)}) async-start(), calls=%async_computation.9 | async-start | bytes 2785280 | tf_op jit(solution)/shard_map/all_gather | solution.py:116
  212.5 3.3 copy-start.3
  212.5 3.3 copy-start.4
  212.5 178.8 %reduce-scatter.2.cloned.1.call-start = ((), (), s32[]{:S(2)}) async-start(), calls=%async_computation.8 | async-start | bytes 4456448 | tf_op jit(solution)/shard_map/reduce_scatter | solution.py:106
  215.8 1.6 copy-start.2
  220.0 16.3 %copy-start = (bf16[1,2048,512]{2,1,0:T(8,128)(2,1)S(1)}, bf16[1,2048,512]{2,1,0:T(8,128)(2,1)}, u32[]{:S(2)}) copy-start(bf16[1,2048,512]{2,1,0:T(8,128)(2,1)} %all-gather.5.cloned.1.call-done) | copy-start | bytes 6291460
  222.4 67.8 %all-to-all-start.1 = ((bf16[32,5,2048]{2,1,0:T(8,128)(2,1)}), bf16[32,5,2048]{2,1,0:T(8,128)(2,1)}, u32[]{:S(2)}, u32[]{:S(2)}) async-start(bf16[32,5,2048]{2,1,0:T(8,128)(2,1)} %reshape.55), calls=%async_computation.1 | async-start | bytes 2097152 | tf_op jit(solution)/shard_map/all_to_all | solution.py:79
  236.3 1.9 copy-start.1
  236.3 1.9 copy-start.5
  290.2 58.8 %all-to-all-start.2 = ((bf16[32,5,2048]{2,1,0:T(8,128)(2,1)}), bf16[32,5,2048]{2,1,0:T(8,128)(2,1)S(1)}, u32[]{:S(2)}, u32[]{:S(2)}) async-start(bf16[32,5,2048]{2,1,0:T(8,128)(2,1)} %reshape.57), calls=%async_computation.2 | async-start | bytes 2097152 | tf_op jit(solution)/shard_map/all_to_all | solution.py:94
  349.0 17.8 %all-to-all-start.3 = ((bf16[160,16,128]{2,0,1:T(8,128)(2,1)}), bf16[160,16,128]{2,0,1:T(8,128)(2,1)S(1)}, u32[]{:S(2)}, u32[]{:S(2)}) async-start(bf16[160,16,128]{2,0,1:T(8,128)(2,1)} %copy_bitcast_fusion), calls=%async_computation.4 | async-start | bytes 1310720 | tf_op jit(solution)/shard_map/all_to_all | solution.py:114
Sparse Core Ops, SparseCore 0:
  11.3 67.3 all-gather.4
  82.1 62.3 all-gather.6
  147.8 61.7 all-gather.8
  212.8 64.3 all-gather.10
  281.9 109.2 reduce-scatter.1
where the time goes:
time: 401 us; the launch traced here: 399 us
  waiting for transfers between devices  305 us (76%)
  starting transfers between devices  42.8 us (11%)
  matrix products  22.1 us (6%)
  between operations  13.9 us (3%)
  local copies, waits for them, and re-layouts  11.9 us (3%)
    all_to_all x1, waiting for transfers between devices, local(): lax.all_to_all(packed.reshape(expert_count, capacity, 2 * model_width), '...  98.5 us
    all_gather x1, waiting for transfers between devices, local(): lax.all_gather(w_down, 'fsdp', axis=1, tiled=True)  63.1 us
    all_to_all x1, waiting for transfers between devices, local(): lax.all_to_all(rows_dx.reshape(expert_count, capacity, model_width), 'ep'...  52.4 us
    all_to_all x1, waiting for transfers between devices, local(): lax.all_to_all(rows_y.reshape(expert_count, capacity, model_width), 'ep',...  50 us
    reduce_scatter x1, waiting for transfers between devices, local(): lax.psum_scatter(contract_rows(rows_x, both_grads).astype(jnp.bfloat16),...  20.9 us
    all_to_all x1, starting transfers between devices, local(): lax.all_to_all(packed.reshape(expert_count, capacity, 2 * model_width), '...  16.7 us
    all_to_all x1, starting transfers between devices, local(): lax.all_to_all(rows_y.reshape(expert_count, capacity, model_width), 'ep',...  13.9 us
    all_gather x1, waiting for transfers between devices, local(): lax.all_gather(w_up, 'fsdp', axis=1, tiled=True)  11.4 us
  transfers between devices with their start and end apart: 9, of which 7 were waited for; matrix products, arithmetic and copies ran while one was open for 8% of the time, Pallas kernels for 0%

commit v1 on v0

v1 whole, which is shorter than its diff:
```python
import jax
import jax.numpy as jnp
from jax import lax
from jax.sharding import PartitionSpec as P


def slot_matrix(bucket, expert_count, capacity):
    token_count = bucket.shape[0]
    labels = lax.broadcasted_iota(jnp.int32, (token_count, expert_count), 1)
    chosen = (bucket == labels).astype(jnp.int32)
    earlier = jnp.cumsum(chosen, axis=0) - chosen
    slot_index = jnp.sum(earlier * chosen, axis=1)
    position = bucket[:, 0] * capacity + slot_index
    targets = lax.broadcasted_iota(jnp.int32, (expert_count * capacity, token_count), 0)
    return (targets == position[None, :]).astype(jnp.bfloat16)


def contract_rows(left_rows, right_rows):
    return lax.dot_general(
        left_rows, right_rows, (((0,), (0,)), ((), ())), preferred_element_type=jnp.float32
    )


def contract_cols(left_rows, right_rows):
    return lax.dot_general(
        left_rows, right_rows, (((1,), (1,)), ((), ())), preferred_element_type=jnp.float32
    )


def exchange(rows, expert_count):
    row_count, width = rows.shape
    chunk = row_count // expert_count * (width // 128)
    sent = rows.reshape(row_count, width // 128, 128).reshape(expert_count, chunk, 128)
    arrived = lax.all_to_all(sent, "ep", split_axis=0, concat_axis=0, tiled=True)
    return arrived.reshape(row_count, width // 128, 128).reshape(row_count, width)


Y, X_HI = 4, 2


def core_swap(array):
    return lax.ppermute(array, "fsdp", [(f, f ^ 1) for f in range(2 * Y * X_HI)])


def chip_shift(array, dy, dx):
    pairs = []
    for y in range(Y):
        for x in range(X_HI):
            for core in range(2):
                pairs.append(
                    ((y * X_HI + x) * 2 + core, ((y + dy) % Y * X_HI + (x ^ dx)) * 2 + core)
                )
    return lax.ppermute(array, "fsdp", pairs)


def local(tokens, cotangent, bucket, w_gate, w_up, w_down):
    token_count = tokens.shape[0]
    model_width = tokens.shape[1]
    expert_count = lax.axis_size("ep")
    capacity = max(2, 5 * token_count // (4 * expert_count))
    slot_rows = expert_count * capacity
    shard_width = w_gate.shape[1]
    hidden_width = w_gate.shape[2]
    chips = Y * X_HI
    place = lax.axis_index("fsdp")
    core = place % 2
    chip = place // 2

    weights = lax.all_gather(
        jnp.concatenate([w_gate[0], w_up[0], w_down[0]], axis=1), "fsdp", axis=0, tiled=True
    )
    selector = slot_matrix(bucket, expert_count, capacity)
    joined = jnp.concatenate([tokens, cotangent], axis=1)
    packed = jnp.dot(selector, joined, preferred_element_type=jnp.float32).astype(jnp.bfloat16)
    arrived = exchange(packed, expert_count)
    rows_x = arrived[:, :model_width]
    rows_dy = arrived[:, model_width:]

    blocks = arrived.reshape(slot_rows, 2 * chips, 2, shard_width)
    own = jnp.where(core == 0, blocks[:, :, 0], blocks[:, :, 1])
    other = core_swap(jnp.where(core == 0, blocks[:, :, 1], blocks[:, :, 0]))

    w_gate_up = weights[:, : 2 * hidden_width]
    w_out = weights[:, 2 * hidden_width :]
    pre = jnp.dot(rows_x, w_gate_up, preferred_element_type=jnp.float32)
    gate_pre = pre[:, :hidden_width]
    up_proj = pre[:, hidden_width:]
    sigmoid_gate = jax.nn.sigmoid(gate_pre)
    activated = gate_pre * sigmoid_gate
    hidden = (activated * up_proj).astype(jnp.bfloat16)
    rows_y = contract_cols(hidden, w_out).astype(jnp.bfloat16)
    back_y = exchange(rows_y, expert_count)
    grad_hidden = jnp.dot(rows_dy, w_out, preferred_element_type=jnp.float32)
    grad_pre_gate = (
        grad_hidden * up_proj * sigmoid_gate * (1.0 + gate_pre * (1.0 - sigmoid_gate))
    ).astype(jnp.bfloat16)
    grad_pre_up = (grad_hidden * activated).astype(jnp.bfloat16)
    grads_pre = jnp.concatenate([grad_pre_gate, grad_pre_up], axis=1)
    rows_dx = contract_cols(grads_pre, w_gate_up).astype(jnp.bfloat16)
    back_dx = exchange(rows_dx, expert_count)

    sides = jnp.concatenate([grads_pre, hidden], axis=1)
    other_sides = core_swap(sides)
    pair_rows = jnp.concatenate([own, other], axis=0)
    pair_sides = jnp.concatenate([sides, other_sides], axis=0)

    def terms(target):
        x_block = lax.dynamic_index_in_dim(pair_rows, target, 1, keepdims=False)
        dy_block = lax.dynamic_index_in_dim(pair_rows, target + chips, 1, keepdims=False)
        gate_up = contract_rows(x_block, pair_sides[:, : 2 * hidden_width])
        down = contract_rows(dy_block, pair_sides[:, 2 * hidden_width :])
        return jnp.concatenate([gate_up, down], axis=1).astype(jnp.bfloat16)

    total = terms(chip).astype(jnp.float32)
    y_index, x_index = chip // X_HI, chip % X_HI
    for dy, dx in ((2, 1), (2, 0), (1, 1), (3, 1), (1, 0), (3, 0), (0, 1)):
        target = (y_index + dy) % Y * X_HI + (x_index ^ dx)
        total = total + chip_shift(terms(target), dy, dx).astype(jnp.float32)

    grads = total.astype(jnp.bfloat16)
    grad_wg = grads[None, :, :hidden_width]
    grad_wu = grads[None, :, hidden_width : 2 * hidden_width]
    grad_wd = grads[None, :, 2 * hidden_width :]
    outputs = contract_rows(selector, back_y).astype(jnp.bfloat16)
    input_grad = contract_rows(selector, back_dx).astype(jnp.bfloat16)
    return (outputs, input_grad, grad_wg, grad_wu, grad_wd)


def solution(mesh):
    in_specs = (
        P(("ep", "fsdp"), None),
        P(("ep", "fsdp"), None),
        P(("ep", "fsdp"), None),
        P("ep", "fsdp", None),
        P("ep", "fsdp", None),
        P("ep", "fsdp", None),
    )
    out_specs = (
        P(("ep", "fsdp"), None),
        P(("ep", "fsdp"), None),
        P("ep", "fsdp", None),
        P("ep", "fsdp", None),
        P("ep", "fsdp", None),
    )
    return jax.shard_map(local, mesh=mesh, in_specs=in_specs, out_specs=out_specs, check_vma=False)
```

time: 401 us -> 214 us (0.53)
  waiting for transfers between devices: 305 us -> 92.3 us
  starting transfers between devices: 42.8 us -> 61.4 us
  other arithmetic: 3.37 us -> 17.6 us
  matrix products: 22.1 us -> 17.5 us
    all_to_all x4 -> x3, waiting for transfers between devices: 208 us -> 80.3 us  [exchange(): lax.all_to_all(sent, 'ep', split_axis=0, concat_axis=0, tiled=True)]
    all_gather x4 -> x1, waiting for transfers between devices: 74.5 us -> 0.01 us  [local(): lax.all_gather(jnp.concatenate([w_gate[0], w_up[0], w_down[0]], axis=1),...]
    ppermute x0 -> x9, starting transfers between devices: none -> 31.7 us  [the longest x7 27.3 us: chip_shift(): return lax.ppermute(array, 'fsdp', pairs)]
    reduce_scatter x1 -> x0, waiting for transfers between devices: 20.9 us -> none  [local(): lax.psum_scatter(contract_rows(rows_x, both_grads).astype(jnp.bfloat16),...]
    all_to_all x4 -> x3, starting transfers between devices: 42.6 us -> 29.7 us  [exchange(): lax.all_to_all(sent, 'ep', split_axis=0, concat_axis=0, tiled=True)]
    ppermute x0 -> x9, waiting for transfers between devices: none -> 12 us  [the longest x7 12 us: chip_shift(): return lax.ppermute(array, 'fsdp', pairs)]
    concatenate x0 -> x13, other arithmetic: none -> 11 us  [the longest x3 5.1 us: local(): pair_rows = jnp.concatenate([own, other], axis=0)]
    reshape x7 -> x0, local copies, waits for them, and re-layouts: 9.28 us -> none  [the longest x1 2.42 us: local(): rows_y.reshape(expert_count, capacity, model_width)]
  transfers between devices with their start and end apart: 9 -> 13, of which waited for: 7 -> 4; matrix products, arithmetic and copies ran while one was open for 8% -> 17% of each run, Pallas kernels for 0% -> 0%
where the time goes in v1:
time: 214 us; the launch traced here: 213 us
  waiting for transfers between devices  92.3 us (43%)
  starting transfers between devices  61.4 us (29%)
  other arithmetic  17.6 us (8%)
  matrix products  17.5 us (8%)
  between operations  14.8 us (7%)
  local copies, waits for them, and re-layouts  8.92 us (4%)
    all_to_all x3, waiting for transfers between devices, exchange(): lax.all_to_all(sent, 'ep', split_axis=0, concat_axis=0, tiled=True)  80.3 us
    all_to_all x3, starting transfers between devices, exchange(): lax.all_to_all(sent, 'ep', split_axis=0, concat_axis=0, tiled=True)  29.7 us
    ppermute x7, starting transfers between devices, chip_shift(): return lax.ppermute(array, 'fsdp', pairs)  27.3 us
    ppermute x7, waiting for transfers between devices, chip_shift(): return lax.ppermute(array, 'fsdp', pairs)  12 us
    dot_general x18, matrix products, contract_rows(): lax.dot_general(left_rows, right_rows, (((0,), (0,)), ((), ())), preferre...  8.75 us
    concatenate x3, other arithmetic, local(): pair_rows = jnp.concatenate([own, other], axis=0)  5.1 us
    dot_general x2, matrix products, contract_cols(): lax.dot_general(left_rows, right_rows, (((1,), (1,)), ((), ())), preferre...  4.55 us
    ppermute x2, starting transfers between devices, core_swap(): lax.ppermute(array, 'fsdp', [(f, f ^ 1) for f in range(2 * Y * X_HI)])  4.33 us
  transfers between devices with their start and end apart: 13, of which 4 were waited for; matrix products, arithmetic and copies ran while one was open for 17% of the time, Pallas kernels for 0%

profile of v1, /device:TPU:6, one launch (start us, length us, event | category | flops | bytes accessed | tf_op | source)
XLA Modules:
  0.0 212.6 jit_solution(15751175552032394849)
XLA Ops:
  7.2 1.9 pad_maximum_fusion.2
  10.8 1.5 reshape_reshape.18
  12.3 16.7 %all-to-all-start = ((bf16[32,160,128]{2,1,0:T(8,128)(2,1)}), bf16[32,160,128]{2,1,0:T(8,128)(2,1)S(1)}, u32[]{:S(2)}, u32[]{:S(2)}) async-start(bf16[32,160,128]{2,1,0:T(8,128)(2,1)} %reshape_reshape.18), calls=%async_computation | async-start | bytes 2621440 | tf_op jit(solution)/shard_map/all_to_all | solution.py:34
  29.0 64.8 %all-to-all-done = bf16[32,160,128]{2,1,0:T(8,128)(2,1)S(1)} async-done(((bf16[32,160,128]{2,1,0:T(8,128)(2,1)}), bf16[32,160,128]{2,1,0:T(8,128)(2,1)S(1)}, u32[]{:S(2)}, u32[]{:S(2)}) %all-to-all-start) | async-done | bytes 1310752 | tf_op jit(solution)/shard_map/all_to_all | solution.py:34
  93.8 3.9 %broadcast_select_fusion = (bf16[160,16,1,128]{3,2,1,0:T(2,128)(2,1)S(1)}, bf16[160,16,1,128]{3,2,1,0:T(2,128)(2,1)}) fusion(pred[]{:T(512)S(6)} %eq.34, bf16[160,16,2,128]{3,2,1,0:T(2,128)(2,1)S(1)} %bitcast.77), kind=kLoop, calls=%fused_computation.37 | loop fusion | flops 655360 | bytes 2621441 | tf_op jit(solution)/shard_map/jit(_where)/select_n | solution.py:81
  97.7 1.9 collective-permute-start
  104.0 1.9 fusion.26
  105.9 1.9 fusion.20
  107.8 3.2 %fusion.2 = f32[160,1024]{1,0:T(8,128)S(1)} fusion(bf16[2048,1536]{1,0:T(8,128)(2,1)} %all-gather.2.cloned.1.call-done, bf16[160,4096]{1,0:T(8,128)(2,1)S(1)} %copy-done), kind=kOutput, calls=%fused_computation.35 | convolution fusion | flops 671088640 | bytes 5505024 | tf_op jit(solution)/shard_map/dot_general | solution.py:85
  112.5 2.4 %collective-permute-start.1 = (bf16[160,1536]{1,0:T(8,128)(2,1)S(1)}, bf16[160,1536]{1,0:T(8,128)(2,1)S(1)}, u32[]{:S(2)}, u32[]{:S(2)}) collective-permute-start(bf16[160,1536]{1,0:T(8,128)(2,1)S(1)} %pad_maximum_fusion.1), channel_id=1, source_target_pairs={{0,1},{1,0},{2,3},{3,2},{4,5},{5,4},{6,7},{7,6},{8,9},{9,8},{10,11... | collective-permute-start | bytes 1474568 | tf_op jit(solution)/shard_map/ppermute | solution.py:42
  116.9 5.9 %all-to-all-start.1 = ((bf16[32,80,128]{2,1,0:T(8,128)(2,1)}), bf16[32,80,128]{2,1,0:T(8,128)(2,1)S(1)}, u32[]{:S(2)}, u32[]{:S(2)}) async-start(bf16[32,80,128]{2,1,0:T(8,128)(2,1)} %reshape_reshape.20), calls=%async_computation.1 | async-start | bytes 1310720 | tf_op jit(solution)/shard_map/all_to_all | solution.py:34
  122.8 3.7 %fusion.4 = bf16[160,2048]{1,0:T(8,128)(2,1)S(1)} fusion(bf16[2048,1536]{1,0:T(8,128)(2,1)} %all-gather.2.cloned.1.call-done, bf16[160,512]{1,0:T(8,128)(2,1)S(1)} %get-tuple-element.24, bf16[160,512]{1,0:T(8,128)(2,1)S(1)} %get-tuple-element.23), kind=kOutput, calls=%fused_computation.39 | convolution fusion | flops 672071680 | bytes 5177344 | tf_op jit(solution)/shard_map/dot_general | solution.py:25
  129.2 4.8 %collective-permute-start.8 = (bf16[128,1536]{1,0:T(8,128)(2,1)}, bf16[128,1536]{1,0:T(8,128)(2,1)S(1)}, u32[]{:S(2)}, u32[]{:S(2)}) collective-permute-start(bf16[128,1536]{1,0:T(8,128)(2,1)} %pad_maximum_fusion.9), channel_id=1, source_target_pairs={{0,2},{1,3},{2,0},{3,1},{4,6},{5,7},{6,4},{7,5},{8,10},{9,11},{10,... | collective-permute-start | bytes 1179656 | tf_op jit(solution)/shard_map/ppermute | solution.py:53
  135.3 3.1 %collective-permute-start.7 = (bf16[128,1536]{1,0:T(8,128)(2,1)}, bf16[128,1536]{1,0:T(8,128)(2,1)S(1)}, u32[]{:S(2)}, u32[]{:S(2)}) collective-permute-start(bf16[128,1536]{1,0:T(8,128)(2,1)} %pad_maximum_fusion.8), channel_id=1, source_target_pairs={{0,12},{1,13},{2,14},{3,15},{4,0},{5,1},{6,2},{7,3},{8,4},{9,5},{1... | collective-permute-start | bytes 1179656 | tf_op jit(solution)/shard_map/ppermute | solution.py:53
  139.9 3.1 %collective-permute-start.6 = (bf16[128,1536]{1,0:T(8,128)(2,1)}, bf16[128,1536]{1,0:T(8,128)(2,1)}, u32[]{:S(2)}, u32[]{:S(2)}) collective-permute-start(bf16[128,1536]{1,0:T(8,128)(2,1)} %pad_maximum_fusion.7), channel_id=1, source_target_pairs={{0,4},{1,5},{2,6},{3,7},{4,8},{5,9},{6,10},{7,11},{8,12},{9,13},{1... | collective-permute-start | bytes 1179656 | tf_op jit(solution)/shard_map/ppermute | solution.py:53
  144.4 5.8 %collective-permute-start.5 = (bf16[128,1536]{1,0:T(8,128)(2,1)}, bf16[128,1536]{1,0:T(8,128)(2,1)}, u32[]{:S(2)}, u32[]{:S(2)}) collective-permute-start(bf16[128,1536]{1,0:T(8,128)(2,1)} %pad_maximum_fusion.6), channel_id=1, source_target_pairs={{0,14},{1,15},{2,12},{3,13},{4,2},{5,3},{6,0},{7,1},{8,6},{9,7},{1... | collective-permute-start | bytes 1179656 | tf_op jit(solution)/shard_map/ppermute | solution.py:53
  151.6 2.5 %collective-permute-start.4 = (bf16[128,1536]{1,0:T(8,128)(2,1)}, bf16[128,1536]{1,0:T(8,128)(2,1)}, u32[]{:S(2)}, u32[]{:S(2)}) collective-permute-start(bf16[128,1536]{1,0:T(8,128)(2,1)} %pad_maximum_fusion.5), channel_id=1, source_target_pairs={{0,6},{1,7},{2,4},{3,5},{4,10},{5,11},{6,8},{7,9},{8,14},{9,15},{1... | collective-permute-start | bytes 1179656 | tf_op jit(solution)/shard_map/ppermute | solution.py:53
  154.5 6.1 %all-to-all-done.1 = bf16[32,80,128]{2,1,0:T(8,128)(2,1)S(1)} async-done(((bf16[32,80,128]{2,1,0:T(8,128)(2,1)}), bf16[32,80,128]{2,1,0:T(8,128)(2,1)S(1)}, u32[]{:S(2)}, u32[]{:S(2)}) %all-to-all-start.1) | async-done | bytes 655392 | tf_op jit(solution)/shard_map/all_to_all | solution.py:34
  160.5 7.0 %all-to-all-start.2 = ((bf16[32,80,128]{2,1,0:T(8,128)(2,1)}), bf16[32,80,128]{2,1,0:T(8,128)(2,1)S(1)}, u32[]{:S(2)}, u32[]{:S(2)}) async-start(bf16[32,80,128]{2,1,0:T(8,128)(2,1)} %reshape_reshape.22), calls=%async_computation.2 | async-start | bytes 1310720 | tf_op jit(solution)/shard_map/all_to_all | solution.py:34
  170.5 3.3 %collective-permute-start.3 = (bf16[128,1536]{1,0:T(8,128)(2,1)S(1)}, bf16[128,1536]{1,0:T(8,128)(2,1)S(1)}, u32[]{:S(2)}, u32[]{:S(2)}) collective-permute-start(bf16[128,1536]{1,0:T(8,128)(2,1)S(1)} %pad_maximum_fusion.4), channel_id=1, source_target_pairs={{0,8},{1,9},{2,10},{3,11},{4,12},{5,13},{6,14},{7,15},{8,0},{9,1},... | collective-permute-start | bytes 1179656 | tf_op jit(solution)/shard_map/ppermute | solution.py:53
  173.8 4.6 %collective-permute-start.2 = (bf16[128,1536]{1,0:T(8,128)(2,1)S(1)}, bf16[128,1536]{1,0:T(8,128)(2,1)S(1)}, u32[]{:S(2)}, u32[]{:S(2)}) collective-permute-start(bf16[128,1536]{1,0:T(8,128)(2,1)S(1)} %pad_maximum_fusion.3), channel_id=1, source_target_pairs={{0,10},{1,11},{2,8},{3,9},{4,14},{5,15},{6,12},{7,13},{8,2},{9,3},... | collective-permute-start | bytes 1179656 | tf_op jit(solution)/shard_map/ppermute | solution.py:53
  179.0 12.0 %collective-permute-done.3 = bf16[128,1536]{1,0:T(8,128)(2,1)S(1)} collective-permute-done((bf16[128,1536]{1,0:T(8,128)(2,1)S(1)}, bf16[128,1536]{1,0:T(8,128)(2,1)S(1)}, u32[]{:S(2)}, u32[]{:S(2)}) %collective-permute-start.3) | collective-permute-done | bytes 393248 | tf_op jit(solution)/shard_map/ppermute | solution.py:53
  191.0 1.6 add_convert_fusion
  194.9 9.4 %all-to-all-done.2 = bf16[32,80,128]{2,1,0:T(8,128)(2,1)S(1)} async-done(((bf16[32,80,128]{2,1,0:T(8,128)(2,1)}), bf16[32,80,128]{2,1,0:T(8,128)(2,1)S(1)}, u32[]{:S(2)}, u32[]{:S(2)}) %all-to-all-start.2) | async-done | bytes 655392 | tf_op jit(solution)/shard_map/all_to_all | solution.py:34
  (87 shorter events, 24.6 us)
Async XLA Ops:
  7.2 3.1 %copy-start.1 = (bf16[128,2048]{1,0:T(8,128)(2,1)S(1)}, bf16[128,2048]{1,0:T(8,128)(2,1)}, u32[]{:S(2)}) copy-start(bf16[128,2048]{1,0:T(8,128)(2,1)} %param.7) | copy-start | bytes 1572868
  7.2 100.6 %all-gather.2.cloned.1.call-start = ((), (), s32[]{:S(2)}) async-start(), calls=%async_computation.3 | async-start | bytes 6684672 | tf_op jit(solution)/shard_map/all_gather | solution.py:69
  12.3 81.5 %all-to-all-start = ((bf16[32,160,128]{2,1,0:T(8,128)(2,1)}), bf16[32,160,128]{2,1,0:T(8,128)(2,1)S(1)}, u32[]{:S(2)}, u32[]{:S(2)}) async-start(bf16[32,160,128]{2,1,0:T(8,128)(2,1)} %reshape_reshape.18), calls=%async_computation | async-start | bytes 2621440 | tf_op jit(solution)/shard_map/all_to_all | solution.py:34
  97.7 5.0 %collective-permute-start = (bf16[160,16,128]{2,1,0:T(8,128)(2,1)S(1)}, bf16[160,16,128]{2,1,0:T(8,128)(2,1)S(1)}, u32[]{:S(2)}, u32[]{:S(2)}) collective-permute-start(bf16[160,16,128]{2,1,0:T(8,128)(2,1)S(1)} %bitcast.81), channel_id=1, source_target_pairs={{0,1},{1,0},{2,3},{3,2},{4,5},{5,4},{6,7},{7,6},{8,9},{9,8},{10,11... | collective-permute-start | bytes 1966088 | tf_op jit(solution)/shard_map/ppermute | solution.py:42
  107.8 4.0 %copy-start.15 = (bf16[2048,1536]{1,0:T(8,128)(2,1)S(1)}, bf16[2048,1536]{1,0:T(8,128)(2,1)}, u32[]{:S(2)}) copy-start(bf16[2048,1536]{1,0:T(8,128)(2,1)} %all-gather.2.cloned.1.call-done) | copy-start | bytes 18874372
  112.5 15.2 %collective-permute-start.1 = (bf16[160,1536]{1,0:T(8,128)(2,1)S(1)}, bf16[160,1536]{1,0:T(8,128)(2,1)S(1)}, u32[]{:S(2)}, u32[]{:S(2)}) collective-permute-start(bf16[160,1536]{1,0:T(8,128)(2,1)S(1)} %pad_maximum_fusion.1), channel_id=1, source_target_pairs={{0,1},{1,0},{2,3},{3,2},{4,5},{5,4},{6,7},{7,6},{8,9},{9,8},{10,11... | collective-permute-start | bytes 1474568 | tf_op jit(solution)/shard_map/ppermute | solution.py:42
  116.9 43.7 %all-to-all-start.1 = ((bf16[32,80,128]{2,1,0:T(8,128)(2,1)}), bf16[32,80,128]{2,1,0:T(8,128)(2,1)S(1)}, u32[]{:S(2)}, u32[]{:S(2)}) async-start(bf16[32,80,128]{2,1,0:T(8,128)(2,1)} %reshape_reshape.20), calls=%async_computation.1 | async-start | bytes 1310720 | tf_op jit(solution)/shard_map/all_to_all | solution.py:34
  129.2 9.3 %copy-start.12 = (bf16[320,1,128]{2,1,0:T(2,128)(2,1)S(1)}, bf16[320,1,128]{2,1,0:T(2,128)(2,1)}, u32[]{:S(2)}) copy-start(bf16[320,1,128]{2,1,0:T(2,128)(2,1)} %get-tuple-element.16) | copy-start | bytes 245764
  129.2 41.3 %collective-permute-start.8 = (bf16[128,1536]{1,0:T(8,128)(2,1)}, bf16[128,1536]{1,0:T(8,128)(2,1)S(1)}, u32[]{:S(2)}, u32[]{:S(2)}) collective-permute-start(bf16[128,1536]{1,0:T(8,128)(2,1)} %pad_maximum_fusion.9), channel_id=1, source_target_pairs={{0,2},{1,3},{2,0},{3,1},{4,6},{5,7},{6,4},{7,5},{8,10},{9,11},{10,... | collective-permute-start | bytes 1179656 | tf_op jit(solution)/shard_map/ppermute | solution.py:53
  134.0 4.8 %copy-start.11 = (bf16[320,1,128]{2,1,0:T(2,128)(2,1)S(1)}, bf16[320,1,128]{2,1,0:T(2,128)(2,1)}, u32[]{:S(2)}) copy-start(bf16[320,1,128]{2,1,0:T(2,128)(2,1)} %get-tuple-element.15) | copy-start | bytes 245764
  135.3 7.7 %copy-start.10 = (bf16[320,1,128]{2,1,0:T(2,128)(2,1)S(1)}, bf16[320,1,128]{2,1,0:T(2,128)(2,1)}, u32[]{:S(2)}) copy-start(bf16[320,1,128]{2,1,0:T(2,128)(2,1)} %get-tuple-element.14) | copy-start | bytes 245764
  135.3 38.5 %collective-permute-start.7 = (bf16[128,1536]{1,0:T(8,128)(2,1)}, bf16[128,1536]{1,0:T(8,128)(2,1)S(1)}, u32[]{:S(2)}, u32[]{:S(2)}) collective-permute-start(bf16[128,1536]{1,0:T(8,128)(2,1)} %pad_maximum_fusion.8), channel_id=1, source_target_pairs={{0,12},{1,13},{2,14},{3,15},{4,0},{5,1},{6,2},{7,3},{8,4},{9,5},{1... | collective-permute-start | bytes 1179656 | tf_op jit(solution)/shard_map/ppermute | solution.py:53
  138.5 4.8 %copy-start.9 = (bf16[320,1,128]{2,1,0:T(2,128)(2,1)S(1)}, bf16[320,1,128]{2,1,0:T(2,128)(2,1)}, u32[]{:S(2)}) copy-start(bf16[320,1,128]{2,1,0:T(2,128)(2,1)} %get-tuple-element.13) | copy-start | bytes 245764
  139.9 10.4 %copy-start.8 = (bf16[320,1,128]{2,1,0:T(2,128)(2,1)S(1)}, bf16[320,1,128]{2,1,0:T(2,128)(2,1)}, u32[]{:S(2)}) copy-start(bf16[320,1,128]{2,1,0:T(2,128)(2,1)} %get-tuple-element.12) | copy-start | bytes 245764
  139.9 39.1 %collective-permute-start.6 = (bf16[128,1536]{1,0:T(8,128)(2,1)}, bf16[128,1536]{1,0:T(8,128)(2,1)}, u32[]{:S(2)}, u32[]{:S(2)}) collective-permute-start(bf16[128,1536]{1,0:T(8,128)(2,1)} %pad_maximum_fusion.7), channel_id=1, source_target_pairs={{0,4},{1,5},{2,6},{3,7},{4,8},{5,9},{6,10},{7,11},{8,12},{9,13},{1... | collective-permute-start | bytes 1179656 | tf_op jit(solution)/shard_map/ppermute | solution.py:53
  143.0 7.5 %copy-start.7 = (bf16[320,1,128]{2,1,0:T(2,128)(2,1)S(1)}, bf16[320,1,128]{2,1,0:T(2,128)(2,1)}, u32[]{:S(2)}) copy-start(bf16[320,1,128]{2,1,0:T(2,128)(2,1)} %get-tuple-element.11) | copy-start | bytes 245764
  144.4 9.8 %copy-start.6 = (bf16[320,1,128]{2,1,0:T(2,128)(2,1)S(1)}, bf16[320,1,128]{2,1,0:T(2,128)(2,1)}, u32[]{:S(2)}) copy-start(bf16[320,1,128]{2,1,0:T(2,128)(2,1)} %get-tuple-element.10) | copy-start | bytes 245764
  144.4 34.6 %collective-permute-start.5 = (bf16[128,1536]{1,0:T(8,128)(2,1)}, bf16[128,1536]{1,0:T(8,128)(2,1)}, u32[]{:S(2)}, u32[]{:S(2)}) collective-permute-start(bf16[128,1536]{1,0:T(8,128)(2,1)} %pad_maximum_fusion.6), channel_id=1, source_target_pairs={{0,14},{1,15},{2,12},{3,13},{4,2},{5,3},{6,0},{7,1},{8,6},{9,7},{1... | collective-permute-start | bytes 1179656 | tf_op jit(solution)/shard_map/ppermute | solution.py:53
  151.6 27.4 %collective-permute-start.4 = (bf16[128,1536]{1,0:T(8,128)(2,1)}, bf16[128,1536]{1,0:T(8,128)(2,1)}, u32[]{:S(2)}, u32[]{:S(2)}) collective-permute-start(bf16[128,1536]{1,0:T(8,128)(2,1)} %pad_maximum_fusion.5), channel_id=1, source_target_pairs={{0,6},{1,7},{2,4},{3,5},{4,10},{5,11},{6,8},{7,9},{8,14},{9,15},{1... | collective-permute-start | bytes 1179656 | tf_op jit(solution)/shard_map/ppermute | solution.py:53
  160.5 43.8 %all-to-all-start.2 = ((bf16[32,80,128]{2,1,0:T(8,128)(2,1)}), bf16[32,80,128]{2,1,0:T(8,128)(2,1)S(1)}, u32[]{:S(2)}, u32[]{:S(2)}) async-start(bf16[32,80,128]{2,1,0:T(8,128)(2,1)} %reshape_reshape.22), calls=%async_computation.2 | async-start | bytes 1310720 | tf_op jit(solution)/shard_map/all_to_all | solution.py:34
  170.0 8.4 %copy-start.4 = (bf16[320,1,128]{2,1,0:T(2,128)(2,1)S(1)}, bf16[320,1,128]{2,1,0:T(2,128)(2,1)}, u32[]{:S(2)}) copy-start(bf16[320,1,128]{2,1,0:T(2,128)(2,1)} %get-tuple-element.6) | copy-start | bytes 245764
  170.0 8.6 %copy-start.3 = (bf16[320,1,128]{2,1,0:T(2,128)(2,1)S(1)}, bf16[320,1,128]{2,1,0:T(2,128)(2,1)}, u32[]{:S(2)}) copy-start(bf16[320,1,128]{2,1,0:T(2,128)(2,1)} %get-tuple-element.5) | copy-start | bytes 245764
  170.5 20.6 %collective-permute-start.3 = (bf16[128,1536]{1,0:T(8,128)(2,1)S(1)}, bf16[128,1536]{1,0:T(8,128)(2,1)S(1)}, u32[]{:S(2)}, u32[]{:S(2)}) collective-permute-start(bf16[128,1536]{1,0:T(8,128)(2,1)S(1)} %pad_maximum_fusion.4), channel_id=1, source_target_pairs={{0,8},{1,9},{2,10},{3,11},{4,12},{5,13},{6,14},{7,15},{8,0},{9,1},... | collective-permute-start | bytes 1179656 | tf_op jit(solution)/shard_map/ppermute | solution.py:53
  173.8 17.2 %collective-permute-start.2 = (bf16[128,1536]{1,0:T(8,128)(2,1)S(1)}, bf16[128,1536]{1,0:T(8,128)(2,1)S(1)}, u32[]{:S(2)}, u32[]{:S(2)}) collective-permute-start(bf16[128,1536]{1,0:T(8,128)(2,1)S(1)} %pad_maximum_fusion.3), channel_id=1, source_target_pairs={{0,10},{1,11},{2,8},{3,9},{4,14},{5,15},{6,12},{7,13},{8,2},{9,3},... | collective-permute-start | bytes 1179656 | tf_op jit(solution)/shard_map/ppermute | solution.py:53
  (5 other events, 11.5 us)
Sparse Core Ops, SparseCore 0:
  11.9 88.6 all-gather.1

commit v2 on v1

--- a/solution.py
+++ b/solution.py
@@ -36,6 +36,7 @@
 
 
 Y, X_HI = 4, 2
+SHIFTS = ((2, 1), (2, 0), (1, 1), (3, 1), (1, 0), (3, 0), (0, 1))
 
 
 def core_swap(array):
@@ -53,22 +54,40 @@
     return lax.ppermute(array, "fsdp", pairs)
 
 
+def chip_at(chip, dy, dx):
+    return lax.bitwise_and(chip // X_HI + dy, Y - 1) * X_HI + lax.bitwise_xor(chip % X_HI, dx)
+
+
+def gather_weights(shard, chip, core):
+    rows = shard.shape[0]
+    gathered = jnp.zeros((2 * Y * X_HI * rows, shard.shape[1]), shard.dtype)
+    parts = [(chip, shard)]
+    for dy, dx in SHIFTS:
+        parts.append((chip_at(chip, Y - dy, dx), chip_shift(shard, dy, dx)))
+    for origin, part in parts:
+        gathered = lax.dynamic_update_slice(gathered, part, ((origin * 2 + core) * rows, 0))
+    for group in (parts[:4], parts[4:]):
+        swapped = core_swap(jnp.concatenate([part for _, part in group], axis=0))
+        for number, (origin, _) in enumerate(group):
+            gathered = lax.dynamic_update_slice(
+                gathered,
+                swapped[number * rows : (number + 1) * rows],
+                ((origin * 2 + 1 - core) * rows, 0),
+            )
+    return gathered
+
+
 def local(tokens, cotangent, bucket, w_gate, w_up, w_down):
     token_count = tokens.shape[0]
     model_width = tokens.shape[1]
     expert_count = lax.axis_size("ep")
     capacity = max(2, 5 * token_count // (4 * expert_count))
-    slot_rows = expert_count * capacity
     shard_width = w_gate.shape[1]
     hidden_width = w_gate.shape[2]
-    chips = Y * X_HI
     place = lax.axis_index("fsdp")
-    core = place % 2
-    chip = place // 2
+    core = lax.bitwise_and(place, 1)
+    chip = lax.shift_right_logical(place, 1)
 
-    weights = lax.all_gather(
-        jnp.concatenate([w_gate[0], w_up[0], w_down[0]], axis=1), "fsdp", axis=0, tiled=True
-    )
     selector = slot_matrix(bucket, expert_count, capacity)
     joined = jnp.concatenate([tokens, cotangent], axis=1)
     packed = jnp.dot(selector, joined, preferred_element_type=jnp.float32).astype(jnp.bfloat16)
@@ -76,10 +95,9 @@
     rows_x = arrived[:, :model_width]
     rows_dy = arrived[:, model_width:]
 
-    blocks = arrived.reshape(slot_rows, 2 * chips, 2, shard_width)
-    own = jnp.where(core == 0, blocks[:, :, 0], blocks[:, :, 1])
-    other = core_swap(jnp.where(core == 0, blocks[:, :, 1], blocks[:, :, 0]))
-
+    weights = gather_weights(
+        jnp.concatenate([w_gate[0], w_up[0], w_down[0]], axis=1), chip, core
+    )
     w_gate_up = weights[:, : 2 * hidden_width]
     w_out = weights[:, 2 * hidden_width :]
     pre = jnp.dot(rows_x, w_gate_up, preferred_element_type=jnp.float32)
@@ -89,7 +107,6 @@
     activated = gate_pre * sigmoid_gate
     hidden = (activated * up_proj).astype(jnp.bfloat16)
     rows_y = contract_cols(hidden, w_out).astype(jnp.bfloat16)
-    back_y = exchange(rows_y, expert_count)
     grad_hidden = jnp.dot(rows_dy, w_out, preferred_element_type=jnp.float32)
     grad_pre_gate = (
         grad_hidden * up_proj * sigmoid_gate * (1.0 + gate_pre * (1.0 - sigmoid_gate))
@@ -97,32 +114,41 @@
     grad_pre_up = (grad_hidden * activated).astype(jnp.bfloat16)
     grads_pre = jnp.concatenate([grad_pre_gate, grad_pre_up], axis=1)
     rows_dx = contract_cols(grads_pre, w_gate_up).astype(jnp.bfloat16)
-    back_dx = exchange(rows_dx, expert_count)
+    returned = jnp.concatenate([rows_y, rows_dx], axis=1)
+    sides = jnp.concatenate([grads_pre, hidden], axis=1)
+    returned, arrived, sides = lax.optimization_barrier((returned, arrived, sides))
+    back = exchange(returned, expert_count)
 
-    sides = jnp.concatenate([grads_pre, hidden], axis=1)
+    other_rows = core_swap(arrived)
     other_sides = core_swap(sides)
-    pair_rows = jnp.concatenate([own, other], axis=0)
-    pair_sides = jnp.concatenate([sides, other_sides], axis=0)
 
     def terms(target):
-        x_block = lax.dynamic_index_in_dim(pair_rows, target, 1, keepdims=False)
-        dy_block = lax.dynamic_index_in_dim(pair_rows, target + chips, 1, keepdims=False)
-        gate_up = contract_rows(x_block, pair_sides[:, : 2 * hidden_width])
-        down = contract_rows(dy_block, pair_sides[:, 2 * hidden_width :])
+        column = (target * 2 + core) * shard_width
+
+        def block(start):
+            return jnp.concatenate(
+                [
+                    lax.dynamic_slice_in_dim(rows, start, shard_width, axis=1)
+                    for rows in (arrived, other_rows)
+                ],
+                axis=0,
+            )
+
+        both = jnp.concatenate([sides, other_sides], axis=0)
+        gate_up = contract_rows(block(column), both[:, : 2 * hidden_width])
+        down = contract_rows(block(model_width + column), both[:, 2 * hidden_width :])
         return jnp.concatenate([gate_up, down], axis=1).astype(jnp.bfloat16)
 
     total = terms(chip).astype(jnp.float32)
-    y_index, x_index = chip // X_HI, chip % X_HI
-    for dy, dx in ((2, 1), (2, 0), (1, 1), (3, 1), (1, 0), (3, 0), (0, 1)):
-        target = (y_index + dy) % Y * X_HI + (x_index ^ dx)
-        total = total + chip_shift(terms(target), dy, dx).astype(jnp.float32)
+    for dy, dx in SHIFTS:
+        total = total + chip_shift(terms(chip_at(chip, dy, dx)), dy, dx).astype(jnp.float32)
 
     grads = total.astype(jnp.bfloat16)
     grad_wg = grads[None, :, :hidden_width]
     grad_wu = grads[None, :, hidden_width : 2 * hidden_width]
     grad_wd = grads[None, :, 2 * hidden_width :]
-    outputs = contract_rows(selector, back_y).astype(jnp.bfloat16)
-    input_grad = contract_rows(selector, back_dx).astype(jnp.bfloat16)
+    outputs = contract_rows(selector, back[:, :model_width]).astype(jnp.bfloat16)
+    input_grad = contract_rows(selector, back[:, model_width:]).astype(jnp.bfloat16)
     return (outputs, input_grad, grad_wg, grad_wu, grad_wd)
 
 

time: 214 us -> 220 us (1.028)
  starting transfers between devices: 61.4 us -> 88.3 us
  local copies, waits for them, and re-layouts: 8.92 us -> 24.2 us
  between operations: 14.8 us -> 1.49 us
  other arithmetic: 17.6 us -> 4.33 us
  waiting for transfers between devices: 92.3 us -> 79.4 us
  matrix products: 17.5 us -> 19.9 us
    ppermute x7 -> x14, starting transfers between devices: 27.3 us -> 57.7 us  [chip_shift(): return lax.ppermute(array, 'fsdp', pairs)]
    all_to_all x3 -> x2, waiting for transfers between devices: 80.3 us -> 52.9 us  [exchange(): lax.all_to_all(sent, 'ep', split_axis=0, concat_axis=0, tiled=True)]
    ppermute x7 -> x14, waiting for transfers between devices: 12 us -> 26.5 us  [chip_shift(): return lax.ppermute(array, 'fsdp', pairs)]
    dynamic_update_slice x0 -> x15, local copies, waits for them, and re-layouts: none -> 13.7 us  [the longest x7 7.46 us: gather_weights(): lax.dynamic_update_slice(gathered, part, ((origin * 2 + core) * rows, 0))]
    all_to_all x3 -> x2, starting transfers between devices: 29.7 us -> 21.9 us  [exchange(): lax.all_to_all(sent, 'ep', split_axis=0, concat_axis=0, tiled=True)]
    ppermute x2 -> x4, starting transfers between devices: 4.33 us -> 8.66 us  [core_swap(): lax.ppermute(array, 'fsdp', [(f, f ^ 1) for f in range(2 * Y * X_HI)])]
    select_n x1 -> x0, other arithmetic: 3.89 us -> none  [local(): other = core_swap(jnp.where(core == 0, blocks[:, :, 1], blocks[:, :, 0]))]
    concatenate x7, other arithmetic: 3.93 us -> 0.2 us  [terms(): return jnp.concatenate([gate_up, down], axis=1).astype(jnp.bfloat16)]
  transfers between devices with their start and end apart: 13 -> 20, of which waited for: 4 -> 8; matrix products, arithmetic and copies ran while one was open for 17% -> 14% of each run, Pallas kernels for 0% -> 0%
where the time goes in v2:
time: 220 us; the launch traced here: 218 us
  starting transfers between devices  88.3 us (40%)
  waiting for transfers between devices  79.4 us (36%)
  local copies, waits for them, and re-layouts  24.2 us (11%)
  matrix products  19.9 us (9%)
  other arithmetic  4.33 us (2%)
    ppermute x14, starting transfers between devices, chip_shift(): return lax.ppermute(array, 'fsdp', pairs)  57.7 us
    all_to_all x2, waiting for transfers between devices, exchange(): lax.all_to_all(sent, 'ep', split_axis=0, concat_axis=0, tiled=True)  52.9 us
    ppermute x14, waiting for transfers between devices, chip_shift(): return lax.ppermute(array, 'fsdp', pairs)  26.5 us
    all_to_all x2, starting transfers between devices, exchange(): lax.all_to_all(sent, 'ep', split_axis=0, concat_axis=0, tiled=True)  21.9 us
    ppermute x4, starting transfers between devices, core_swap(): lax.ppermute(array, 'fsdp', [(f, f ^ 1) for f in range(2 * Y * X_HI)])  8.66 us
    dynamic_update_slice x7, local copies, waits for them, and re-layouts, gather_weights(): lax.dynamic_update_slice(gathered, part, ((origin * 2 + core) * rows, 0))  7.46 us
    dot_general x18, matrix products, contract_rows(): lax.dot_general(left_rows, right_rows, (((0,), (0,)), ((), ())), preferre...  6.82 us
    dynamic_update_slice x8, local copies, waits for them, and re-layouts, gather_weights(): lax.dynamic_update_slice(gathered, swapped[number * rows:(number + 1) * r...  6.22 us
  transfers between devices with their start and end apart: 20, of which 8 were waited for; matrix products, arithmetic and copies ran while one was open for 14% of the time, Pallas kernels for 0%

profile of v2, /device:TPU:6, one launch (start us, length us, event | category | flops | bytes accessed | tf_op | source)
XLA Modules:
  0.0 217.7 jit_solution(10447515007644921937)
XLA Ops:
  0.7 3.1 %broadcast_in_dim.13 = bf16[2048,1536]{1,0:T(8,128)(2,1)} broadcast(bf16[]{:T(256)} %constant.99.clone.1), dimensions={} | broadcast | bytes 6291458 | tf_op jit(solution)/shard_map/broadcast_in_dim | solution.py:63
  4.7 5.9 %collective-permute-start = (bf16[128,1536]{1,0:T(8,128)(2,1)}, bf16[128,1536]{1,0:T(8,128)(2,1)S(1)}, u32[]{:S(2)}, u32[]{:S(2)}) collective-permute-start(bf16[128,1536]{1,0:T(8,128)(2,1)} %get-tuple-element.49), channel_id=1, source_target_pairs={{0,10},{1,11},{2,8},{3,9},{4,14},{5,15},{6,12},{7,13},{8,2},{9,3},... | collective-permute-start | bytes 1179656 | tf_op jit(solution)/shard_map/ppermute | solution.py:54
  12.9 5.1 %collective-permute-start.2 = (bf16[128,1536]{1,0:T(8,128)(2,1)}, bf16[128,1536]{1,0:T(8,128)(2,1)S(1)}, u32[]{:S(2)}, u32[]{:S(2)}) collective-permute-start(bf16[128,1536]{1,0:T(8,128)(2,1)} %get-tuple-element.49), channel_id=1, source_target_pairs={{0,6},{1,7},{2,4},{3,5},{4,10},{5,11},{6,8},{7,9},{8,14},{9,15},{1... | collective-permute-start | bytes 1179656 | tf_op jit(solution)/shard_map/ppermute | solution.py:54
  17.9 4.4 %collective-permute-start.3 = (bf16[128,1536]{1,0:T(8,128)(2,1)}, bf16[128,1536]{1,0:T(8,128)(2,1)S(1)}, u32[]{:S(2)}, u32[]{:S(2)}) collective-permute-start(bf16[128,1536]{1,0:T(8,128)(2,1)} %get-tuple-element.49), channel_id=1, source_target_pairs={{0,14},{1,15},{2,12},{3,13},{4,2},{5,3},{6,0},{7,1},{8,6},{9,7},{1... | collective-permute-start | bytes 1179656 | tf_op jit(solution)/shard_map/ppermute | solution.py:54
  25.1 4.7 %collective-permute-start.5 = (bf16[128,1536]{1,0:T(8,128)(2,1)}, bf16[128,1536]{1,0:T(8,128)(2,1)}, u32[]{:S(2)}, u32[]{:S(2)}) collective-permute-start(bf16[128,1536]{1,0:T(8,128)(2,1)} %get-tuple-element.49), channel_id=1, source_target_pairs={{0,12},{1,13},{2,14},{3,15},{4,0},{5,1},{6,2},{7,3},{8,4},{9,5},{1... | collective-permute-start | bytes 1179656 | tf_op jit(solution)/shard_map/ppermute | solution.py:54
  29.9 9.2 %collective-permute-done.1 = bf16[128,1536]{1,0:T(8,128)(2,1)S(1)} collective-permute-done((bf16[128,1536]{1,0:T(8,128)(2,1)}, bf16[128,1536]{1,0:T(8,128)(2,1)S(1)}, u32[]{:S(2)}, u32[]{:S(2)}) %collective-permute-start.1) | collective-permute-done | bytes 393248 | tf_op jit(solution)/shard_map/ppermute | solution.py:54
  39.1 2.7 %collective-permute-start.6 = (bf16[128,1536]{1,0:T(8,128)(2,1)}, bf16[128,1536]{1,0:T(8,128)(2,1)}, u32[]{:S(2)}, u32[]{:S(2)}) collective-permute-start(bf16[128,1536]{1,0:T(8,128)(2,1)} %get-tuple-element.49), channel_id=1, source_target_pairs={{0,2},{1,3},{2,0},{3,1},{4,6},{5,7},{6,4},{7,5},{8,10},{9,11},{10,... | collective-permute-start | bytes 1179656 | tf_op jit(solution)/shard_map/ppermute | solution.py:54
  45.0 16.7 %all-to-all-start = ((bf16[32,160,128]{2,1,0:T(8,128)(2,1)}), bf16[32,160,128]{2,1,0:T(8,128)(2,1)S(1)}, u32[]{:S(2)}, u32[]{:S(2)}) async-start(bf16[32,160,128]{2,1,0:T(8,128)(2,1)} %reshape_reshape.12), calls=%async_computation | async-start | bytes 2621440 | tf_op jit(solution)/shard_map/all_to_all | solution.py:34
  66.1 2.4 %collective-permute-start.8 = (bf16[512,1536]{1,0:T(8,128)(2,1)S(1)}, bf16[512,1536]{1,0:T(8,128)(2,1)S(1)}, u32[]{:S(2)}, u32[]{:S(2)}) collective-permute-start(bf16[512,1536]{1,0:T(8,128)(2,1)S(1)} %pad_maximum_fusion.1), channel_id=1, source_target_pairs={{0,1},{1,0},{2,3},{3,2},{4,5},{5,4},{6,7},{7,6},{8,9},{9,8},{10,11... | collective-permute-start | bytes 4718600 | tf_op jit(solution)/shard_map/ppermute | solution.py:43
  82.2 44.2 %all-to-all-done = bf16[32,160,128]{2,1,0:T(8,128)(2,1)S(1)} async-done(((bf16[32,160,128]{2,1,0:T(8,128)(2,1)}), bf16[32,160,128]{2,1,0:T(8,128)(2,1)S(1)}, u32[]{:S(2)}, u32[]{:S(2)}) %all-to-all-start) | async-done | bytes 1310752 | tf_op jit(solution)/shard_map/all_to_all | solution.py:34
  127.0 3.0 %fusion.2 = f32[160,1024]{1,0:T(8,128)S(1)} fusion(bf16[2048,1536]{1,0:T(8,128)(2,1)} %slice_dynamic-update-slice_fusion, bf16[160,4096]{1,0:T(8,128)(2,1)S(1)} %reshape_reshape.13), kind=kOutput, calls=%fused_computation.3 | convolution fusion | flops 671088640 | bytes 5505024 | tf_op jit(solution)/shard_map/dot_general | solution.py:103
  132.2 2.4 %convolution_convert_fusion.1 = bf16[160,2048]{1,0:T(8,128)(2,1)S(1)} fusion(bf16[160,512]{1,0:T(8,128)(2,1)S(1)} %get-tuple-element.45, bf16[2048,1536]{1,0:T(8,128)(2,1)} %slice_dynamic-update-slice_fusion), kind=kOutput, calls=%fused_computation.6 | convolution fusion | flops 335872000 | bytes 2916352 | tf_op jit(solution)/shard_map/dot_general | solution.py:25
  134.7 3.7 %fusion.4 = bf16[160,2048]{1,0:T(8,128)(2,1)S(1)} fusion(bf16[2048,1536]{1,0:T(8,128)(2,1)} %slice_dynamic-update-slice_fusion, bf16[160,512]{1,0:T(8,128)(2,1)S(1)} %get-tuple-element.44, bf16[160,512]{1,0:T(8,128)(2,1)S(1)} %get-tuple-element.43), kind=kOutput, calls=%fused_computation.5 | convolution fusion | flops 672071680 | bytes 5177344 | tf_op jit(solution)/shard_map/dot_general | solution.py:25
  140.4 2.4 %collective-permute-start.10 = (bf16[160,1536]{1,0:T(8,128)(2,1)S(1)}, bf16[160,1536]{1,0:T(8,128)(2,1)}, u32[]{:S(2)}, u32[]{:S(2)}) collective-permute-start(bf16[160,1536]{1,0:T(8,128)(2,1)S(1)} %pad_maximum_fusion.3), channel_id=1, source_target_pairs={{0,1},{1,0},{2,3},{3,2},{4,5},{5,4},{6,7},{7,6},{8,9},{9,8},{10,11... | collective-permute-start | bytes 1474568 | tf_op jit(solution)/shard_map/ppermute | solution.py:43
  144.4 5.2 %all-to-all-start.1 = ((bf16[32,160,128]{2,1,0:T(8,128)(2,1)}), bf16[32,160,128]{2,1,0:T(8,128)(2,1)S(1)}, u32[]{:S(2)}, u32[]{:S(2)}) async-start(bf16[32,160,128]{2,1,0:T(8,128)(2,1)} %reshape_reshape.14), calls=%async_computation.1 | async-start | bytes 2621440 | tf_op jit(solution)/shard_map/all_to_all | solution.py:34
  152.9 6.7 %collective-permute-start.11 = (bf16[128,1536]{1,0:T(8,128)(2,1)S(1)}, bf16[128,1536]{1,0:T(8,128)(2,1)S(1)}, u32[]{:S(2)}, u32[]{:S(2)}) collective-permute-start(bf16[128,1536]{1,0:T(8,128)(2,1)S(1)} %pad_maximum_fusion.5), channel_id=1, source_target_pairs={{0,10},{1,11},{2,8},{3,9},{4,14},{5,15},{6,12},{7,13},{8,2},{9,3},... | collective-permute-start | bytes 1179656 | tf_op jit(solution)/shard_map/ppermute | solution.py:54
  160.2 2.9 %collective-permute-start.12 = (bf16[128,1536]{1,0:T(8,128)(2,1)S(1)}, bf16[128,1536]{1,0:T(8,128)(2,1)S(1)}, u32[]{:S(2)}, u32[]{:S(2)}) collective-permute-start(bf16[128,1536]{1,0:T(8,128)(2,1)S(1)} %pad_maximum_fusion.6), channel_id=1, source_target_pairs={{0,8},{1,9},{2,10},{3,11},{4,12},{5,13},{6,14},{7,15},{8,0},{9,1},... | collective-permute-start | bytes 1179656 | tf_op jit(solution)/shard_map/ppermute | solution.py:54
  163.7 2.9 %collective-permute-start.13 = (bf16[128,1536]{1,0:T(8,128)(2,1)S(1)}, bf16[128,1536]{1,0:T(8,128)(2,1)S(1)}, u32[]{:S(2)}, u32[]{:S(2)}) collective-permute-start(bf16[128,1536]{1,0:T(8,128)(2,1)S(1)} %pad_maximum_fusion.7), channel_id=1, source_target_pairs={{0,6},{1,7},{2,4},{3,5},{4,10},{5,11},{6,8},{7,9},{8,14},{9,15},{1... | collective-permute-start | bytes 1179656 | tf_op jit(solution)/shard_map/ppermute | solution.py:54
  167.2 6.5 %collective-permute-start.14 = (bf16[128,1536]{1,0:T(8,128)(2,1)S(1)}, bf16[128,1536]{1,0:T(8,128)(2,1)S(1)}, u32[]{:S(2)}, u32[]{:S(2)}) collective-permute-start(bf16[128,1536]{1,0:T(8,128)(2,1)S(1)} %pad_maximum_fusion.8), channel_id=1, source_target_pairs={{0,14},{1,15},{2,12},{3,13},{4,2},{5,3},{6,0},{7,1},{8,6},{9,7},{1... | collective-permute-start | bytes 1179656 | tf_op jit(solution)/shard_map/ppermute | solution.py:54
  177.6 5.1 %collective-permute-start.16 = (bf16[128,1536]{1,0:T(8,128)(2,1)S(1)}, bf16[128,1536]{1,0:T(8,128)(2,1)S(1)}, u32[]{:S(2)}, u32[]{:S(2)}) collective-permute-start(bf16[128,1536]{1,0:T(8,128)(2,1)S(1)} %pad_maximum_fusion.10), channel_id=1, source_target_pairs={{0,12},{1,13},{2,14},{3,15},{4,0},{5,1},{6,2},{7,3},{8,4},{9,5},{1... | collective-permute-start | bytes 1179656 | tf_op jit(solution)/shard_map/ppermute | solution.py:54
  182.7 5.1 %collective-permute-done.12 = bf16[128,1536]{1,0:T(8,128)(2,1)S(1)} collective-permute-done((bf16[128,1536]{1,0:T(8,128)(2,1)S(1)}, bf16[128,1536]{1,0:T(8,128)(2,1)S(1)}, u32[]{:S(2)}, u32[]{:S(2)}) %collective-permute-start.12) | collective-permute-done | bytes 393248 | tf_op jit(solution)/shard_map/ppermute | solution.py:54
  187.8 4.3 %collective-permute-start.17 = (bf16[128,1536]{1,0:T(8,128)(2,1)S(1)}, bf16[128,1536]{1,0:T(8,128)(2,1)S(1)}, u32[]{:S(2)}, u32[]{:S(2)}) collective-permute-start(bf16[128,1536]{1,0:T(8,128)(2,1)S(1)} %pad_maximum_fusion.11), channel_id=1, source_target_pairs={{0,2},{1,3},{2,0},{3,1},{4,6},{5,7},{6,4},{7,5},{8,10},{9,11},{10,... | collective-permute-start | bytes 1179656 | tf_op jit(solution)/shard_map/ppermute | solution.py:54
  197.5 7.3 %collective-permute-done.17 = bf16[128,1536]{1,0:T(8,128)(2,1)S(1)} collective-permute-done((bf16[128,1536]{1,0:T(8,128)(2,1)S(1)}, bf16[128,1536]{1,0:T(8,128)(2,1)S(1)}, u32[]{:S(2)}, u32[]{:S(2)}) %collective-permute-start.17) | collective-permute-done | bytes 393248 | tf_op jit(solution)/shard_map/ppermute | solution.py:54
  206.0 8.7 %all-to-all-done.1 = bf16[32,160,128]{2,1,0:T(8,128)(2,1)S(1)} async-done(((bf16[32,160,128]{2,1,0:T(8,128)(2,1)}), bf16[32,160,128]{2,1,0:T(8,128)(2,1)S(1)}, u32[]{:S(2)}, u32[]{:S(2)}) %all-to-all-start.1) | async-done | bytes 1310752 | tf_op jit(solution)/shard_map/all_to_all | solution.py:34
  (89 shorter events, 51.4 us)
Async XLA Ops:
  0.6 3.1 %copy-start = (bf16[1,128,512]{2,1,0:T(8,128)(2,1)S(1)}, bf16[1,128,512]{2,1,0:T(8,128)(2,1)}, u32[]{:S(2)}) copy-start(bf16[1,128,512]{2,1,0:T(8,128)(2,1)} %param.11) | copy-start | bytes 393220
  0.6 3.1 %copy-start.1 = (bf16[1,128,512]{2,1,0:T(8,128)(2,1)S(1)}, bf16[1,128,512]{2,1,0:T(8,128)(2,1)}, u32[]{:S(2)}) copy-start(bf16[1,128,512]{2,1,0:T(8,128)(2,1)} %param.10) | copy-start | bytes 393220
  0.7 3.1 %copy-start.2 = (bf16[1,128,512]{2,1,0:T(8,128)(2,1)S(1)}, bf16[1,128,512]{2,1,0:T(8,128)(2,1)}, u32[]{:S(2)}) copy-start(bf16[1,128,512]{2,1,0:T(8,128)(2,1)} %param.9) | copy-start | bytes 393220
  0.7 24.0 %copy-start.3 = (s32[128,1]{0,1:T(1,128)S(1)}, s32[128,1]{0,1:T(1,128)}, u32[]{:S(2)}) copy-start(s32[128,1]{0,1:T(1,128)} %param.8) | copy-start | bytes 1540
  4.7 20.4 %collective-permute-start = (bf16[128,1536]{1,0:T(8,128)(2,1)}, bf16[128,1536]{1,0:T(8,128)(2,1)S(1)}, u32[]{:S(2)}, u32[]{:S(2)}) collective-permute-start(bf16[128,1536]{1,0:T(8,128)(2,1)} %get-tuple-element.49), channel_id=1, source_target_pairs={{0,10},{1,11},{2,8},{3,9},{4,14},{5,15},{6,12},{7,13},{8,2},{9,3},... | collective-permute-start | bytes 1179656 | tf_op jit(solution)/shard_map/ppermute | solution.py:54
  10.6 28.5 %collective-permute-start.1 = (bf16[128,1536]{1,0:T(8,128)(2,1)}, bf16[128,1536]{1,0:T(8,128)(2,1)S(1)}, u32[]{:S(2)}, u32[]{:S(2)}) collective-permute-start(bf16[128,1536]{1,0:T(8,128)(2,1)} %get-tuple-element.49), channel_id=1, source_target_pairs={{0,8},{1,9},{2,10},{3,11},{4,12},{5,13},{6,14},{7,15},{8,0},{9,1},... | collective-permute-start | bytes 1179656 | tf_op jit(solution)/shard_map/ppermute | solution.py:54
  12.9 49.0 %collective-permute-start.2 = (bf16[128,1536]{1,0:T(8,128)(2,1)}, bf16[128,1536]{1,0:T(8,128)(2,1)S(1)}, u32[]{:S(2)}, u32[]{:S(2)}) collective-permute-start(bf16[128,1536]{1,0:T(8,128)(2,1)} %get-tuple-element.49), channel_id=1, source_target_pairs={{0,6},{1,7},{2,4},{3,5},{4,10},{5,11},{6,8},{7,9},{8,14},{9,15},{1... | collective-permute-start | bytes 1179656 | tf_op jit(solution)/shard_map/ppermute | solution.py:54
  17.9 46.9 %collective-permute-start.3 = (bf16[128,1536]{1,0:T(8,128)(2,1)}, bf16[128,1536]{1,0:T(8,128)(2,1)S(1)}, u32[]{:S(2)}, u32[]{:S(2)}) collective-permute-start(bf16[128,1536]{1,0:T(8,128)(2,1)} %get-tuple-element.49), channel_id=1, source_target_pairs={{0,14},{1,15},{2,12},{3,13},{4,2},{5,3},{6,0},{7,1},{8,6},{9,7},{1... | collective-permute-start | bytes 1179656 | tf_op jit(solution)/shard_map/ppermute | solution.py:54
  22.3 42.5 %collective-permute-start.4 = (bf16[128,1536]{1,0:T(8,128)(2,1)}, bf16[128,1536]{1,0:T(8,128)(2,1)S(1)}, u32[]{:S(2)}, u32[]{:S(2)}) collective-permute-start(bf16[128,1536]{1,0:T(8,128)(2,1)} %get-tuple-element.49), channel_id=1, source_target_pairs={{0,4},{1,5},{2,6},{3,7},{4,8},{5,9},{6,10},{7,11},{8,12},{9,13},{1... | collective-permute-start | bytes 1179656 | tf_op jit(solution)/shard_map/ppermute | solution.py:54
  25.1 39.7 %collective-permute-start.5 = (bf16[128,1536]{1,0:T(8,128)(2,1)}, bf16[128,1536]{1,0:T(8,128)(2,1)}, u32[]{:S(2)}, u32[]{:S(2)}) collective-permute-start(bf16[128,1536]{1,0:T(8,128)(2,1)} %get-tuple-element.49), channel_id=1, source_target_pairs={{0,12},{1,13},{2,14},{3,15},{4,0},{5,1},{6,2},{7,3},{8,4},{9,5},{1... | collective-permute-start | bytes 1179656 | tf_op jit(solution)/shard_map/ppermute | solution.py:54
  39.1 25.8 %collective-permute-start.6 = (bf16[128,1536]{1,0:T(8,128)(2,1)}, bf16[128,1536]{1,0:T(8,128)(2,1)}, u32[]{:S(2)}, u32[]{:S(2)}) collective-permute-start(bf16[128,1536]{1,0:T(8,128)(2,1)} %get-tuple-element.49), channel_id=1, source_target_pairs={{0,2},{1,3},{2,0},{3,1},{4,6},{5,7},{6,4},{7,5},{8,10},{9,11},{10,... | collective-permute-start | bytes 1179656 | tf_op jit(solution)/shard_map/ppermute | solution.py:54
  45.0 81.4 %all-to-all-start = ((bf16[32,160,128]{2,1,0:T(8,128)(2,1)}), bf16[32,160,128]{2,1,0:T(8,128)(2,1)S(1)}, u32[]{:S(2)}, u32[]{:S(2)}) async-start(bf16[32,160,128]{2,1,0:T(8,128)(2,1)} %reshape_reshape.12), calls=%async_computation | async-start | bytes 2621440 | tf_op jit(solution)/shard_map/all_to_all | solution.py:34
  62.9 13.1 %collective-permute-start.7 = (bf16[512,1536]{1,0:T(8,128)(2,1)S(1)}, bf16[512,1536]{1,0:T(8,128)(2,1)S(1)}, u32[]{:S(2)}, u32[]{:S(2)}) collective-permute-start(bf16[512,1536]{1,0:T(8,128)(2,1)S(1)} %pad_maximum_fusion), channel_id=1, source_target_pairs={{0,1},{1,0},{2,3},{3,2},{4,5},{5,4},{6,7},{7,6},{8,9},{9,8},{10,11... | collective-permute-start | bytes 4718600 | tf_op jit(solution)/shard_map/ppermute | solution.py:43
  66.1 13.0 %collective-permute-start.8 = (bf16[512,1536]{1,0:T(8,128)(2,1)S(1)}, bf16[512,1536]{1,0:T(8,128)(2,1)S(1)}, u32[]{:S(2)}, u32[]{:S(2)}) collective-permute-start(bf16[512,1536]{1,0:T(8,128)(2,1)S(1)} %pad_maximum_fusion.1), channel_id=1, source_target_pairs={{0,1},{1,0},{2,3},{3,2},{4,5},{5,4},{6,7},{7,6},{8,9},{9,8},{10,11... | collective-permute-start | bytes 4718600 | tf_op jit(solution)/shard_map/ppermute | solution.py:43
  138.5 12.5 %collective-permute-start.9 = (bf16[160,4096]{1,0:T(8,128)(2,1)S(1)}, bf16[160,4096]{1,0:T(8,128)(2,1)}, u32[]{:S(2)}, u32[]{:S(2)}) collective-permute-start(bf16[160,4096]{1,0:T(8,128)(2,1)S(1)} %reshape_reshape.13), channel_id=1, source_target_pairs={{0,1},{1,0},{2,3},{3,2},{4,5},{5,4},{6,7},{7,6},{8,9},{9,8},{10,11... | collective-permute-start | bytes 3932168 | tf_op jit(solution)/shard_map/ppermute | solution.py:43
  140.4 9.5 %collective-permute-start.10 = (bf16[160,1536]{1,0:T(8,128)(2,1)S(1)}, bf16[160,1536]{1,0:T(8,128)(2,1)}, u32[]{:S(2)}, u32[]{:S(2)}) collective-permute-start(bf16[160,1536]{1,0:T(8,128)(2,1)S(1)} %pad_maximum_fusion.3), channel_id=1, source_target_pairs={{0,1},{1,0},{2,3},{3,2},{4,5},{5,4},{6,7},{7,6},{8,9},{9,8},{10,11... | collective-permute-start | bytes 1474568 | tf_op jit(solution)/shard_map/ppermute | solution.py:43
  144.4 70.3 %all-to-all-start.1 = ((bf16[32,160,128]{2,1,0:T(8,128)(2,1)}), bf16[32,160,128]{2,1,0:T(8,128)(2,1)S(1)}, u32[]{:S(2)}, u32[]{:S(2)}) async-start(bf16[32,160,128]{2,1,0:T(8,128)(2,1)} %reshape_reshape.14), calls=%async_computation.1 | async-start | bytes 2621440 | tf_op jit(solution)/shard_map/all_to_all | solution.py:34
  152.9 24.7 %collective-permute-start.11 = (bf16[128,1536]{1,0:T(8,128)(2,1)S(1)}, bf16[128,1536]{1,0:T(8,128)(2,1)S(1)}, u32[]{:S(2)}, u32[]{:S(2)}) collective-permute-start(bf16[128,1536]{1,0:T(8,128)(2,1)S(1)} %pad_maximum_fusion.5), channel_id=1, source_target_pairs={{0,10},{1,11},{2,8},{3,9},{4,14},{5,15},{6,12},{7,13},{8,2},{9,3},... | collective-permute-start | bytes 1179656 | tf_op jit(solution)/shard_map/ppermute | solution.py:54
  160.2 27.6 %collective-permute-start.12 = (bf16[128,1536]{1,0:T(8,128)(2,1)S(1)}, bf16[128,1536]{1,0:T(8,128)(2,1)S(1)}, u32[]{:S(2)}, u32[]{:S(2)}) collective-permute-start(bf16[128,1536]{1,0:T(8,128)(2,1)S(1)} %pad_maximum_fusion.6), channel_id=1, source_target_pairs={{0,8},{1,9},{2,10},{3,11},{4,12},{5,13},{6,14},{7,15},{8,0},{9,1},... | collective-permute-start | bytes 1179656 | tf_op jit(solution)/shard_map/ppermute | solution.py:54
  163.7 29.0 %collective-permute-start.13 = (bf16[128,1536]{1,0:T(8,128)(2,1)S(1)}, bf16[128,1536]{1,0:T(8,128)(2,1)S(1)}, u32[]{:S(2)}, u32[]{:S(2)}) collective-permute-start(bf16[128,1536]{1,0:T(8,128)(2,1)S(1)} %pad_maximum_fusion.7), channel_id=1, source_target_pairs={{0,6},{1,7},{2,4},{3,5},{4,10},{5,11},{6,8},{7,9},{8,14},{9,15},{1... | collective-permute-start | bytes 1179656 | tf_op jit(solution)/shard_map/ppermute | solution.py:54
  167.2 26.3 %collective-permute-start.14 = (bf16[128,1536]{1,0:T(8,128)(2,1)S(1)}, bf16[128,1536]{1,0:T(8,128)(2,1)S(1)}, u32[]{:S(2)}, u32[]{:S(2)}) collective-permute-start(bf16[128,1536]{1,0:T(8,128)(2,1)S(1)} %pad_maximum_fusion.8), channel_id=1, source_target_pairs={{0,14},{1,15},{2,12},{3,13},{4,2},{5,3},{6,0},{7,1},{8,6},{9,7},{1... | collective-permute-start | bytes 1179656 | tf_op jit(solution)/shard_map/ppermute | solution.py:54
  174.4 21.5 %collective-permute-start.15 = (bf16[128,1536]{1,0:T(8,128)(2,1)S(1)}, bf16[128,1536]{1,0:T(8,128)(2,1)S(1)}, u32[]{:S(2)}, u32[]{:S(2)}) collective-permute-start(bf16[128,1536]{1,0:T(8,128)(2,1)S(1)} %pad_maximum_fusion.9), channel_id=1, source_target_pairs={{0,4},{1,5},{2,6},{3,7},{4,8},{5,9},{6,10},{7,11},{8,12},{9,13},{1... | collective-permute-start | bytes 1179656 | tf_op jit(solution)/shard_map/ppermute | solution.py:54
  177.6 19.9 %collective-permute-start.16 = (bf16[128,1536]{1,0:T(8,128)(2,1)S(1)}, bf16[128,1536]{1,0:T(8,128)(2,1)S(1)}, u32[]{:S(2)}, u32[]{:S(2)}) collective-permute-start(bf16[128,1536]{1,0:T(8,128)(2,1)S(1)} %pad_maximum_fusion.10), channel_id=1, source_target_pairs={{0,12},{1,13},{2,14},{3,15},{4,0},{5,1},{6,2},{7,3},{8,4},{9,5},{1... | collective-permute-start | bytes 1179656 | tf_op jit(solution)/shard_map/ppermute | solution.py:54
  187.8 17.1 %collective-permute-start.17 = (bf16[128,1536]{1,0:T(8,128)(2,1)S(1)}, bf16[128,1536]{1,0:T(8,128)(2,1)S(1)}, u32[]{:S(2)}, u32[]{:S(2)}) collective-permute-start(bf16[128,1536]{1,0:T(8,128)(2,1)S(1)} %pad_maximum_fusion.11), channel_id=1, source_target_pairs={{0,2},{1,3},{2,0},{3,1},{4,6},{5,7},{6,4},{7,5},{8,10},{9,11},{10,... | collective-permute-start | bytes 1179656 | tf_op jit(solution)/shard_map/ppermute | solution.py:54

commit v3 on v2

--- a/solution.py
+++ b/solution.py
@@ -1,6 +1,8 @@
 import jax
 import jax.numpy as jnp
 from jax import lax
+from jax.experimental import pallas as pl
+from jax.experimental.pallas import tpu as pltpu
 from jax.sharding import PartitionSpec as P
 
 
@@ -59,22 +61,122 @@
 
 
 def gather_weights(shard, chip, core):
-    rows = shard.shape[0]
-    gathered = jnp.zeros((2 * Y * X_HI * rows, shard.shape[1]), shard.dtype)
-    parts = [(chip, shard)]
-    for dy, dx in SHIFTS:
-        parts.append((chip_at(chip, Y - dy, dx), chip_shift(shard, dy, dx)))
-    for origin, part in parts:
-        gathered = lax.dynamic_update_slice(gathered, part, ((origin * 2 + core) * rows, 0))
-    for group in (parts[:4], parts[4:]):
-        swapped = core_swap(jnp.concatenate([part for _, part in group], axis=0))
-        for number, (origin, _) in enumerate(group):
-            gathered = lax.dynamic_update_slice(
-                gathered,
-                swapped[number * rows : (number + 1) * rows],
-                ((origin * 2 + 1 - core) * rows, 0),
+    origins = [chip] + [chip_at(chip, Y - dy, dx) for dy, dx in SHIFTS]
+    parts = [shard] + [chip_shift(shard, dy, dx) for dy, dx in SHIFTS]
+    groups, numbers = [], []
+    for first in (4, 0):
+        held = jnp.concatenate(parts[first : first + 4], axis=0)
+        for array, side in ((held, core), (core_swap(held), 1 - core)):
+            groups.append(array)
+            numbers += [origin * 2 + side for origin in origins[first : first + 4]]
+    return groups, jnp.stack(numbers).astype(jnp.int32)
+
+
+def expert_kernel(numbers, rows, *refs):
+    groups, (back, sides, pre, grad_hidden) = refs[:4], refs[4:]
+    block = groups[0].shape[0] // 4
+    width = rows.shape[1] // 2
+    hidden_width = sides.shape[1] // 3
+
+    def columns(number):
+        return pl.ds(pl.multiple_of(numbers[number] * block, block), block)
+
+    def dy_columns(number):
+        return pl.ds(pl.multiple_of(width + numbers[number] * block, block), block)
+
+    for group in range(4):
+        for half in range(2):
+            first = group * 4 + half * 2
+            weights = groups[group].at[pl.ds(half * 2 * block, 2 * block)]
+            x = jnp.concatenate([rows[:, columns(first)], rows[:, columns(first + 1)]], axis=1)
+            dy = jnp.concatenate(
+                [rows[:, dy_columns(first)], rows[:, dy_columns(first + 1)]], axis=1
             )
-    return gathered
+            x_part = jnp.dot(
+                x, weights[:, : 2 * hidden_width], preferred_element_type=jnp.float32
+            )
+            dy_part = jnp.dot(
+                dy, weights[:, 2 * hidden_width :], preferred_element_type=jnp.float32
+            )
+            if first == 0:
+                pre[...] = x_part
+                grad_hidden[...] = dy_part
+            else:
+                pre[...] += x_part
+                grad_hidden[...] += dy_part
+
+    gate_pre = pre[:, :hidden_width]
+    up_proj = pre[:, hidden_width:]
+    upstream = grad_hidden[...]
+    sigmoid_gate = jax.nn.sigmoid(gate_pre)
+    activated = gate_pre * sigmoid_gate
+    sides[:, :hidden_width] = (
+        upstream * up_proj * sigmoid_gate * (1.0 + gate_pre * (1.0 - sigmoid_gate))
+    ).astype(sides.dtype)
+    sides[:, hidden_width : 2 * hidden_width] = (upstream * activated).astype(sides.dtype)
+    sides[:, 2 * hidden_width :] = (activated * up_proj).astype(sides.dtype)
+
+    hidden = sides[:, 2 * hidden_width :]
+    grads_pre = sides[:, : 2 * hidden_width]
+    for group in range(4):
+        for half in range(2):
+            first = group * 4 + half * 2
+            weights = groups[group].at[pl.ds(half * 2 * block, 2 * block)]
+            y = contract_cols(hidden, weights[:, 2 * hidden_width :]).astype(back.dtype)
+            dx = contract_cols(grads_pre, weights[:, : 2 * hidden_width]).astype(back.dtype)
+            for number in range(2):
+                part = slice(number * block, (number + 1) * block)
+                back[:, columns(first + number)] = y[:, part]
+                back[:, dy_columns(first + number)] = dx[:, part]
+
+
+def expert_rows(rows, groups, numbers, hidden_width):
+    row_count, width = rows.shape
+    vmem = pl.BlockSpec(memory_space=pltpu.VMEM)
+    return pl.pallas_call(
+        expert_kernel,
+        out_shape=(
+            jax.ShapeDtypeStruct((row_count, width), rows.dtype),
+            jax.ShapeDtypeStruct((row_count, 3 * hidden_width), rows.dtype),
+        ),
+        in_specs=[pl.BlockSpec(memory_space=pltpu.SMEM)] + [vmem] * 5,
+        out_specs=(vmem, vmem),
+        scratch_shapes=[
+            pltpu.VMEM((row_count, 2 * hidden_width), jnp.float32),
+            pltpu.VMEM((row_count, hidden_width), jnp.float32),
+        ],
+        compiler_params=pltpu.CompilerParams(vmem_limit_bytes=32 * 1024 * 1024),
+    )(numbers, rows, *groups)
+
+
+def terms_kernel(numbers, own, other, own_sides, other_sides, *terms):
+    block = terms[0].shape[0]
+    width = own.shape[1] // 2
+    hidden_width = own_sides.shape[1] // 3
+    for number, term in enumerate(terms):
+        start = numbers[number] * block
+
+        def rows(first):
+            columns = pl.ds(pl.multiple_of(first + start, block), block)
+            return own[:, columns], other[:, columns]
+
+        for first, sides in ((0, slice(0, 2 * hidden_width)), (width, slice(2 * hidden_width, None))):
+            own_rows, other_rows = rows(first)
+            total = contract_rows(own_rows, own_sides[:, sides])
+            total += contract_rows(other_rows, other_sides[:, sides])
+            term[:, sides] = total.astype(term.dtype)
+
+
+def gradient_terms(numbers, own, other, own_sides, other_sides, block):
+    vmem = pl.BlockSpec(memory_space=pltpu.VMEM)
+    count = numbers.shape[0]
+    return pl.pallas_call(
+        terms_kernel,
+        out_shape=[jax.ShapeDtypeStruct((block, own_sides.shape[1]), own.dtype)] * count,
+        in_specs=[pl.BlockSpec(memory_space=pltpu.SMEM)] + [vmem] * 4,
+        out_specs=[vmem] * count,
+        compiler_params=pltpu.CompilerParams(vmem_limit_bytes=32 * 1024 * 1024),
+    )(numbers, own, other, own_sides, other_sides)
 
 
 def local(tokens, cotangent, bucket, w_gate, w_up, w_down):
@@ -91,57 +193,23 @@
     selector = slot_matrix(bucket, expert_count, capacity)
     joined = jnp.concatenate([tokens, cotangent], axis=1)
     packed = jnp.dot(selector, joined, preferred_element_type=jnp.float32).astype(jnp.bfloat16)
+    shard = jnp.concatenate([w_gate[0], w_up[0], w_down[0]], axis=1)
+    packed, shard = lax.optimization_barrier((packed, shard))
     arrived = exchange(packed, expert_count)
-    rows_x = arrived[:, :model_width]
-    rows_dy = arrived[:, model_width:]
-
-    weights = gather_weights(
-        jnp.concatenate([w_gate[0], w_up[0], w_down[0]], axis=1), chip, core
-    )
-    w_gate_up = weights[:, : 2 * hidden_width]
-    w_out = weights[:, 2 * hidden_width :]
-    pre = jnp.dot(rows_x, w_gate_up, preferred_element_type=jnp.float32)
-    gate_pre = pre[:, :hidden_width]
-    up_proj = pre[:, hidden_width:]
-    sigmoid_gate = jax.nn.sigmoid(gate_pre)
-    activated = gate_pre * sigmoid_gate
-    hidden = (activated * up_proj).astype(jnp.bfloat16)
-    rows_y = contract_cols(hidden, w_out).astype(jnp.bfloat16)
-    grad_hidden = jnp.dot(rows_dy, w_out, preferred_element_type=jnp.float32)
-    grad_pre_gate = (
-        grad_hidden * up_proj * sigmoid_gate * (1.0 + gate_pre * (1.0 - sigmoid_gate))
-    ).astype(jnp.bfloat16)
-    grad_pre_up = (grad_hidden * activated).astype(jnp.bfloat16)
-    grads_pre = jnp.concatenate([grad_pre_gate, grad_pre_up], axis=1)
-    rows_dx = contract_cols(grads_pre, w_gate_up).astype(jnp.bfloat16)
-    returned = jnp.concatenate([rows_y, rows_dx], axis=1)
-    sides = jnp.concatenate([grads_pre, hidden], axis=1)
+    groups, numbers = gather_weights(shard, chip, core)
+    returned, sides = expert_rows(arrived, groups, numbers, hidden_width)
     returned, arrived, sides = lax.optimization_barrier((returned, arrived, sides))
     back = exchange(returned, expert_count)
 
     other_rows = core_swap(arrived)
     other_sides = core_swap(sides)
 
-    def terms(target):
-        column = (target * 2 + core) * shard_width
-
-        def block(start):
-            return jnp.concatenate(
-                [
-                    lax.dynamic_slice_in_dim(rows, start, shard_width, axis=1)
-                    for rows in (arrived, other_rows)
-                ],
-                axis=0,
-            )
-
-        both = jnp.concatenate([sides, other_sides], axis=0)
-        gate_up = contract_rows(block(column), both[:, : 2 * hidden_width])
-        down = contract_rows(block(model_width + column), both[:, 2 * hidden_width :])
-        return jnp.concatenate([gate_up, down], axis=1).astype(jnp.bfloat16)
-
-    total = terms(chip).astype(jnp.float32)
-    for dy, dx in SHIFTS:
-        total = total + chip_shift(terms(chip_at(chip, dy, dx)), dy, dx).astype(jnp.float32)
+    targets = [chip] + [chip_at(chip, dy, dx) for dy, dx in SHIFTS]
+    columns = jnp.stack([target * 2 + core for target in targets]).astype(jnp.int32)
+    terms = gradient_terms(columns, arrived, other_rows, sides, other_sides, shard_width)
+    total = terms[0].astype(jnp.float32)
+    for (dy, dx), term in zip(SHIFTS, terms[1:]):
+        total = total + chip_shift(term, dy, dx).astype(jnp.float32)
 
     grads = total.astype(jnp.bfloat16)
     grad_wg = grads[None, :, :hidden_width]

time: 220 us -> 182 us (0.83)
  matrix products: 19.9 us -> 3.98 us
  waiting for transfers between devices: 79.4 us -> 64.2 us
  local copies, waits for them, and re-layouts: 24.2 us -> 14.7 us
  Pallas kernels: 0 us -> 8.81 us
  starting transfers between devices: 88.3 us -> 84.4 us
    all_to_all x2, waiting for transfers between devices: 52.9 us -> 9.04 us  [exchange(): lax.all_to_all(sent, 'ep', split_axis=0, concat_axis=0, tiled=True)]
    ppermute x14, waiting for transfers between devices: 26.5 us -> 53.7 us  [chip_shift(): return lax.ppermute(array, 'fsdp', pairs)]
    dynamic_update_slice x15 -> x0, local copies, waits for them, and re-layouts: 13.7 us -> none  [the longest x7 7.46 us: gather_weights(): lax.dynamic_update_slice(gathered, part, ((origin * 2 + core) * rows, 0))]
    dot_general x4 -> x0, matrix products: 11.4 us -> none  [the longest x2 6.18 us: contract_cols(): lax.dot_general(left_rows, right_rows, (((1,), (1,)), ((), ())), preferre...]
    pallas_call x0 -> x2, Pallas kernels: none -> 8.81 us  [the longest x1 5.91 us: expert_rows(): pl.pallas_call(expert_kernel, out_shape=(jax.ShapeDtypeStruct((row_count,...]
    ppermute x14, starting transfers between devices: 57.7 us -> 50.1 us  [chip_shift(): return lax.ppermute(array, 'fsdp', pairs)]
    dot_general x18 -> x2, matrix products: 6.82 us -> 2.29 us  [contract_rows(): lax.dot_general(left_rows, right_rows, (((0,), (0,)), ((), ())), preferre...]
    all_to_all x2, starting transfers between devices: 21.9 us -> 26.1 us  [exchange(): lax.all_to_all(sent, 'ep', split_axis=0, concat_axis=0, tiled=True)]
  transfers between devices with their start and end apart: 20 -> 20, of which waited for: 8 -> 11; matrix products, arithmetic and copies ran while one was open for 14% -> 4% of each run, Pallas kernels for 0% -> 2%
where the time goes in v3:
time: 182 us; the launch traced here: 181 us
  starting transfers between devices  84.4 us (46%)
  waiting for transfers between devices  64.2 us (35%)
  local copies, waits for them, and re-layouts  14.7 us (8%)
  Pallas kernels  8.81 us (5%)
  matrix products  3.98 us (2%)
  other arithmetic  3.86 us (2%)
    ppermute x14, waiting for transfers between devices, chip_shift(): return lax.ppermute(array, 'fsdp', pairs)  53.7 us
    ppermute x14, starting transfers between devices, chip_shift(): return lax.ppermute(array, 'fsdp', pairs)  50.1 us
    all_to_all x2, starting transfers between devices, exchange(): lax.all_to_all(sent, 'ep', split_axis=0, concat_axis=0, tiled=True)  26.1 us
    all_to_all x2, waiting for transfers between devices, exchange(): lax.all_to_all(sent, 'ep', split_axis=0, concat_axis=0, tiled=True)  9.04 us
    ppermute x4, starting transfers between devices, core_swap(): lax.ppermute(array, 'fsdp', [(f, f ^ 1) for f in range(2 * Y * X_HI)])  8.16 us
    pallas_call x1, Pallas kernels, expert_rows(): pl.pallas_call(expert_kernel, out_shape=(jax.ShapeDtypeStruct((row_count,...  5.91 us
    another operation x2, local copies, waits for them, and re-layouts, exchange(): rows.reshape(row_count, width // 128, 128).reshape(expert_count, chunk, 128)  4.76 us
    another operation x2, local copies, waits for them, and re-layouts, exchange(): arrived.reshape(row_count, width // 128, 128).reshape(row_count, width)  4.71 us
  transfers between devices with their start and end apart: 20, of which 11 were waited for; matrix products, arithmetic and copies ran while one was open for 4% of the time, Pallas kernels for 2%

profile of v3, /device:TPU:6, one launch (start us, length us, event | category | flops | bytes accessed | tf_op | source)
XLA Modules:
  0.0 180.9 jit_solution(8702754478038038826)
XLA Ops:
  7.3 16.8 %all-to-all-start = ((bf16[32,160,128]{2,1,0:T(8,128)(2,1)}), bf16[32,160,128]{2,1,0:T(8,128)(2,1)}, u32[]{:S(2)}, u32[]{:S(2)}) async-start(bf16[32,160,128]{2,1,0:T(8,128)(2,1)} %reshape_reshape.12), calls=%async_computation | async-start | bytes 2621440 | tf_op jit(solution)/shard_map/all_to_all | solution.py:36
  24.0 5.9 %collective-permute-start.5 = (bf16[128,1536]{1,0:T(8,128)(2,1)S(1)}, bf16[128,1536]{1,0:T(8,128)(2,1)S(1)}, u32[]{:S(2)}, u32[]{:S(2)}) collective-permute-start(bf16[128,1536]{1,0:T(8,128)(2,1)S(1)} %pad_maximum_fusion), channel_id=1, source_target_pairs={{0,10},{1,11},{2,8},{3,9},{4,14},{5,15},{6,12},{7,13},{8,2},{9,3},... | collective-permute-start | bytes 1179656 | tf_op jit(solution)/shard_map/ppermute | solution.py:56
  30.0 4.1 %collective-permute-start.7 = (bf16[128,1536]{1,0:T(8,128)(2,1)S(1)}, bf16[128,1536]{1,0:T(8,128)(2,1)S(1)}, u32[]{:S(2)}, u32[]{:S(2)}) collective-permute-start(bf16[128,1536]{1,0:T(8,128)(2,1)S(1)} %pad_maximum_fusion), channel_id=1, source_target_pairs={{0,6},{1,7},{2,4},{3,5},{4,10},{5,11},{6,8},{7,9},{8,14},{9,15},{1... | collective-permute-start | bytes 1179656 | tf_op jit(solution)/shard_map/ppermute | solution.py:56
  34.2 3.7 %collective-permute-start.6 = (bf16[128,1536]{1,0:T(8,128)(2,1)S(1)}, bf16[128,1536]{1,0:T(8,128)(2,1)S(1)}, u32[]{:S(2)}, u32[]{:S(2)}) collective-permute-start(bf16[128,1536]{1,0:T(8,128)(2,1)S(1)} %pad_maximum_fusion), channel_id=1, source_target_pairs={{0,8},{1,9},{2,10},{3,11},{4,12},{5,13},{6,14},{7,15},{8,0},{9,1},... | collective-permute-start | bytes 1179656 | tf_op jit(solution)/shard_map/ppermute | solution.py:56
  37.9 3.3 %collective-permute-start.3 = (bf16[128,1536]{1,0:T(8,128)(2,1)S(1)}, bf16[128,1536]{1,0:T(8,128)(2,1)S(1)}, u32[]{:S(2)}, u32[]{:S(2)}) collective-permute-start(bf16[128,1536]{1,0:T(8,128)(2,1)S(1)} %pad_maximum_fusion), channel_id=1, source_target_pairs={{0,2},{1,3},{2,0},{3,1},{4,6},{5,7},{6,4},{7,5},{8,10},{9,11},{10,... | collective-permute-start | bytes 1179656 | tf_op jit(solution)/shard_map/ppermute | solution.py:56
  41.2 2.6 %collective-permute-start.2 = (bf16[128,1536]{1,0:T(8,128)(2,1)S(1)}, bf16[128,1536]{1,0:T(8,128)(2,1)S(1)}, u32[]{:S(2)}, u32[]{:S(2)}) collective-permute-start(bf16[128,1536]{1,0:T(8,128)(2,1)S(1)} %pad_maximum_fusion), channel_id=1, source_target_pairs={{0,12},{1,13},{2,14},{3,15},{4,0},{5,1},{6,2},{7,3},{8,4},{9,5},{1... | collective-permute-start | bytes 1179656 | tf_op jit(solution)/shard_map/ppermute | solution.py:56
  45.6 3.6 %collective-permute-start.1 = (bf16[128,1536]{1,0:T(8,128)(2,1)S(1)}, bf16[128,1536]{1,0:T(8,128)(2,1)S(1)}, u32[]{:S(2)}, u32[]{:S(2)}) collective-permute-start(bf16[128,1536]{1,0:T(8,128)(2,1)S(1)} %pad_maximum_fusion), channel_id=1, source_target_pairs={{0,4},{1,5},{2,6},{3,7},{4,8},{5,9},{6,10},{7,11},{8,12},{9,13},{1... | collective-permute-start | bytes 1179656 | tf_op jit(solution)/shard_map/ppermute | solution.py:56
  49.2 10.8 %collective-permute-done.6 = bf16[128,1536]{1,0:T(8,128)(2,1)S(1)} collective-permute-done((bf16[128,1536]{1,0:T(8,128)(2,1)S(1)}, bf16[128,1536]{1,0:T(8,128)(2,1)S(1)}, u32[]{:S(2)}, u32[]{:S(2)}) %collective-permute-start.6) | collective-permute-done | bytes 393248 | tf_op jit(solution)/shard_map/ppermute | solution.py:56
  64.0 14.1 %collective-permute-done = bf16[128,1536]{1,0:T(8,128)(2,1)S(1)} collective-permute-done((bf16[128,1536]{1,0:T(8,128)(2,1)S(1)}, bf16[128,1536]{1,0:T(8,128)(2,1)S(1)}, u32[]{:S(2)}, u32[]{:S(2)}) %collective-permute-start) | collective-permute-done | bytes 393248 | tf_op jit(solution)/shard_map/ppermute | solution.py:56
  83.4 5.5 %all-to-all-done = bf16[32,160,128]{2,1,0:T(8,128)(2,1)} async-done(((bf16[32,160,128]{2,1,0:T(8,128)(2,1)}), bf16[32,160,128]{2,1,0:T(8,128)(2,1)}, u32[]{:S(2)}, u32[]{:S(2)}) %all-to-all-start) | async-done | bytes 1310752 | tf_op jit(solution)/shard_map/all_to_all | solution.py:36
  91.3 5.9 %shard_map.101 = (bf16[160,4096]{1,0:T(8,128)(2,1)S(1)}, bf16[160,1536]{1,0:T(8,128)(2,1)S(1)}) custom-call(s32[16]{0:T(128)S(1)} %stack.80.numbers, bf16[160,4096]{1,0:T(8,128)(2,1)S(1)} %reshape_reshape.13.rows.own, bf16[512,1536]{1,0:T(8,128)(2,1)} %constant_dynamic-update-slice_fusion.refs_0_, bf16[512,1536]{1,0:T(8,128)(2,1)} %collective-permute-done.4.refs_1_, ...), custom_call_target="tpu_custom_call" | custom-call | tf_op jit(solution)/shard_map/pallas_call | solution.py:136
  98.3 3.3 %reshape_reshape.14 = bf16[32,160,128]{2,1,0:T(8,128)(2,1)} reshape(bf16[160,4096]{1,0:T(8,128)(2,1)} %copy-done) | data formatting | bytes 2621440 | tf_op jit(solution)/shard_map/reshape;reshape | solution.py:35
  101.6 9.4 %all-to-all-start.1 = ((bf16[32,160,128]{2,1,0:T(8,128)(2,1)}), bf16[32,160,128]{2,1,0:T(8,128)(2,1)}, u32[]{:S(2)}, u32[]{:S(2)}) async-start(bf16[32,160,128]{2,1,0:T(8,128)(2,1)} %reshape_reshape.14), calls=%async_computation.1 | async-start | bytes 2621440 | tf_op jit(solution)/shard_map/all_to_all | solution.py:36
  116.9 2.9 %shard_map.102 = (bf16[128,1536]{1,0:T(8,128)(2,1)S(1)}, bf16[128,1536]{1,0:T(8,128)(2,1)S(1)}, bf16[128,1536]{1,0:T(8,128)(2,1)S(1)}, bf16[128,1536]{1,0:T(8,12...) custom-call(s32[8]{0:T(128)S(1)} %stack.82.numbers, ...), custom_call_target="tpu_custom_call" | custom-call | tf_op jit(solution)/shard_map/pallas_call | solution.py:173
  119.8 3.6 %collective-permute-start.11 = (bf16[128,1536]{1,0:T(8,128)(2,1)S(1)}, bf16[128,1536]{1,0:T(8,128)(2,1)S(1)}, u32[]{:S(2)}, u32[]{:S(2)}) collective-permute-start(bf16[128,1536]{1,0:T(8,128)(2,1)S(1)} %get-tuple-element.28), channel_id=1, source_target_pairs={{0,10},{1,11},{2,8},{3,9},{4,14},{5,15},{6,12},{7,13},{8,2},{9,3},... | collective-permute-start | bytes 1179656 | tf_op jit(solution)/shard_map/ppermute | solution.py:56
  123.4 4.5 %collective-permute-start.12 = (bf16[128,1536]{1,0:T(8,128)(2,1)S(1)}, bf16[128,1536]{1,0:T(8,128)(2,1)S(1)}, u32[]{:S(2)}, u32[]{:S(2)}) collective-permute-start(bf16[128,1536]{1,0:T(8,128)(2,1)S(1)} %get-tuple-element.29), channel_id=1, source_target_pairs={{0,8},{1,9},{2,10},{3,11},{4,12},{5,13},{6,14},{7,15},{8,0},{9,1},... | collective-permute-start | bytes 1179656 | tf_op jit(solution)/shard_map/ppermute | solution.py:56
  129.9 7.5 %collective-permute-start.14 = (bf16[128,1536]{1,0:T(8,128)(2,1)S(1)}, bf16[128,1536]{1,0:T(8,128)(2,1)S(1)}, u32[]{:S(2)}, u32[]{:S(2)}) collective-permute-start(bf16[128,1536]{1,0:T(8,128)(2,1)S(1)} %get-tuple-element.31), channel_id=1, source_target_pairs={{0,14},{1,15},{2,12},{3,13},{4,2},{5,3},{6,0},{7,1},{8,6},{9,7},{1... | collective-permute-start | bytes 1179656 | tf_op jit(solution)/shard_map/ppermute | solution.py:56
  139.3 2.7 %collective-permute-done.11 = bf16[128,1536]{1,0:T(8,128)(2,1)S(1)} collective-permute-done((bf16[128,1536]{1,0:T(8,128)(2,1)S(1)}, bf16[128,1536]{1,0:T(8,128)(2,1)S(1)}, u32[]{:S(2)}, u32[]{:S(2)}) %collective-permute-start.11) | collective-permute-done | bytes 393248 | tf_op jit(solution)/shard_map/ppermute | solution.py:56
  142.0 2.4 %collective-permute-start.16 = (bf16[128,1536]{1,0:T(8,128)(2,1)S(1)}, bf16[128,1536]{1,0:T(8,128)(2,1)S(1)}, u32[]{:S(2)}, u32[]{:S(2)}) collective-permute-start(bf16[128,1536]{1,0:T(8,128)(2,1)S(1)} %get-tuple-element.33), channel_id=1, source_target_pairs={{0,12},{1,13},{2,14},{3,15},{4,0},{5,1},{6,2},{7,3},{8,4},{9,5},{1... | collective-permute-start | bytes 1179656 | tf_op jit(solution)/shard_map/ppermute | solution.py:56
  144.5 10.9 %collective-permute-done.12 = bf16[128,1536]{1,0:T(8,128)(2,1)S(1)} collective-permute-done((bf16[128,1536]{1,0:T(8,128)(2,1)S(1)}, bf16[128,1536]{1,0:T(8,128)(2,1)S(1)}, u32[]{:S(2)}, u32[]{:S(2)}) %collective-permute-start.12) | collective-permute-done | bytes 393248 | tf_op jit(solution)/shard_map/ppermute | solution.py:56
  155.4 2.8 %collective-permute-start.17 = (bf16[128,1536]{1,0:T(8,128)(2,1)S(1)}, bf16[128,1536]{1,0:T(8,128)(2,1)S(1)}, u32[]{:S(2)}, u32[]{:S(2)}) collective-permute-start(bf16[128,1536]{1,0:T(8,128)(2,1)S(1)} %get-tuple-element.34), channel_id=1, source_target_pairs={{0,2},{1,3},{2,0},{3,1},{4,6},{5,7},{6,4},{7,5},{8,10},{9,11},{10,... | collective-permute-start | bytes 1179656 | tf_op jit(solution)/shard_map/ppermute | solution.py:56
  158.8 4.0 %collective-permute-done.15 = bf16[128,1536]{1,0:T(8,128)(2,1)S(1)} collective-permute-done((bf16[128,1536]{1,0:T(8,128)(2,1)S(1)}, bf16[128,1536]{1,0:T(8,128)(2,1)S(1)}, u32[]{:S(2)}, u32[]{:S(2)}) %collective-permute-start.15) | collective-permute-done | bytes 393248 | tf_op jit(solution)/shard_map/ppermute | solution.py:56
  162.8 8.9 %collective-permute-done.17 = bf16[128,1536]{1,0:T(8,128)(2,1)S(1)} collective-permute-done((bf16[128,1536]{1,0:T(8,128)(2,1)S(1)}, bf16[128,1536]{1,0:T(8,128)(2,1)S(1)}, u32[]{:S(2)}, u32[]{:S(2)}) %collective-permute-start.17) | collective-permute-done | bytes 393248 | tf_op jit(solution)/shard_map/ppermute | solution.py:56
  172.8 3.5 %all-to-all-done.1 = bf16[32,160,128]{2,1,0:T(8,128)(2,1)} async-done(((bf16[32,160,128]{2,1,0:T(8,128)(2,1)}), bf16[32,160,128]{2,1,0:T(8,128)(2,1)}, u32[]{:S(2)}, u32[]{:S(2)}) %all-to-all-start.1) | async-done | bytes 1310752 | tf_op jit(solution)/shard_map/all_to_all | solution.py:36
  (44 shorter events, 36.9 us)
Async XLA Ops:
  7.3 81.6 %all-to-all-start = ((bf16[32,160,128]{2,1,0:T(8,128)(2,1)}), bf16[32,160,128]{2,1,0:T(8,128)(2,1)}, u32[]{:S(2)}, u32[]{:S(2)}) async-start(bf16[32,160,128]{2,1,0:T(8,128)(2,1)} %reshape_reshape.12), calls=%async_computation | async-start | bytes 2621440 | tf_op jit(solution)/shard_map/all_to_all | solution.py:36
  24.0 21.5 %collective-permute-start.5 = (bf16[128,1536]{1,0:T(8,128)(2,1)S(1)}, bf16[128,1536]{1,0:T(8,128)(2,1)S(1)}, u32[]{:S(2)}, u32[]{:S(2)}) collective-permute-start(bf16[128,1536]{1,0:T(8,128)(2,1)S(1)} %pad_maximum_fusion), channel_id=1, source_target_pairs={{0,10},{1,11},{2,8},{3,9},{4,14},{5,15},{6,12},{7,13},{8,2},{9,3},... | collective-permute-start | bytes 1179656 | tf_op jit(solution)/shard_map/ppermute | solution.py:56
  30.0 32.1 %collective-permute-start.7 = (bf16[128,1536]{1,0:T(8,128)(2,1)S(1)}, bf16[128,1536]{1,0:T(8,128)(2,1)S(1)}, u32[]{:S(2)}, u32[]{:S(2)}) collective-permute-start(bf16[128,1536]{1,0:T(8,128)(2,1)S(1)} %pad_maximum_fusion), channel_id=1, source_target_pairs={{0,6},{1,7},{2,4},{3,5},{4,10},{5,11},{6,8},{7,9},{8,14},{9,15},{1... | collective-permute-start | bytes 1179656 | tf_op jit(solution)/shard_map/ppermute | solution.py:56
  34.2 25.9 %collective-permute-start.6 = (bf16[128,1536]{1,0:T(8,128)(2,1)S(1)}, bf16[128,1536]{1,0:T(8,128)(2,1)S(1)}, u32[]{:S(2)}, u32[]{:S(2)}) collective-permute-start(bf16[128,1536]{1,0:T(8,128)(2,1)S(1)} %pad_maximum_fusion), channel_id=1, source_target_pairs={{0,8},{1,9},{2,10},{3,11},{4,12},{5,13},{6,14},{7,15},{8,0},{9,1},... | collective-permute-start | bytes 1179656 | tf_op jit(solution)/shard_map/ppermute | solution.py:56
  37.9 42.6 %collective-permute-start.3 = (bf16[128,1536]{1,0:T(8,128)(2,1)S(1)}, bf16[128,1536]{1,0:T(8,128)(2,1)S(1)}, u32[]{:S(2)}, u32[]{:S(2)}) collective-permute-start(bf16[128,1536]{1,0:T(8,128)(2,1)S(1)} %pad_maximum_fusion), channel_id=1, source_target_pairs={{0,2},{1,3},{2,0},{3,1},{4,6},{5,7},{6,4},{7,5},{8,10},{9,11},{10,... | collective-permute-start | bytes 1179656 | tf_op jit(solution)/shard_map/ppermute | solution.py:56
  41.2 38.5 %collective-permute-start.2 = (bf16[128,1536]{1,0:T(8,128)(2,1)S(1)}, bf16[128,1536]{1,0:T(8,128)(2,1)S(1)}, u32[]{:S(2)}, u32[]{:S(2)}) collective-permute-start(bf16[128,1536]{1,0:T(8,128)(2,1)S(1)} %pad_maximum_fusion), channel_id=1, source_target_pairs={{0,12},{1,13},{2,14},{3,15},{4,0},{5,1},{6,2},{7,3},{8,4},{9,5},{1... | collective-permute-start | bytes 1179656 | tf_op jit(solution)/shard_map/ppermute | solution.py:56
  45.6 33.4 %collective-permute-start.1 = (bf16[128,1536]{1,0:T(8,128)(2,1)S(1)}, bf16[128,1536]{1,0:T(8,128)(2,1)S(1)}, u32[]{:S(2)}, u32[]{:S(2)}) collective-permute-start(bf16[128,1536]{1,0:T(8,128)(2,1)S(1)} %pad_maximum_fusion), channel_id=1, source_target_pairs={{0,4},{1,5},{2,6},{3,7},{4,8},{5,9},{6,10},{7,11},{8,12},{9,13},{1... | collective-permute-start | bytes 1179656 | tf_op jit(solution)/shard_map/ppermute | solution.py:56
  60.1 18.1 %collective-permute-start = (bf16[128,1536]{1,0:T(8,128)(2,1)S(1)}, bf16[128,1536]{1,0:T(8,128)(2,1)S(1)}, u32[]{:S(2)}, u32[]{:S(2)}) collective-permute-start(bf16[128,1536]{1,0:T(8,128)(2,1)S(1)} %pad_maximum_fusion), channel_id=1, source_target_pairs={{0,14},{1,15},{2,12},{3,13},{4,2},{5,3},{6,0},{7,1},{8,6},{9,7},{1... | collective-permute-start | bytes 1179656 | tf_op jit(solution)/shard_map/ppermute | solution.py:56
  62.1 29.2 %collective-permute-start.8 = (bf16[512,1536]{1,0:T(8,128)(2,1)S(1)}, bf16[512,1536]{1,0:T(8,128)(2,1)}, u32[]{:S(2)}, u32[]{:S(2)}) collective-permute-start(bf16[512,1536]{1,0:T(8,128)(2,1)S(1)} %constant_dynamic-update-slice_fusion.4.refs_2_), channel_id=1, source_target_pairs={{0,1},{1,0},{2,3},{3,2},{4,5},{5,4},{6,7},{7,6},{8,9},{9,8},{10,11... | collective-permute-start | bytes 4718600 | tf_op jit(solution)/shard_map/ppermute | solution.py:45
  81.3 10.0 %collective-permute-start.4 = (bf16[512,1536]{1,0:T(8,128)(2,1)}, bf16[512,1536]{1,0:T(8,128)(2,1)}, u32[]{:S(2)}, u32[]{:S(2)}) collective-permute-start(bf16[512,1536]{1,0:T(8,128)(2,1)} %constant_dynamic-update-slice_fusion.refs_0_), channel_id=1, source_target_pairs={{0,1},{1,0},{2,3},{3,2},{4,5},{5,4},{6,7},{7,6},{8,9},{9,8},{10,11... | collective-permute-start | bytes 4718600 | tf_op jit(solution)/shard_map/ppermute | solution.py:45
  97.2 1.1 copy-start
  101.6 74.7 %all-to-all-start.1 = ((bf16[32,160,128]{2,1,0:T(8,128)(2,1)}), bf16[32,160,128]{2,1,0:T(8,128)(2,1)}, u32[]{:S(2)}, u32[]{:S(2)}) async-start(bf16[32,160,128]{2,1,0:T(8,128)(2,1)} %reshape_reshape.14), calls=%async_computation.1 | async-start | bytes 2621440 | tf_op jit(solution)/shard_map/all_to_all | solution.py:36
  110.9 5.9 %collective-permute-start.9 = (bf16[160,4096]{1,0:T(8,128)(2,1)S(1)}, bf16[160,4096]{1,0:T(8,128)(2,1)S(1)}, u32[]{:S(2)}, u32[]{:S(2)}) collective-permute-start(bf16[160,4096]{1,0:T(8,128)(2,1)S(1)} %reshape_reshape.13.rows.own), channel_id=1, source_target_pairs={{0,1},{1,0},{2,3},{3,2},{4,5},{5,4},{6,7},{7,6},{8,9},{9,8},{10,11... | collective-permute-start | bytes 3932168 | tf_op jit(solution)/shard_map/ppermute | solution.py:45
  112.9 4.0 %collective-permute-start.10 = (bf16[160,1536]{1,0:T(8,128)(2,1)S(1)}, bf16[160,1536]{1,0:T(8,128)(2,1)}, u32[]{:S(2)}, u32[]{:S(2)}) collective-permute-start(bf16[160,1536]{1,0:T(8,128)(2,1)S(1)} %get-tuple-element.26.own_sides), channel_id=1, source_target_pairs={{0,1},{1,0},{2,3},{3,2},{4,5},{5,4},{6,7},{7,6},{8,9},{9,8},{10,11... | collective-permute-start | bytes 1474568 | tf_op jit(solution)/shard_map/ppermute | solution.py:45
  119.8 22.3 %collective-permute-start.11 = (bf16[128,1536]{1,0:T(8,128)(2,1)S(1)}, bf16[128,1536]{1,0:T(8,128)(2,1)S(1)}, u32[]{:S(2)}, u32[]{:S(2)}) collective-permute-start(bf16[128,1536]{1,0:T(8,128)(2,1)S(1)} %get-tuple-element.28), channel_id=1, source_target_pairs={{0,10},{1,11},{2,8},{3,9},{4,14},{5,15},{6,12},{7,13},{8,2},{9,3},... | collective-permute-start | bytes 1179656 | tf_op jit(solution)/shard_map/ppermute | solution.py:56
  123.4 32.0 %collective-permute-start.12 = (bf16[128,1536]{1,0:T(8,128)(2,1)S(1)}, bf16[128,1536]{1,0:T(8,128)(2,1)S(1)}, u32[]{:S(2)}, u32[]{:S(2)}) collective-permute-start(bf16[128,1536]{1,0:T(8,128)(2,1)S(1)} %get-tuple-element.29), channel_id=1, source_target_pairs={{0,8},{1,9},{2,10},{3,11},{4,12},{5,13},{6,14},{7,15},{8,0},{9,1},... | collective-permute-start | bytes 1179656 | tf_op jit(solution)/shard_map/ppermute | solution.py:56
  127.9 30.3 %collective-permute-start.13 = (bf16[128,1536]{1,0:T(8,128)(2,1)S(1)}, bf16[128,1536]{1,0:T(8,128)(2,1)S(1)}, u32[]{:S(2)}, u32[]{:S(2)}) collective-permute-start(bf16[128,1536]{1,0:T(8,128)(2,1)S(1)} %get-tuple-element.30), channel_id=1, source_target_pairs={{0,6},{1,7},{2,4},{3,5},{4,10},{5,11},{6,8},{7,9},{8,14},{9,15},{1... | collective-permute-start | bytes 1179656 | tf_op jit(solution)/shard_map/ppermute | solution.py:56
  129.9 28.9 %collective-permute-start.14 = (bf16[128,1536]{1,0:T(8,128)(2,1)S(1)}, bf16[128,1536]{1,0:T(8,128)(2,1)S(1)}, u32[]{:S(2)}, u32[]{:S(2)}) collective-permute-start(bf16[128,1536]{1,0:T(8,128)(2,1)S(1)} %get-tuple-element.31), channel_id=1, source_target_pairs={{0,14},{1,15},{2,12},{3,13},{4,2},{5,3},{6,0},{7,1},{8,6},{9,7},{1... | collective-permute-start | bytes 1179656 | tf_op jit(solution)/shard_map/ppermute | solution.py:56
  137.4 25.4 %collective-permute-start.15 = (bf16[128,1536]{1,0:T(8,128)(2,1)S(1)}, bf16[128,1536]{1,0:T(8,128)(2,1)S(1)}, u32[]{:S(2)}, u32[]{:S(2)}) collective-permute-start(bf16[128,1536]{1,0:T(8,128)(2,1)S(1)} %get-tuple-element.32), channel_id=1, source_target_pairs={{0,4},{1,5},{2,6},{3,7},{4,8},{5,9},{6,10},{7,11},{8,12},{9,13},{1... | collective-permute-start | bytes 1179656 | tf_op jit(solution)/shard_map/ppermute | solution.py:56
  142.0 20.7 %collective-permute-start.16 = (bf16[128,1536]{1,0:T(8,128)(2,1)S(1)}, bf16[128,1536]{1,0:T(8,128)(2,1)S(1)}, u32[]{:S(2)}, u32[]{:S(2)}) collective-permute-start(bf16[128,1536]{1,0:T(8,128)(2,1)S(1)} %get-tuple-element.33), channel_id=1, source_target_pairs={{0,12},{1,13},{2,14},{3,15},{4,0},{5,1},{6,2},{7,3},{8,4},{9,5},{1... | collective-permute-start | bytes 1179656 | tf_op jit(solution)/shard_map/ppermute | solution.py:56
  155.4 16.2 %collective-permute-start.17 = (bf16[128,1536]{1,0:T(8,128)(2,1)S(1)}, bf16[128,1536]{1,0:T(8,128)(2,1)S(1)}, u32[]{:S(2)}, u32[]{:S(2)}) collective-permute-start(bf16[128,1536]{1,0:T(8,128)(2,1)S(1)} %get-tuple-element.34), channel_id=1, source_target_pairs={{0,2},{1,3},{2,0},{3,1},{4,6},{5,7},{6,4},{7,5},{8,10},{9,11},{10,... | collective-permute-start | bytes 1179656 | tf_op jit(solution)/shard_map/ppermute | solution.py:56

commit v4 on v3

v4 whole, which is shorter than its diff:
```python
import functools
import jax
import jax.numpy as jnp
from jax import lax
from jax.experimental import pallas as pl
from jax.experimental.pallas import tpu as pltpu
from jax.sharding import PartitionSpec as P


def contract_rows(left_rows, right_rows):
    return lax.dot_general(
        left_rows, right_rows, (((0,), (0,)), ((), ())), preferred_element_type=jnp.float32
    )


def contract_cols(left_rows, right_rows):
    return lax.dot_general(
        left_rows, right_rows, (((1,), (1,)), ((), ())), preferred_element_type=jnp.float32
    )


def slot_matrix(bucket, expert_count, capacity):
    token_count = bucket.shape[1]
    labels = lax.broadcasted_iota(jnp.int32, (expert_count, token_count), 0)
    chosen = jnp.where(bucket == labels, 1.0, 0.0)
    before = lax.broadcasted_iota(jnp.int32, (token_count, token_count), 0)
    after = lax.broadcasted_iota(jnp.int32, (token_count, token_count), 1)
    earlier = jnp.dot(
        chosen.astype(jnp.bfloat16),
        jnp.where(before < after, 1.0, 0.0).astype(jnp.bfloat16),
        preferred_element_type=jnp.float32,
    )
    slot = jnp.sum(earlier * chosen, axis=0, keepdims=True).astype(jnp.int32)
    position = bucket * capacity + slot
    targets = lax.broadcasted_iota(jnp.int32, (expert_count * capacity, token_count), 0)
    return jnp.where(targets == position, 1.0, 0.0).astype(jnp.bfloat16)


def vmem_call(kernel, out_shape, small, *arrays, scratch_shapes=()):
    vmem = pl.BlockSpec(memory_space=pltpu.VMEM)
    in_specs = [vmem] * len(arrays)
    if small is not None:
        in_specs = [pl.BlockSpec(memory_space=pltpu.SMEM)] + in_specs
        arrays = (small, *arrays)
    return pl.pallas_call(
        kernel,
        out_shape=out_shape,
        in_specs=in_specs,
        out_specs=jax.tree.map(lambda _: vmem, out_shape),
        scratch_shapes=scratch_shapes,
        compiler_params=pltpu.CompilerParams(vmem_limit_bytes=20 * 1024 * 1024),
    )(*arrays)


def pack_kernel(expert_count, capacity, bucket, tokens, cotangent, packed):
    selector = slot_matrix(bucket[...], expert_count, capacity)
    lanes = packed.shape[2]
    columns = []
    for array in (tokens, cotangent):
        rows = jnp.dot(selector, array[...], preferred_element_type=jnp.float32)
        rows = rows.astype(packed.dtype)
        columns += [rows[:, i : i + lanes] for i in range(0, rows.shape[1], lanes)]
    packed[...] = jnp.swapaxes(jnp.stack(columns, axis=0), 0, 1)


def unpack_kernel(expert_count, capacity, bucket, back, outputs, input_grad):
    selector = slot_matrix(bucket[...], expert_count, capacity)
    lanes = back.shape[2]
    blocks = jnp.swapaxes(back[...], 0, 1)
    count = blocks.shape[0] // 2
    for first, result in ((0, outputs), (count, input_grad)):
        for pair in range(0, count, 2):
            rows = jnp.concatenate([blocks[first + pair], blocks[first + pair + 1]], axis=1)
            result[:, pair * lanes : (pair + 2) * lanes] = contract_rows(selector, rows).astype(
                result.dtype
            )


def exchange(rows, expert_count):
    row_count, blocks, lanes = rows.shape
    sent = rows.reshape(expert_count, row_count // expert_count * blocks, lanes)
    arrived = lax.all_to_all(sent, "ep", split_axis=0, concat_axis=0, tiled=True)
    return arrived.reshape(rows.shape)


Y, X_HI = 4, 2
SHIFTS = ((2, 1), (2, 0), (1, 1), (3, 1), (1, 0), (3, 0), (0, 1))


def core_swap(array):
    return lax.ppermute(array, "fsdp", [(f, f ^ 1) for f in range(2 * Y * X_HI)])


def chip_shift(array, dy, dx):
    pairs = []
    for y in range(Y):
        for x in range(X_HI):
            for core in range(2):
                pairs.append(
                    ((y * X_HI + x) * 2 + core, ((y + dy) % Y * X_HI + (x ^ dx)) * 2 + core)
                )
    return lax.ppermute(array, "fsdp", pairs)


def chip_at(chip, dy, dx):
    return lax.bitwise_and(chip // X_HI + dy, Y - 1) * X_HI + lax.bitwise_xor(chip % X_HI, dx)


def gather_weights(shard, chip, core):
    origins = [chip] + [chip_at(chip, Y - dy, dx) for dy, dx in SHIFTS]
    parts = [shard] + [chip_shift(shard, dy, dx) for dy, dx in SHIFTS]
    groups, numbers = [], []
    for first in (4, 0):
        held = jnp.concatenate(parts[first : first + 4], axis=0)
        for array, side in ((held, core), (core_swap(held), 1 - core)):
            groups.append(array)
            numbers += [origin * 2 + side for origin in origins[first : first + 4]]
    return groups, jnp.stack(numbers).astype(jnp.int32)


def expert_kernel(numbers, arrived, *refs):
    groups, (back, sides, rows, results, pre, grad_hidden) = refs[:4], refs[4:]
    block = arrived.shape[2]
    blocks = arrived.shape[1] // 2
    hidden_width = sides.shape[1] // 3
    rows[...] = jnp.swapaxes(arrived[...], 0, 1)

    for first in range(0, 16, 2):
        weights = groups[first // 4].at[pl.ds(first % 4 * block, 2 * block)]
        one, two = numbers[first], numbers[first + 1]
        x = jnp.concatenate([rows[one], rows[two]], axis=1)
        dy = jnp.concatenate([rows[blocks + one], rows[blocks + two]], axis=1)
        x_part = jnp.dot(x, weights[:, : 2 * hidden_width], preferred_element_type=jnp.float32)
        dy_part = jnp.dot(dy, weights[:, 2 * hidden_width :], preferred_element_type=jnp.float32)
        if first == 0:
            pre[...] = x_part
            grad_hidden[...] = dy_part
        else:
            pre[...] += x_part
            grad_hidden[...] += dy_part

    gate_pre = pre[:, :hidden_width]
    up_proj = pre[:, hidden_width:]
    upstream = grad_hidden[...]
    sigmoid_gate = jax.nn.sigmoid(gate_pre)
    activated = gate_pre * sigmoid_gate
    sides[:, :hidden_width] = (
        upstream * up_proj * sigmoid_gate * (1.0 + gate_pre * (1.0 - sigmoid_gate))
    ).astype(sides.dtype)
    sides[:, hidden_width : 2 * hidden_width] = (upstream * activated).astype(sides.dtype)
    sides[:, 2 * hidden_width :] = (activated * up_proj).astype(sides.dtype)

    hidden = sides[:, 2 * hidden_width :]
    grads_pre = sides[:, : 2 * hidden_width]
    for first in range(0, 16, 2):
        weights = groups[first // 4].at[pl.ds(first % 4 * block, 2 * block)]
        y = contract_cols(hidden, weights[:, 2 * hidden_width :]).astype(back.dtype)
        dx = contract_cols(grads_pre, weights[:, : 2 * hidden_width]).astype(back.dtype)
        for half in range(2):
            number = numbers[first + half]
            results[number] = y[:, half * block : (half + 1) * block]
            results[blocks + number] = dx[:, half * block : (half + 1) * block]
    back[...] = jnp.swapaxes(results[...], 0, 1)


def expert_rows(arrived, groups, numbers, hidden_width):
    row_count, blocks, lanes = arrived.shape
    return vmem_call(
        expert_kernel,
        (
            jax.ShapeDtypeStruct(arrived.shape, arrived.dtype),
            jax.ShapeDtypeStruct((row_count, 3 * hidden_width), arrived.dtype),
            jax.ShapeDtypeStruct((blocks, row_count, lanes), arrived.dtype),
        ),
        numbers,
        arrived,
        *groups,
        scratch_shapes=[
            pltpu.VMEM((blocks, row_count, lanes), arrived.dtype),
            pltpu.VMEM((row_count, 2 * hidden_width), jnp.float32),
            pltpu.VMEM((row_count, hidden_width), jnp.float32),
        ],
    )


def terms_kernel(numbers, own, other, own_sides, other_sides, *terms):
    blocks = own.shape[0] // 2
    hidden_width = own_sides.shape[1] // 3
    for place, term in enumerate(terms):
        number = numbers[place]
        for first, sides in ((0, slice(0, 2 * hidden_width)), (blocks, slice(2 * hidden_width, None))):
            total = contract_rows(own[first + number], own_sides[:, sides])
            total += contract_rows(other[first + number], other_sides[:, sides])
            term[:, sides] = total.astype(term.dtype)


def local(tokens, cotangent, bucket, w_gate, w_up, w_down):
    token_count, model_width = tokens.shape
    expert_count = lax.axis_size("ep")
    capacity = max(2, 5 * token_count // (4 * expert_count))
    slot_rows = expert_count * capacity
    shard_width = w_gate.shape[1]
    hidden_width = w_gate.shape[2]
    place = lax.axis_index("fsdp")
    core = lax.bitwise_and(place, 1)
    chip = lax.shift_right_logical(place, 1)
    sizes = (expert_count, capacity)
    choice = bucket.reshape(1, token_count)

    blocked = jax.ShapeDtypeStruct(
        (slot_rows, 2 * model_width // shard_width, shard_width), tokens.dtype
    )
    packed = vmem_call(
        functools.partial(pack_kernel, *sizes), blocked, None, choice, tokens, cotangent
    )
    packed, w_gate, w_up, w_down = lax.optimization_barrier((packed, w_gate, w_up, w_down))
    arrived = exchange(packed, expert_count)
    shard = jnp.concatenate([w_gate[0], w_up[0], w_down[0]], axis=1)
    groups, numbers = gather_weights(shard, chip, core)
    returned, sides, rows = expert_rows(arrived, groups, numbers, hidden_width)
    returned, rows, sides = lax.optimization_barrier((returned, rows, sides))
    back = exchange(returned, expert_count)

    other_rows = core_swap(rows)
    other_sides = core_swap(sides)
    targets = [chip] + [chip_at(chip, dy, dx) for dy, dx in SHIFTS]
    columns = jnp.stack([target * 2 + core for target in targets]).astype(jnp.int32)
    term = jax.ShapeDtypeStruct((shard_width, 3 * hidden_width), tokens.dtype)
    terms = vmem_call(
        terms_kernel, [term] * len(targets), columns, rows, other_rows, sides, other_sides
    )
    total = terms[0].astype(jnp.float32)
    for (dy, dx), term in zip(SHIFTS, terms[1:]):
        total = total + chip_shift(term, dy, dx).astype(jnp.float32)

    grads = total.astype(jnp.bfloat16)
    grad_wg = grads[None, :, :hidden_width]
    grad_wu = grads[None, :, hidden_width : 2 * hidden_width]
    grad_wd = grads[None, :, 2 * hidden_width :]
    result = jax.ShapeDtypeStruct(tokens.shape, tokens.dtype)
    outputs, input_grad = vmem_call(
        functools.partial(unpack_kernel, *sizes), (result, result), None, choice, back
    )
    return (outputs, input_grad, grad_wg, grad_wu, grad_wd)


def solution(mesh):
    in_specs = (
        P(("ep", "fsdp"), None),
        P(("ep", "fsdp"), None),
        P(("ep", "fsdp"), None),
        P("ep", "fsdp", None),
        P("ep", "fsdp", None),
        P("ep", "fsdp", None),
    )
    out_specs = (
        P(("ep", "fsdp"), None),
        P(("ep", "fsdp"), None),
        P("ep", "fsdp", None),
        P("ep", "fsdp", None),
        P("ep", "fsdp", None),
    )
    return jax.shard_map(local, mesh=mesh, in_specs=in_specs, out_specs=out_specs, check_vma=False)
```

time: 182 us -> 178 us (0.978); the launches traced: 181 us -> 175 us
  starting transfers between devices: 84.4 us -> 99 us
  waiting for transfers between devices: 64.2 us -> 51.9 us
  local copies, waits for them, and re-layouts: 14.7 us -> 8.94 us
  Pallas kernels: 8.81 us -> 13.6 us
  matrix products: 3.98 us -> 0 us
  other arithmetic: 3.86 us -> 0.53 us
    ppermute x14, starting transfers between devices: 50.1 us -> 59.7 us  [chip_shift(): return lax.ppermute(array, 'fsdp', pairs)]
    another operation x4 -> x0, local copies, waits for them, and re-layouts: 9.48 us -> none  [the longest x2 4.76 us: exchange(): rows.reshape(row_count, width // 128, 128).reshape(expert_count, chunk, 128)]
    ppermute x14, waiting for transfers between devices: 53.7 us -> 45.1 us  [chip_shift(): return lax.ppermute(array, 'fsdp', pairs)]
    all_to_all x2, waiting for transfers between devices: 9.04 us -> 2.27 us  [exchange(): lax.all_to_all(sent, 'ep', split_axis=0, concat_axis=0, tiled=True)]
    pallas_call x2 -> x4, Pallas kernels: 8.81 us -> 13.6 us  [vmem_call(): pl.pallas_call(kernel, out_shape=out_shape, in_specs=in_specs, out_specs=...]
    all_to_all x2, starting transfers between devices: 26.1 us -> 30.6 us  [exchange(): lax.all_to_all(sent, 'ep', split_axis=0, concat_axis=0, tiled=True)]
    dot_general x3 -> x0, matrix products: 3.98 us -> none  [the longest x2 2.29 us: contract_rows(): lax.dot_general(left_rows, right_rows, (((0,), (0,)), ((), ())), preferre...]
    unnamed x8 -> x23, local copies, waits for them, and re-layouts: 3.48 us -> 7.22 us
  transfers between devices with their start and end apart: 20 -> 20, of which waited for: 11 -> 11; matrix products, arithmetic and copies ran while one was open for 4% -> 3% of each run, Pallas kernels for 2% -> 2%
where the time goes in v4:
time: 178 us; the launch traced here: 175 us
  starting transfers between devices  99 us (56%)
  waiting for transfers between devices  51.9 us (29%)
  Pallas kernels  13.6 us (8%)
  local copies, waits for them, and re-layouts  8.94 us (5%)
    ppermute x14, starting transfers between devices, chip_shift(): return lax.ppermute(array, 'fsdp', pairs)  59.7 us
    ppermute x14, waiting for transfers between devices, chip_shift(): return lax.ppermute(array, 'fsdp', pairs)  45.1 us
    all_to_all x2, starting transfers between devices, exchange(): lax.all_to_all(sent, 'ep', split_axis=0, concat_axis=0, tiled=True)  30.6 us
    pallas_call x4, Pallas kernels, vmem_call(): pl.pallas_call(kernel, out_shape=out_shape, in_specs=in_specs, out_specs=...  13.6 us
    ppermute x4, starting transfers between devices, core_swap(): lax.ppermute(array, 'fsdp', [(f, f ^ 1) for f in range(2 * Y * X_HI)])  8.65 us
    unnamed x23, local copies, waits for them, and re-layouts  7.22 us
    ppermute x4, waiting for transfers between devices, core_swap(): lax.ppermute(array, 'fsdp', [(f, f ^ 1) for f in range(2 * Y * X_HI)])  4.55 us
  transfers between devices with their start and end apart: 20, of which 11 were waited for; matrix products, arithmetic and copies ran while one was open for 3% of the time, Pallas kernels for 2%

profile of v4, /device:TPU:6, one launch (start us, length us, event | category | flops | bytes accessed | tf_op | source)
XLA Modules:
  0.0 175.1 jit_solution(14704074902206058831)
XLA Ops:
  3.4 2.0 %shard_map.101 = bf16[160,32,128]{2,1,0:T(8,128)(2,1)} custom-call(s32[1,128]{1,0:T(1,128)S(1)} %bitcast.34, bf16[128,2048]{1,0:T(8,128)(2,1)S(1)} %copy-done.3, bf16[128,2048]{1,0:T(8,128)(2,1)S(1)} %copy-done.4), custom_call_target="tpu_custom_call" | custom-call | tf_op jit(solution)/shard_map/pallas_call | solution.py:45
  5.4 16.8 %all-to-all-start = ((bf16[32,160,128]{2,1,0:T(8,128)(2,1)}), bf16[32,160,128]{2,1,0:T(8,128)(2,1)S(1)}, u32[]{:S(2)}, u32[]{:S(2)}) async-start(bf16[32,160,128]{2,1,0:T(8,128)(2,1)} %bitcast.17), calls=%async_computation | async-start | bytes 2621440 | tf_op jit(solution)/shard_map/all_to_all | solution.py:82
  22.3 5.8 %collective-permute-start = (bf16[128,1536]{1,0:T(8,128)(2,1)S(1)}, bf16[128,1536]{1,0:T(8,128)(2,1)S(1)}, u32[]{:S(2)}, u32[]{:S(2)}) collective-permute-start(bf16[128,1536]{1,0:T(8,128)(2,1)S(1)} %pad_maximum_fusion.1), channel_id=1, source_target_pairs={{0,14},{1,15},{2,12},{3,13},{4,2},{5,3},{6,0},{7,1},{8,6},{9,7},{1... | collective-permute-start | bytes 1179656 | tf_op jit(solution)/shard_map/ppermute | solution.py:102
  30.0 4.0 %collective-permute-start.7 = (bf16[128,1536]{1,0:T(8,128)(2,1)S(1)}, bf16[128,1536]{1,0:T(8,128)(2,1)S(1)}, u32[]{:S(2)}, u32[]{:S(2)}) collective-permute-start(bf16[128,1536]{1,0:T(8,128)(2,1)S(1)} %pad_maximum_fusion.1), channel_id=1, source_target_pairs={{0,6},{1,7},{2,4},{3,5},{4,10},{5,11},{6,8},{7,9},{8,14},{9,15},{1... | collective-permute-start | bytes 1179656 | tf_op jit(solution)/shard_map/ppermute | solution.py:102
  34.1 6.0 %collective-permute-start.6 = (bf16[128,1536]{1,0:T(8,128)(2,1)S(1)}, bf16[128,1536]{1,0:T(8,128)(2,1)S(1)}, u32[]{:S(2)}, u32[]{:S(2)}) collective-permute-start(bf16[128,1536]{1,0:T(8,128)(2,1)S(1)} %pad_maximum_fusion.1), channel_id=1, source_target_pairs={{0,8},{1,9},{2,10},{3,11},{4,12},{5,13},{6,14},{7,15},{8,0},{9,1},... | collective-permute-start | bytes 1179656 | tf_op jit(solution)/shard_map/ppermute | solution.py:102
  40.1 2.8 %collective-permute-start.5 = (bf16[128,1536]{1,0:T(8,128)(2,1)S(1)}, bf16[128,1536]{1,0:T(8,128)(2,1)S(1)}, u32[]{:S(2)}, u32[]{:S(2)}) collective-permute-start(bf16[128,1536]{1,0:T(8,128)(2,1)S(1)} %pad_maximum_fusion.1), channel_id=1, source_target_pairs={{0,10},{1,11},{2,8},{3,9},{4,14},{5,15},{6,12},{7,13},{8,2},{9,3},... | collective-permute-start | bytes 1179656 | tf_op jit(solution)/shard_map/ppermute | solution.py:102
  42.9 6.7 %collective-permute-start.2 = (bf16[128,1536]{1,0:T(8,128)(2,1)S(1)}, bf16[128,1536]{1,0:T(8,128)(2,1)S(1)}, u32[]{:S(2)}, u32[]{:S(2)}) collective-permute-start(bf16[128,1536]{1,0:T(8,128)(2,1)S(1)} %pad_maximum_fusion.1), channel_id=1, source_target_pairs={{0,12},{1,13},{2,14},{3,15},{4,0},{5,1},{6,2},{7,3},{8,4},{9,5},{1... | collective-permute-start | bytes 1179656 | tf_op jit(solution)/shard_map/ppermute | solution.py:102
  50.4 16.1 %collective-permute-done.1 = bf16[128,1536]{1,0:T(8,128)(2,1)S(1)} collective-permute-done((bf16[128,1536]{1,0:T(8,128)(2,1)S(1)}, bf16[128,1536]{1,0:T(8,128)(2,1)S(1)}, u32[]{:S(2)}, u32[]{:S(2)}) %collective-permute-start.1) | collective-permute-done | bytes 393248 | tf_op jit(solution)/shard_map/ppermute | solution.py:102
  66.5 4.0 %collective-permute-start.3 = (bf16[128,1536]{1,0:T(8,128)(2,1)S(1)}, bf16[128,1536]{1,0:T(8,128)(2,1)S(1)}, u32[]{:S(2)}, u32[]{:S(2)}) collective-permute-start(bf16[128,1536]{1,0:T(8,128)(2,1)S(1)} %pad_maximum_fusion.1), channel_id=1, source_target_pairs={{0,2},{1,3},{2,0},{3,1},{4,6},{5,7},{6,4},{7,5},{8,10},{9,11},{10,... | collective-permute-start | bytes 1179656 | tf_op jit(solution)/shard_map/ppermute | solution.py:102
  72.1 6.0 %collective-permute-done.3 = bf16[128,1536]{1,0:T(8,128)(2,1)S(1)} collective-permute-done((bf16[128,1536]{1,0:T(8,128)(2,1)S(1)}, bf16[128,1536]{1,0:T(8,128)(2,1)S(1)}, u32[]{:S(2)}, u32[]{:S(2)}) %collective-permute-start.3) | collective-permute-done | bytes 393248 | tf_op jit(solution)/shard_map/ppermute | solution.py:102
  80.9 2.4 %collective-permute-start.8 = (bf16[512,1536]{1,0:T(8,128)(2,1)S(1)}, bf16[512,1536]{1,0:T(8,128)(2,1)}, u32[]{:S(2)}, u32[]{:S(2)}) collective-permute-start(bf16[512,1536]{1,0:T(8,128)(2,1)S(1)} %pad_maximum_fusion.refs_2_), channel_id=1, source_target_pairs={{0,1},{1,0},{2,3},{3,2},{4,5},{5,4},{6,7},{7,6},{8,9},{9,8},{10,11... | collective-permute-start | bytes 4718600 | tf_op jit(solution)/shard_map/ppermute | solution.py:91
  84.5 2.0 %collective-permute-done.8.refs_3_ = bf16[512,1536]{1,0:T(8,128)(2,1)} collective-permute-done((bf16[512,1536]{1,0:T(8,128)(2,1)S(1)}, bf16[512,1536]{1,0:T(8,128)(2,1)}, u32[]{:S(2)}, u32[]{:S(2)}) %collective-permute-start.8) | collective-permute-done | bytes 1572896 | tf_op jit(solution)/shard_map/ppermute | solution.py:91
  87.0 6.7 %shard_map.102 = (bf16[160,32,128]{2,1,0:T(8,128)(2,1)S(1)}, bf16[160,1536]{1,0:T(8,128)(2,1)S(1)}, bf16[32,160,128]{2,1,0:T(8,128)(2,1)S(1)}) custom-call(s32[16]{0:T(128)S(1)} %stack.80.numbers, bf16[160,32,128]{2,1,0:T(8,128)(2,1)S(1)} %bitcast.32, bf16[512,1536]{1,0:T(8,128)(2,1)} %constant_dynamic-update-slice_fusion.refs_0_, ...), custom_call_target="tpu_custom_call" | custom-call | tf_op jit(solution)/shard_map/pallas_call | solution.py:45
  95.9 13.8 %all-to-all-start.1 = ((bf16[32,160,128]{2,1,0:T(8,128)(2,1)}), bf16[32,160,128]{2,1,0:T(8,128)(2,1)S(1)}, u32[]{:S(2)}, u32[]{:S(2)}) async-start(bf16[32,160,128]{2,1,0:T(8,128)(2,1)} %bitcast.33), calls=%async_computation.1 | async-start | bytes 2621440 | tf_op jit(solution)/shard_map/all_to_all | solution.py:82
  109.7 1.9 %collective-permute-start.9 = (bf16[32,160,128]{2,1,0:T(8,128)(2,1)S(1)}, bf16[32,160,128]{2,1,0:T(8,128)(2,1)}, u32[]{:S(2)}, u32[]{:S(2)}) collective-permute-start(bf16[32,160,128]{2,1,0:T(8,128)(2,1)S(1)} %copy-done.2), channel_id=1, source_target_pairs={{0,1},{1,0},{2,3},{3,2},{4,5},{5,4},{6,7},{7,6},{8,9},{9,8},{10,11... | collective-permute-start | bytes 3932168 | tf_op jit(solution)/shard_map/ppermute | solution.py:91
  111.7 2.4 %collective-permute-start.10 = (bf16[160,1536]{1,0:T(8,128)(2,1)S(1)}, bf16[160,1536]{1,0:T(8,128)(2,1)}, u32[]{:S(2)}, u32[]{:S(2)}) collective-permute-start(bf16[160,1536]{1,0:T(8,128)(2,1)S(1)} %get-tuple-element.36.own_sides), channel_id=1, source_target_pairs={{0,1},{1,0},{2,3},{3,2},{4,5},{5,4},{6,7},{7,6},{8,9},{9,8},{10,11... | collective-permute-start | bytes 1474568 | tf_op jit(solution)/shard_map/ppermute | solution.py:91
  115.7 3.3 %shard_map.104 = (bf16[128,1536]{1,0:T(8,128)(2,1)S(1)}, bf16[128,1536]{1,0:T(8,128)(2,1)S(1)}, bf16[128,1536]{1,0:T(8,128)(2,1)S(1)}, bf16[128,1536]{1,0:T(8,12...) custom-call(s32[8]{0:T(128)S(1)} %stack.82.numbers, ...), custom_call_target="tpu_custom_call" | custom-call | tf_op jit(solution)/shard_map/pallas_call | solution.py:45
  120.9 7.0 %collective-permute-start.12 = (bf16[128,1536]{1,0:T(8,128)(2,1)S(1)}, bf16[128,1536]{1,0:T(8,128)(2,1)S(1)}, u32[]{:S(2)}, u32[]{:S(2)}) collective-permute-start(bf16[128,1536]{1,0:T(8,128)(2,1)S(1)} %get-tuple-element.39), channel_id=1, source_target_pairs={{0,8},{1,9},{2,10},{3,11},{4,12},{5,13},{6,14},{7,15},{8,0},{9,1},... | collective-permute-start | bytes 1179656 | tf_op jit(solution)/shard_map/ppermute | solution.py:102
  129.8 7.5 %collective-permute-start.14 = (bf16[128,1536]{1,0:T(8,128)(2,1)S(1)}, bf16[128,1536]{1,0:T(8,128)(2,1)S(1)}, u32[]{:S(2)}, u32[]{:S(2)}) collective-permute-start(bf16[128,1536]{1,0:T(8,128)(2,1)S(1)} %get-tuple-element.41), channel_id=1, source_target_pairs={{0,14},{1,15},{2,12},{3,13},{4,2},{5,3},{6,0},{7,1},{8,6},{9,7},{1... | collective-permute-start | bytes 1179656 | tf_op jit(solution)/shard_map/ppermute | solution.py:102
  140.6 3.9 %collective-permute-start.16 = (bf16[128,1536]{1,0:T(8,128)(2,1)S(1)}, bf16[128,1536]{1,0:T(8,128)(2,1)S(1)}, u32[]{:S(2)}, u32[]{:S(2)}) collective-permute-start(bf16[128,1536]{1,0:T(8,128)(2,1)S(1)} %get-tuple-element.43), channel_id=1, source_target_pairs={{0,12},{1,13},{2,14},{3,15},{4,0},{5,1},{6,2},{7,3},{8,4},{9,5},{1... | collective-permute-start | bytes 1179656 | tf_op jit(solution)/shard_map/ppermute | solution.py:102
  144.4 9.8 %collective-permute-done.12 = bf16[128,1536]{1,0:T(8,128)(2,1)S(1)} collective-permute-done((bf16[128,1536]{1,0:T(8,128)(2,1)S(1)}, bf16[128,1536]{1,0:T(8,128)(2,1)S(1)}, u32[]{:S(2)}, u32[]{:S(2)}) %collective-permute-start.12) | collective-permute-done | bytes 393248 | tf_op jit(solution)/shard_map/ppermute | solution.py:102
  154.3 4.3 %collective-permute-start.17 = (bf16[128,1536]{1,0:T(8,128)(2,1)S(1)}, bf16[128,1536]{1,0:T(8,128)(2,1)S(1)}, u32[]{:S(2)}, u32[]{:S(2)}) collective-permute-start(bf16[128,1536]{1,0:T(8,128)(2,1)S(1)} %get-tuple-element.44), channel_id=1, source_target_pairs={{0,2},{1,3},{2,0},{3,1},{4,6},{5,7},{6,4},{7,5},{8,10},{9,11},{10,... | collective-permute-start | bytes 1179656 | tf_op jit(solution)/shard_map/ppermute | solution.py:102
  158.6 3.1 %collective-permute-done.15 = bf16[128,1536]{1,0:T(8,128)(2,1)S(1)} collective-permute-done((bf16[128,1536]{1,0:T(8,128)(2,1)S(1)}, bf16[128,1536]{1,0:T(8,128)(2,1)S(1)}, u32[]{:S(2)}, u32[]{:S(2)}) %collective-permute-start.15) | collective-permute-done | bytes 393248 | tf_op jit(solution)/shard_map/ppermute | solution.py:102
  161.7 8.9 %collective-permute-done.17 = bf16[128,1536]{1,0:T(8,128)(2,1)S(1)} collective-permute-done((bf16[128,1536]{1,0:T(8,128)(2,1)S(1)}, bf16[128,1536]{1,0:T(8,128)(2,1)S(1)}, u32[]{:S(2)}, u32[]{:S(2)}) %collective-permute-start.17) | collective-permute-done | bytes 393248 | tf_op jit(solution)/shard_map/ppermute | solution.py:102
  (50 shorter events, 26.8 us)
Async XLA Ops:
  5.4 16.9 %copy-start.7 = (bf16[1,128,512]{2,1,0:T(8,128)(2,1)S(1)}, bf16[1,128,512]{2,1,0:T(8,128)(2,1)}, u32[]{:S(2)}) copy-start(bf16[1,128,512]{2,1,0:T(8,128)(2,1)} %param.11) | copy-start | bytes 393220
  5.4 16.9 %copy-start.8 = (bf16[1,128,512]{2,1,0:T(8,128)(2,1)S(1)}, bf16[1,128,512]{2,1,0:T(8,128)(2,1)}, u32[]{:S(2)}) copy-start(bf16[1,128,512]{2,1,0:T(8,128)(2,1)} %param.10) | copy-start | bytes 393220
  5.4 16.9 %copy-start.9 = (bf16[1,128,512]{2,1,0:T(8,128)(2,1)S(1)}, bf16[1,128,512]{2,1,0:T(8,128)(2,1)}, u32[]{:S(2)}) copy-start(bf16[1,128,512]{2,1,0:T(8,128)(2,1)} %param.9) | copy-start | bytes 393220
  5.4 81.6 %all-to-all-start = ((bf16[32,160,128]{2,1,0:T(8,128)(2,1)}), bf16[32,160,128]{2,1,0:T(8,128)(2,1)S(1)}, u32[]{:S(2)}, u32[]{:S(2)}) async-start(bf16[32,160,128]{2,1,0:T(8,128)(2,1)} %bitcast.17), calls=%async_computation | async-start | bytes 2621440 | tf_op jit(solution)/shard_map/all_to_all | solution.py:82
  22.3 20.6 %collective-permute-start = (bf16[128,1536]{1,0:T(8,128)(2,1)S(1)}, bf16[128,1536]{1,0:T(8,128)(2,1)S(1)}, u32[]{:S(2)}, u32[]{:S(2)}) collective-permute-start(bf16[128,1536]{1,0:T(8,128)(2,1)S(1)} %pad_maximum_fusion.1), channel_id=1, source_target_pairs={{0,14},{1,15},{2,12},{3,13},{4,2},{5,3},{6,0},{7,1},{8,6},{9,7},{1... | collective-permute-start | bytes 1179656 | tf_op jit(solution)/shard_map/ppermute | solution.py:102
  28.1 38.4 %collective-permute-start.1 = (bf16[128,1536]{1,0:T(8,128)(2,1)S(1)}, bf16[128,1536]{1,0:T(8,128)(2,1)S(1)}, u32[]{:S(2)}, u32[]{:S(2)}) collective-permute-start(bf16[128,1536]{1,0:T(8,128)(2,1)S(1)} %pad_maximum_fusion.1), channel_id=1, source_target_pairs={{0,4},{1,5},{2,6},{3,7},{4,8},{5,9},{6,10},{7,11},{8,12},{9,13},{1... | collective-permute-start | bytes 1179656 | tf_op jit(solution)/shard_map/ppermute | solution.py:102
  30.0 50.7 %collective-permute-start.7 = (bf16[128,1536]{1,0:T(8,128)(2,1)S(1)}, bf16[128,1536]{1,0:T(8,128)(2,1)S(1)}, u32[]{:S(2)}, u32[]{:S(2)}) collective-permute-start(bf16[128,1536]{1,0:T(8,128)(2,1)S(1)} %pad_maximum_fusion.1), channel_id=1, source_target_pairs={{0,6},{1,7},{2,4},{3,5},{4,10},{5,11},{6,8},{7,9},{8,14},{9,15},{1... | collective-permute-start | bytes 1179656 | tf_op jit(solution)/shard_map/ppermute | solution.py:102
  34.1 46.7 %collective-permute-start.6 = (bf16[128,1536]{1,0:T(8,128)(2,1)S(1)}, bf16[128,1536]{1,0:T(8,128)(2,1)S(1)}, u32[]{:S(2)}, u32[]{:S(2)}) collective-permute-start(bf16[128,1536]{1,0:T(8,128)(2,1)S(1)} %pad_maximum_fusion.1), channel_id=1, source_target_pairs={{0,8},{1,9},{2,10},{3,11},{4,12},{5,13},{6,14},{7,15},{8,0},{9,1},... | collective-permute-start | bytes 1179656 | tf_op jit(solution)/shard_map/ppermute | solution.py:102
  40.1 40.7 %collective-permute-start.5 = (bf16[128,1536]{1,0:T(8,128)(2,1)S(1)}, bf16[128,1536]{1,0:T(8,128)(2,1)S(1)}, u32[]{:S(2)}, u32[]{:S(2)}) collective-permute-start(bf16[128,1536]{1,0:T(8,128)(2,1)S(1)} %pad_maximum_fusion.1), channel_id=1, source_target_pairs={{0,10},{1,11},{2,8},{3,9},{4,14},{5,15},{6,12},{7,13},{8,2},{9,3},... | collective-permute-start | bytes 1179656 | tf_op jit(solution)/shard_map/ppermute | solution.py:102
  42.9 28.4 %collective-permute-start.2 = (bf16[128,1536]{1,0:T(8,128)(2,1)S(1)}, bf16[128,1536]{1,0:T(8,128)(2,1)S(1)}, u32[]{:S(2)}, u32[]{:S(2)}) collective-permute-start(bf16[128,1536]{1,0:T(8,128)(2,1)S(1)} %pad_maximum_fusion.1), channel_id=1, source_target_pairs={{0,12},{1,13},{2,14},{3,15},{4,0},{5,1},{6,2},{7,3},{8,4},{9,5},{1... | collective-permute-start | bytes 1179656 | tf_op jit(solution)/shard_map/ppermute | solution.py:102
  66.5 11.6 %collective-permute-start.3 = (bf16[128,1536]{1,0:T(8,128)(2,1)S(1)}, bf16[128,1536]{1,0:T(8,128)(2,1)S(1)}, u32[]{:S(2)}, u32[]{:S(2)}) collective-permute-start(bf16[128,1536]{1,0:T(8,128)(2,1)S(1)} %pad_maximum_fusion.1), channel_id=1, source_target_pairs={{0,2},{1,3},{2,0},{3,1},{4,6},{5,7},{6,4},{7,5},{8,10},{9,11},{10,... | collective-permute-start | bytes 1179656 | tf_op jit(solution)/shard_map/ppermute | solution.py:102
  78.8 5.6 %collective-permute-start.4 = (bf16[512,1536]{1,0:T(8,128)(2,1)}, bf16[512,1536]{1,0:T(8,128)(2,1)}, u32[]{:S(2)}, u32[]{:S(2)}) collective-permute-start(bf16[512,1536]{1,0:T(8,128)(2,1)} %constant_dynamic-update-slice_fusion.refs_0_), channel_id=1, source_target_pairs={{0,1},{1,0},{2,3},{3,2},{4,5},{5,4},{6,7},{7,6},{8,9},{9,8},{10,11... | collective-permute-start | bytes 4718600 | tf_op jit(solution)/shard_map/ppermute | solution.py:91
  80.9 5.6 %collective-permute-start.8 = (bf16[512,1536]{1,0:T(8,128)(2,1)S(1)}, bf16[512,1536]{1,0:T(8,128)(2,1)}, u32[]{:S(2)}, u32[]{:S(2)}) collective-permute-start(bf16[512,1536]{1,0:T(8,128)(2,1)S(1)} %pad_maximum_fusion.refs_2_), channel_id=1, source_target_pairs={{0,1},{1,0},{2,3},{3,2},{4,5},{5,4},{6,7},{7,6},{8,9},{9,8},{10,11... | collective-permute-start | bytes 4718600 | tf_op jit(solution)/shard_map/ppermute | solution.py:91
  95.9 13.8 %copy-start.2 = (bf16[32,160,128]{2,1,0:T(8,128)(2,1)S(1)}, bf16[32,160,128]{2,1,0:T(8,128)(2,1)}, u32[]{:S(2)}) copy-start(bf16[32,160,128]{2,1,0:T(8,128)(2,1)} %copy-done.1) | copy-start | bytes 3932164
  95.9 77.5 %all-to-all-start.1 = ((bf16[32,160,128]{2,1,0:T(8,128)(2,1)}), bf16[32,160,128]{2,1,0:T(8,128)(2,1)S(1)}, u32[]{:S(2)}, u32[]{:S(2)}) async-start(bf16[32,160,128]{2,1,0:T(8,128)(2,1)} %bitcast.33), calls=%async_computation.1 | async-start | bytes 2621440 | tf_op jit(solution)/shard_map/all_to_all | solution.py:82
  109.7 5.9 %collective-permute-start.9 = (bf16[32,160,128]{2,1,0:T(8,128)(2,1)S(1)}, bf16[32,160,128]{2,1,0:T(8,128)(2,1)}, u32[]{:S(2)}, u32[]{:S(2)}) collective-permute-start(bf16[32,160,128]{2,1,0:T(8,128)(2,1)S(1)} %copy-done.2), channel_id=1, source_target_pairs={{0,1},{1,0},{2,3},{3,2},{4,5},{5,4},{6,7},{7,6},{8,9},{9,8},{10,11... | collective-permute-start | bytes 3932168 | tf_op jit(solution)/shard_map/ppermute | solution.py:91
  111.7 4.0 %collective-permute-start.10 = (bf16[160,1536]{1,0:T(8,128)(2,1)S(1)}, bf16[160,1536]{1,0:T(8,128)(2,1)}, u32[]{:S(2)}, u32[]{:S(2)}) collective-permute-start(bf16[160,1536]{1,0:T(8,128)(2,1)S(1)} %get-tuple-element.36.own_sides), channel_id=1, source_target_pairs={{0,1},{1,0},{2,3},{3,2},{4,5},{5,4},{6,7},{7,6},{8,9},{9,8},{10,11... | collective-permute-start | bytes 1474568 | tf_op jit(solution)/shard_map/ppermute | solution.py:91
  119.0 21.6 %collective-permute-start.11 = (bf16[128,1536]{1,0:T(8,128)(2,1)S(1)}, bf16[128,1536]{1,0:T(8,128)(2,1)S(1)}, u32[]{:S(2)}, u32[]{:S(2)}) collective-permute-start(bf16[128,1536]{1,0:T(8,128)(2,1)S(1)} %get-tuple-element.38), channel_id=1, source_target_pairs={{0,10},{1,11},{2,8},{3,9},{4,14},{5,15},{6,12},{7,13},{8,2},{9,3},... | collective-permute-start | bytes 1179656 | tf_op jit(solution)/shard_map/ppermute | solution.py:102
  120.9 33.4 %collective-permute-start.12 = (bf16[128,1536]{1,0:T(8,128)(2,1)S(1)}, bf16[128,1536]{1,0:T(8,128)(2,1)S(1)}, u32[]{:S(2)}, u32[]{:S(2)}) collective-permute-start(bf16[128,1536]{1,0:T(8,128)(2,1)S(1)} %get-tuple-element.39), channel_id=1, source_target_pairs={{0,8},{1,9},{2,10},{3,11},{4,12},{5,13},{6,14},{7,15},{8,0},{9,1},... | collective-permute-start | bytes 1179656 | tf_op jit(solution)/shard_map/ppermute | solution.py:102
  127.9 30.7 %collective-permute-start.13 = (bf16[128,1536]{1,0:T(8,128)(2,1)S(1)}, bf16[128,1536]{1,0:T(8,128)(2,1)S(1)}, u32[]{:S(2)}, u32[]{:S(2)}) collective-permute-start(bf16[128,1536]{1,0:T(8,128)(2,1)S(1)} %get-tuple-element.40), channel_id=1, source_target_pairs={{0,6},{1,7},{2,4},{3,5},{4,10},{5,11},{6,8},{7,9},{8,14},{9,15},{1... | collective-permute-start | bytes 1179656 | tf_op jit(solution)/shard_map/ppermute | solution.py:102
  129.8 28.8 %collective-permute-start.14 = (bf16[128,1536]{1,0:T(8,128)(2,1)S(1)}, bf16[128,1536]{1,0:T(8,128)(2,1)S(1)}, u32[]{:S(2)}, u32[]{:S(2)}) collective-permute-start(bf16[128,1536]{1,0:T(8,128)(2,1)S(1)} %get-tuple-element.41), channel_id=1, source_target_pairs={{0,14},{1,15},{2,12},{3,13},{4,2},{5,3},{6,0},{7,1},{8,6},{9,7},{1... | collective-permute-start | bytes 1179656 | tf_op jit(solution)/shard_map/ppermute | solution.py:102
  137.4 24.3 %collective-permute-start.15 = (bf16[128,1536]{1,0:T(8,128)(2,1)S(1)}, bf16[128,1536]{1,0:T(8,128)(2,1)S(1)}, u32[]{:S(2)}, u32[]{:S(2)}) collective-permute-start(bf16[128,1536]{1,0:T(8,128)(2,1)S(1)} %get-tuple-element.42), channel_id=1, source_target_pairs={{0,4},{1,5},{2,6},{3,7},{4,8},{5,9},{6,10},{7,11},{8,12},{9,13},{1... | collective-permute-start | bytes 1179656 | tf_op jit(solution)/shard_map/ppermute | solution.py:102
  140.6 21.1 %collective-permute-start.16 = (bf16[128,1536]{1,0:T(8,128)(2,1)S(1)}, bf16[128,1536]{1,0:T(8,128)(2,1)S(1)}, u32[]{:S(2)}, u32[]{:S(2)}) collective-permute-start(bf16[128,1536]{1,0:T(8,128)(2,1)S(1)} %get-tuple-element.43), channel_id=1, source_target_pairs={{0,12},{1,13},{2,14},{3,15},{4,0},{5,1},{6,2},{7,3},{8,4},{9,5},{1... | collective-permute-start | bytes 1179656 | tf_op jit(solution)/shard_map/ppermute | solution.py:102
  154.3 16.3 %collective-permute-start.17 = (bf16[128,1536]{1,0:T(8,128)(2,1)S(1)}, bf16[128,1536]{1,0:T(8,128)(2,1)S(1)}, u32[]{:S(2)}, u32[]{:S(2)}) collective-permute-start(bf16[128,1536]{1,0:T(8,128)(2,1)S(1)} %get-tuple-element.44), channel_id=1, source_target_pairs={{0,2},{1,3},{2,0},{3,1},{4,6},{5,7},{6,4},{7,5},{8,10},{9,11},{10,... | collective-permute-start | bytes 1179656 | tf_op jit(solution)/shard_map/ppermute | solution.py:102
  (6 other events, 7.8 us)

commit v5 on v4

--- a/solution.py
+++ b/solution.py
@@ -36,31 +36,68 @@
     return jnp.where(targets == position, 1.0, 0.0).astype(jnp.bfloat16)
 
 
-def vmem_call(kernel, out_shape, small, *arrays, scratch_shapes=()):
-    vmem = pl.BlockSpec(memory_space=pltpu.VMEM)
+def vmem_call(kernel, out_shape, small, *arrays, scratch_shapes=(), far_out=False):
+    vmem, far = pl.BlockSpec(memory_space=pltpu.VMEM), pl.BlockSpec(memory_space=pltpu.HBM)
     in_specs = [vmem] * len(arrays)
     if small is not None:
         in_specs = [pl.BlockSpec(memory_space=pltpu.SMEM)] + in_specs
         arrays = (small, *arrays)
     return pl.pallas_call(
         kernel,
-        out_shape=out_shape,
+        out_shape=jax.tree.map(lambda s: pltpu.HBM(s.shape, s.dtype), out_shape) if far_out else out_shape,
         in_specs=in_specs,
-        out_specs=jax.tree.map(lambda _: vmem, out_shape),
+        out_specs=jax.tree.map(lambda _: far if far_out else vmem, out_shape),
         scratch_shapes=scratch_shapes,
         compiler_params=pltpu.CompilerParams(vmem_limit_bytes=20 * 1024 * 1024),
     )(*arrays)
 
 
-def pack_kernel(expert_count, capacity, bucket, tokens, cotangent, packed):
-    selector = slot_matrix(bucket[...], expert_count, capacity)
+def pack_kernel(
+    expert_count, capacity, bucket, tokens, cotangent, packed, choice, near, result, sems
+):
+    lookup = pltpu.make_async_copy(bucket, choice, sems.at[4])
+    lookup.start()
+    loads = [
+        pltpu.make_async_copy(array, near.at[number], sems.at[number])
+        for number, array in enumerate((tokens, cotangent))
+    ]
+    for load in loads:
+        load.start()
+    lookup.wait()
+    selector = slot_matrix(choice[...], expert_count, capacity)
     lanes = packed.shape[2]
-    columns = []
-    for array in (tokens, cotangent):
-        rows = jnp.dot(selector, array[...], preferred_element_type=jnp.float32)
+    count = packed.shape[1] // 2
+    stores = []
+    for number, load in enumerate(loads):
+        load.wait()
+        rows = jnp.dot(selector, near[number], preferred_element_type=jnp.float32)
         rows = rows.astype(packed.dtype)
-        columns += [rows[:, i : i + lanes] for i in range(0, rows.shape[1], lanes)]
-    packed[...] = jnp.swapaxes(jnp.stack(columns, axis=0), 0, 1)
+        columns = [rows[:, i : i + lanes] for i in range(0, rows.shape[1], lanes)]
+        part = pl.ds(number * count, count)
+        result[:, part, :] = jnp.swapaxes(jnp.stack(columns, axis=0), 0, 1)
+        stores.append(
+            pltpu.make_async_copy(result.at[:, part], packed.at[:, part], sems.at[2 + number])
+        )
+        stores[-1].start()
+    for store in stores:
+        store.wait()
+
+
+def pack_rows(kernel, out_shape, choice, tokens, cotangent):
+    far = pl.BlockSpec(memory_space=pltpu.HBM)
+    return pl.pallas_call(
+        kernel,
+        out_shape=pltpu.HBM(out_shape.shape, out_shape.dtype),
+        in_specs=[far, far, far],
+        out_specs=far,
+        scratch_shapes=[
+            pltpu.VMEM(choice.shape, choice.dtype),
+            pltpu.VMEM((2, *tokens.shape), tokens.dtype),
+            pltpu.VMEM(out_shape.shape, out_shape.dtype),
+            pltpu.SemaphoreType.DMA((5,)),
+        ],
+        compiler_params=pltpu.CompilerParams(vmem_limit_bytes=20 * 1024 * 1024),
+    )(*(pltpu.with_memory_space_constraint(a, pltpu.HBM) for a in (choice, tokens, cotangent)))
 
 
 def unpack_kernel(expert_count, capacity, bucket, back, outputs, input_grad):
@@ -84,7 +121,6 @@
 
 
 Y, X_HI = 4, 2
-SHIFTS = ((2, 1), (2, 0), (1, 1), (3, 1), (1, 0), (3, 0), (0, 1))
 
 
 def core_swap(array):
@@ -107,23 +143,33 @@
 
 
 def gather_weights(shard, chip, core):
-    origins = [chip] + [chip_at(chip, Y - dy, dx) for dy, dx in SHIFTS]
-    parts = [shard] + [chip_shift(shard, dy, dx) for dy, dx in SHIFTS]
+    across, two = chip_shift(shard, 0, 1), chip_shift(shard, 2, 0)
+    one, three = chip_shift(shard, 1, 0), chip_shift(shard, 3, 0)
+    early = [(shard, 0, 0), (across, 0, 1), (one, 3, 0), (three, 1, 0)]
+    late = [
+        (two, 2, 0),
+        (chip_shift(across, 1, 0), 3, 1),
+        (chip_shift(across, 3, 0), 1, 1),
+        (chip_shift(two, 0, 1), 2, 1),
+    ]
     groups, numbers = [], []
-    for first in (4, 0):
-        held = jnp.concatenate(parts[first : first + 4], axis=0)
+    for parts in (early, late):
+        held = jnp.concatenate([part for part, _, _ in parts], axis=0)
         for array, side in ((held, core), (core_swap(held), 1 - core)):
             groups.append(array)
-            numbers += [origin * 2 + side for origin in origins[first : first + 4]]
+            numbers += [chip_at(chip, dy, dx) * 2 + side for _, dy, dx in parts]
     return groups, jnp.stack(numbers).astype(jnp.int32)
 
 
 def expert_kernel(numbers, arrived, *refs):
-    groups, (back, sides, rows, results, pre, grad_hidden) = refs[:4], refs[4:]
+    groups, (back, sides_out, rows_out) = refs[:4], refs[4:7]
+    rows, results, returned, sides, pre, grad_hidden, sems = refs[7:]
     block = arrived.shape[2]
     blocks = arrived.shape[1] // 2
     hidden_width = sides.shape[1] // 3
     rows[...] = jnp.swapaxes(arrived[...], 0, 1)
+    stores = [pltpu.make_async_copy(rows, rows_out, sems.at[0])]
+    stores[0].start()
 
     for first in range(0, 16, 2):
         weights = groups[first // 4].at[pl.ds(first % 4 * block, 2 * block)]
@@ -149,6 +195,8 @@
     ).astype(sides.dtype)
     sides[:, hidden_width : 2 * hidden_width] = (upstream * activated).astype(sides.dtype)
     sides[:, 2 * hidden_width :] = (activated * up_proj).astype(sides.dtype)
+    stores.append(pltpu.make_async_copy(sides, sides_out, sems.at[1]))
+    stores[1].start()
 
     hidden = sides[:, 2 * hidden_width :]
     grads_pre = sides[:, : 2 * hidden_width]
@@ -160,7 +208,16 @@
             number = numbers[first + half]
             results[number] = y[:, half * block : (half + 1) * block]
             results[blocks + number] = dx[:, half * block : (half + 1) * block]
-    back[...] = jnp.swapaxes(results[...], 0, 1)
+    step = back.shape[0] // 5
+    for number in range(5):
+        part = pl.ds(number * step, step)
+        returned[part] = jnp.swapaxes(results[:, part], 0, 1)
+        stores.append(
+            pltpu.make_async_copy(returned.at[part], back.at[part], sems.at[2 + number])
+        )
+        stores[-1].start()
+    for store in stores:
+        store.wait()
 
 
 def expert_rows(arrived, groups, numbers, hidden_width):
@@ -177,9 +234,14 @@
         *groups,
         scratch_shapes=[
             pltpu.VMEM((blocks, row_count, lanes), arrived.dtype),
+            pltpu.VMEM((blocks, row_count, lanes), arrived.dtype),
+            pltpu.VMEM(arrived.shape, arrived.dtype),
+            pltpu.VMEM((row_count, 3 * hidden_width), arrived.dtype),
             pltpu.VMEM((row_count, 2 * hidden_width), jnp.float32),
             pltpu.VMEM((row_count, hidden_width), jnp.float32),
+            pltpu.SemaphoreType.DMA((7,)),
         ],
+        far_out=True,
     )
 
 
@@ -210,9 +272,7 @@
     blocked = jax.ShapeDtypeStruct(
         (slot_rows, 2 * model_width // shard_width, shard_width), tokens.dtype
     )
-    packed = vmem_call(
-        functools.partial(pack_kernel, *sizes), blocked, None, choice, tokens, cotangent
-    )
+    packed = pack_rows(functools.partial(pack_kernel, *sizes), blocked, choice, tokens, cotangent)
     packed, w_gate, w_up, w_down = lax.optimization_barrier((packed, w_gate, w_up, w_down))
     arrived = exchange(packed, expert_count)
     shard = jnp.concatenate([w_gate[0], w_up[0], w_down[0]], axis=1)
@@ -223,15 +283,31 @@
 
     other_rows = core_swap(rows)
     other_sides = core_swap(sides)
-    targets = [chip] + [chip_at(chip, dy, dx) for dy, dx in SHIFTS]
-    columns = jnp.stack([target * 2 + core for target in targets]).astype(jnp.int32)
-    term = jax.ShapeDtypeStruct((shard_width, 3 * hidden_width), tokens.dtype)
+    targets = [(dy, dx) for dy in range(Y) for dx in range(X_HI)]
+    columns = jnp.stack([chip_at(chip, dy, dx) * 2 + core for dy, dx in targets]).astype(jnp.int32)
+    shape = jax.ShapeDtypeStruct((shard_width, 3 * hidden_width), tokens.dtype)
     terms = vmem_call(
-        terms_kernel, [term] * len(targets), columns, rows, other_rows, sides, other_sides
-    )
-    total = terms[0].astype(jnp.float32)
-    for (dy, dx), term in zip(SHIFTS, terms[1:]):
-        total = total + chip_shift(term, dy, dx).astype(jnp.float32)
+        terms_kernel, [shape] * len(targets), columns, rows, other_rows, sides, other_sides
+    )
+    terms = dict(zip(targets, terms))
+
+    def add(*arrays):
+        return sum(array.astype(jnp.float32) for array in arrays)
+
+    def summed(*arrays):
+        return add(*arrays).astype(tokens.dtype)
+
+    two = summed(terms[2, 0], chip_shift(terms[2, 1], 0, 1))
+    across = summed(
+        terms[0, 1], chip_shift(terms[1, 1], 1, 0), chip_shift(terms[3, 1], 3, 0)
+    )
+    total = add(
+        terms[0, 0],
+        chip_shift(terms[1, 0], 1, 0),
+        chip_shift(terms[3, 0], 3, 0),
+        chip_shift(two, 2, 0),
+        chip_shift(across, 0, 1),
+    )
 
     grads = total.astype(jnp.bfloat16)
     grad_wg = grads[None, :, :hidden_width]

time: 178 us -> 170 us (0.955)
  starting transfers between devices: 99 us -> 80.2 us
  waiting for transfers between devices: 51.9 us -> 66.2 us
  local copies, waits for them, and re-layouts: 8.94 us -> 4.08 us
    ppermute x14, starting transfers between devices: 59.7 us -> 47.4 us  [chip_shift(): return lax.ppermute(array, 'fsdp', pairs)]
    ppermute x14, waiting for transfers between devices: 45.1 us -> 53 us  [chip_shift(): return lax.ppermute(array, 'fsdp', pairs)]
    all_to_all x2, starting transfers between devices: 30.6 us -> 24.6 us  [exchange(): lax.all_to_all(sent, 'ep', split_axis=0, concat_axis=0, tiled=True)]
    all_to_all x2, waiting for transfers between devices: 2.27 us -> 8.12 us  [exchange(): lax.all_to_all(sent, 'ep', split_axis=0, concat_axis=0, tiled=True)]
    unnamed x23 -> x15, local copies, waits for them, and re-layouts: 7.22 us -> 2.34 us
where the time goes in v5:
time: 170 us; the launch traced here: 167 us
  starting transfers between devices  80.2 us (47%)
  waiting for transfers between devices  66.2 us (39%)
  Pallas kernels  15.3 us (9%)
  local copies, waits for them, and re-layouts  4.08 us (2%)
    ppermute x14, waiting for transfers between devices, chip_shift(): return lax.ppermute(array, 'fsdp', pairs)  53 us
    ppermute x14, starting transfers between devices, chip_shift(): return lax.ppermute(array, 'fsdp', pairs)  47.4 us
    all_to_all x2, starting transfers between devices, exchange(): lax.all_to_all(sent, 'ep', split_axis=0, concat_axis=0, tiled=True)  24.6 us
    pallas_call x3, Pallas kernels, vmem_call(): pl.pallas_call(kernel, out_shape=jax.tree.map(lambda s: pltpu.HBM(s.shape...  12.4 us
    ppermute x4, starting transfers between devices, core_swap(): lax.ppermute(array, 'fsdp', [(f, f ^ 1) for f in range(2 * Y * X_HI)])  8.16 us
    all_to_all x2, waiting for transfers between devices, exchange(): lax.all_to_all(sent, 'ep', split_axis=0, concat_axis=0, tiled=True)  8.12 us
    ppermute x4, waiting for transfers between devices, core_swap(): lax.ppermute(array, 'fsdp', [(f, f ^ 1) for f in range(2 * Y * X_HI)])  5.08 us
  transfers between devices with their start and end apart: 20, of which 11 were waited for; matrix products, arithmetic and copies ran while one was open for 3% of the time, Pallas kernels for 2%

profile of v5, /device:TPU:6, one launch (start us, length us, event | category | flops | bytes accessed | tf_op | source)
XLA Modules:
  0.0 167.4 jit_solution(3852650178323989891)
XLA Ops:
  0.6 2.9 %shard_map.101 = bf16[160,32,128]{2,1,0:T(8,128)(2,1)} custom-call(s32[1,128]{1,0:T(1,128)} %bitcast.32, bf16[128,2048]{1,0:T(8,128)(2,1)} %tokens.1, bf16[128,2048]{1,0:T(8,128)(2,1)} %cotangent.1), custom_call_target="tpu_custom_call" | custom-call | tf_op jit(solution)/shard_map/pallas_call | solution.py:88
  3.6 16.9 %all-to-all-start = ((bf16[32,160,128]{2,1,0:T(8,128)(2,1)}), bf16[32,160,128]{2,1,0:T(8,128)(2,1)S(1)}, u32[]{:S(2)}, u32[]{:S(2)}) async-start(bf16[32,160,128]{2,1,0:T(8,128)(2,1)} %bitcast.34), calls=%async_computation | async-start | bytes 2621440 | tf_op jit(solution)/shard_map/all_to_all | solution.py:119
  20.5 3.3 %collective-permute-start = (bf16[128,1536]{1,0:T(8,128)(2,1)S(1)}, bf16[128,1536]{1,0:T(8,128)(2,1)S(1)}, u32[]{:S(2)}, u32[]{:S(2)}) collective-permute-start(bf16[128,1536]{1,0:T(8,128)(2,1)S(1)} %pad_maximum_fusion.1), channel_id=1, source_target_pairs={{0,2},{1,3},{2,0},{3,1},{4,6},{5,7},{6,4},{7,5},{8,10},{9,11},{10,... | collective-permute-start | bytes 1179656 | tf_op jit(solution)/shard_map/ppermute | solution.py:138
  23.8 4.9 %collective-permute-start.2 = (bf16[128,1536]{1,0:T(8,128)(2,1)S(1)}, bf16[128,1536]{1,0:T(8,128)(2,1)S(1)}, u32[]{:S(2)}, u32[]{:S(2)}) collective-permute-start(bf16[128,1536]{1,0:T(8,128)(2,1)S(1)} %pad_maximum_fusion.1), channel_id=1, source_target_pairs={{0,12},{1,13},{2,14},{3,15},{4,0},{5,1},{6,2},{7,3},{8,4},{9,5},{1... | collective-permute-start | bytes 1179656 | tf_op jit(solution)/shard_map/ppermute | solution.py:138
  30.7 4.1 %collective-permute-start.4 = (bf16[128,1536]{1,0:T(8,128)(2,1)S(1)}, bf16[128,1536]{1,0:T(8,128)(2,1)S(1)}, u32[]{:S(2)}, u32[]{:S(2)}) collective-permute-start(bf16[128,1536]{1,0:T(8,128)(2,1)S(1)} %pad_maximum_fusion.1), channel_id=1, source_target_pairs={{0,8},{1,9},{2,10},{3,11},{4,12},{5,13},{6,14},{7,15},{8,0},{9,1},... | collective-permute-start | bytes 1179656 | tf_op jit(solution)/shard_map/ppermute | solution.py:138
  34.8 2.6 %collective-permute-done = bf16[128,1536]{1,0:T(8,128)(2,1)S(1)} collective-permute-done((bf16[128,1536]{1,0:T(8,128)(2,1)S(1)}, bf16[128,1536]{1,0:T(8,128)(2,1)S(1)}, u32[]{:S(2)}, u32[]{:S(2)}) %collective-permute-start) | collective-permute-done | bytes 393248 | tf_op jit(solution)/shard_map/ppermute | solution.py:138
  37.5 3.5 %collective-permute-start.5 = (bf16[128,1536]{1,0:T(8,128)(2,1)S(1)}, bf16[128,1536]{1,0:T(8,128)(2,1)S(1)}, u32[]{:S(2)}, u32[]{:S(2)}) collective-permute-start(bf16[128,1536]{1,0:T(8,128)(2,1)S(1)} %collective-permute-done), channel_id=1, source_target_pairs={{0,4},{1,5},{2,6},{3,7},{4,8},{5,9},{6,10},{7,11},{8,12},{9,13},{1... | collective-permute-start | bytes 1179656 | tf_op jit(solution)/shard_map/ppermute | solution.py:138
  41.0 3.8 %collective-permute-done.2 = bf16[128,1536]{1,0:T(8,128)(2,1)S(1)} collective-permute-done((bf16[128,1536]{1,0:T(8,128)(2,1)S(1)}, bf16[128,1536]{1,0:T(8,128)(2,1)S(1)}, u32[]{:S(2)}, u32[]{:S(2)}) %collective-permute-start.2) | collective-permute-done | bytes 393248 | tf_op jit(solution)/shard_map/ppermute | solution.py:138
  44.7 7.1 %collective-permute-done.1 = bf16[128,1536]{1,0:T(8,128)(2,1)S(1)} collective-permute-done((bf16[128,1536]{1,0:T(8,128)(2,1)S(1)}, bf16[128,1536]{1,0:T(8,128)(2,1)S(1)}, u32[]{:S(2)}, u32[]{:S(2)}) %collective-permute-start.1) | collective-permute-done | bytes 393248 | tf_op jit(solution)/shard_map/ppermute | solution.py:138
  55.8 4.4 %collective-permute-start.7 = (bf16[128,1536]{1,0:T(8,128)(2,1)S(1)}, bf16[128,1536]{1,0:T(8,128)(2,1)S(1)}, u32[]{:S(2)}, u32[]{:S(2)}) collective-permute-start(bf16[128,1536]{1,0:T(8,128)(2,1)S(1)} %collective-permute-done.4), channel_id=1, source_target_pairs={{0,2},{1,3},{2,0},{3,1},{4,6},{5,7},{6,4},{7,5},{8,10},{9,11},{10,... | collective-permute-start | bytes 1179656 | tf_op jit(solution)/shard_map/ppermute | solution.py:138
  61.7 5.5 %collective-permute-done.6 = bf16[128,1536]{1,0:T(8,128)(2,1)S(1)} collective-permute-done((bf16[128,1536]{1,0:T(8,128)(2,1)S(1)}, bf16[128,1536]{1,0:T(8,128)(2,1)S(1)}, u32[]{:S(2)}, u32[]{:S(2)}) %collective-permute-start.6) | collective-permute-done | bytes 393248 | tf_op jit(solution)/shard_map/ppermute | solution.py:138
  68.0 5.7 %collective-permute-done.7 = bf16[128,1536]{1,0:T(8,128)(2,1)S(1)} collective-permute-done((bf16[128,1536]{1,0:T(8,128)(2,1)S(1)}, bf16[128,1536]{1,0:T(8,128)(2,1)S(1)}, u32[]{:S(2)}, u32[]{:S(2)}) %collective-permute-start.7) | collective-permute-done | bytes 393248 | tf_op jit(solution)/shard_map/ppermute | solution.py:138
  76.7 3.6 %collective-permute-done.8.refs_3_ = bf16[512,1536]{1,0:T(8,128)(2,1)} collective-permute-done((bf16[512,1536]{1,0:T(8,128)(2,1)}, bf16[512,1536]{1,0:T(8,128)(2,1)}, u32[]{:S(2)}, u32[]{:S(2)}) %collective-permute-start.8) | collective-permute-done | bytes 1572896 | tf_op jit(solution)/shard_map/ppermute | solution.py:127
  80.2 5.0 %all-to-all-done = bf16[32,160,128]{2,1,0:T(8,128)(2,1)S(1)} async-done(((bf16[32,160,128]{2,1,0:T(8,128)(2,1)}), bf16[32,160,128]{2,1,0:T(8,128)(2,1)S(1)}, u32[]{:S(2)}, u32[]{:S(2)}) %all-to-all-start) | async-done | bytes 1310752 | tf_op jit(solution)/shard_map/all_to_all | solution.py:119
  85.2 7.5 %shard_map.102 = (bf16[160,32,128]{2,1,0:T(8,128)(2,1)}, bf16[160,1536]{1,0:T(8,128)(2,1)}, bf16[32,160,128]{2,1,0:T(8,128)(2,1)}) custom-call(s32[16]{0:T(128)S(1)} %stack.78.numbers, bf16[160,32,128]{2,1,0:T(8,128)(2,1)S(1)} %bitcast.31, bf16[512,1536]{1,0:T(8,128)(2,1)S(1)} %pad_maximum_fusion.refs_0_, bf16[512,1536]{1,0:T(8,128)(2,1)} %collective-permute-done.3.refs_1_, ...), custom_call_target="tpu_custom_call" | custom-call | tf_op jit(solution)/shard_map/pallas_call | solution.py:45
  92.8 7.7 %all-to-all-start.1 = ((bf16[32,160,128]{2,1,0:T(8,128)(2,1)}), bf16[32,160,128]{2,1,0:T(8,128)(2,1)S(1)}, u32[]{:S(2)}, u32[]{:S(2)}) async-start(bf16[32,160,128]{2,1,0:T(8,128)(2,1)} %bitcast.35), calls=%async_computation.1 | async-start | bytes 2621440 | tf_op jit(solution)/shard_map/all_to_all | solution.py:119
  106.4 3.3 %shard_map.104 = (bf16[128,1536]{1,0:T(8,128)(2,1)S(1)}, bf16[128,1536]{1,0:T(8,128)(2,1)S(1)}, bf16[128,1536]{1,0:T(8,128)(2,1)S(1)}, bf16[128,1536]{1,0:T(8,12...) custom-call(s32[8]{0:T(128)S(1)} %stack.79.numbers, ...), custom_call_target="tpu_custom_call" | custom-call | tf_op jit(solution)/shard_map/pallas_call | solution.py:45
  109.7 4.8 %collective-permute-start.13 = (bf16[128,1536]{1,0:T(8,128)(2,1)S(1)}, bf16[128,1536]{1,0:T(8,128)(2,1)S(1)}, u32[]{:S(2)}, u32[]{:S(2)}) collective-permute-start(bf16[128,1536]{1,0:T(8,128)(2,1)S(1)} %get-tuple-element.41), channel_id=1, source_target_pairs={{0,2},{1,3},{2,0},{3,1},{4,6},{5,7},{6,4},{7,5},{8,10},{9,11},{10,... | collective-permute-start | bytes 1179656 | tf_op jit(solution)/shard_map/ppermute | solution.py:138
  114.5 3.6 %collective-permute-start.11 = (bf16[128,1536]{1,0:T(8,128)(2,1)S(1)}, bf16[128,1536]{1,0:T(8,128)(2,1)S(1)}, u32[]{:S(2)}, u32[]{:S(2)}) collective-permute-start(bf16[128,1536]{1,0:T(8,128)(2,1)S(1)} %get-tuple-element.38), channel_id=1, source_target_pairs={{0,4},{1,5},{2,6},{3,7},{4,8},{5,9},{6,10},{7,11},{8,12},{9,13},{1... | collective-permute-start | bytes 1179656 | tf_op jit(solution)/shard_map/ppermute | solution.py:138
  118.1 3.4 %collective-permute-start.12 = (bf16[128,1536]{1,0:T(8,128)(2,1)S(1)}, bf16[128,1536]{1,0:T(8,128)(2,1)S(1)}, u32[]{:S(2)}, u32[]{:S(2)}) collective-permute-start(bf16[128,1536]{1,0:T(8,128)(2,1)S(1)} %get-tuple-element.39), channel_id=1, source_target_pairs={{0,12},{1,13},{2,14},{3,15},{4,0},{5,1},{6,2},{7,3},{8,4},{9,5},{1... | collective-permute-start | bytes 1179656 | tf_op jit(solution)/shard_map/ppermute | solution.py:138
  124.0 4.6 %collective-permute-start.16 = (bf16[128,1536]{1,0:T(8,128)(2,1)S(1)}, bf16[128,1536]{1,0:T(8,128)(2,1)S(1)}, u32[]{:S(2)}, u32[]{:S(2)}) collective-permute-start(bf16[128,1536]{1,0:T(8,128)(2,1)S(1)} %get-tuple-element.44), channel_id=1, source_target_pairs={{0,12},{1,13},{2,14},{3,15},{4,0},{5,1},{6,2},{7,3},{8,4},{9,5},{1... | collective-permute-start | bytes 1179656 | tf_op jit(solution)/shard_map/ppermute | solution.py:138
  130.7 14.9 %collective-permute-done.15 = bf16[128,1536]{1,0:T(8,128)(2,1)S(1)} collective-permute-done((bf16[128,1536]{1,0:T(8,128)(2,1)S(1)}, bf16[128,1536]{1,0:T(8,128)(2,1)S(1)}, u32[]{:S(2)}, u32[]{:S(2)}) %collective-permute-start.15) | collective-permute-done | bytes 393248 | tf_op jit(solution)/shard_map/ppermute | solution.py:138
  148.3 13.4 %collective-permute-done.17 = bf16[128,1536]{1,0:T(8,128)(2,1)S(1)} collective-permute-done((bf16[128,1536]{1,0:T(8,128)(2,1)S(1)}, bf16[128,1536]{1,0:T(8,128)(2,1)S(1)}, u32[]{:S(2)}, u32[]{:S(2)}) %collective-permute-start.17) | collective-permute-done | bytes 393248 | tf_op jit(solution)/shard_map/ppermute | solution.py:138
  162.7 3.1 %all-to-all-done.1 = bf16[32,160,128]{2,1,0:T(8,128)(2,1)S(1)} async-done(((bf16[32,160,128]{2,1,0:T(8,128)(2,1)}), bf16[32,160,128]{2,1,0:T(8,128)(2,1)S(1)}, u32[]{:S(2)}, u32[]{:S(2)}) %all-to-all-start.1) | async-done | bytes 1310752 | tf_op jit(solution)/shard_map/all_to_all | solution.py:119
  (44 shorter events, 26.8 us)
Async XLA Ops:
  3.6 16.9 %copy-start.3 = (bf16[1,128,512]{2,1,0:T(8,128)(2,1)S(1)}, bf16[1,128,512]{2,1,0:T(8,128)(2,1)}, u32[]{:S(2)}) copy-start(bf16[1,128,512]{2,1,0:T(8,128)(2,1)} %param.11) | copy-start | bytes 393220
  3.6 16.9 %copy-start.4 = (bf16[1,128,512]{2,1,0:T(8,128)(2,1)S(1)}, bf16[1,128,512]{2,1,0:T(8,128)(2,1)}, u32[]{:S(2)}) copy-start(bf16[1,128,512]{2,1,0:T(8,128)(2,1)} %param.10) | copy-start | bytes 393220
  3.6 16.9 %copy-start.5 = (bf16[1,128,512]{2,1,0:T(8,128)(2,1)S(1)}, bf16[1,128,512]{2,1,0:T(8,128)(2,1)}, u32[]{:S(2)}) copy-start(bf16[1,128,512]{2,1,0:T(8,128)(2,1)} %param.9) | copy-start | bytes 393220
  3.6 81.6 %all-to-all-start = ((bf16[32,160,128]{2,1,0:T(8,128)(2,1)}), bf16[32,160,128]{2,1,0:T(8,128)(2,1)S(1)}, u32[]{:S(2)}, u32[]{:S(2)}) async-start(bf16[32,160,128]{2,1,0:T(8,128)(2,1)} %bitcast.34), calls=%async_computation | async-start | bytes 2621440 | tf_op jit(solution)/shard_map/all_to_all | solution.py:119
  20.5 16.9 %collective-permute-start = (bf16[128,1536]{1,0:T(8,128)(2,1)S(1)}, bf16[128,1536]{1,0:T(8,128)(2,1)S(1)}, u32[]{:S(2)}, u32[]{:S(2)}) collective-permute-start(bf16[128,1536]{1,0:T(8,128)(2,1)S(1)} %pad_maximum_fusion.1), channel_id=1, source_target_pairs={{0,2},{1,3},{2,0},{3,1},{4,6},{5,7},{6,4},{7,5},{8,10},{9,11},{10,... | collective-permute-start | bytes 1179656 | tf_op jit(solution)/shard_map/ppermute | solution.py:138
  23.8 20.9 %collective-permute-start.2 = (bf16[128,1536]{1,0:T(8,128)(2,1)S(1)}, bf16[128,1536]{1,0:T(8,128)(2,1)S(1)}, u32[]{:S(2)}, u32[]{:S(2)}) collective-permute-start(bf16[128,1536]{1,0:T(8,128)(2,1)S(1)} %pad_maximum_fusion.1), channel_id=1, source_target_pairs={{0,12},{1,13},{2,14},{3,15},{4,0},{5,1},{6,2},{7,3},{8,4},{9,5},{1... | collective-permute-start | bytes 1179656 | tf_op jit(solution)/shard_map/ppermute | solution.py:138
  28.8 23.0 %collective-permute-start.1 = (bf16[128,1536]{1,0:T(8,128)(2,1)S(1)}, bf16[128,1536]{1,0:T(8,128)(2,1)S(1)}, u32[]{:S(2)}, u32[]{:S(2)}) collective-permute-start(bf16[128,1536]{1,0:T(8,128)(2,1)S(1)} %pad_maximum_fusion.1), channel_id=1, source_target_pairs={{0,4},{1,5},{2,6},{3,7},{4,8},{5,9},{6,10},{7,11},{8,12},{9,13},{1... | collective-permute-start | bytes 1179656 | tf_op jit(solution)/shard_map/ppermute | solution.py:138
  30.7 25.1 %collective-permute-start.4 = (bf16[128,1536]{1,0:T(8,128)(2,1)S(1)}, bf16[128,1536]{1,0:T(8,128)(2,1)S(1)}, u32[]{:S(2)}, u32[]{:S(2)}) collective-permute-start(bf16[128,1536]{1,0:T(8,128)(2,1)S(1)} %pad_maximum_fusion.1), channel_id=1, source_target_pairs={{0,8},{1,9},{2,10},{3,11},{4,12},{5,13},{6,14},{7,15},{8,0},{9,1},... | collective-permute-start | bytes 1179656 | tf_op jit(solution)/shard_map/ppermute | solution.py:138
  37.5 23.5 %collective-permute-start.5 = (bf16[128,1536]{1,0:T(8,128)(2,1)S(1)}, bf16[128,1536]{1,0:T(8,128)(2,1)S(1)}, u32[]{:S(2)}, u32[]{:S(2)}) collective-permute-start(bf16[128,1536]{1,0:T(8,128)(2,1)S(1)} %collective-permute-done), channel_id=1, source_target_pairs={{0,4},{1,5},{2,6},{3,7},{4,8},{5,9},{6,10},{7,11},{8,12},{9,13},{1... | collective-permute-start | bytes 1179656 | tf_op jit(solution)/shard_map/ppermute | solution.py:138
  51.9 24.7 %collective-permute-start.3 = (bf16[512,1536]{1,0:T(8,128)(2,1)S(1)}, bf16[512,1536]{1,0:T(8,128)(2,1)}, u32[]{:S(2)}, u32[]{:S(2)}) collective-permute-start(bf16[512,1536]{1,0:T(8,128)(2,1)S(1)} %pad_maximum_fusion.refs_0_), channel_id=1, source_target_pairs={{0,1},{1,0},{2,3},{3,2},{4,5},{5,4},{6,7},{7,6},{8,9},{9,8},{10,11... | collective-permute-start | bytes 4718600 | tf_op jit(solution)/shard_map/ppermute | solution.py:127
  53.8 13.4 %collective-permute-start.6 = (bf16[128,1536]{1,0:T(8,128)(2,1)S(1)}, bf16[128,1536]{1,0:T(8,128)(2,1)S(1)}, u32[]{:S(2)}, u32[]{:S(2)}) collective-permute-start(bf16[128,1536]{1,0:T(8,128)(2,1)S(1)} %collective-permute-done), channel_id=1, source_target_pairs={{0,12},{1,13},{2,14},{3,15},{4,0},{5,1},{6,2},{7,3},{8,4},{9,5},{1... | collective-permute-start | bytes 1179656 | tf_op jit(solution)/shard_map/ppermute | solution.py:138
  55.8 18.0 %collective-permute-start.7 = (bf16[128,1536]{1,0:T(8,128)(2,1)S(1)}, bf16[128,1536]{1,0:T(8,128)(2,1)S(1)}, u32[]{:S(2)}, u32[]{:S(2)}) collective-permute-start(bf16[128,1536]{1,0:T(8,128)(2,1)S(1)} %collective-permute-done.4), channel_id=1, source_target_pairs={{0,2},{1,3},{2,0},{3,1},{4,6},{5,7},{6,4},{7,5},{8,10},{9,11},{10,... | collective-permute-start | bytes 1179656 | tf_op jit(solution)/shard_map/ppermute | solution.py:138
  74.6 5.6 %collective-permute-start.8 = (bf16[512,1536]{1,0:T(8,128)(2,1)}, bf16[512,1536]{1,0:T(8,128)(2,1)}, u32[]{:S(2)}, u32[]{:S(2)}) collective-permute-start(bf16[512,1536]{1,0:T(8,128)(2,1)} %constant_dynamic-update-slice_fusion.refs_2_), channel_id=1, source_target_pairs={{0,1},{1,0},{2,3},{3,2},{4,5},{5,4},{6,7},{7,6},{8,9},{9,8},{10,11... | collective-permute-start | bytes 4718600 | tf_op jit(solution)/shard_map/ppermute | solution.py:127
  92.7 9.7 %copy-start.1 = (bf16[160,1536]{1,0:T(8,128)(2,1)S(1)}, bf16[160,1536]{1,0:T(8,128)(2,1)}, u32[]{:S(2)}) copy-start(bf16[160,1536]{1,0:T(8,128)(2,1)} %get-tuple-element.36.own_sides) | copy-start | bytes 1474564
  92.8 73.0 %all-to-all-start.1 = ((bf16[32,160,128]{2,1,0:T(8,128)(2,1)}), bf16[32,160,128]{2,1,0:T(8,128)(2,1)S(1)}, u32[]{:S(2)}, u32[]{:S(2)}) async-start(bf16[32,160,128]{2,1,0:T(8,128)(2,1)} %bitcast.35), calls=%async_computation.1 | async-start | bytes 2621440 | tf_op jit(solution)/shard_map/all_to_all | solution.py:119
  100.5 6.0 %collective-permute-start.9 = (bf16[32,160,128]{2,1,0:T(8,128)(2,1)S(1)}, bf16[32,160,128]{2,1,0:T(8,128)(2,1)}, u32[]{:S(2)}, u32[]{:S(2)}) collective-permute-start(bf16[32,160,128]{2,1,0:T(8,128)(2,1)S(1)} %copy-done), channel_id=1, source_target_pairs={{0,1},{1,0},{2,3},{3,2},{4,5},{5,4},{6,7},{7,6},{8,9},{9,8},{10,11... | collective-permute-start | bytes 3932168 | tf_op jit(solution)/shard_map/ppermute | solution.py:127
  102.4 4.0 %collective-permute-start.10 = (bf16[160,1536]{1,0:T(8,128)(2,1)S(1)}, bf16[160,1536]{1,0:T(8,128)(2,1)}, u32[]{:S(2)}, u32[]{:S(2)}) collective-permute-start(bf16[160,1536]{1,0:T(8,128)(2,1)S(1)} %copy-done.1), channel_id=1, source_target_pairs={{0,1},{1,0},{2,3},{3,2},{4,5},{5,4},{6,7},{7,6},{8,9},{9,8},{10,11... | collective-permute-start | bytes 1474568 | tf_op jit(solution)/shard_map/ppermute | solution.py:127
  109.7 18.9 %collective-permute-start.13 = (bf16[128,1536]{1,0:T(8,128)(2,1)S(1)}, bf16[128,1536]{1,0:T(8,128)(2,1)S(1)}, u32[]{:S(2)}, u32[]{:S(2)}) collective-permute-start(bf16[128,1536]{1,0:T(8,128)(2,1)S(1)} %get-tuple-element.41), channel_id=1, source_target_pairs={{0,2},{1,3},{2,0},{3,1},{4,6},{5,7},{6,4},{7,5},{8,10},{9,11},{10,... | collective-permute-start | bytes 1179656 | tf_op jit(solution)/shard_map/ppermute | solution.py:138
  114.5 33.8 %collective-permute-start.11 = (bf16[128,1536]{1,0:T(8,128)(2,1)S(1)}, bf16[128,1536]{1,0:T(8,128)(2,1)S(1)}, u32[]{:S(2)}, u32[]{:S(2)}) collective-permute-start(bf16[128,1536]{1,0:T(8,128)(2,1)S(1)} %get-tuple-element.38), channel_id=1, source_target_pairs={{0,4},{1,5},{2,6},{3,7},{4,8},{5,9},{6,10},{7,11},{8,12},{9,13},{1... | collective-permute-start | bytes 1179656 | tf_op jit(solution)/shard_map/ppermute | solution.py:138
  118.1 30.2 %collective-permute-start.12 = (bf16[128,1536]{1,0:T(8,128)(2,1)S(1)}, bf16[128,1536]{1,0:T(8,128)(2,1)S(1)}, u32[]{:S(2)}, u32[]{:S(2)}) collective-permute-start(bf16[128,1536]{1,0:T(8,128)(2,1)S(1)} %get-tuple-element.39), channel_id=1, source_target_pairs={{0,12},{1,13},{2,14},{3,15},{4,0},{5,1},{6,2},{7,3},{8,4},{9,5},{1... | collective-permute-start | bytes 1179656 | tf_op jit(solution)/shard_map/ppermute | solution.py:138
  121.6 24.0 %collective-permute-start.15 = (bf16[128,1536]{1,0:T(8,128)(2,1)S(1)}, bf16[128,1536]{1,0:T(8,128)(2,1)S(1)}, u32[]{:S(2)}, u32[]{:S(2)}) collective-permute-start(bf16[128,1536]{1,0:T(8,128)(2,1)S(1)} %get-tuple-element.43), channel_id=1, source_target_pairs={{0,4},{1,5},{2,6},{3,7},{4,8},{5,9},{6,10},{7,11},{8,12},{9,13},{1... | collective-permute-start | bytes 1179656 | tf_op jit(solution)/shard_map/ppermute | solution.py:138
  124.0 21.6 %collective-permute-start.16 = (bf16[128,1536]{1,0:T(8,128)(2,1)S(1)}, bf16[128,1536]{1,0:T(8,128)(2,1)S(1)}, u32[]{:S(2)}, u32[]{:S(2)}) collective-permute-start(bf16[128,1536]{1,0:T(8,128)(2,1)S(1)} %get-tuple-element.44), channel_id=1, source_target_pairs={{0,12},{1,13},{2,14},{3,15},{4,0},{5,1},{6,2},{7,3},{8,4},{9,5},{1... | collective-permute-start | bytes 1179656 | tf_op jit(solution)/shard_map/ppermute | solution.py:138
  128.8 19.6 %collective-permute-start.14 = (bf16[128,1536]{1,0:T(8,128)(2,1)S(1)}, bf16[128,1536]{1,0:T(8,128)(2,1)S(1)}, u32[]{:S(2)}, u32[]{:S(2)}) collective-permute-start(bf16[128,1536]{1,0:T(8,128)(2,1)S(1)} %add_convert_fusion.2), channel_id=1, source_target_pairs={{0,8},{1,9},{2,10},{3,11},{4,12},{5,13},{6,14},{7,15},{8,0},{9,1},... | collective-permute-start | bytes 1179656 | tf_op jit(solution)/shard_map/ppermute | solution.py:138
  145.7 16.0 %collective-permute-start.17 = (bf16[128,1536]{1,0:T(8,128)(2,1)S(1)}, bf16[128,1536]{1,0:T(8,128)(2,1)S(1)}, u32[]{:S(2)}, u32[]{:S(2)}) collective-permute-start(bf16[128,1536]{1,0:T(8,128)(2,1)S(1)} %add_convert_fusion.1), channel_id=1, source_target_pairs={{0,2},{1,3},{2,0},{3,1},{4,6},{5,7},{6,4},{7,5},{8,10},{9,11},{10,... | collective-permute-start | bytes 1179656 | tf_op jit(solution)/shard_map/ppermute | solution.py:138
  (2 other events, 11.8 us)

commit v6 on v5

--- a/solution.py
+++ b/solution.py
@@ -145,13 +145,8 @@
 def gather_weights(shard, chip, core):
     across, two = chip_shift(shard, 0, 1), chip_shift(shard, 2, 0)
     one, three = chip_shift(shard, 1, 0), chip_shift(shard, 3, 0)
-    early = [(shard, 0, 0), (across, 0, 1), (one, 3, 0), (three, 1, 0)]
-    late = [
-        (two, 2, 0),
-        (chip_shift(across, 1, 0), 3, 1),
-        (chip_shift(across, 3, 0), 1, 1),
-        (chip_shift(two, 0, 1), 2, 1),
-    ]
+    early = [(shard, 0, 0), (one, 3, 0), (three, 1, 0), (chip_shift(across, 1, 0), 3, 1)]
+    late = [(across, 0, 1), (two, 2, 0), (chip_shift(across, 3, 0), 1, 1), (chip_shift(two, 0, 1), 2, 1)]
     groups, numbers = [], []
     for parts in (early, late):
         held = jnp.concatenate([part for part, _, _ in parts], axis=0)
@@ -163,61 +158,73 @@
 
 def expert_kernel(numbers, arrived, *refs):
     groups, (back, sides_out, rows_out) = refs[:4], refs[4:7]
-    rows, results, returned, sides, pre, grad_hidden, sems = refs[7:]
+    x_rows, dy_rows, y_blocks, dx_blocks, y_back, dx_back, sides, pre, grad_hidden, sems = refs[7:]
     block = arrived.shape[2]
     blocks = arrived.shape[1] // 2
     hidden_width = sides.shape[1] // 3
-    rows[...] = jnp.swapaxes(arrived[...], 0, 1)
-    stores = [pltpu.make_async_copy(rows, rows_out, sems.at[0])]
-    stores[0].start()
-
-    for first in range(0, 16, 2):
-        weights = groups[first // 4].at[pl.ds(first % 4 * block, 2 * block)]
-        one, two = numbers[first], numbers[first + 1]
-        x = jnp.concatenate([rows[one], rows[two]], axis=1)
-        dy = jnp.concatenate([rows[blocks + one], rows[blocks + two]], axis=1)
-        x_part = jnp.dot(x, weights[:, : 2 * hidden_width], preferred_element_type=jnp.float32)
-        dy_part = jnp.dot(dy, weights[:, 2 * hidden_width :], preferred_element_type=jnp.float32)
-        if first == 0:
-            pre[...] = x_part
-            grad_hidden[...] = dy_part
-        else:
-            pre[...] += x_part
-            grad_hidden[...] += dy_part
-
+    stores = []
+
+    def store(source, target):
+        stores.append(pltpu.make_async_copy(source, target, sems.at[len(stores)]))
+        stores[-1].start()
+
+    pairs = [
+        group.at[pl.ds(start, 2 * block)]
+        for group in groups
+        for start in range(0, group.shape[0], 2 * block)
+    ]
+
+    def product(rows, columns, total):
+        for place, weights in enumerate(pairs):
+            both = [rows[numbers[2 * place + half]] for half in range(2)]
+            part = jnp.dot(
+                jnp.concatenate(both, axis=1),
+                weights[:, columns],
+                preferred_element_type=jnp.float32,
+            )
+            if place == 0:
+                total[...] = part
+            else:
+                total[...] += part
+
+    def back_product(left, columns, result):
+        for place, weights in enumerate(pairs):
+            part = contract_cols(left, weights[:, columns]).astype(result.dtype)
+            for half in range(2):
+                result[numbers[2 * place + half]] = part[:, half * block : (half + 1) * block]
+
+    gate_up, down = slice(0, 2 * hidden_width), slice(2 * hidden_width, 3 * hidden_width)
+    x_rows[...] = jnp.swapaxes(arrived[:, :blocks], 0, 1)
+    store(x_rows, rows_out.at[pl.ds(0, blocks)])
+    dy_rows[...] = jnp.swapaxes(arrived[:, blocks:], 0, 1)
+    store(dy_rows, rows_out.at[pl.ds(blocks, blocks)])
+
+    product(x_rows, gate_up, pre)
+    product(dy_rows, down, grad_hidden)
     gate_pre = pre[:, :hidden_width]
     up_proj = pre[:, hidden_width:]
     upstream = grad_hidden[...]
     sigmoid_gate = jax.nn.sigmoid(gate_pre)
     activated = gate_pre * sigmoid_gate
+    hidden = (activated * up_proj).astype(sides.dtype)
+    sides[:, down] = hidden
     sides[:, :hidden_width] = (
         upstream * up_proj * sigmoid_gate * (1.0 + gate_pre * (1.0 - sigmoid_gate))
     ).astype(sides.dtype)
     sides[:, hidden_width : 2 * hidden_width] = (upstream * activated).astype(sides.dtype)
-    sides[:, 2 * hidden_width :] = (activated * up_proj).astype(sides.dtype)
-    stores.append(pltpu.make_async_copy(sides, sides_out, sems.at[1]))
-    stores[1].start()
-
-    hidden = sides[:, 2 * hidden_width :]
-    grads_pre = sides[:, : 2 * hidden_width]
-    for first in range(0, 16, 2):
-        weights = groups[first // 4].at[pl.ds(first % 4 * block, 2 * block)]
-        y = contract_cols(hidden, weights[:, 2 * hidden_width :]).astype(back.dtype)
-        dx = contract_cols(grads_pre, weights[:, : 2 * hidden_width]).astype(back.dtype)
-        for half in range(2):
-            number = numbers[first + half]
-            results[number] = y[:, half * block : (half + 1) * block]
-            results[blocks + number] = dx[:, half * block : (half + 1) * block]
+    store(sides, sides_out)
+
+    back_product(hidden, down, y_blocks)
+    y_back[...] = jnp.swapaxes(y_blocks[...], 0, 1)
+    store(y_back, back.at[:, pl.ds(0, blocks)])
+    back_product(sides[:, gate_up], gate_up, dx_blocks)
     step = back.shape[0] // 5
     for number in range(5):
         part = pl.ds(number * step, step)
-        returned[part] = jnp.swapaxes(results[:, part], 0, 1)
-        stores.append(
-            pltpu.make_async_copy(returned.at[part], back.at[part], sems.at[2 + number])
-        )
-        stores[-1].start()
-    for store in stores:
-        store.wait()
+        dx_back[part] = jnp.swapaxes(dx_blocks[:, part], 0, 1)
+        store(dx_back.at[part], back.at[part, pl.ds(blocks, blocks)])
+    for copy in stores:
+        copy.wait()
 
 
 def expert_rows(arrived, groups, numbers, hidden_width):
@@ -233,13 +240,12 @@
         arrived,
         *groups,
         scratch_shapes=[
-            pltpu.VMEM((blocks, row_count, lanes), arrived.dtype),
-            pltpu.VMEM((blocks, row_count, lanes), arrived.dtype),
-            pltpu.VMEM(arrived.shape, arrived.dtype),
+            *[pltpu.VMEM((blocks // 2, row_count, lanes), arrived.dtype)] * 4,
+            *[pltpu.VMEM((row_count, blocks // 2, lanes), arrived.dtype)] * 2,
             pltpu.VMEM((row_count, 3 * hidden_width), arrived.dtype),
             pltpu.VMEM((row_count, 2 * hidden_width), jnp.float32),
             pltpu.VMEM((row_count, hidden_width), jnp.float32),
-            pltpu.SemaphoreType.DMA((7,)),
+            pltpu.SemaphoreType.DMA((9,)),
         ],
         far_out=True,
     )

time: 170 us -> 165 us (0.971); the launches traced: 167 us -> 164 us
  waiting for transfers between devices: 66.2 us -> 61.5 us
  starting transfers between devices: 80.2 us -> 81.9 us
    ppermute x14, waiting for transfers between devices: 53 us -> 28.8 us  [chip_shift(): return lax.ppermute(array, 'fsdp', pairs)]
    all_to_all x2, waiting for transfers between devices: 8.12 us -> 28.2 us  [exchange(): lax.all_to_all(sent, 'ep', split_axis=0, concat_axis=0, tiled=True)]
    ppermute x14, starting transfers between devices: 47.4 us -> 50.9 us  [chip_shift(): return lax.ppermute(array, 'fsdp', pairs)]
    all_to_all x2, starting transfers between devices: 24.6 us -> 22.3 us  [exchange(): lax.all_to_all(sent, 'ep', split_axis=0, concat_axis=0, tiled=True)]
  transfers between devices with their start and end apart: 20 -> 20, of which waited for: 11 -> 13; matrix products, arithmetic and copies ran while one was open for 3% -> 3% of each run, Pallas kernels for 2% -> 2%
where the time goes in v6:
time: 165 us; the launch traced here: 164 us
  starting transfers between devices  81.9 us (50%)
  waiting for transfers between devices  61.5 us (37%)
  Pallas kernels  15.1 us (9%)
  local copies, waits for them, and re-layouts  4.08 us (2%)
    ppermute x14, starting transfers between devices, chip_shift(): return lax.ppermute(array, 'fsdp', pairs)  50.9 us
    ppermute x14, waiting for transfers between devices, chip_shift(): return lax.ppermute(array, 'fsdp', pairs)  28.8 us
    all_to_all x2, waiting for transfers between devices, exchange(): lax.all_to_all(sent, 'ep', split_axis=0, concat_axis=0, tiled=True)  28.2 us
    all_to_all x2, starting transfers between devices, exchange(): lax.all_to_all(sent, 'ep', split_axis=0, concat_axis=0, tiled=True)  22.3 us
    pallas_call x3, Pallas kernels, vmem_call(): pl.pallas_call(kernel, out_shape=jax.tree.map(lambda s: pltpu.HBM(s.shape...  12.1 us
    ppermute x4, starting transfers between devices, core_swap(): lax.ppermute(array, 'fsdp', [(f, f ^ 1) for f in range(2 * Y * X_HI)])  8.65 us
    ppermute x4, waiting for transfers between devices, core_swap(): lax.ppermute(array, 'fsdp', [(f, f ^ 1) for f in range(2 * Y * X_HI)])  4.56 us
  transfers between devices with their start and end apart: 20, of which 13 were waited for; matrix products, arithmetic and copies ran while one was open for 3% of the time, Pallas kernels for 2%

profile of v6, /device:TPU:6, one launch (start us, length us, event | category | flops | bytes accessed | tf_op | source)
XLA Modules:
  0.0 164.1 jit_solution(16203582943988087155)
XLA Ops:
  0.6 2.9 %shard_map.101 = bf16[160,32,128]{2,1,0:T(8,128)(2,1)} custom-call(s32[1,128]{1,0:T(1,128)} %bitcast.32, bf16[128,2048]{1,0:T(8,128)(2,1)} %tokens.1, bf16[128,2048]{1,0:T(8,128)(2,1)} %cotangent.1), custom_call_target="tpu_custom_call" | custom-call | tf_op jit(solution)/shard_map/pallas_call | solution.py:88
  3.6 16.9 %all-to-all-start = ((bf16[32,160,128]{2,1,0:T(8,128)(2,1)}), bf16[32,160,128]{2,1,0:T(8,128)(2,1)S(1)}, u32[]{:S(2)}, u32[]{:S(2)}) async-start(bf16[32,160,128]{2,1,0:T(8,128)(2,1)} %bitcast.34), calls=%async_computation | async-start | bytes 2621440 | tf_op jit(solution)/shard_map/all_to_all | solution.py:119
  20.5 3.3 %collective-permute-start.2 = (bf16[128,1536]{1,0:T(8,128)(2,1)S(1)}, bf16[128,1536]{1,0:T(8,128)(2,1)S(1)}, u32[]{:S(2)}, u32[]{:S(2)}) collective-permute-start(bf16[128,1536]{1,0:T(8,128)(2,1)S(1)} %pad_maximum_fusion.1), channel_id=1, source_target_pairs={{0,2},{1,3},{2,0},{3,1},{4,6},{5,7},{6,4},{7,5},{8,10},{9,11},{10,... | collective-permute-start | bytes 1179656 | tf_op jit(solution)/shard_map/ppermute | solution.py:138
  23.8 5.1 %collective-permute-start.5 = (bf16[128,1536]{1,0:T(8,128)(2,1)S(1)}, bf16[128,1536]{1,0:T(8,128)(2,1)S(1)}, u32[]{:S(2)}, u32[]{:S(2)}) collective-permute-start(bf16[128,1536]{1,0:T(8,128)(2,1)S(1)} %pad_maximum_fusion.1), channel_id=1, source_target_pairs={{0,8},{1,9},{2,10},{3,11},{4,12},{5,13},{6,14},{7,15},{8,0},{9,1},... | collective-permute-start | bytes 1179656 | tf_op jit(solution)/shard_map/ppermute | solution.py:138
  29.0 3.0 %collective-permute-start.1 = (bf16[128,1536]{1,0:T(8,128)(2,1)S(1)}, bf16[128,1536]{1,0:T(8,128)(2,1)S(1)}, u32[]{:S(2)}, u32[]{:S(2)}) collective-permute-start(bf16[128,1536]{1,0:T(8,128)(2,1)S(1)} %pad_maximum_fusion.1), channel_id=1, source_target_pairs={{0,12},{1,13},{2,14},{3,15},{4,0},{5,1},{6,2},{7,3},{8,4},{9,5},{1... | collective-permute-start | bytes 1179656 | tf_op jit(solution)/shard_map/ppermute | solution.py:138
  31.9 2.9 %collective-permute-start = (bf16[128,1536]{1,0:T(8,128)(2,1)S(1)}, bf16[128,1536]{1,0:T(8,128)(2,1)S(1)}, u32[]{:S(2)}, u32[]{:S(2)}) collective-permute-start(bf16[128,1536]{1,0:T(8,128)(2,1)S(1)} %pad_maximum_fusion.1), channel_id=1, source_target_pairs={{0,4},{1,5},{2,6},{3,7},{4,8},{5,9},{6,10},{7,11},{8,12},{9,13},{1... | collective-permute-start | bytes 1179656 | tf_op jit(solution)/shard_map/ppermute | solution.py:138
  37.5 4.9 %collective-permute-start.6 = (bf16[128,1536]{1,0:T(8,128)(2,1)S(1)}, bf16[128,1536]{1,0:T(8,128)(2,1)S(1)}, u32[]{:S(2)}, u32[]{:S(2)}) collective-permute-start(bf16[128,1536]{1,0:T(8,128)(2,1)S(1)} %collective-permute-done.2), channel_id=1, source_target_pairs={{0,12},{1,13},{2,14},{3,15},{4,0},{5,1},{6,2},{7,3},{8,4},{9,5},{1... | collective-permute-start | bytes 1179656 | tf_op jit(solution)/shard_map/ppermute | solution.py:138
  44.3 3.2 %collective-permute-start.7 = (bf16[128,1536]{1,0:T(8,128)(2,1)S(1)}, bf16[128,1536]{1,0:T(8,128)(2,1)S(1)}, u32[]{:S(2)}, u32[]{:S(2)}) collective-permute-start(bf16[128,1536]{1,0:T(8,128)(2,1)S(1)} %collective-permute-done.5), channel_id=1, source_target_pairs={{0,2},{1,3},{2,0},{3,1},{4,6},{5,7},{6,4},{7,5},{8,10},{9,11},{10,... | collective-permute-start | bytes 1179656 | tf_op jit(solution)/shard_map/ppermute | solution.py:138
  49.1 5.4 %collective-permute-done.6 = bf16[128,1536]{1,0:T(8,128)(2,1)S(1)} collective-permute-done((bf16[128,1536]{1,0:T(8,128)(2,1)S(1)}, bf16[128,1536]{1,0:T(8,128)(2,1)S(1)}, u32[]{:S(2)}, u32[]{:S(2)}) %collective-permute-start.6) | collective-permute-done | bytes 393248 | tf_op jit(solution)/shard_map/ppermute | solution.py:138
  55.3 3.2 %collective-permute-done.7 = bf16[128,1536]{1,0:T(8,128)(2,1)S(1)} collective-permute-done((bf16[128,1536]{1,0:T(8,128)(2,1)S(1)}, bf16[128,1536]{1,0:T(8,128)(2,1)S(1)}, u32[]{:S(2)}, u32[]{:S(2)}) %collective-permute-start.7) | collective-permute-done | bytes 393248 | tf_op jit(solution)/shard_map/ppermute | solution.py:138
  67.0 18.3 %all-to-all-done = bf16[32,160,128]{2,1,0:T(8,128)(2,1)S(1)} async-done(((bf16[32,160,128]{2,1,0:T(8,128)(2,1)}), bf16[32,160,128]{2,1,0:T(8,128)(2,1)S(1)}, u32[]{:S(2)}, u32[]{:S(2)}) %all-to-all-start) | async-done | bytes 1310752 | tf_op jit(solution)/shard_map/all_to_all | solution.py:119
  85.2 7.2 %shard_map.102 = (bf16[160,32,128]{2,1,0:T(8,128)(2,1)}, bf16[160,1536]{1,0:T(8,128)(2,1)}, bf16[32,160,128]{2,1,0:T(8,128)(2,1)}) custom-call(s32[16]{0:T(128)S(1)} %stack.78.numbers, bf16[160,32,128]{2,1,0:T(8,128)(2,1)S(1)} %bitcast.31, bf16[512,1536]{1,0:T(8,128)(2,1)S(1)} %pad_maximum_fusion.refs_0_, bf16[512,1536]{1,0:T(8,128)(2,1)} %collective-permute-done.4.refs_1_, ...), custom_call_target="tpu_custom_call" | custom-call | tf_op jit(solution)/shard_map/pallas_call | solution.py:45
  92.5 5.5 %all-to-all-start.1 = ((bf16[32,160,128]{2,1,0:T(8,128)(2,1)}), bf16[32,160,128]{2,1,0:T(8,128)(2,1)S(1)}, u32[]{:S(2)}, u32[]{:S(2)}) async-start(bf16[32,160,128]{2,1,0:T(8,128)(2,1)} %bitcast.35), calls=%async_computation.1 | async-start | bytes 2621440 | tf_op jit(solution)/shard_map/all_to_all | solution.py:119
  103.9 3.3 %shard_map.104 = (bf16[128,1536]{1,0:T(8,128)(2,1)S(1)}, bf16[128,1536]{1,0:T(8,128)(2,1)S(1)}, bf16[128,1536]{1,0:T(8,128)(2,1)S(1)}, bf16[128,1536]{1,0:T(8,12...) custom-call(s32[8]{0:T(128)S(1)} %stack.79.numbers, ...), custom_call_target="tpu_custom_call" | custom-call | tf_op jit(solution)/shard_map/pallas_call | solution.py:45
  107.2 3.3 %collective-permute-start.13 = (bf16[128,1536]{1,0:T(8,128)(2,1)S(1)}, bf16[128,1536]{1,0:T(8,128)(2,1)S(1)}, u32[]{:S(2)}, u32[]{:S(2)}) collective-permute-start(bf16[128,1536]{1,0:T(8,128)(2,1)S(1)} %get-tuple-element.41), channel_id=1, source_target_pairs={{0,2},{1,3},{2,0},{3,1},{4,6},{5,7},{6,4},{7,5},{8,10},{9,11},{10,... | collective-permute-start | bytes 1179656 | tf_op jit(solution)/shard_map/ppermute | solution.py:138
  110.5 3.5 %collective-permute-start.11 = (bf16[128,1536]{1,0:T(8,128)(2,1)S(1)}, bf16[128,1536]{1,0:T(8,128)(2,1)S(1)}, u32[]{:S(2)}, u32[]{:S(2)}) collective-permute-start(bf16[128,1536]{1,0:T(8,128)(2,1)S(1)} %get-tuple-element.38), channel_id=1, source_target_pairs={{0,4},{1,5},{2,6},{3,7},{4,8},{5,9},{6,10},{7,11},{8,12},{9,13},{1... | collective-permute-start | bytes 1179656 | tf_op jit(solution)/shard_map/ppermute | solution.py:138
  114.0 3.6 %collective-permute-start.12 = (bf16[128,1536]{1,0:T(8,128)(2,1)S(1)}, bf16[128,1536]{1,0:T(8,128)(2,1)S(1)}, u32[]{:S(2)}, u32[]{:S(2)}) collective-permute-start(bf16[128,1536]{1,0:T(8,128)(2,1)S(1)} %get-tuple-element.39), channel_id=1, source_target_pairs={{0,12},{1,13},{2,14},{3,15},{4,0},{5,1},{6,2},{7,3},{8,4},{9,5},{1... | collective-permute-start | bytes 1179656 | tf_op jit(solution)/shard_map/ppermute | solution.py:138
  119.9 4.8 %collective-permute-start.16 = (bf16[128,1536]{1,0:T(8,128)(2,1)S(1)}, bf16[128,1536]{1,0:T(8,128)(2,1)S(1)}, u32[]{:S(2)}, u32[]{:S(2)}) collective-permute-start(bf16[128,1536]{1,0:T(8,128)(2,1)S(1)} %get-tuple-element.44), channel_id=1, source_target_pairs={{0,12},{1,13},{2,14},{3,15},{4,0},{5,1},{6,2},{7,3},{8,4},{9,5},{1... | collective-permute-start | bytes 1179656 | tf_op jit(solution)/shard_map/ppermute | solution.py:138
  124.9 5.1 %collective-permute-start.14 = (bf16[128,1536]{1,0:T(8,128)(2,1)S(1)}, bf16[128,1536]{1,0:T(8,128)(2,1)S(1)}, u32[]{:S(2)}, u32[]{:S(2)}) collective-permute-start(bf16[128,1536]{1,0:T(8,128)(2,1)S(1)} %add_convert_fusion.2), channel_id=1, source_target_pairs={{0,8},{1,9},{2,10},{3,11},{4,12},{5,13},{6,14},{7,15},{8,0},{9,1},... | collective-permute-start | bytes 1179656 | tf_op jit(solution)/shard_map/ppermute | solution.py:138
  130.1 3.2 %collective-permute-done.15 = bf16[128,1536]{1,0:T(8,128)(2,1)S(1)} collective-permute-done((bf16[128,1536]{1,0:T(8,128)(2,1)S(1)}, bf16[128,1536]{1,0:T(8,128)(2,1)S(1)}, u32[]{:S(2)}, u32[]{:S(2)}) %collective-permute-start.15) | collective-permute-done | bytes 393248 | tf_op jit(solution)/shard_map/ppermute | solution.py:138
  133.2 3.1 %collective-permute-done.16 = bf16[128,1536]{1,0:T(8,128)(2,1)S(1)} collective-permute-done((bf16[128,1536]{1,0:T(8,128)(2,1)S(1)}, bf16[128,1536]{1,0:T(8,128)(2,1)S(1)}, u32[]{:S(2)}, u32[]{:S(2)}) %collective-permute-start.16) | collective-permute-done | bytes 393248 | tf_op jit(solution)/shard_map/ppermute | solution.py:138
  136.5 4.0 %collective-permute-start.17 = (bf16[128,1536]{1,0:T(8,128)(2,1)S(1)}, bf16[128,1536]{1,0:T(8,128)(2,1)S(1)}, u32[]{:S(2)}, u32[]{:S(2)}) collective-permute-start(bf16[128,1536]{1,0:T(8,128)(2,1)S(1)} %add_convert_fusion.1), channel_id=1, source_target_pairs={{0,2},{1,3},{2,0},{3,1},{4,6},{5,7},{6,4},{7,5},{8,10},{9,11},{10,... | collective-permute-start | bytes 1179656 | tf_op jit(solution)/shard_map/ppermute | solution.py:138
  142.8 8.8 %collective-permute-done.17 = bf16[128,1536]{1,0:T(8,128)(2,1)S(1)} collective-permute-done((bf16[128,1536]{1,0:T(8,128)(2,1)S(1)}, bf16[128,1536]{1,0:T(8,128)(2,1)S(1)}, u32[]{:S(2)}, u32[]{:S(2)}) %collective-permute-start.17) | collective-permute-done | bytes 393248 | tf_op jit(solution)/shard_map/ppermute | solution.py:138
  152.6 9.9 %all-to-all-done.1 = bf16[32,160,128]{2,1,0:T(8,128)(2,1)S(1)} async-done(((bf16[32,160,128]{2,1,0:T(8,128)(2,1)}), bf16[32,160,128]{2,1,0:T(8,128)(2,1)S(1)}, u32[]{:S(2)}, u32[]{:S(2)}) %all-to-all-start.1) | async-done | bytes 1310752 | tf_op jit(solution)/shard_map/all_to_all | solution.py:119
  (44 shorter events, 28.8 us)
Async XLA Ops:
  3.6 16.9 %copy-start.3 = (bf16[1,128,512]{2,1,0:T(8,128)(2,1)S(1)}, bf16[1,128,512]{2,1,0:T(8,128)(2,1)}, u32[]{:S(2)}) copy-start(bf16[1,128,512]{2,1,0:T(8,128)(2,1)} %param.11) | copy-start | bytes 393220
  3.6 16.9 %copy-start.4 = (bf16[1,128,512]{2,1,0:T(8,128)(2,1)S(1)}, bf16[1,128,512]{2,1,0:T(8,128)(2,1)}, u32[]{:S(2)}) copy-start(bf16[1,128,512]{2,1,0:T(8,128)(2,1)} %param.10) | copy-start | bytes 393220
  3.6 16.9 %copy-start.5 = (bf16[1,128,512]{2,1,0:T(8,128)(2,1)S(1)}, bf16[1,128,512]{2,1,0:T(8,128)(2,1)}, u32[]{:S(2)}) copy-start(bf16[1,128,512]{2,1,0:T(8,128)(2,1)} %param.9) | copy-start | bytes 393220
  3.6 81.6 %all-to-all-start = ((bf16[32,160,128]{2,1,0:T(8,128)(2,1)}), bf16[32,160,128]{2,1,0:T(8,128)(2,1)S(1)}, u32[]{:S(2)}, u32[]{:S(2)}) async-start(bf16[32,160,128]{2,1,0:T(8,128)(2,1)} %bitcast.34), calls=%async_computation | async-start | bytes 2621440 | tf_op jit(solution)/shard_map/all_to_all | solution.py:119
  20.5 16.9 %collective-permute-start.2 = (bf16[128,1536]{1,0:T(8,128)(2,1)S(1)}, bf16[128,1536]{1,0:T(8,128)(2,1)S(1)}, u32[]{:S(2)}, u32[]{:S(2)}) collective-permute-start(bf16[128,1536]{1,0:T(8,128)(2,1)S(1)} %pad_maximum_fusion.1), channel_id=1, source_target_pairs={{0,2},{1,3},{2,0},{3,1},{4,6},{5,7},{6,4},{7,5},{8,10},{9,11},{10,... | collective-permute-start | bytes 1179656 | tf_op jit(solution)/shard_map/ppermute | solution.py:138
  23.8 20.5 %collective-permute-start.5 = (bf16[128,1536]{1,0:T(8,128)(2,1)S(1)}, bf16[128,1536]{1,0:T(8,128)(2,1)S(1)}, u32[]{:S(2)}, u32[]{:S(2)}) collective-permute-start(bf16[128,1536]{1,0:T(8,128)(2,1)S(1)} %pad_maximum_fusion.1), channel_id=1, source_target_pairs={{0,8},{1,9},{2,10},{3,11},{4,12},{5,13},{6,14},{7,15},{8,0},{9,1},... | collective-permute-start | bytes 1179656 | tf_op jit(solution)/shard_map/ppermute | solution.py:138
  29.0 32.2 %collective-permute-start.1 = (bf16[128,1536]{1,0:T(8,128)(2,1)S(1)}, bf16[128,1536]{1,0:T(8,128)(2,1)S(1)}, u32[]{:S(2)}, u32[]{:S(2)}) collective-permute-start(bf16[128,1536]{1,0:T(8,128)(2,1)S(1)} %pad_maximum_fusion.1), channel_id=1, source_target_pairs={{0,12},{1,13},{2,14},{3,15},{4,0},{5,1},{6,2},{7,3},{8,4},{9,5},{1... | collective-permute-start | bytes 1179656 | tf_op jit(solution)/shard_map/ppermute | solution.py:138
  31.9 29.3 %collective-permute-start = (bf16[128,1536]{1,0:T(8,128)(2,1)S(1)}, bf16[128,1536]{1,0:T(8,128)(2,1)S(1)}, u32[]{:S(2)}, u32[]{:S(2)}) collective-permute-start(bf16[128,1536]{1,0:T(8,128)(2,1)S(1)} %pad_maximum_fusion.1), channel_id=1, source_target_pairs={{0,4},{1,5},{2,6},{3,7},{4,8},{5,9},{6,10},{7,11},{8,12},{9,13},{1... | collective-permute-start | bytes 1179656 | tf_op jit(solution)/shard_map/ppermute | solution.py:138
  37.5 17.0 %collective-permute-start.6 = (bf16[128,1536]{1,0:T(8,128)(2,1)S(1)}, bf16[128,1536]{1,0:T(8,128)(2,1)S(1)}, u32[]{:S(2)}, u32[]{:S(2)}) collective-permute-start(bf16[128,1536]{1,0:T(8,128)(2,1)S(1)} %collective-permute-done.2), channel_id=1, source_target_pairs={{0,12},{1,13},{2,14},{3,15},{4,0},{5,1},{6,2},{7,3},{8,4},{9,5},{1... | collective-permute-start | bytes 1179656 | tf_op jit(solution)/shard_map/ppermute | solution.py:138
  42.4 18.8 %collective-permute-start.3 = (bf16[128,1536]{1,0:T(8,128)(2,1)S(1)}, bf16[128,1536]{1,0:T(8,128)(2,1)S(1)}, u32[]{:S(2)}, u32[]{:S(2)}) collective-permute-start(bf16[128,1536]{1,0:T(8,128)(2,1)S(1)} %collective-permute-done.2), channel_id=1, source_target_pairs={{0,4},{1,5},{2,6},{3,7},{4,8},{5,9},{6,10},{7,11},{8,12},{9,13},{1... | collective-permute-start | bytes 1179656 | tf_op jit(solution)/shard_map/ppermute | solution.py:138
  44.3 14.1 %collective-permute-start.7 = (bf16[128,1536]{1,0:T(8,128)(2,1)S(1)}, bf16[128,1536]{1,0:T(8,128)(2,1)S(1)}, u32[]{:S(2)}, u32[]{:S(2)}) collective-permute-start(bf16[128,1536]{1,0:T(8,128)(2,1)S(1)} %collective-permute-done.5), channel_id=1, source_target_pairs={{0,2},{1,3},{2,0},{3,1},{4,6},{5,7},{6,4},{7,5},{8,10},{9,11},{10,... | collective-permute-start | bytes 1179656 | tf_op jit(solution)/shard_map/ppermute | solution.py:138
  59.3 5.6 %collective-permute-start.8 = (bf16[512,1536]{1,0:T(8,128)(2,1)}, bf16[512,1536]{1,0:T(8,128)(2,1)}, u32[]{:S(2)}, u32[]{:S(2)}) collective-permute-start(bf16[512,1536]{1,0:T(8,128)(2,1)} %constant_dynamic-update-slice_fusion.refs_2_), channel_id=1, source_target_pairs={{0,1},{1,0},{2,3},{3,2},{4,5},{5,4},{6,7},{7,6},{8,9},{9,8},{10,11... | collective-permute-start | bytes 4718600 | tf_op jit(solution)/shard_map/ppermute | solution.py:127
  61.3 5.6 %collective-permute-start.4 = (bf16[512,1536]{1,0:T(8,128)(2,1)S(1)}, bf16[512,1536]{1,0:T(8,128)(2,1)}, u32[]{:S(2)}, u32[]{:S(2)}) collective-permute-start(bf16[512,1536]{1,0:T(8,128)(2,1)S(1)} %pad_maximum_fusion.refs_0_), channel_id=1, source_target_pairs={{0,1},{1,0},{2,3},{3,2},{4,5},{5,4},{6,7},{7,6},{8,9},{9,8},{10,11... | collective-permute-start | bytes 4718600 | tf_op jit(solution)/shard_map/ppermute | solution.py:127
  92.5 70.0 %all-to-all-start.1 = ((bf16[32,160,128]{2,1,0:T(8,128)(2,1)}), bf16[32,160,128]{2,1,0:T(8,128)(2,1)S(1)}, u32[]{:S(2)}, u32[]{:S(2)}) async-start(bf16[32,160,128]{2,1,0:T(8,128)(2,1)} %bitcast.35), calls=%async_computation.1 | async-start | bytes 2621440 | tf_op jit(solution)/shard_map/all_to_all | solution.py:119
  98.0 6.0 %collective-permute-start.9 = (bf16[32,160,128]{2,1,0:T(8,128)(2,1)S(1)}, bf16[32,160,128]{2,1,0:T(8,128)(2,1)}, u32[]{:S(2)}, u32[]{:S(2)}) collective-permute-start(bf16[32,160,128]{2,1,0:T(8,128)(2,1)S(1)} %copy-done), channel_id=1, source_target_pairs={{0,1},{1,0},{2,3},{3,2},{4,5},{5,4},{6,7},{7,6},{8,9},{9,8},{10,11... | collective-permute-start | bytes 3932168 | tf_op jit(solution)/shard_map/ppermute | solution.py:127
  99.9 4.0 %collective-permute-start.10 = (bf16[160,1536]{1,0:T(8,128)(2,1)S(1)}, bf16[160,1536]{1,0:T(8,128)(2,1)}, u32[]{:S(2)}, u32[]{:S(2)}) collective-permute-start(bf16[160,1536]{1,0:T(8,128)(2,1)S(1)} %copy-done.1), channel_id=1, source_target_pairs={{0,1},{1,0},{2,3},{3,2},{4,5},{5,4},{6,7},{7,6},{8,9},{9,8},{10,11... | collective-permute-start | bytes 1474568 | tf_op jit(solution)/shard_map/ppermute | solution.py:127
  107.2 17.6 %collective-permute-start.13 = (bf16[128,1536]{1,0:T(8,128)(2,1)S(1)}, bf16[128,1536]{1,0:T(8,128)(2,1)S(1)}, u32[]{:S(2)}, u32[]{:S(2)}) collective-permute-start(bf16[128,1536]{1,0:T(8,128)(2,1)S(1)} %get-tuple-element.41), channel_id=1, source_target_pairs={{0,2},{1,3},{2,0},{3,1},{4,6},{5,7},{6,4},{7,5},{8,10},{9,11},{10,... | collective-permute-start | bytes 1179656 | tf_op jit(solution)/shard_map/ppermute | solution.py:138
  110.5 30.0 %collective-permute-start.11 = (bf16[128,1536]{1,0:T(8,128)(2,1)S(1)}, bf16[128,1536]{1,0:T(8,128)(2,1)S(1)}, u32[]{:S(2)}, u32[]{:S(2)}) collective-permute-start(bf16[128,1536]{1,0:T(8,128)(2,1)S(1)} %get-tuple-element.38), channel_id=1, source_target_pairs={{0,4},{1,5},{2,6},{3,7},{4,8},{5,9},{6,10},{7,11},{8,12},{9,13},{1... | collective-permute-start | bytes 1179656 | tf_op jit(solution)/shard_map/ppermute | solution.py:138
  114.0 26.5 %collective-permute-start.12 = (bf16[128,1536]{1,0:T(8,128)(2,1)S(1)}, bf16[128,1536]{1,0:T(8,128)(2,1)S(1)}, u32[]{:S(2)}, u32[]{:S(2)}) collective-permute-start(bf16[128,1536]{1,0:T(8,128)(2,1)S(1)} %get-tuple-element.39), channel_id=1, source_target_pairs={{0,12},{1,13},{2,14},{3,15},{4,0},{5,1},{6,2},{7,3},{8,4},{9,5},{1... | collective-permute-start | bytes 1179656 | tf_op jit(solution)/shard_map/ppermute | solution.py:138
  117.6 15.6 %collective-permute-start.15 = (bf16[128,1536]{1,0:T(8,128)(2,1)S(1)}, bf16[128,1536]{1,0:T(8,128)(2,1)S(1)}, u32[]{:S(2)}, u32[]{:S(2)}) collective-permute-start(bf16[128,1536]{1,0:T(8,128)(2,1)S(1)} %get-tuple-element.43), channel_id=1, source_target_pairs={{0,4},{1,5},{2,6},{3,7},{4,8},{5,9},{6,10},{7,11},{8,12},{9,13},{1... | collective-permute-start | bytes 1179656 | tf_op jit(solution)/shard_map/ppermute | solution.py:138
  119.9 16.5 %collective-permute-start.16 = (bf16[128,1536]{1,0:T(8,128)(2,1)S(1)}, bf16[128,1536]{1,0:T(8,128)(2,1)S(1)}, u32[]{:S(2)}, u32[]{:S(2)}) collective-permute-start(bf16[128,1536]{1,0:T(8,128)(2,1)S(1)} %get-tuple-element.44), channel_id=1, source_target_pairs={{0,12},{1,13},{2,14},{3,15},{4,0},{5,1},{6,2},{7,3},{8,4},{9,5},{1... | collective-permute-start | bytes 1179656 | tf_op jit(solution)/shard_map/ppermute | solution.py:138
  124.9 17.9 %collective-permute-start.14 = (bf16[128,1536]{1,0:T(8,128)(2,1)S(1)}, bf16[128,1536]{1,0:T(8,128)(2,1)S(1)}, u32[]{:S(2)}, u32[]{:S(2)}) collective-permute-start(bf16[128,1536]{1,0:T(8,128)(2,1)S(1)} %add_convert_fusion.2), channel_id=1, source_target_pairs={{0,8},{1,9},{2,10},{3,11},{4,12},{5,13},{6,14},{7,15},{8,0},{9,1},... | collective-permute-start | bytes 1179656 | tf_op jit(solution)/shard_map/ppermute | solution.py:138
  136.5 15.1 %collective-permute-start.17 = (bf16[128,1536]{1,0:T(8,128)(2,1)S(1)}, bf16[128,1536]{1,0:T(8,128)(2,1)S(1)}, u32[]{:S(2)}, u32[]{:S(2)}) collective-permute-start(bf16[128,1536]{1,0:T(8,128)(2,1)S(1)} %add_convert_fusion.1), channel_id=1, source_target_pairs={{0,2},{1,3},{2,0},{3,1},{4,6},{5,7},{6,4},{7,5},{8,10},{9,11},{10,... | collective-permute-start | bytes 1179656 | tf_op jit(solution)/shard_map/ppermute | solution.py:138
  151.6 10.9 %copy-start.2 = (s32[128,1]{0,1:T(1,128)S(1)}, s32[128,1]{0,1:T(1,128)}, u32[]{:S(2)}) copy-start(s32[128,1]{0,1:T(1,128)} %param.8) | copy-start | bytes 1540
  (2 other events, 12.9 us)

commit v7 on v6

--- a/solution.py
+++ b/solution.py
@@ -13,10 +13,7 @@
     )
 
 
-def contract_cols(left_rows, right_rows):
-    return lax.dot_general(
-        left_rows, right_rows, (((1,), (1,)), ((), ())), preferred_element_type=jnp.float32
-    )
+STRIDE = 5
 
 
 def slot_matrix(bucket, expert_count, capacity):
@@ -31,7 +28,8 @@
         preferred_element_type=jnp.float32,
     )
     slot = jnp.sum(earlier * chosen, axis=0, keepdims=True).astype(jnp.int32)
-    position = bucket * capacity + slot
+    place = lax.rem(bucket * pow(STRIDE, -1, expert_count), expert_count)
+    position = place * capacity + slot
     targets = lax.broadcasted_iota(jnp.int32, (expert_count * capacity, token_count), 0)
     return jnp.where(targets == position, 1.0, 0.0).astype(jnp.bfloat16)
 
@@ -53,7 +51,18 @@
 
 
 def pack_kernel(
-    expert_count, capacity, bucket, tokens, cotangent, packed, choice, near, result, sems
+    expert_count,
+    capacity,
+    bucket,
+    tokens,
+    cotangent,
+    packed,
+    selector_out,
+    choice,
+    near,
+    result,
+    selector,
+    sems,
 ):
     lookup = pltpu.make_async_copy(bucket, choice, sems.at[4])
     lookup.start()
@@ -64,13 +73,14 @@
     for load in loads:
         load.start()
     lookup.wait()
-    selector = slot_matrix(choice[...], expert_count, capacity)
+    selector[...] = slot_matrix(choice[...], expert_count, capacity)
+    stores = [pltpu.make_async_copy(selector, selector_out, sems.at[5])]
+    stores[0].start()
     lanes = packed.shape[2]
     count = packed.shape[1] // 2
-    stores = []
     for number, load in enumerate(loads):
         load.wait()
-        rows = jnp.dot(selector, near[number], preferred_element_type=jnp.float32)
+        rows = jnp.dot(selector[...], near[number], preferred_element_type=jnp.float32)
         rows = rows.astype(packed.dtype)
         columns = [rows[:, i : i + lanes] for i in range(0, rows.shape[1], lanes)]
         part = pl.ds(number * count, count)
@@ -84,39 +94,48 @@
 
 
 def pack_rows(kernel, out_shape, choice, tokens, cotangent):
+    selector = jax.ShapeDtypeStruct((out_shape.shape[0], tokens.shape[0]), tokens.dtype)
     far = pl.BlockSpec(memory_space=pltpu.HBM)
     return pl.pallas_call(
         kernel,
-        out_shape=pltpu.HBM(out_shape.shape, out_shape.dtype),
+        out_shape=tuple(pltpu.HBM(shape.shape, shape.dtype) for shape in (out_shape, selector)),
         in_specs=[far, far, far],
-        out_specs=far,
+        out_specs=(far, far),
         scratch_shapes=[
             pltpu.VMEM(choice.shape, choice.dtype),
             pltpu.VMEM((2, *tokens.shape), tokens.dtype),
             pltpu.VMEM(out_shape.shape, out_shape.dtype),
-            pltpu.SemaphoreType.DMA((5,)),
+            pltpu.VMEM(selector.shape, selector.dtype),
+            pltpu.SemaphoreType.DMA((6,)),
         ],
         compiler_params=pltpu.CompilerParams(vmem_limit_bytes=20 * 1024 * 1024),
     )(*(pltpu.with_memory_space_constraint(a, pltpu.HBM) for a in (choice, tokens, cotangent)))
 
 
-def unpack_kernel(expert_count, capacity, bucket, back, outputs, input_grad):
-    selector = slot_matrix(bucket[...], expert_count, capacity)
+def unpack_kernel(selector, back, outputs, input_grad, results, sems):
     lanes = back.shape[2]
-    blocks = jnp.swapaxes(back[...], 0, 1)
-    count = blocks.shape[0] // 2
-    for first, result in ((0, outputs), (count, input_grad)):
+    count = back.shape[1] // 2
+    stores = []
+    for number, target in enumerate((outputs, input_grad)):
+        blocks = jnp.swapaxes(back[:, number * count : (number + 1) * count], 0, 1)
         for pair in range(0, count, 2):
-            rows = jnp.concatenate([blocks[first + pair], blocks[first + pair + 1]], axis=1)
-            result[:, pair * lanes : (pair + 2) * lanes] = contract_rows(selector, rows).astype(
-                result.dtype
-            )
+            rows = jnp.concatenate([blocks[pair], blocks[pair + 1]], axis=1)
+            results[number, :, pair * lanes : (pair + 2) * lanes] = contract_rows(
+                selector[...], rows
+            ).astype(results.dtype)
+        stores.append(pltpu.make_async_copy(results.at[number], target, sems.at[number]))
+        stores[-1].start()
+    for store in stores:
+        store.wait()
 
 
 def exchange(rows, expert_count):
     row_count, blocks, lanes = rows.shape
     sent = rows.reshape(expert_count, row_count // expert_count * blocks, lanes)
-    arrived = lax.all_to_all(sent, "ep", split_axis=0, concat_axis=0, tiled=True)
+    order = [number * STRIDE % expert_count for number in range(expert_count)]
+    arrived = lax.all_to_all(
+        sent, "ep", split_axis=0, concat_axis=0, tiled=True, axis_index_groups=[order]
+    )
     return arrived.reshape(rows.shape)
 
 
@@ -188,8 +207,10 @@
                 total[...] += part
 
     def back_product(left, columns, result):
+        left = left.T
         for place, weights in enumerate(pairs):
-            part = contract_cols(left, weights[:, columns]).astype(result.dtype)
+            part = jnp.dot(weights[:, columns], left, preferred_element_type=jnp.float32)
+            part = part.T.astype(result.dtype)
             for half in range(2):
                 result[numbers[2 * place + half]] = part[:, half * block : (half + 1) * block]
 
@@ -278,7 +299,7 @@
     blocked = jax.ShapeDtypeStruct(
         (slot_rows, 2 * model_width // shard_width, shard_width), tokens.dtype
     )
-    packed = pack_rows(functools.partial(pack_kernel, *sizes), blocked, choice, tokens, cotangent)
+    packed, selector = pack_rows(functools.partial(pack_kernel, *sizes), blocked, choice, tokens, cotangent)
     packed, w_gate, w_up, w_down = lax.optimization_barrier((packed, w_gate, w_up, w_down))
     arrived = exchange(packed, expert_count)
     shard = jnp.concatenate([w_gate[0], w_up[0], w_down[0]], axis=1)
@@ -321,7 +342,16 @@
     grad_wd = grads[None, :, 2 * hidden_width :]
     result = jax.ShapeDtypeStruct(tokens.shape, tokens.dtype)
     outputs, input_grad = vmem_call(
-        functools.partial(unpack_kernel, *sizes), (result, result), None, choice, back
+        unpack_kernel,
+        (result, result),
+        None,
+        selector,
+        back,
+        scratch_shapes=[
+            pltpu.VMEM((2, *tokens.shape), tokens.dtype),
+            pltpu.SemaphoreType.DMA((2,)),
+        ],
+        far_out=True,
     )
     return (outputs, input_grad, grad_wg, grad_wu, grad_wd)
 

time: 165 us -> 167 us (1.012)
  waiting for transfers between devices: 61.5 us -> 64.3 us
  transfers between devices with their start and end apart: 20 -> 20, of which waited for: 13 -> 12; matrix products, arithmetic and copies ran while one was open for 3% -> 3% of each run, Pallas kernels for 2% -> 2%
where the time goes in v7:
time: 167 us; the launch traced here: 166 us
  starting transfers between devices  80.7 us (48%)
  waiting for transfers between devices  64.3 us (39%)
  Pallas kernels  15.2 us (9%)
  local copies, waits for them, and re-layouts  4.1 us (2%)
    ppermute x14, starting transfers between devices, chip_shift(): return lax.ppermute(array, 'fsdp', pairs)  49.9 us
    ppermute x14, waiting for transfers between devices, chip_shift(): return lax.ppermute(array, 'fsdp', pairs)  29.9 us
    all_to_all x2, waiting for transfers between devices, exchange(): lax.all_to_all(sent, 'ep', split_axis=0, concat_axis=0, tiled=True, axis_...  29.8 us
    all_to_all x2, starting transfers between devices, exchange(): lax.all_to_all(sent, 'ep', split_axis=0, concat_axis=0, tiled=True, axis_...  22.1 us
    pallas_call x3, Pallas kernels, vmem_call(): pl.pallas_call(kernel, out_shape=jax.tree.map(lambda s: pltpu.HBM(s.shape...  12.3 us
    ppermute x4, starting transfers between devices, core_swap(): lax.ppermute(array, 'fsdp', [(f, f ^ 1) for f in range(2 * Y * X_HI)])  8.65 us
    ppermute x4, waiting for transfers between devices, core_swap(): lax.ppermute(array, 'fsdp', [(f, f ^ 1) for f in range(2 * Y * X_HI)])  4.56 us
  transfers between devices with their start and end apart: 20, of which 12 were waited for; matrix products, arithmetic and copies ran while one was open for 3% of the time, Pallas kernels for 2%

profile of v7, /device:TPU:6, one launch (start us, length us, event | category | flops | bytes accessed | tf_op | source)
XLA Modules:
  0.0 165.9 jit_solution(4971191263073169804)
XLA Ops:
  0.6 2.9 %shard_map.101 = (bf16[160,32,128]{2,1,0:T(8,128)(2,1)}, bf16[160,128]{1,0:T(8,128)(2,1)}) custom-call(s32[1,128]{1,0:T(1,128)} %bitcast.40, bf16[128,2048]{1,0:T(8,128)(2,1)} %tokens.1, bf16[128,2048]{1,0:T(8,128)(2,1)} %cotangent.1), custom_call_target="tpu_custom_call" | custom-call | tf_op jit(solution)/shard_map/pallas_call | solution.py:99
  3.6 16.9 %all-to-all-start = ((bf16[32,160,128]{2,1,0:T(8,128)(2,1)}), bf16[32,160,128]{2,1,0:T(8,128)(2,1)S(1)}, u32[]{:S(2)}, u32[]{:S(2)}) async-start(bf16[32,160,128]{2,1,0:T(8,128)(2,1)} %bitcast.32), calls=%async_computation | async-start | bytes 2621440 | tf_op jit(solution)/shard_map/all_to_all | solution.py:136
  20.5 3.3 %collective-permute-start.2 = (bf16[128,1536]{1,0:T(8,128)(2,1)S(1)}, bf16[128,1536]{1,0:T(8,128)(2,1)S(1)}, u32[]{:S(2)}, u32[]{:S(2)}) collective-permute-start(bf16[128,1536]{1,0:T(8,128)(2,1)S(1)} %pad_maximum_fusion.1), channel_id=1, source_target_pairs={{0,2},{1,3},{2,0},{3,1},{4,6},{5,7},{6,4},{7,5},{8,10},{9,11},{10,... | collective-permute-start | bytes 1179656 | tf_op jit(solution)/shard_map/ppermute | solution.py:157
  23.9 5.1 %collective-permute-start.5 = (bf16[128,1536]{1,0:T(8,128)(2,1)S(1)}, bf16[128,1536]{1,0:T(8,128)(2,1)S(1)}, u32[]{:S(2)}, u32[]{:S(2)}) collective-permute-start(bf16[128,1536]{1,0:T(8,128)(2,1)S(1)} %pad_maximum_fusion.1), channel_id=1, source_target_pairs={{0,8},{1,9},{2,10},{3,11},{4,12},{5,13},{6,14},{7,15},{8,0},{9,1},... | collective-permute-start | bytes 1179656 | tf_op jit(solution)/shard_map/ppermute | solution.py:157
  29.0 3.0 %collective-permute-start.1 = (bf16[128,1536]{1,0:T(8,128)(2,1)S(1)}, bf16[128,1536]{1,0:T(8,128)(2,1)S(1)}, u32[]{:S(2)}, u32[]{:S(2)}) collective-permute-start(bf16[128,1536]{1,0:T(8,128)(2,1)S(1)} %pad_maximum_fusion.1), channel_id=1, source_target_pairs={{0,12},{1,13},{2,14},{3,15},{4,0},{5,1},{6,2},{7,3},{8,4},{9,5},{1... | collective-permute-start | bytes 1179656 | tf_op jit(solution)/shard_map/ppermute | solution.py:157
  31.9 2.9 %collective-permute-start = (bf16[128,1536]{1,0:T(8,128)(2,1)S(1)}, bf16[128,1536]{1,0:T(8,128)(2,1)S(1)}, u32[]{:S(2)}, u32[]{:S(2)}) collective-permute-start(bf16[128,1536]{1,0:T(8,128)(2,1)S(1)} %pad_maximum_fusion.1), channel_id=1, source_target_pairs={{0,4},{1,5},{2,6},{3,7},{4,8},{5,9},{6,10},{7,11},{8,12},{9,13},{1... | collective-permute-start | bytes 1179656 | tf_op jit(solution)/shard_map/ppermute | solution.py:157
  34.8 3.0 %collective-permute-done.2 = bf16[128,1536]{1,0:T(8,128)(2,1)S(1)} collective-permute-done((bf16[128,1536]{1,0:T(8,128)(2,1)S(1)}, bf16[128,1536]{1,0:T(8,128)(2,1)S(1)}, u32[]{:S(2)}, u32[]{:S(2)}) %collective-permute-start.2) | collective-permute-done | bytes 393248 | tf_op jit(solution)/shard_map/ppermute | solution.py:157
  37.8 4.9 %collective-permute-start.6 = (bf16[128,1536]{1,0:T(8,128)(2,1)S(1)}, bf16[128,1536]{1,0:T(8,128)(2,1)S(1)}, u32[]{:S(2)}, u32[]{:S(2)}) collective-permute-start(bf16[128,1536]{1,0:T(8,128)(2,1)S(1)} %collective-permute-done.2), channel_id=1, source_target_pairs={{0,12},{1,13},{2,14},{3,15},{4,0},{5,1},{6,2},{7,3},{8,4},{9,5},{1... | collective-permute-start | bytes 1179656 | tf_op jit(solution)/shard_map/ppermute | solution.py:157
  48.8 5.7 %collective-permute-done.6 = bf16[128,1536]{1,0:T(8,128)(2,1)S(1)} collective-permute-done((bf16[128,1536]{1,0:T(8,128)(2,1)S(1)}, bf16[128,1536]{1,0:T(8,128)(2,1)S(1)}, u32[]{:S(2)}, u32[]{:S(2)}) %collective-permute-start.6) | collective-permute-done | bytes 393248 | tf_op jit(solution)/shard_map/ppermute | solution.py:157
  55.3 3.8 %collective-permute-done.7 = bf16[128,1536]{1,0:T(8,128)(2,1)S(1)} collective-permute-done((bf16[128,1536]{1,0:T(8,128)(2,1)S(1)}, bf16[128,1536]{1,0:T(8,128)(2,1)S(1)}, u32[]{:S(2)}, u32[]{:S(2)}) %collective-permute-start.7) | collective-permute-done | bytes 393248 | tf_op jit(solution)/shard_map/ppermute | solution.py:157
  67.6 18.5 %all-to-all-done = bf16[32,160,128]{2,1,0:T(8,128)(2,1)S(1)} async-done(((bf16[32,160,128]{2,1,0:T(8,128)(2,1)}), bf16[32,160,128]{2,1,0:T(8,128)(2,1)S(1)}, u32[]{:S(2)}, u32[]{:S(2)}) %all-to-all-start) | async-done | bytes 1310752 | tf_op jit(solution)/shard_map/all_to_all | solution.py:136
  86.1 7.4 %shard_map.102 = (bf16[160,32,128]{2,1,0:T(8,128)(2,1)}, bf16[160,1536]{1,0:T(8,128)(2,1)}, bf16[32,160,128]{2,1,0:T(8,128)(2,1)}) custom-call(s32[16]{0:T(128)S(1)} %stack.78.numbers, bf16[160,32,128]{2,1,0:T(8,128)(2,1)S(1)} %bitcast.31, bf16[512,1536]{1,0:T(8,128)(2,1)S(1)} %pad_maximum_fusion.refs_0_, bf16[512,1536]{1,0:T(8,128)(2,1)} %collective-permute-done.4.refs_1_, ...), custom_call_target="tpu_custom_call" | custom-call | tf_op jit(solution)/shard_map/pallas_call | solution.py:43
  93.6 5.3 %all-to-all-start.1 = ((bf16[32,160,128]{2,1,0:T(8,128)(2,1)}), bf16[32,160,128]{2,1,0:T(8,128)(2,1)S(1)}, u32[]{:S(2)}, u32[]{:S(2)}) async-start(bf16[32,160,128]{2,1,0:T(8,128)(2,1)} %bitcast.33), calls=%async_computation.1 | async-start | bytes 2621440 | tf_op jit(solution)/shard_map/all_to_all | solution.py:136
  104.8 3.3 %shard_map.104 = (bf16[128,1536]{1,0:T(8,128)(2,1)S(1)}, bf16[128,1536]{1,0:T(8,128)(2,1)S(1)}, bf16[128,1536]{1,0:T(8,128)(2,1)S(1)}, bf16[128,1536]{1,0:T(8,12...) custom-call(s32[8]{0:T(128)S(1)} %stack.79.numbers, ...), custom_call_target="tpu_custom_call" | custom-call | tf_op jit(solution)/shard_map/pallas_call | solution.py:43
  108.1 3.3 %collective-permute-start.13 = (bf16[128,1536]{1,0:T(8,128)(2,1)S(1)}, bf16[128,1536]{1,0:T(8,128)(2,1)S(1)}, u32[]{:S(2)}, u32[]{:S(2)}) collective-permute-start(bf16[128,1536]{1,0:T(8,128)(2,1)S(1)} %get-tuple-element.45), channel_id=1, source_target_pairs={{0,2},{1,3},{2,0},{3,1},{4,6},{5,7},{6,4},{7,5},{8,10},{9,11},{10,... | collective-permute-start | bytes 1179656 | tf_op jit(solution)/shard_map/ppermute | solution.py:157
  111.4 3.5 %collective-permute-start.11 = (bf16[128,1536]{1,0:T(8,128)(2,1)S(1)}, bf16[128,1536]{1,0:T(8,128)(2,1)S(1)}, u32[]{:S(2)}, u32[]{:S(2)}) collective-permute-start(bf16[128,1536]{1,0:T(8,128)(2,1)S(1)} %get-tuple-element.42), channel_id=1, source_target_pairs={{0,4},{1,5},{2,6},{3,7},{4,8},{5,9},{6,10},{7,11},{8,12},{9,13},{1... | collective-permute-start | bytes 1179656 | tf_op jit(solution)/shard_map/ppermute | solution.py:157
  114.9 3.6 %collective-permute-start.12 = (bf16[128,1536]{1,0:T(8,128)(2,1)S(1)}, bf16[128,1536]{1,0:T(8,128)(2,1)S(1)}, u32[]{:S(2)}, u32[]{:S(2)}) collective-permute-start(bf16[128,1536]{1,0:T(8,128)(2,1)S(1)} %get-tuple-element.43), channel_id=1, source_target_pairs={{0,12},{1,13},{2,14},{3,15},{4,0},{5,1},{6,2},{7,3},{8,4},{9,5},{1... | collective-permute-start | bytes 1179656 | tf_op jit(solution)/shard_map/ppermute | solution.py:157
  120.8 4.8 %collective-permute-start.16 = (bf16[128,1536]{1,0:T(8,128)(2,1)S(1)}, bf16[128,1536]{1,0:T(8,128)(2,1)S(1)}, u32[]{:S(2)}, u32[]{:S(2)}) collective-permute-start(bf16[128,1536]{1,0:T(8,128)(2,1)S(1)} %get-tuple-element.48), channel_id=1, source_target_pairs={{0,12},{1,13},{2,14},{3,15},{4,0},{5,1},{6,2},{7,3},{8,4},{9,5},{1... | collective-permute-start | bytes 1179656 | tf_op jit(solution)/shard_map/ppermute | solution.py:157
  125.7 4.7 %collective-permute-start.14 = (bf16[128,1536]{1,0:T(8,128)(2,1)S(1)}, bf16[128,1536]{1,0:T(8,128)(2,1)S(1)}, u32[]{:S(2)}, u32[]{:S(2)}) collective-permute-start(bf16[128,1536]{1,0:T(8,128)(2,1)S(1)} %add_convert_fusion.2), channel_id=1, source_target_pairs={{0,8},{1,9},{2,10},{3,11},{4,12},{5,13},{6,14},{7,15},{8,0},{9,1},... | collective-permute-start | bytes 1179656 | tf_op jit(solution)/shard_map/ppermute | solution.py:157
  130.4 3.7 %collective-permute-done.15 = bf16[128,1536]{1,0:T(8,128)(2,1)S(1)} collective-permute-done((bf16[128,1536]{1,0:T(8,128)(2,1)S(1)}, bf16[128,1536]{1,0:T(8,128)(2,1)S(1)}, u32[]{:S(2)}, u32[]{:S(2)}) %collective-permute-start.15) | collective-permute-done | bytes 393248 | tf_op jit(solution)/shard_map/ppermute | solution.py:157
  134.1 3.1 %collective-permute-done.16 = bf16[128,1536]{1,0:T(8,128)(2,1)S(1)} collective-permute-done((bf16[128,1536]{1,0:T(8,128)(2,1)S(1)}, bf16[128,1536]{1,0:T(8,128)(2,1)S(1)}, u32[]{:S(2)}, u32[]{:S(2)}) %collective-permute-start.16) | collective-permute-done | bytes 393248 | tf_op jit(solution)/shard_map/ppermute | solution.py:157
  137.4 4.0 %collective-permute-start.17 = (bf16[128,1536]{1,0:T(8,128)(2,1)S(1)}, bf16[128,1536]{1,0:T(8,128)(2,1)S(1)}, u32[]{:S(2)}, u32[]{:S(2)}) collective-permute-start(bf16[128,1536]{1,0:T(8,128)(2,1)S(1)} %add_convert_fusion.1), channel_id=1, source_target_pairs={{0,2},{1,3},{2,0},{3,1},{4,6},{5,7},{6,4},{7,5},{8,10},{9,11},{10,... | collective-permute-start | bytes 1179656 | tf_op jit(solution)/shard_map/ppermute | solution.py:157
  143.7 8.3 %collective-permute-done.17 = bf16[128,1536]{1,0:T(8,128)(2,1)S(1)} collective-permute-done((bf16[128,1536]{1,0:T(8,128)(2,1)S(1)}, bf16[128,1536]{1,0:T(8,128)(2,1)S(1)}, u32[]{:S(2)}, u32[]{:S(2)}) %collective-permute-start.17) | collective-permute-done | bytes 393248 | tf_op jit(solution)/shard_map/ppermute | solution.py:157
  153.1 11.2 %all-to-all-done.1 = bf16[32,160,128]{2,1,0:T(8,128)(2,1)S(1)} async-done(((bf16[32,160,128]{2,1,0:T(8,128)(2,1)}), bf16[32,160,128]{2,1,0:T(8,128)(2,1)S(1)}, u32[]{:S(2)}, u32[]{:S(2)}) %all-to-all-start.1) | async-done | bytes 1310752 | tf_op jit(solution)/shard_map/all_to_all | solution.py:136
  (44 shorter events, 28.6 us)
Async XLA Ops:
  3.6 16.9 %copy-start.3 = (bf16[1,128,512]{2,1,0:T(8,128)(2,1)S(1)}, bf16[1,128,512]{2,1,0:T(8,128)(2,1)}, u32[]{:S(2)}) copy-start(bf16[1,128,512]{2,1,0:T(8,128)(2,1)} %param.11) | copy-start | bytes 393220
  3.6 16.9 %copy-start.4 = (bf16[1,128,512]{2,1,0:T(8,128)(2,1)S(1)}, bf16[1,128,512]{2,1,0:T(8,128)(2,1)}, u32[]{:S(2)}) copy-start(bf16[1,128,512]{2,1,0:T(8,128)(2,1)} %param.10) | copy-start | bytes 393220
  3.6 16.9 %copy-start.5 = (bf16[1,128,512]{2,1,0:T(8,128)(2,1)S(1)}, bf16[1,128,512]{2,1,0:T(8,128)(2,1)}, u32[]{:S(2)}) copy-start(bf16[1,128,512]{2,1,0:T(8,128)(2,1)} %param.9) | copy-start | bytes 393220
  3.6 82.5 %all-to-all-start = ((bf16[32,160,128]{2,1,0:T(8,128)(2,1)}), bf16[32,160,128]{2,1,0:T(8,128)(2,1)S(1)}, u32[]{:S(2)}, u32[]{:S(2)}) async-start(bf16[32,160,128]{2,1,0:T(8,128)(2,1)} %bitcast.32), calls=%async_computation | async-start | bytes 2621440 | tf_op jit(solution)/shard_map/all_to_all | solution.py:136
  20.5 17.3 %collective-permute-start.2 = (bf16[128,1536]{1,0:T(8,128)(2,1)S(1)}, bf16[128,1536]{1,0:T(8,128)(2,1)S(1)}, u32[]{:S(2)}, u32[]{:S(2)}) collective-permute-start(bf16[128,1536]{1,0:T(8,128)(2,1)S(1)} %pad_maximum_fusion.1), channel_id=1, source_target_pairs={{0,2},{1,3},{2,0},{3,1},{4,6},{5,7},{6,4},{7,5},{8,10},{9,11},{10,... | collective-permute-start | bytes 1179656 | tf_op jit(solution)/shard_map/ppermute | solution.py:157
  23.9 20.8 %collective-permute-start.5 = (bf16[128,1536]{1,0:T(8,128)(2,1)S(1)}, bf16[128,1536]{1,0:T(8,128)(2,1)S(1)}, u32[]{:S(2)}, u32[]{:S(2)}) collective-permute-start(bf16[128,1536]{1,0:T(8,128)(2,1)S(1)} %pad_maximum_fusion.1), channel_id=1, source_target_pairs={{0,8},{1,9},{2,10},{3,11},{4,12},{5,13},{6,14},{7,15},{8,0},{9,1},... | collective-permute-start | bytes 1179656 | tf_op jit(solution)/shard_map/ppermute | solution.py:157
  29.0 32.9 %collective-permute-start.1 = (bf16[128,1536]{1,0:T(8,128)(2,1)S(1)}, bf16[128,1536]{1,0:T(8,128)(2,1)S(1)}, u32[]{:S(2)}, u32[]{:S(2)}) collective-permute-start(bf16[128,1536]{1,0:T(8,128)(2,1)S(1)} %pad_maximum_fusion.1), channel_id=1, source_target_pairs={{0,12},{1,13},{2,14},{3,15},{4,0},{5,1},{6,2},{7,3},{8,4},{9,5},{1... | collective-permute-start | bytes 1179656 | tf_op jit(solution)/shard_map/ppermute | solution.py:157
  31.9 29.9 %collective-permute-start = (bf16[128,1536]{1,0:T(8,128)(2,1)S(1)}, bf16[128,1536]{1,0:T(8,128)(2,1)S(1)}, u32[]{:S(2)}, u32[]{:S(2)}) collective-permute-start(bf16[128,1536]{1,0:T(8,128)(2,1)S(1)} %pad_maximum_fusion.1), channel_id=1, source_target_pairs={{0,4},{1,5},{2,6},{3,7},{4,8},{5,9},{6,10},{7,11},{8,12},{9,13},{1... | collective-permute-start | bytes 1179656 | tf_op jit(solution)/shard_map/ppermute | solution.py:157
  37.8 16.7 %collective-permute-start.6 = (bf16[128,1536]{1,0:T(8,128)(2,1)S(1)}, bf16[128,1536]{1,0:T(8,128)(2,1)S(1)}, u32[]{:S(2)}, u32[]{:S(2)}) collective-permute-start(bf16[128,1536]{1,0:T(8,128)(2,1)S(1)} %collective-permute-done.2), channel_id=1, source_target_pairs={{0,12},{1,13},{2,14},{3,15},{4,0},{5,1},{6,2},{7,3},{8,4},{9,5},{1... | collective-permute-start | bytes 1179656 | tf_op jit(solution)/shard_map/ppermute | solution.py:157
  42.7 19.2 %collective-permute-start.3 = (bf16[128,1536]{1,0:T(8,128)(2,1)S(1)}, bf16[128,1536]{1,0:T(8,128)(2,1)S(1)}, u32[]{:S(2)}, u32[]{:S(2)}) collective-permute-start(bf16[128,1536]{1,0:T(8,128)(2,1)S(1)} %collective-permute-done.2), channel_id=1, source_target_pairs={{0,4},{1,5},{2,6},{3,7},{4,8},{5,9},{6,10},{7,11},{8,12},{9,13},{1... | collective-permute-start | bytes 1179656 | tf_op jit(solution)/shard_map/ppermute | solution.py:157
  44.6 14.5 %collective-permute-start.7 = (bf16[128,1536]{1,0:T(8,128)(2,1)S(1)}, bf16[128,1536]{1,0:T(8,128)(2,1)S(1)}, u32[]{:S(2)}, u32[]{:S(2)}) collective-permute-start(bf16[128,1536]{1,0:T(8,128)(2,1)S(1)} %collective-permute-done.5), channel_id=1, source_target_pairs={{0,2},{1,3},{2,0},{3,1},{4,6},{5,7},{6,4},{7,5},{8,10},{9,11},{10,... | collective-permute-start | bytes 1179656 | tf_op jit(solution)/shard_map/ppermute | solution.py:157
  59.9 5.6 %collective-permute-start.8 = (bf16[512,1536]{1,0:T(8,128)(2,1)}, bf16[512,1536]{1,0:T(8,128)(2,1)}, u32[]{:S(2)}, u32[]{:S(2)}) collective-permute-start(bf16[512,1536]{1,0:T(8,128)(2,1)} %constant_dynamic-update-slice_fusion.refs_2_), channel_id=1, source_target_pairs={{0,1},{1,0},{2,3},{3,2},{4,5},{5,4},{6,7},{7,6},{8,9},{9,8},{10,11... | collective-permute-start | bytes 4718600 | tf_op jit(solution)/shard_map/ppermute | solution.py:146
  62.0 5.6 %collective-permute-start.4 = (bf16[512,1536]{1,0:T(8,128)(2,1)S(1)}, bf16[512,1536]{1,0:T(8,128)(2,1)}, u32[]{:S(2)}, u32[]{:S(2)}) collective-permute-start(bf16[512,1536]{1,0:T(8,128)(2,1)S(1)} %pad_maximum_fusion.refs_0_), channel_id=1, source_target_pairs={{0,1},{1,0},{2,3},{3,2},{4,5},{5,4},{6,7},{7,6},{8,9},{9,8},{10,11... | collective-permute-start | bytes 4718600 | tf_op jit(solution)/shard_map/ppermute | solution.py:146
  93.6 70.7 %all-to-all-start.1 = ((bf16[32,160,128]{2,1,0:T(8,128)(2,1)}), bf16[32,160,128]{2,1,0:T(8,128)(2,1)S(1)}, u32[]{:S(2)}, u32[]{:S(2)}) async-start(bf16[32,160,128]{2,1,0:T(8,128)(2,1)} %bitcast.33), calls=%async_computation.1 | async-start | bytes 2621440 | tf_op jit(solution)/shard_map/all_to_all | solution.py:136
  98.9 6.0 %collective-permute-start.9 = (bf16[32,160,128]{2,1,0:T(8,128)(2,1)S(1)}, bf16[32,160,128]{2,1,0:T(8,128)(2,1)}, u32[]{:S(2)}, u32[]{:S(2)}) collective-permute-start(bf16[32,160,128]{2,1,0:T(8,128)(2,1)S(1)} %copy-done), channel_id=1, source_target_pairs={{0,1},{1,0},{2,3},{3,2},{4,5},{5,4},{6,7},{7,6},{8,9},{9,8},{10,11... | collective-permute-start | bytes 3932168 | tf_op jit(solution)/shard_map/ppermute | solution.py:146
  100.8 4.0 %collective-permute-start.10 = (bf16[160,1536]{1,0:T(8,128)(2,1)S(1)}, bf16[160,1536]{1,0:T(8,128)(2,1)}, u32[]{:S(2)}, u32[]{:S(2)}) collective-permute-start(bf16[160,1536]{1,0:T(8,128)(2,1)S(1)} %copy-done.1), channel_id=1, source_target_pairs={{0,1},{1,0},{2,3},{3,2},{4,5},{5,4},{6,7},{7,6},{8,9},{9,8},{10,11... | collective-permute-start | bytes 1474568 | tf_op jit(solution)/shard_map/ppermute | solution.py:146
  108.1 17.5 %collective-permute-start.13 = (bf16[128,1536]{1,0:T(8,128)(2,1)S(1)}, bf16[128,1536]{1,0:T(8,128)(2,1)S(1)}, u32[]{:S(2)}, u32[]{:S(2)}) collective-permute-start(bf16[128,1536]{1,0:T(8,128)(2,1)S(1)} %get-tuple-element.45), channel_id=1, source_target_pairs={{0,2},{1,3},{2,0},{3,1},{4,6},{5,7},{6,4},{7,5},{8,10},{9,11},{10,... | collective-permute-start | bytes 1179656 | tf_op jit(solution)/shard_map/ppermute | solution.py:157
  111.4 30.0 %collective-permute-start.11 = (bf16[128,1536]{1,0:T(8,128)(2,1)S(1)}, bf16[128,1536]{1,0:T(8,128)(2,1)S(1)}, u32[]{:S(2)}, u32[]{:S(2)}) collective-permute-start(bf16[128,1536]{1,0:T(8,128)(2,1)S(1)} %get-tuple-element.42), channel_id=1, source_target_pairs={{0,4},{1,5},{2,6},{3,7},{4,8},{5,9},{6,10},{7,11},{8,12},{9,13},{1... | collective-permute-start | bytes 1179656 | tf_op jit(solution)/shard_map/ppermute | solution.py:157
  114.9 26.5 %collective-permute-start.12 = (bf16[128,1536]{1,0:T(8,128)(2,1)S(1)}, bf16[128,1536]{1,0:T(8,128)(2,1)S(1)}, u32[]{:S(2)}, u32[]{:S(2)}) collective-permute-start(bf16[128,1536]{1,0:T(8,128)(2,1)S(1)} %get-tuple-element.43), channel_id=1, source_target_pairs={{0,12},{1,13},{2,14},{3,15},{4,0},{5,1},{6,2},{7,3},{8,4},{9,5},{1... | collective-permute-start | bytes 1179656 | tf_op jit(solution)/shard_map/ppermute | solution.py:157
  118.5 15.6 %collective-permute-start.15 = (bf16[128,1536]{1,0:T(8,128)(2,1)S(1)}, bf16[128,1536]{1,0:T(8,128)(2,1)S(1)}, u32[]{:S(2)}, u32[]{:S(2)}) collective-permute-start(bf16[128,1536]{1,0:T(8,128)(2,1)S(1)} %get-tuple-element.47), channel_id=1, source_target_pairs={{0,4},{1,5},{2,6},{3,7},{4,8},{5,9},{6,10},{7,11},{8,12},{9,13},{1... | collective-permute-start | bytes 1179656 | tf_op jit(solution)/shard_map/ppermute | solution.py:157
  120.8 16.5 %collective-permute-start.16 = (bf16[128,1536]{1,0:T(8,128)(2,1)S(1)}, bf16[128,1536]{1,0:T(8,128)(2,1)S(1)}, u32[]{:S(2)}, u32[]{:S(2)}) collective-permute-start(bf16[128,1536]{1,0:T(8,128)(2,1)S(1)} %get-tuple-element.48), channel_id=1, source_target_pairs={{0,12},{1,13},{2,14},{3,15},{4,0},{5,1},{6,2},{7,3},{8,4},{9,5},{1... | collective-permute-start | bytes 1179656 | tf_op jit(solution)/shard_map/ppermute | solution.py:157
  125.7 18.0 %collective-permute-start.14 = (bf16[128,1536]{1,0:T(8,128)(2,1)S(1)}, bf16[128,1536]{1,0:T(8,128)(2,1)S(1)}, u32[]{:S(2)}, u32[]{:S(2)}) collective-permute-start(bf16[128,1536]{1,0:T(8,128)(2,1)S(1)} %add_convert_fusion.2), channel_id=1, source_target_pairs={{0,8},{1,9},{2,10},{3,11},{4,12},{5,13},{6,14},{7,15},{8,0},{9,1},... | collective-permute-start | bytes 1179656 | tf_op jit(solution)/shard_map/ppermute | solution.py:157
  137.4 14.6 %collective-permute-start.17 = (bf16[128,1536]{1,0:T(8,128)(2,1)S(1)}, bf16[128,1536]{1,0:T(8,128)(2,1)S(1)}, u32[]{:S(2)}, u32[]{:S(2)}) collective-permute-start(bf16[128,1536]{1,0:T(8,128)(2,1)S(1)} %add_convert_fusion.1), channel_id=1, source_target_pairs={{0,2},{1,3},{2,0},{3,1},{4,6},{5,7},{6,4},{7,5},{8,10},{9,11},{10,... | collective-permute-start | bytes 1179656 | tf_op jit(solution)/shard_map/ppermute | solution.py:157
  152.1 12.2 %copy-start.2 = (bf16[160,128]{1,0:T(8,128)(2,1)S(1)}, bf16[160,128]{1,0:T(8,128)(2,1)}, u32[]{:S(2)}) copy-start(bf16[160,128]{1,0:T(8,128)(2,1)} %get-tuple-element.27.selector) | copy-start | bytes 122884
  (2 other events, 12.6 us)

commit v8 on v7

--- a/solution.py
+++ b/solution.py
@@ -11,9 +11,6 @@
     return lax.dot_general(
         left_rows, right_rows, (((0,), (0,)), ((), ())), preferred_element_type=jnp.float32
     )
-
-
-STRIDE = 5
 
 
 def slot_matrix(bucket, expert_count, capacity):
@@ -28,8 +25,7 @@
         preferred_element_type=jnp.float32,
     )
     slot = jnp.sum(earlier * chosen, axis=0, keepdims=True).astype(jnp.int32)
-    place = lax.rem(bucket * pow(STRIDE, -1, expert_count), expert_count)
-    position = place * capacity + slot
+    position = bucket * capacity + slot
     targets = lax.broadcasted_iota(jnp.int32, (expert_count * capacity, token_count), 0)
     return jnp.where(targets == position, 1.0, 0.0).astype(jnp.bfloat16)
 
@@ -132,10 +128,7 @@
 def exchange(rows, expert_count):
     row_count, blocks, lanes = rows.shape
     sent = rows.reshape(expert_count, row_count // expert_count * blocks, lanes)
-    order = [number * STRIDE % expert_count for number in range(expert_count)]
-    arrived = lax.all_to_all(
-        sent, "ep", split_axis=0, concat_axis=0, tiled=True, axis_index_groups=[order]
-    )
+    arrived = lax.all_to_all(sent, "ep", split_axis=0, concat_axis=0, tiled=True)
     return arrived.reshape(rows.shape)
 
 

time: 167 us -> 166 us (level)
  waiting for transfers between devices: 64.3 us -> 61.5 us
  transfers between devices with their start and end apart: 20 -> 20, of which waited for: 12 -> 13; matrix products, arithmetic and copies ran while one was open for 3% -> 3% of each run, Pallas kernels for 2% -> 2%
where the time goes in v8:
time: 166 us; the launch traced here: 164 us
  starting transfers between devices  81.9 us (49%)
  waiting for transfers between devices  61.5 us (37%)
  Pallas kernels  15.2 us (9%)
  local copies, waits for them, and re-layouts  4.1 us (2%)
    ppermute x14, starting transfers between devices, chip_shift(): return lax.ppermute(array, 'fsdp', pairs)  50.9 us
    ppermute x14, waiting for transfers between devices, chip_shift(): return lax.ppermute(array, 'fsdp', pairs)  28.7 us
    all_to_all x2, waiting for transfers between devices, exchange(): lax.all_to_all(sent, 'ep', split_axis=0, concat_axis=0, tiled=True)  28.2 us
    all_to_all x2, starting transfers between devices, exchange(): lax.all_to_all(sent, 'ep', split_axis=0, concat_axis=0, tiled=True)  22.3 us
    pallas_call x3, Pallas kernels, vmem_call(): pl.pallas_call(kernel, out_shape=jax.tree.map(lambda s: pltpu.HBM(s.shape...  12.2 us
    ppermute x4, starting transfers between devices, core_swap(): lax.ppermute(array, 'fsdp', [(f, f ^ 1) for f in range(2 * Y * X_HI)])  8.65 us
    ppermute x4, waiting for transfers between devices, core_swap(): lax.ppermute(array, 'fsdp', [(f, f ^ 1) for f in range(2 * Y * X_HI)])  4.56 us
  transfers between devices with their start and end apart: 20, of which 13 were waited for; matrix products, arithmetic and copies ran while one was open for 3% of the time, Pallas kernels for 2%

profile of v8, /device:TPU:6, one launch (start us, length us, event | category | flops | bytes accessed | tf_op | source)
XLA Modules:
  0.0 164.2 jit_solution(2879019762757761742)
XLA Ops:
  0.6 2.9 %shard_map.101 = (bf16[160,32,128]{2,1,0:T(8,128)(2,1)}, bf16[160,128]{1,0:T(8,128)(2,1)}) custom-call(s32[1,128]{1,0:T(1,128)} %bitcast.40, bf16[128,2048]{1,0:T(8,128)(2,1)} %tokens.1, bf16[128,2048]{1,0:T(8,128)(2,1)} %cotangent.1), custom_call_target="tpu_custom_call" | custom-call | tf_op jit(solution)/shard_map/pallas_call | solution.py:95
  3.6 16.9 %all-to-all-start = ((bf16[32,160,128]{2,1,0:T(8,128)(2,1)}), bf16[32,160,128]{2,1,0:T(8,128)(2,1)S(1)}, u32[]{:S(2)}, u32[]{:S(2)}) async-start(bf16[32,160,128]{2,1,0:T(8,128)(2,1)} %bitcast.32), calls=%async_computation | async-start | bytes 2621440 | tf_op jit(solution)/shard_map/all_to_all | solution.py:131
  20.5 3.3 %collective-permute-start.2 = (bf16[128,1536]{1,0:T(8,128)(2,1)S(1)}, bf16[128,1536]{1,0:T(8,128)(2,1)S(1)}, u32[]{:S(2)}, u32[]{:S(2)}) collective-permute-start(bf16[128,1536]{1,0:T(8,128)(2,1)S(1)} %pad_maximum_fusion.1), channel_id=1, source_target_pairs={{0,2},{1,3},{2,0},{3,1},{4,6},{5,7},{6,4},{7,5},{8,10},{9,11},{10,... | collective-permute-start | bytes 1179656 | tf_op jit(solution)/shard_map/ppermute | solution.py:150
  23.9 5.1 %collective-permute-start.5 = (bf16[128,1536]{1,0:T(8,128)(2,1)S(1)}, bf16[128,1536]{1,0:T(8,128)(2,1)S(1)}, u32[]{:S(2)}, u32[]{:S(2)}) collective-permute-start(bf16[128,1536]{1,0:T(8,128)(2,1)S(1)} %pad_maximum_fusion.1), channel_id=1, source_target_pairs={{0,8},{1,9},{2,10},{3,11},{4,12},{5,13},{6,14},{7,15},{8,0},{9,1},... | collective-permute-start | bytes 1179656 | tf_op jit(solution)/shard_map/ppermute | solution.py:150
  29.0 3.0 %collective-permute-start.1 = (bf16[128,1536]{1,0:T(8,128)(2,1)S(1)}, bf16[128,1536]{1,0:T(8,128)(2,1)S(1)}, u32[]{:S(2)}, u32[]{:S(2)}) collective-permute-start(bf16[128,1536]{1,0:T(8,128)(2,1)S(1)} %pad_maximum_fusion.1), channel_id=1, source_target_pairs={{0,12},{1,13},{2,14},{3,15},{4,0},{5,1},{6,2},{7,3},{8,4},{9,5},{1... | collective-permute-start | bytes 1179656 | tf_op jit(solution)/shard_map/ppermute | solution.py:150
  31.9 2.9 %collective-permute-start = (bf16[128,1536]{1,0:T(8,128)(2,1)S(1)}, bf16[128,1536]{1,0:T(8,128)(2,1)S(1)}, u32[]{:S(2)}, u32[]{:S(2)}) collective-permute-start(bf16[128,1536]{1,0:T(8,128)(2,1)S(1)} %pad_maximum_fusion.1), channel_id=1, source_target_pairs={{0,4},{1,5},{2,6},{3,7},{4,8},{5,9},{6,10},{7,11},{8,12},{9,13},{1... | collective-permute-start | bytes 1179656 | tf_op jit(solution)/shard_map/ppermute | solution.py:150
  37.5 4.9 %collective-permute-start.6 = (bf16[128,1536]{1,0:T(8,128)(2,1)S(1)}, bf16[128,1536]{1,0:T(8,128)(2,1)S(1)}, u32[]{:S(2)}, u32[]{:S(2)}) collective-permute-start(bf16[128,1536]{1,0:T(8,128)(2,1)S(1)} %collective-permute-done.2), channel_id=1, source_target_pairs={{0,12},{1,13},{2,14},{3,15},{4,0},{5,1},{6,2},{7,3},{8,4},{9,5},{1... | collective-permute-start | bytes 1179656 | tf_op jit(solution)/shard_map/ppermute | solution.py:150
  44.3 3.2 %collective-permute-start.7 = (bf16[128,1536]{1,0:T(8,128)(2,1)S(1)}, bf16[128,1536]{1,0:T(8,128)(2,1)S(1)}, u32[]{:S(2)}, u32[]{:S(2)}) collective-permute-start(bf16[128,1536]{1,0:T(8,128)(2,1)S(1)} %collective-permute-done.5), channel_id=1, source_target_pairs={{0,2},{1,3},{2,0},{3,1},{4,6},{5,7},{6,4},{7,5},{8,10},{9,11},{10,... | collective-permute-start | bytes 1179656 | tf_op jit(solution)/shard_map/ppermute | solution.py:150
  49.1 5.4 %collective-permute-done.6 = bf16[128,1536]{1,0:T(8,128)(2,1)S(1)} collective-permute-done((bf16[128,1536]{1,0:T(8,128)(2,1)S(1)}, bf16[128,1536]{1,0:T(8,128)(2,1)S(1)}, u32[]{:S(2)}, u32[]{:S(2)}) %collective-permute-start.6) | collective-permute-done | bytes 393248 | tf_op jit(solution)/shard_map/ppermute | solution.py:150
  55.3 3.2 %collective-permute-done.7 = bf16[128,1536]{1,0:T(8,128)(2,1)S(1)} collective-permute-done((bf16[128,1536]{1,0:T(8,128)(2,1)S(1)}, bf16[128,1536]{1,0:T(8,128)(2,1)S(1)}, u32[]{:S(2)}, u32[]{:S(2)}) %collective-permute-start.7) | collective-permute-done | bytes 393248 | tf_op jit(solution)/shard_map/ppermute | solution.py:150
  67.0 18.3 %all-to-all-done = bf16[32,160,128]{2,1,0:T(8,128)(2,1)S(1)} async-done(((bf16[32,160,128]{2,1,0:T(8,128)(2,1)}), bf16[32,160,128]{2,1,0:T(8,128)(2,1)S(1)}, u32[]{:S(2)}, u32[]{:S(2)}) %all-to-all-start) | async-done | bytes 1310752 | tf_op jit(solution)/shard_map/all_to_all | solution.py:131
  85.3 7.4 %shard_map.102 = (bf16[160,32,128]{2,1,0:T(8,128)(2,1)}, bf16[160,1536]{1,0:T(8,128)(2,1)}, bf16[32,160,128]{2,1,0:T(8,128)(2,1)}) custom-call(s32[16]{0:T(128)S(1)} %stack.78.numbers, bf16[160,32,128]{2,1,0:T(8,128)(2,1)S(1)} %bitcast.31, bf16[512,1536]{1,0:T(8,128)(2,1)S(1)} %pad_maximum_fusion.refs_0_, bf16[512,1536]{1,0:T(8,128)(2,1)} %collective-permute-done.4.refs_1_, ...), custom_call_target="tpu_custom_call" | custom-call | tf_op jit(solution)/shard_map/pallas_call | solution.py:39
  92.7 5.4 %all-to-all-start.1 = ((bf16[32,160,128]{2,1,0:T(8,128)(2,1)}), bf16[32,160,128]{2,1,0:T(8,128)(2,1)S(1)}, u32[]{:S(2)}, u32[]{:S(2)}) async-start(bf16[32,160,128]{2,1,0:T(8,128)(2,1)} %bitcast.33), calls=%async_computation.1 | async-start | bytes 2621440 | tf_op jit(solution)/shard_map/all_to_all | solution.py:131
  104.1 3.3 %shard_map.104 = (bf16[128,1536]{1,0:T(8,128)(2,1)S(1)}, bf16[128,1536]{1,0:T(8,128)(2,1)S(1)}, bf16[128,1536]{1,0:T(8,128)(2,1)S(1)}, bf16[128,1536]{1,0:T(8,12...) custom-call(s32[8]{0:T(128)S(1)} %stack.79.numbers, ...), custom_call_target="tpu_custom_call" | custom-call | tf_op jit(solution)/shard_map/pallas_call | solution.py:39
  107.4 3.3 %collective-permute-start.13 = (bf16[128,1536]{1,0:T(8,128)(2,1)S(1)}, bf16[128,1536]{1,0:T(8,128)(2,1)S(1)}, u32[]{:S(2)}, u32[]{:S(2)}) collective-permute-start(bf16[128,1536]{1,0:T(8,128)(2,1)S(1)} %get-tuple-element.45), channel_id=1, source_target_pairs={{0,2},{1,3},{2,0},{3,1},{4,6},{5,7},{6,4},{7,5},{8,10},{9,11},{10,... | collective-permute-start | bytes 1179656 | tf_op jit(solution)/shard_map/ppermute | solution.py:150
  110.7 3.5 %collective-permute-start.11 = (bf16[128,1536]{1,0:T(8,128)(2,1)S(1)}, bf16[128,1536]{1,0:T(8,128)(2,1)S(1)}, u32[]{:S(2)}, u32[]{:S(2)}) collective-permute-start(bf16[128,1536]{1,0:T(8,128)(2,1)S(1)} %get-tuple-element.42), channel_id=1, source_target_pairs={{0,4},{1,5},{2,6},{3,7},{4,8},{5,9},{6,10},{7,11},{8,12},{9,13},{1... | collective-permute-start | bytes 1179656 | tf_op jit(solution)/shard_map/ppermute | solution.py:150
  114.2 3.6 %collective-permute-start.12 = (bf16[128,1536]{1,0:T(8,128)(2,1)S(1)}, bf16[128,1536]{1,0:T(8,128)(2,1)S(1)}, u32[]{:S(2)}, u32[]{:S(2)}) collective-permute-start(bf16[128,1536]{1,0:T(8,128)(2,1)S(1)} %get-tuple-element.43), channel_id=1, source_target_pairs={{0,12},{1,13},{2,14},{3,15},{4,0},{5,1},{6,2},{7,3},{8,4},{9,5},{1... | collective-permute-start | bytes 1179656 | tf_op jit(solution)/shard_map/ppermute | solution.py:150
  120.1 4.8 %collective-permute-start.16 = (bf16[128,1536]{1,0:T(8,128)(2,1)S(1)}, bf16[128,1536]{1,0:T(8,128)(2,1)S(1)}, u32[]{:S(2)}, u32[]{:S(2)}) collective-permute-start(bf16[128,1536]{1,0:T(8,128)(2,1)S(1)} %get-tuple-element.48), channel_id=1, source_target_pairs={{0,12},{1,13},{2,14},{3,15},{4,0},{5,1},{6,2},{7,3},{8,4},{9,5},{1... | collective-permute-start | bytes 1179656 | tf_op jit(solution)/shard_map/ppermute | solution.py:150
  125.1 5.1 %collective-permute-start.14 = (bf16[128,1536]{1,0:T(8,128)(2,1)S(1)}, bf16[128,1536]{1,0:T(8,128)(2,1)S(1)}, u32[]{:S(2)}, u32[]{:S(2)}) collective-permute-start(bf16[128,1536]{1,0:T(8,128)(2,1)S(1)} %add_convert_fusion.2), channel_id=1, source_target_pairs={{0,8},{1,9},{2,10},{3,11},{4,12},{5,13},{6,14},{7,15},{8,0},{9,1},... | collective-permute-start | bytes 1179656 | tf_op jit(solution)/shard_map/ppermute | solution.py:150
  130.2 3.2 %collective-permute-done.15 = bf16[128,1536]{1,0:T(8,128)(2,1)S(1)} collective-permute-done((bf16[128,1536]{1,0:T(8,128)(2,1)S(1)}, bf16[128,1536]{1,0:T(8,128)(2,1)S(1)}, u32[]{:S(2)}, u32[]{:S(2)}) %collective-permute-start.15) | collective-permute-done | bytes 393248 | tf_op jit(solution)/shard_map/ppermute | solution.py:150
  133.4 3.1 %collective-permute-done.16 = bf16[128,1536]{1,0:T(8,128)(2,1)S(1)} collective-permute-done((bf16[128,1536]{1,0:T(8,128)(2,1)S(1)}, bf16[128,1536]{1,0:T(8,128)(2,1)S(1)}, u32[]{:S(2)}, u32[]{:S(2)}) %collective-permute-start.16) | collective-permute-done | bytes 393248 | tf_op jit(solution)/shard_map/ppermute | solution.py:150
  136.7 4.1 %collective-permute-start.17 = (bf16[128,1536]{1,0:T(8,128)(2,1)S(1)}, bf16[128,1536]{1,0:T(8,128)(2,1)S(1)}, u32[]{:S(2)}, u32[]{:S(2)}) collective-permute-start(bf16[128,1536]{1,0:T(8,128)(2,1)S(1)} %add_convert_fusion.1), channel_id=1, source_target_pairs={{0,2},{1,3},{2,0},{3,1},{4,6},{5,7},{6,4},{7,5},{8,10},{9,11},{10,... | collective-permute-start | bytes 1179656 | tf_op jit(solution)/shard_map/ppermute | solution.py:150
  143.0 8.8 %collective-permute-done.17 = bf16[128,1536]{1,0:T(8,128)(2,1)S(1)} collective-permute-done((bf16[128,1536]{1,0:T(8,128)(2,1)S(1)}, bf16[128,1536]{1,0:T(8,128)(2,1)S(1)}, u32[]{:S(2)}, u32[]{:S(2)}) %collective-permute-start.17) | collective-permute-done | bytes 393248 | tf_op jit(solution)/shard_map/ppermute | solution.py:150
  152.8 9.9 %all-to-all-done.1 = bf16[32,160,128]{2,1,0:T(8,128)(2,1)S(1)} async-done(((bf16[32,160,128]{2,1,0:T(8,128)(2,1)}), bf16[32,160,128]{2,1,0:T(8,128)(2,1)S(1)}, u32[]{:S(2)}, u32[]{:S(2)}) %all-to-all-start.1) | async-done | bytes 1310752 | tf_op jit(solution)/shard_map/all_to_all | solution.py:131
  (44 shorter events, 28.8 us)
Async XLA Ops:
  3.6 16.9 %copy-start.3 = (bf16[1,128,512]{2,1,0:T(8,128)(2,1)S(1)}, bf16[1,128,512]{2,1,0:T(8,128)(2,1)}, u32[]{:S(2)}) copy-start(bf16[1,128,512]{2,1,0:T(8,128)(2,1)} %param.11) | copy-start | bytes 393220
  3.6 16.9 %copy-start.4 = (bf16[1,128,512]{2,1,0:T(8,128)(2,1)S(1)}, bf16[1,128,512]{2,1,0:T(8,128)(2,1)}, u32[]{:S(2)}) copy-start(bf16[1,128,512]{2,1,0:T(8,128)(2,1)} %param.10) | copy-start | bytes 393220
  3.6 16.9 %copy-start.5 = (bf16[1,128,512]{2,1,0:T(8,128)(2,1)S(1)}, bf16[1,128,512]{2,1,0:T(8,128)(2,1)}, u32[]{:S(2)}) copy-start(bf16[1,128,512]{2,1,0:T(8,128)(2,1)} %param.9) | copy-start | bytes 393220
  3.6 81.6 %all-to-all-start = ((bf16[32,160,128]{2,1,0:T(8,128)(2,1)}), bf16[32,160,128]{2,1,0:T(8,128)(2,1)S(1)}, u32[]{:S(2)}, u32[]{:S(2)}) async-start(bf16[32,160,128]{2,1,0:T(8,128)(2,1)} %bitcast.32), calls=%async_computation | async-start | bytes 2621440 | tf_op jit(solution)/shard_map/all_to_all | solution.py:131
  20.5 16.9 %collective-permute-start.2 = (bf16[128,1536]{1,0:T(8,128)(2,1)S(1)}, bf16[128,1536]{1,0:T(8,128)(2,1)S(1)}, u32[]{:S(2)}, u32[]{:S(2)}) collective-permute-start(bf16[128,1536]{1,0:T(8,128)(2,1)S(1)} %pad_maximum_fusion.1), channel_id=1, source_target_pairs={{0,2},{1,3},{2,0},{3,1},{4,6},{5,7},{6,4},{7,5},{8,10},{9,11},{10,... | collective-permute-start | bytes 1179656 | tf_op jit(solution)/shard_map/ppermute | solution.py:150
  23.9 20.5 %collective-permute-start.5 = (bf16[128,1536]{1,0:T(8,128)(2,1)S(1)}, bf16[128,1536]{1,0:T(8,128)(2,1)S(1)}, u32[]{:S(2)}, u32[]{:S(2)}) collective-permute-start(bf16[128,1536]{1,0:T(8,128)(2,1)S(1)} %pad_maximum_fusion.1), channel_id=1, source_target_pairs={{0,8},{1,9},{2,10},{3,11},{4,12},{5,13},{6,14},{7,15},{8,0},{9,1},... | collective-permute-start | bytes 1179656 | tf_op jit(solution)/shard_map/ppermute | solution.py:150
  29.0 32.2 %collective-permute-start.1 = (bf16[128,1536]{1,0:T(8,128)(2,1)S(1)}, bf16[128,1536]{1,0:T(8,128)(2,1)S(1)}, u32[]{:S(2)}, u32[]{:S(2)}) collective-permute-start(bf16[128,1536]{1,0:T(8,128)(2,1)S(1)} %pad_maximum_fusion.1), channel_id=1, source_target_pairs={{0,12},{1,13},{2,14},{3,15},{4,0},{5,1},{6,2},{7,3},{8,4},{9,5},{1... | collective-permute-start | bytes 1179656 | tf_op jit(solution)/shard_map/ppermute | solution.py:150
  31.9 29.3 %collective-permute-start = (bf16[128,1536]{1,0:T(8,128)(2,1)S(1)}, bf16[128,1536]{1,0:T(8,128)(2,1)S(1)}, u32[]{:S(2)}, u32[]{:S(2)}) collective-permute-start(bf16[128,1536]{1,0:T(8,128)(2,1)S(1)} %pad_maximum_fusion.1), channel_id=1, source_target_pairs={{0,4},{1,5},{2,6},{3,7},{4,8},{5,9},{6,10},{7,11},{8,12},{9,13},{1... | collective-permute-start | bytes 1179656 | tf_op jit(solution)/shard_map/ppermute | solution.py:150
  37.5 17.0 %collective-permute-start.6 = (bf16[128,1536]{1,0:T(8,128)(2,1)S(1)}, bf16[128,1536]{1,0:T(8,128)(2,1)S(1)}, u32[]{:S(2)}, u32[]{:S(2)}) collective-permute-start(bf16[128,1536]{1,0:T(8,128)(2,1)S(1)} %collective-permute-done.2), channel_id=1, source_target_pairs={{0,12},{1,13},{2,14},{3,15},{4,0},{5,1},{6,2},{7,3},{8,4},{9,5},{1... | collective-permute-start | bytes 1179656 | tf_op jit(solution)/shard_map/ppermute | solution.py:150
  42.4 18.8 %collective-permute-start.3 = (bf16[128,1536]{1,0:T(8,128)(2,1)S(1)}, bf16[128,1536]{1,0:T(8,128)(2,1)S(1)}, u32[]{:S(2)}, u32[]{:S(2)}) collective-permute-start(bf16[128,1536]{1,0:T(8,128)(2,1)S(1)} %collective-permute-done.2), channel_id=1, source_target_pairs={{0,4},{1,5},{2,6},{3,7},{4,8},{5,9},{6,10},{7,11},{8,12},{9,13},{1... | collective-permute-start | bytes 1179656 | tf_op jit(solution)/shard_map/ppermute | solution.py:150
  44.3 14.1 %collective-permute-start.7 = (bf16[128,1536]{1,0:T(8,128)(2,1)S(1)}, bf16[128,1536]{1,0:T(8,128)(2,1)S(1)}, u32[]{:S(2)}, u32[]{:S(2)}) collective-permute-start(bf16[128,1536]{1,0:T(8,128)(2,1)S(1)} %collective-permute-done.5), channel_id=1, source_target_pairs={{0,2},{1,3},{2,0},{3,1},{4,6},{5,7},{6,4},{7,5},{8,10},{9,11},{10,... | collective-permute-start | bytes 1179656 | tf_op jit(solution)/shard_map/ppermute | solution.py:150
  59.3 5.6 %collective-permute-start.8 = (bf16[512,1536]{1,0:T(8,128)(2,1)}, bf16[512,1536]{1,0:T(8,128)(2,1)}, u32[]{:S(2)}, u32[]{:S(2)}) collective-permute-start(bf16[512,1536]{1,0:T(8,128)(2,1)} %constant_dynamic-update-slice_fusion.refs_2_), channel_id=1, source_target_pairs={{0,1},{1,0},{2,3},{3,2},{4,5},{5,4},{6,7},{7,6},{8,9},{9,8},{10,11... | collective-permute-start | bytes 4718600 | tf_op jit(solution)/shard_map/ppermute | solution.py:139
  61.3 5.6 %collective-permute-start.4 = (bf16[512,1536]{1,0:T(8,128)(2,1)S(1)}, bf16[512,1536]{1,0:T(8,128)(2,1)}, u32[]{:S(2)}, u32[]{:S(2)}) collective-permute-start(bf16[512,1536]{1,0:T(8,128)(2,1)S(1)} %pad_maximum_fusion.refs_0_), channel_id=1, source_target_pairs={{0,1},{1,0},{2,3},{3,2},{4,5},{5,4},{6,7},{7,6},{8,9},{9,8},{10,11... | collective-permute-start | bytes 4718600 | tf_op jit(solution)/shard_map/ppermute | solution.py:139
  92.7 70.0 %all-to-all-start.1 = ((bf16[32,160,128]{2,1,0:T(8,128)(2,1)}), bf16[32,160,128]{2,1,0:T(8,128)(2,1)S(1)}, u32[]{:S(2)}, u32[]{:S(2)}) async-start(bf16[32,160,128]{2,1,0:T(8,128)(2,1)} %bitcast.33), calls=%async_computation.1 | async-start | bytes 2621440 | tf_op jit(solution)/shard_map/all_to_all | solution.py:131
  98.1 6.0 %collective-permute-start.9 = (bf16[32,160,128]{2,1,0:T(8,128)(2,1)S(1)}, bf16[32,160,128]{2,1,0:T(8,128)(2,1)}, u32[]{:S(2)}, u32[]{:S(2)}) collective-permute-start(bf16[32,160,128]{2,1,0:T(8,128)(2,1)S(1)} %copy-done), channel_id=1, source_target_pairs={{0,1},{1,0},{2,3},{3,2},{4,5},{5,4},{6,7},{7,6},{8,9},{9,8},{10,11... | collective-permute-start | bytes 3932168 | tf_op jit(solution)/shard_map/ppermute | solution.py:139
  100.1 4.0 %collective-permute-start.10 = (bf16[160,1536]{1,0:T(8,128)(2,1)S(1)}, bf16[160,1536]{1,0:T(8,128)(2,1)}, u32[]{:S(2)}, u32[]{:S(2)}) collective-permute-start(bf16[160,1536]{1,0:T(8,128)(2,1)S(1)} %copy-done.1), channel_id=1, source_target_pairs={{0,1},{1,0},{2,3},{3,2},{4,5},{5,4},{6,7},{7,6},{8,9},{9,8},{10,11... | collective-permute-start | bytes 1474568 | tf_op jit(solution)/shard_map/ppermute | solution.py:139
  107.4 17.7 %collective-permute-start.13 = (bf16[128,1536]{1,0:T(8,128)(2,1)S(1)}, bf16[128,1536]{1,0:T(8,128)(2,1)S(1)}, u32[]{:S(2)}, u32[]{:S(2)}) collective-permute-start(bf16[128,1536]{1,0:T(8,128)(2,1)S(1)} %get-tuple-element.45), channel_id=1, source_target_pairs={{0,2},{1,3},{2,0},{3,1},{4,6},{5,7},{6,4},{7,5},{8,10},{9,11},{10,... | collective-permute-start | bytes 1179656 | tf_op jit(solution)/shard_map/ppermute | solution.py:150
  110.7 30.0 %collective-permute-start.11 = (bf16[128,1536]{1,0:T(8,128)(2,1)S(1)}, bf16[128,1536]{1,0:T(8,128)(2,1)S(1)}, u32[]{:S(2)}, u32[]{:S(2)}) collective-permute-start(bf16[128,1536]{1,0:T(8,128)(2,1)S(1)} %get-tuple-element.42), channel_id=1, source_target_pairs={{0,4},{1,5},{2,6},{3,7},{4,8},{5,9},{6,10},{7,11},{8,12},{9,13},{1... | collective-permute-start | bytes 1179656 | tf_op jit(solution)/shard_map/ppermute | solution.py:150
  114.2 26.6 %collective-permute-start.12 = (bf16[128,1536]{1,0:T(8,128)(2,1)S(1)}, bf16[128,1536]{1,0:T(8,128)(2,1)S(1)}, u32[]{:S(2)}, u32[]{:S(2)}) collective-permute-start(bf16[128,1536]{1,0:T(8,128)(2,1)S(1)} %get-tuple-element.43), channel_id=1, source_target_pairs={{0,12},{1,13},{2,14},{3,15},{4,0},{5,1},{6,2},{7,3},{8,4},{9,5},{1... | collective-permute-start | bytes 1179656 | tf_op jit(solution)/shard_map/ppermute | solution.py:150
  117.8 15.6 %collective-permute-start.15 = (bf16[128,1536]{1,0:T(8,128)(2,1)S(1)}, bf16[128,1536]{1,0:T(8,128)(2,1)S(1)}, u32[]{:S(2)}, u32[]{:S(2)}) collective-permute-start(bf16[128,1536]{1,0:T(8,128)(2,1)S(1)} %get-tuple-element.47), channel_id=1, source_target_pairs={{0,4},{1,5},{2,6},{3,7},{4,8},{5,9},{6,10},{7,11},{8,12},{9,13},{1... | collective-permute-start | bytes 1179656 | tf_op jit(solution)/shard_map/ppermute | solution.py:150
  120.1 16.5 %collective-permute-start.16 = (bf16[128,1536]{1,0:T(8,128)(2,1)S(1)}, bf16[128,1536]{1,0:T(8,128)(2,1)S(1)}, u32[]{:S(2)}, u32[]{:S(2)}) collective-permute-start(bf16[128,1536]{1,0:T(8,128)(2,1)S(1)} %get-tuple-element.48), channel_id=1, source_target_pairs={{0,12},{1,13},{2,14},{3,15},{4,0},{5,1},{6,2},{7,3},{8,4},{9,5},{1... | collective-permute-start | bytes 1179656 | tf_op jit(solution)/shard_map/ppermute | solution.py:150
  125.1 17.9 %collective-permute-start.14 = (bf16[128,1536]{1,0:T(8,128)(2,1)S(1)}, bf16[128,1536]{1,0:T(8,128)(2,1)S(1)}, u32[]{:S(2)}, u32[]{:S(2)}) collective-permute-start(bf16[128,1536]{1,0:T(8,128)(2,1)S(1)} %add_convert_fusion.2), channel_id=1, source_target_pairs={{0,8},{1,9},{2,10},{3,11},{4,12},{5,13},{6,14},{7,15},{8,0},{9,1},... | collective-permute-start | bytes 1179656 | tf_op jit(solution)/shard_map/ppermute | solution.py:150
  136.7 15.1 %collective-permute-start.17 = (bf16[128,1536]{1,0:T(8,128)(2,1)S(1)}, bf16[128,1536]{1,0:T(8,128)(2,1)S(1)}, u32[]{:S(2)}, u32[]{:S(2)}) collective-permute-start(bf16[128,1536]{1,0:T(8,128)(2,1)S(1)} %add_convert_fusion.1), channel_id=1, source_target_pairs={{0,2},{1,3},{2,0},{3,1},{4,6},{5,7},{6,4},{7,5},{8,10},{9,11},{10,... | collective-permute-start | bytes 1179656 | tf_op jit(solution)/shard_map/ppermute | solution.py:150
  151.8 10.9 %copy-start.2 = (bf16[160,128]{1,0:T(8,128)(2,1)S(1)}, bf16[160,128]{1,0:T(8,128)(2,1)}, u32[]{:S(2)}) copy-start(bf16[160,128]{1,0:T(8,128)(2,1)} %get-tuple-element.27.selector) | copy-start | bytes 122884
  (2 other events, 12.9 us)

commit v9 on v7

--- a/solution.py
+++ b/solution.py
@@ -13,7 +13,7 @@
     )
 
 
-STRIDE = 5
+PAIR = 2
 
 
 def slot_matrix(bucket, expert_count, capacity):
@@ -28,7 +28,8 @@
         preferred_element_type=jnp.float32,
     )
     slot = jnp.sum(earlier * chosen, axis=0, keepdims=True).astype(jnp.int32)
-    place = lax.rem(bucket * pow(STRIDE, -1, expert_count), expert_count)
+    within = lax.bitwise_and(bucket, PAIR - 1)
+    place = expert_count - PAIR - (bucket - within) + within
     position = place * capacity + slot
     targets = lax.broadcasted_iota(jnp.int32, (expert_count * capacity, token_count), 0)
     return jnp.where(targets == position, 1.0, 0.0).astype(jnp.bfloat16)
@@ -132,7 +133,11 @@
 def exchange(rows, expert_count):
     row_count, blocks, lanes = rows.shape
     sent = rows.reshape(expert_count, row_count // expert_count * blocks, lanes)
-    order = [number * STRIDE % expert_count for number in range(expert_count)]
+    order = [
+        first + within
+        for first in reversed(range(0, expert_count, PAIR))
+        for within in range(PAIR)
+    ]
     arrived = lax.all_to_all(
         sent, "ep", split_axis=0, concat_axis=0, tiled=True, axis_index_groups=[order]
     )

time: 167 us -> 164 us (0.982)
  the two profiles are of different devices: /device:TPU:6 before, /device:TPU:57 now
where the time goes in v9:
time: 164 us; the launch traced here: 163 us
  starting transfers between devices  78.8 us (48%)
  waiting for transfers between devices  63.1 us (38%)
  Pallas kernels  15.2 us (9%)
  local copies, waits for them, and re-layouts  4.1 us (2%)
    ppermute x14, starting transfers between devices, chip_shift(): return lax.ppermute(array, 'fsdp', pairs)  45.3 us
    ppermute x14, waiting for transfers between devices, chip_shift(): return lax.ppermute(array, 'fsdp', pairs)  29.3 us
    all_to_all x2, waiting for transfers between devices, exchange(): lax.all_to_all(sent, 'ep', split_axis=0, concat_axis=0, tiled=True, axis_...  28.6 us
    all_to_all x2, starting transfers between devices, exchange(): lax.all_to_all(sent, 'ep', split_axis=0, concat_axis=0, tiled=True, axis_...  21.7 us
    pallas_call x3, Pallas kernels, vmem_call(): pl.pallas_call(kernel, out_shape=jax.tree.map(lambda s: pltpu.HBM(s.shape...  12.2 us
    ppermute x4, starting transfers between devices, core_swap(): lax.ppermute(array, 'fsdp', [(f, f ^ 1) for f in range(2 * Y * X_HI)])  11.8 us
    ppermute x4, waiting for transfers between devices, core_swap(): lax.ppermute(array, 'fsdp', [(f, f ^ 1) for f in range(2 * Y * X_HI)])  5.24 us
  transfers between devices with their start and end apart: 20, of which 12 were waited for; matrix products, arithmetic and copies ran while one was open for 3% of the time, Pallas kernels for 2%

profile of v9, /device:TPU:57, one launch (start us, length us, event | category | flops | bytes accessed | tf_op | source)
XLA Modules:
  0.0 162.8 jit_solution(12392988574877534852)
XLA Ops:
  0.6 2.9 %shard_map.101 = (bf16[160,32,128]{2,1,0:T(8,128)(2,1)}, bf16[160,128]{1,0:T(8,128)(2,1)}) custom-call(s32[1,128]{1,0:T(1,128)} %bitcast.40, bf16[128,2048]{1,0:T(8,128)(2,1)} %tokens.1, bf16[128,2048]{1,0:T(8,128)(2,1)} %cotangent.1), custom_call_target="tpu_custom_call" | custom-call | tf_op jit(solution)/shard_map/pallas_call | solution.py:100
  3.6 15.9 %all-to-all-start = ((bf16[32,160,128]{2,1,0:T(8,128)(2,1)}), bf16[32,160,128]{2,1,0:T(8,128)(2,1)S(1)}, u32[]{:S(2)}, u32[]{:S(2)}) async-start(bf16[32,160,128]{2,1,0:T(8,128)(2,1)} %bitcast.32), calls=%async_computation | async-start | bytes 2621440 | tf_op jit(solution)/shard_map/all_to_all | solution.py:141
  19.6 4.4 %collective-permute-start.2 = (bf16[128,1536]{1,0:T(8,128)(2,1)S(1)}, bf16[128,1536]{1,0:T(8,128)(2,1)S(1)}, u32[]{:S(2)}, u32[]{:S(2)}) collective-permute-start(bf16[128,1536]{1,0:T(8,128)(2,1)S(1)} %pad_maximum_fusion.1), channel_id=1, source_target_pairs={{0,2},{1,3},{2,0},{3,1},{4,6},{5,7},{6,4},{7,5},{8,10},{9,11},{10,... | collective-permute-start | bytes 1179656 | tf_op jit(solution)/shard_map/ppermute | solution.py:162
  24.0 2.9 %collective-permute-start.5 = (bf16[128,1536]{1,0:T(8,128)(2,1)S(1)}, bf16[128,1536]{1,0:T(8,128)(2,1)S(1)}, u32[]{:S(2)}, u32[]{:S(2)}) collective-permute-start(bf16[128,1536]{1,0:T(8,128)(2,1)S(1)} %pad_maximum_fusion.1), channel_id=1, source_target_pairs={{0,8},{1,9},{2,10},{3,11},{4,12},{5,13},{6,14},{7,15},{8,0},{9,1},... | collective-permute-start | bytes 1179656 | tf_op jit(solution)/shard_map/ppermute | solution.py:162
  28.8 4.6 %collective-permute-start = (bf16[128,1536]{1,0:T(8,128)(2,1)S(1)}, bf16[128,1536]{1,0:T(8,128)(2,1)S(1)}, u32[]{:S(2)}, u32[]{:S(2)}) collective-permute-start(bf16[128,1536]{1,0:T(8,128)(2,1)S(1)} %pad_maximum_fusion.1), channel_id=1, source_target_pairs={{0,4},{1,5},{2,6},{3,7},{4,8},{5,9},{6,10},{7,11},{8,12},{9,13},{1... | collective-permute-start | bytes 1179656 | tf_op jit(solution)/shard_map/ppermute | solution.py:162
  36.9 4.1 %collective-permute-start.3 = (bf16[128,1536]{1,0:T(8,128)(2,1)S(1)}, bf16[128,1536]{1,0:T(8,128)(2,1)S(1)}, u32[]{:S(2)}, u32[]{:S(2)}) collective-permute-start(bf16[128,1536]{1,0:T(8,128)(2,1)S(1)} %collective-permute-done.2), channel_id=1, source_target_pairs={{0,4},{1,5},{2,6},{3,7},{4,8},{5,9},{6,10},{7,11},{8,12},{9,13},{1... | collective-permute-start | bytes 1179656 | tf_op jit(solution)/shard_map/ppermute | solution.py:162
  41.0 4.8 %collective-permute-start.7 = (bf16[128,1536]{1,0:T(8,128)(2,1)S(1)}, bf16[128,1536]{1,0:T(8,128)(2,1)S(1)}, u32[]{:S(2)}, u32[]{:S(2)}) collective-permute-start(bf16[128,1536]{1,0:T(8,128)(2,1)S(1)} %collective-permute-done.5), channel_id=1, source_target_pairs={{0,2},{1,3},{2,0},{3,1},{4,6},{5,7},{6,4},{7,5},{8,10},{9,11},{10,... | collective-permute-start | bytes 1179656 | tf_op jit(solution)/shard_map/ppermute | solution.py:162
  47.4 7.9 %collective-permute-done.6 = bf16[128,1536]{1,0:T(8,128)(2,1)S(1)} collective-permute-done((bf16[128,1536]{1,0:T(8,128)(2,1)S(1)}, bf16[128,1536]{1,0:T(8,128)(2,1)S(1)}, u32[]{:S(2)}, u32[]{:S(2)}) %collective-permute-start.6) | collective-permute-done | bytes 393248 | tf_op jit(solution)/shard_map/ppermute | solution.py:162
  56.9 4.5 %collective-permute-start.8 = (bf16[512,1536]{1,0:T(8,128)(2,1)}, bf16[512,1536]{1,0:T(8,128)(2,1)}, u32[]{:S(2)}, u32[]{:S(2)}) collective-permute-start(bf16[512,1536]{1,0:T(8,128)(2,1)} %constant_dynamic-update-slice_fusion.refs_2_), channel_id=1, source_target_pairs={{0,1},{1,0},{2,3},{3,2},{4,5},{5,4},{6,7},{7,6},{8,9},{9,8},{10,11... | collective-permute-start | bytes 4718600 | tf_op jit(solution)/shard_map/ppermute | solution.py:151
  67.0 16.8 %all-to-all-done = bf16[32,160,128]{2,1,0:T(8,128)(2,1)S(1)} async-done(((bf16[32,160,128]{2,1,0:T(8,128)(2,1)}), bf16[32,160,128]{2,1,0:T(8,128)(2,1)S(1)}, u32[]{:S(2)}, u32[]{:S(2)}) %all-to-all-start) | async-done | bytes 1310752 | tf_op jit(solution)/shard_map/all_to_all | solution.py:141
  83.8 7.4 %shard_map.102 = (bf16[160,32,128]{2,1,0:T(8,128)(2,1)}, bf16[160,1536]{1,0:T(8,128)(2,1)}, bf16[32,160,128]{2,1,0:T(8,128)(2,1)}) custom-call(s32[16]{0:T(128)S(1)} %stack.78.numbers, bf16[160,32,128]{2,1,0:T(8,128)(2,1)S(1)} %bitcast.31, bf16[512,1536]{1,0:T(8,128)(2,1)S(1)} %pad_maximum_fusion.refs_0_, bf16[512,1536]{1,0:T(8,128)(2,1)} %collective-permute-done.4.refs_1_, ...), custom_call_target="tpu_custom_call" | custom-call | tf_op jit(solution)/shard_map/pallas_call | solution.py:44
  91.2 5.7 %all-to-all-start.1 = ((bf16[32,160,128]{2,1,0:T(8,128)(2,1)}), bf16[32,160,128]{2,1,0:T(8,128)(2,1)S(1)}, u32[]{:S(2)}, u32[]{:S(2)}) async-start(bf16[32,160,128]{2,1,0:T(8,128)(2,1)} %bitcast.33), calls=%async_computation.1 | async-start | bytes 2621440 | tf_op jit(solution)/shard_map/all_to_all | solution.py:141
  96.9 3.4 %collective-permute-start.9 = (bf16[32,160,128]{2,1,0:T(8,128)(2,1)S(1)}, bf16[32,160,128]{2,1,0:T(8,128)(2,1)}, u32[]{:S(2)}, u32[]{:S(2)}) collective-permute-start(bf16[32,160,128]{2,1,0:T(8,128)(2,1)S(1)} %copy-done), channel_id=1, source_target_pairs={{0,1},{1,0},{2,3},{3,2},{4,5},{5,4},{6,7},{7,6},{8,9},{9,8},{10,11... | collective-permute-start | bytes 3932168 | tf_op jit(solution)/shard_map/ppermute | solution.py:151
  104.3 3.3 %shard_map.104 = (bf16[128,1536]{1,0:T(8,128)(2,1)S(1)}, bf16[128,1536]{1,0:T(8,128)(2,1)S(1)}, bf16[128,1536]{1,0:T(8,128)(2,1)S(1)}, bf16[128,1536]{1,0:T(8,12...) custom-call(s32[8]{0:T(128)S(1)} %stack.79.numbers, ...), custom_call_target="tpu_custom_call" | custom-call | tf_op jit(solution)/shard_map/pallas_call | solution.py:44
  107.6 4.4 %collective-permute-start.13 = (bf16[128,1536]{1,0:T(8,128)(2,1)S(1)}, bf16[128,1536]{1,0:T(8,128)(2,1)S(1)}, u32[]{:S(2)}, u32[]{:S(2)}) collective-permute-start(bf16[128,1536]{1,0:T(8,128)(2,1)S(1)} %get-tuple-element.45), channel_id=1, source_target_pairs={{0,2},{1,3},{2,0},{3,1},{4,6},{5,7},{6,4},{7,5},{8,10},{9,11},{10,... | collective-permute-start | bytes 1179656 | tf_op jit(solution)/shard_map/ppermute | solution.py:162
  113.9 3.4 %collective-permute-start.12 = (bf16[128,1536]{1,0:T(8,128)(2,1)S(1)}, bf16[128,1536]{1,0:T(8,128)(2,1)S(1)}, u32[]{:S(2)}, u32[]{:S(2)}) collective-permute-start(bf16[128,1536]{1,0:T(8,128)(2,1)S(1)} %get-tuple-element.43), channel_id=1, source_target_pairs={{0,12},{1,13},{2,14},{3,15},{4,0},{5,1},{6,2},{7,3},{8,4},{9,5},{1... | collective-permute-start | bytes 1179656 | tf_op jit(solution)/shard_map/ppermute | solution.py:162
  117.2 3.1 %collective-permute-start.15 = (bf16[128,1536]{1,0:T(8,128)(2,1)S(1)}, bf16[128,1536]{1,0:T(8,128)(2,1)S(1)}, u32[]{:S(2)}, u32[]{:S(2)}) collective-permute-start(bf16[128,1536]{1,0:T(8,128)(2,1)S(1)} %get-tuple-element.47), channel_id=1, source_target_pairs={{0,4},{1,5},{2,6},{3,7},{4,8},{5,9},{6,10},{7,11},{8,12},{9,13},{1... | collective-permute-start | bytes 1179656 | tf_op jit(solution)/shard_map/ppermute | solution.py:162
  123.7 2.9 %collective-permute-start.14 = (bf16[128,1536]{1,0:T(8,128)(2,1)S(1)}, bf16[128,1536]{1,0:T(8,128)(2,1)S(1)}, u32[]{:S(2)}, u32[]{:S(2)}) collective-permute-start(bf16[128,1536]{1,0:T(8,128)(2,1)S(1)} %add_convert_fusion.2), channel_id=1, source_target_pairs={{0,8},{1,9},{2,10},{3,11},{4,12},{5,13},{6,14},{7,15},{8,0},{9,1},... | collective-permute-start | bytes 1179656 | tf_op jit(solution)/shard_map/ppermute | solution.py:162
  126.5 6.0 %collective-permute-done.15 = bf16[128,1536]{1,0:T(8,128)(2,1)S(1)} collective-permute-done((bf16[128,1536]{1,0:T(8,128)(2,1)S(1)}, bf16[128,1536]{1,0:T(8,128)(2,1)S(1)}, u32[]{:S(2)}, u32[]{:S(2)}) %collective-permute-start.15) | collective-permute-done | bytes 393248 | tf_op jit(solution)/shard_map/ppermute | solution.py:162
  132.5 3.2 %collective-permute-done.16 = bf16[128,1536]{1,0:T(8,128)(2,1)S(1)} collective-permute-done((bf16[128,1536]{1,0:T(8,128)(2,1)S(1)}, bf16[128,1536]{1,0:T(8,128)(2,1)S(1)}, u32[]{:S(2)}, u32[]{:S(2)}) %collective-permute-start.16) | collective-permute-done | bytes 393248 | tf_op jit(solution)/shard_map/ppermute | solution.py:162
  135.9 2.4 %collective-permute-start.17 = (bf16[128,1536]{1,0:T(8,128)(2,1)S(1)}, bf16[128,1536]{1,0:T(8,128)(2,1)S(1)}, u32[]{:S(2)}, u32[]{:S(2)}) collective-permute-start(bf16[128,1536]{1,0:T(8,128)(2,1)S(1)} %add_convert_fusion.1), channel_id=1, source_target_pairs={{0,2},{1,3},{2,0},{3,1},{4,6},{5,7},{6,4},{7,5},{8,10},{9,11},{10,... | collective-permute-start | bytes 1179656 | tf_op jit(solution)/shard_map/ppermute | solution.py:162
  138.4 5.2 %collective-permute-done.14 = bf16[128,1536]{1,0:T(8,128)(2,1)S(1)} collective-permute-done((bf16[128,1536]{1,0:T(8,128)(2,1)S(1)}, bf16[128,1536]{1,0:T(8,128)(2,1)S(1)}, u32[]{:S(2)}, u32[]{:S(2)}) %collective-permute-start.14) | collective-permute-done | bytes 393248 | tf_op jit(solution)/shard_map/ppermute | solution.py:162
  143.6 4.8 %collective-permute-done.17 = bf16[128,1536]{1,0:T(8,128)(2,1)S(1)} collective-permute-done((bf16[128,1536]{1,0:T(8,128)(2,1)S(1)}, bf16[128,1536]{1,0:T(8,128)(2,1)S(1)}, u32[]{:S(2)}, u32[]{:S(2)}) %collective-permute-start.17) | collective-permute-done | bytes 393248 | tf_op jit(solution)/shard_map/ppermute | solution.py:162
  149.4 11.8 %all-to-all-done.1 = bf16[32,160,128]{2,1,0:T(8,128)(2,1)S(1)} async-done(((bf16[32,160,128]{2,1,0:T(8,128)(2,1)}), bf16[32,160,128]{2,1,0:T(8,128)(2,1)S(1)}, u32[]{:S(2)}, u32[]{:S(2)}) %all-to-all-start.1) | async-done | bytes 1310752 | tf_op jit(solution)/shard_map/all_to_all | solution.py:141
  (44 shorter events, 25.9 us)
Async XLA Ops:
  3.6 16.0 %copy-start.3 = (bf16[1,128,512]{2,1,0:T(8,128)(2,1)S(1)}, bf16[1,128,512]{2,1,0:T(8,128)(2,1)}, u32[]{:S(2)}) copy-start(bf16[1,128,512]{2,1,0:T(8,128)(2,1)} %param.11) | copy-start | bytes 393220
  3.6 16.0 %copy-start.4 = (bf16[1,128,512]{2,1,0:T(8,128)(2,1)S(1)}, bf16[1,128,512]{2,1,0:T(8,128)(2,1)}, u32[]{:S(2)}) copy-start(bf16[1,128,512]{2,1,0:T(8,128)(2,1)} %param.10) | copy-start | bytes 393220
  3.6 16.0 %copy-start.5 = (bf16[1,128,512]{2,1,0:T(8,128)(2,1)S(1)}, bf16[1,128,512]{2,1,0:T(8,128)(2,1)}, u32[]{:S(2)}) copy-start(bf16[1,128,512]{2,1,0:T(8,128)(2,1)} %param.9) | copy-start | bytes 393220
  3.6 80.2 %all-to-all-start = ((bf16[32,160,128]{2,1,0:T(8,128)(2,1)}), bf16[32,160,128]{2,1,0:T(8,128)(2,1)S(1)}, u32[]{:S(2)}, u32[]{:S(2)}) async-start(bf16[32,160,128]{2,1,0:T(8,128)(2,1)} %bitcast.32), calls=%async_computation | async-start | bytes 2621440 | tf_op jit(solution)/shard_map/all_to_all | solution.py:141
  19.6 14.9 %collective-permute-start.2 = (bf16[128,1536]{1,0:T(8,128)(2,1)S(1)}, bf16[128,1536]{1,0:T(8,128)(2,1)S(1)}, u32[]{:S(2)}, u32[]{:S(2)}) collective-permute-start(bf16[128,1536]{1,0:T(8,128)(2,1)S(1)} %pad_maximum_fusion.1), channel_id=1, source_target_pairs={{0,2},{1,3},{2,0},{3,1},{4,6},{5,7},{6,4},{7,5},{8,10},{9,11},{10,... | collective-permute-start | bytes 1179656 | tf_op jit(solution)/shard_map/ppermute | solution.py:162
  24.0 17.0 %collective-permute-start.5 = (bf16[128,1536]{1,0:T(8,128)(2,1)S(1)}, bf16[128,1536]{1,0:T(8,128)(2,1)S(1)}, u32[]{:S(2)}, u32[]{:S(2)}) collective-permute-start(bf16[128,1536]{1,0:T(8,128)(2,1)S(1)} %pad_maximum_fusion.1), channel_id=1, source_target_pairs={{0,8},{1,9},{2,10},{3,11},{4,12},{5,13},{6,14},{7,15},{8,0},{9,1},... | collective-permute-start | bytes 1179656 | tf_op jit(solution)/shard_map/ppermute | solution.py:162
  26.9 34.6 %collective-permute-start.1 = (bf16[128,1536]{1,0:T(8,128)(2,1)S(1)}, bf16[128,1536]{1,0:T(8,128)(2,1)S(1)}, u32[]{:S(2)}, u32[]{:S(2)}) collective-permute-start(bf16[128,1536]{1,0:T(8,128)(2,1)S(1)} %pad_maximum_fusion.1), channel_id=1, source_target_pairs={{0,12},{1,13},{2,14},{3,15},{4,0},{5,1},{6,2},{7,3},{8,4},{9,5},{1... | collective-permute-start | bytes 1179656 | tf_op jit(solution)/shard_map/ppermute | solution.py:162
  28.8 32.7 %collective-permute-start = (bf16[128,1536]{1,0:T(8,128)(2,1)S(1)}, bf16[128,1536]{1,0:T(8,128)(2,1)S(1)}, u32[]{:S(2)}, u32[]{:S(2)}) collective-permute-start(bf16[128,1536]{1,0:T(8,128)(2,1)S(1)} %pad_maximum_fusion.1), channel_id=1, source_target_pairs={{0,4},{1,5},{2,6},{3,7},{4,8},{5,9},{6,10},{7,11},{8,12},{9,13},{1... | collective-permute-start | bytes 1179656 | tf_op jit(solution)/shard_map/ppermute | solution.py:162
  34.5 20.8 %collective-permute-start.6 = (bf16[128,1536]{1,0:T(8,128)(2,1)S(1)}, bf16[128,1536]{1,0:T(8,128)(2,1)S(1)}, u32[]{:S(2)}, u32[]{:S(2)}) collective-permute-start(bf16[128,1536]{1,0:T(8,128)(2,1)S(1)} %collective-permute-done.2), channel_id=1, source_target_pairs={{0,12},{1,13},{2,14},{3,15},{4,0},{5,1},{6,2},{7,3},{8,4},{9,5},{1... | collective-permute-start | bytes 1179656 | tf_op jit(solution)/shard_map/ppermute | solution.py:162
  36.9 24.6 %collective-permute-start.3 = (bf16[128,1536]{1,0:T(8,128)(2,1)S(1)}, bf16[128,1536]{1,0:T(8,128)(2,1)S(1)}, u32[]{:S(2)}, u32[]{:S(2)}) collective-permute-start(bf16[128,1536]{1,0:T(8,128)(2,1)S(1)} %collective-permute-done.2), channel_id=1, source_target_pairs={{0,4},{1,5},{2,6},{3,7},{4,8},{5,9},{6,10},{7,11},{8,12},{9,13},{1... | collective-permute-start | bytes 1179656 | tf_op jit(solution)/shard_map/ppermute | solution.py:162
  41.0 15.1 %collective-permute-start.7 = (bf16[128,1536]{1,0:T(8,128)(2,1)S(1)}, bf16[128,1536]{1,0:T(8,128)(2,1)S(1)}, u32[]{:S(2)}, u32[]{:S(2)}) collective-permute-start(bf16[128,1536]{1,0:T(8,128)(2,1)S(1)} %collective-permute-done.5), channel_id=1, source_target_pairs={{0,2},{1,3},{2,0},{3,1},{4,6},{5,7},{6,4},{7,5},{8,10},{9,11},{10,... | collective-permute-start | bytes 1179656 | tf_op jit(solution)/shard_map/ppermute | solution.py:162
  56.9 7.9 %collective-permute-start.8 = (bf16[512,1536]{1,0:T(8,128)(2,1)}, bf16[512,1536]{1,0:T(8,128)(2,1)}, u32[]{:S(2)}, u32[]{:S(2)}) collective-permute-start(bf16[512,1536]{1,0:T(8,128)(2,1)} %constant_dynamic-update-slice_fusion.refs_2_), channel_id=1, source_target_pairs={{0,1},{1,0},{2,3},{3,2},{4,5},{5,4},{6,7},{7,6},{8,9},{9,8},{10,11... | collective-permute-start | bytes 4718600 | tf_op jit(solution)/shard_map/ppermute | solution.py:151
  61.6 5.4 %collective-permute-start.4 = (bf16[512,1536]{1,0:T(8,128)(2,1)S(1)}, bf16[512,1536]{1,0:T(8,128)(2,1)}, u32[]{:S(2)}, u32[]{:S(2)}) collective-permute-start(bf16[512,1536]{1,0:T(8,128)(2,1)S(1)} %pad_maximum_fusion.refs_0_), channel_id=1, source_target_pairs={{0,1},{1,0},{2,3},{3,2},{4,5},{5,4},{6,7},{7,6},{8,9},{9,8},{10,11... | collective-permute-start | bytes 4718600 | tf_op jit(solution)/shard_map/ppermute | solution.py:151
  91.2 70.0 %all-to-all-start.1 = ((bf16[32,160,128]{2,1,0:T(8,128)(2,1)}), bf16[32,160,128]{2,1,0:T(8,128)(2,1)S(1)}, u32[]{:S(2)}, u32[]{:S(2)}) async-start(bf16[32,160,128]{2,1,0:T(8,128)(2,1)} %bitcast.33), calls=%async_computation.1 | async-start | bytes 2621440 | tf_op jit(solution)/shard_map/all_to_all | solution.py:141
  96.9 7.3 %collective-permute-start.9 = (bf16[32,160,128]{2,1,0:T(8,128)(2,1)S(1)}, bf16[32,160,128]{2,1,0:T(8,128)(2,1)}, u32[]{:S(2)}, u32[]{:S(2)}) collective-permute-start(bf16[32,160,128]{2,1,0:T(8,128)(2,1)S(1)} %copy-done), channel_id=1, source_target_pairs={{0,1},{1,0},{2,3},{3,2},{4,5},{5,4},{6,7},{7,6},{8,9},{9,8},{10,11... | collective-permute-start | bytes 3932168 | tf_op jit(solution)/shard_map/ppermute | solution.py:151
  100.4 3.9 %collective-permute-start.10 = (bf16[160,1536]{1,0:T(8,128)(2,1)S(1)}, bf16[160,1536]{1,0:T(8,128)(2,1)}, u32[]{:S(2)}, u32[]{:S(2)}) collective-permute-start(bf16[160,1536]{1,0:T(8,128)(2,1)S(1)} %copy-done.1), channel_id=1, source_target_pairs={{0,1},{1,0},{2,3},{3,2},{4,5},{5,4},{6,7},{7,6},{8,9},{9,8},{10,11... | collective-permute-start | bytes 1474568 | tf_op jit(solution)/shard_map/ppermute | solution.py:151
  107.6 16.0 %collective-permute-start.13 = (bf16[128,1536]{1,0:T(8,128)(2,1)S(1)}, bf16[128,1536]{1,0:T(8,128)(2,1)S(1)}, u32[]{:S(2)}, u32[]{:S(2)}) collective-permute-start(bf16[128,1536]{1,0:T(8,128)(2,1)S(1)} %get-tuple-element.45), channel_id=1, source_target_pairs={{0,2},{1,3},{2,0},{3,1},{4,6},{5,7},{6,4},{7,5},{8,10},{9,11},{10,... | collective-permute-start | bytes 1179656 | tf_op jit(solution)/shard_map/ppermute | solution.py:162
  111.9 26.4 %collective-permute-start.11 = (bf16[128,1536]{1,0:T(8,128)(2,1)S(1)}, bf16[128,1536]{1,0:T(8,128)(2,1)S(1)}, u32[]{:S(2)}, u32[]{:S(2)}) collective-permute-start(bf16[128,1536]{1,0:T(8,128)(2,1)S(1)} %get-tuple-element.42), channel_id=1, source_target_pairs={{0,4},{1,5},{2,6},{3,7},{4,8},{5,9},{6,10},{7,11},{8,12},{9,13},{1... | collective-permute-start | bytes 1179656 | tf_op jit(solution)/shard_map/ppermute | solution.py:162
  113.9 24.5 %collective-permute-start.12 = (bf16[128,1536]{1,0:T(8,128)(2,1)S(1)}, bf16[128,1536]{1,0:T(8,128)(2,1)S(1)}, u32[]{:S(2)}, u32[]{:S(2)}) collective-permute-start(bf16[128,1536]{1,0:T(8,128)(2,1)S(1)} %get-tuple-element.43), channel_id=1, source_target_pairs={{0,12},{1,13},{2,14},{3,15},{4,0},{5,1},{6,2},{7,3},{8,4},{9,5},{1... | collective-permute-start | bytes 1179656 | tf_op jit(solution)/shard_map/ppermute | solution.py:162
  117.2 15.3 %collective-permute-start.15 = (bf16[128,1536]{1,0:T(8,128)(2,1)S(1)}, bf16[128,1536]{1,0:T(8,128)(2,1)S(1)}, u32[]{:S(2)}, u32[]{:S(2)}) collective-permute-start(bf16[128,1536]{1,0:T(8,128)(2,1)S(1)} %get-tuple-element.47), channel_id=1, source_target_pairs={{0,4},{1,5},{2,6},{3,7},{4,8},{5,9},{6,10},{7,11},{8,12},{9,13},{1... | collective-permute-start | bytes 1179656 | tf_op jit(solution)/shard_map/ppermute | solution.py:162
  120.4 15.4 %collective-permute-start.16 = (bf16[128,1536]{1,0:T(8,128)(2,1)S(1)}, bf16[128,1536]{1,0:T(8,128)(2,1)S(1)}, u32[]{:S(2)}, u32[]{:S(2)}) collective-permute-start(bf16[128,1536]{1,0:T(8,128)(2,1)S(1)} %get-tuple-element.48), channel_id=1, source_target_pairs={{0,12},{1,13},{2,14},{3,15},{4,0},{5,1},{6,2},{7,3},{8,4},{9,5},{1... | collective-permute-start | bytes 1179656 | tf_op jit(solution)/shard_map/ppermute | solution.py:162
  123.7 19.9 %collective-permute-start.14 = (bf16[128,1536]{1,0:T(8,128)(2,1)S(1)}, bf16[128,1536]{1,0:T(8,128)(2,1)S(1)}, u32[]{:S(2)}, u32[]{:S(2)}) collective-permute-start(bf16[128,1536]{1,0:T(8,128)(2,1)S(1)} %add_convert_fusion.2), channel_id=1, source_target_pairs={{0,8},{1,9},{2,10},{3,11},{4,12},{5,13},{6,14},{7,15},{8,0},{9,1},... | collective-permute-start | bytes 1179656 | tf_op jit(solution)/shard_map/ppermute | solution.py:162
  135.9 12.5 %collective-permute-start.17 = (bf16[128,1536]{1,0:T(8,128)(2,1)S(1)}, bf16[128,1536]{1,0:T(8,128)(2,1)S(1)}, u32[]{:S(2)}, u32[]{:S(2)}) collective-permute-start(bf16[128,1536]{1,0:T(8,128)(2,1)S(1)} %add_convert_fusion.1), channel_id=1, source_target_pairs={{0,2},{1,3},{2,0},{3,1},{4,6},{5,7},{6,4},{7,5},{8,10},{9,11},{10,... | collective-permute-start | bytes 1179656 | tf_op jit(solution)/shard_map/ppermute | solution.py:162
  148.4 12.8 %copy-start.2 = (bf16[160,128]{1,0:T(8,128)(2,1)S(1)}, bf16[160,128]{1,0:T(8,128)(2,1)}, u32[]{:S(2)}) copy-start(bf16[160,128]{1,0:T(8,128)(2,1)} %get-tuple-element.27.selector) | copy-start | bytes 122884
  (2 other events, 14.9 us)

commit v10 on v9

--- a/solution.py
+++ b/solution.py
@@ -13,7 +13,7 @@
     )
 
 
-PAIR = 2
+PAIR, FIRST = 2, 11
 
 
 def slot_matrix(bucket, expert_count, capacity):
@@ -29,7 +29,7 @@
     )
     slot = jnp.sum(earlier * chosen, axis=0, keepdims=True).astype(jnp.int32)
     within = lax.bitwise_and(bucket, PAIR - 1)
-    place = expert_count - PAIR - (bucket - within) + within
+    place = lax.rem(expert_count + FIRST * PAIR - (bucket - within), expert_count) + within
     position = place * capacity + slot
     targets = lax.broadcasted_iota(jnp.int32, (expert_count * capacity, token_count), 0)
     return jnp.where(targets == position, 1.0, 0.0).astype(jnp.bfloat16)
@@ -134,8 +134,8 @@
     row_count, blocks, lanes = rows.shape
     sent = rows.reshape(expert_count, row_count // expert_count * blocks, lanes)
     order = [
-        first + within
-        for first in reversed(range(0, expert_count, PAIR))
+        (FIRST * PAIR - back) % expert_count + within
+        for back in range(0, expert_count, PAIR)
         for within in range(PAIR)
     ]
     arrived = lax.all_to_all(

time: 164 us -> 162 us (0.988)
  the two profiles are of different devices: /device:TPU:57 before, /device:TPU:24 now
where the time goes in v10:
time: 162 us; the launch traced here: 161 us
  starting transfers between devices  87.7 us (54%)
  waiting for transfers between devices  52.2 us (32%)
  Pallas kernels  15.2 us (9%)
  local copies, waits for them, and re-layouts  4.1 us (3%)
    ppermute x14, starting transfers between devices, chip_shift(): return lax.ppermute(array, 'fsdp', pairs)  48.5 us
    ppermute x14, waiting for transfers between devices, chip_shift(): return lax.ppermute(array, 'fsdp', pairs)  37.1 us
    all_to_all x2, starting transfers between devices, exchange(): lax.all_to_all(sent, 'ep', split_axis=0, concat_axis=0, tiled=True, axis_...  30.6 us
    pallas_call x3, Pallas kernels, vmem_call(): pl.pallas_call(kernel, out_shape=jax.tree.map(lambda s: pltpu.HBM(s.shape...  12.2 us
    all_to_all x2, waiting for transfers between devices, exchange(): lax.all_to_all(sent, 'ep', split_axis=0, concat_axis=0, tiled=True, axis_...  10.5 us
    ppermute x4, starting transfers between devices, core_swap(): lax.ppermute(array, 'fsdp', [(f, f ^ 1) for f in range(2 * Y * X_HI)])  8.65 us
    ppermute x4, waiting for transfers between devices, core_swap(): lax.ppermute(array, 'fsdp', [(f, f ^ 1) for f in range(2 * Y * X_HI)])  4.56 us
  transfers between devices with their start and end apart: 20, of which 10 were waited for; matrix products, arithmetic and copies ran while one was open for 3% of the time, Pallas kernels for 2%

profile of v10, /device:TPU:24, one launch (start us, length us, event | category | flops | bytes accessed | tf_op | source)
XLA Modules:
  0.0 160.8 jit_solution(4464436030541930500)
XLA Ops:
  0.6 2.9 %shard_map.101 = (bf16[160,32,128]{2,1,0:T(8,128)(2,1)}, bf16[160,128]{1,0:T(8,128)(2,1)}) custom-call(s32[1,128]{1,0:T(1,128)} %bitcast.40, bf16[128,2048]{1,0:T(8,128)(2,1)} %tokens.1, bf16[128,2048]{1,0:T(8,128)(2,1)} %cotangent.1), custom_call_target="tpu_custom_call" | custom-call | tf_op jit(solution)/shard_map/pallas_call | solution.py:100
  3.6 17.4 %all-to-all-start = ((bf16[32,160,128]{2,1,0:T(8,128)(2,1)}), bf16[32,160,128]{2,1,0:T(8,128)(2,1)S(1)}, u32[]{:S(2)}, u32[]{:S(2)}) async-start(bf16[32,160,128]{2,1,0:T(8,128)(2,1)} %bitcast.32), calls=%async_computation | async-start | bytes 2621440 | tf_op jit(solution)/shard_map/all_to_all | solution.py:141
  21.1 4.6 %collective-permute-start.2 = (bf16[128,1536]{1,0:T(8,128)(2,1)S(1)}, bf16[128,1536]{1,0:T(8,128)(2,1)S(1)}, u32[]{:S(2)}, u32[]{:S(2)}) collective-permute-start(bf16[128,1536]{1,0:T(8,128)(2,1)S(1)} %pad_maximum_fusion.1), channel_id=1, source_target_pairs={{0,2},{1,3},{2,0},{3,1},{4,6},{5,7},{6,4},{7,5},{8,10},{9,11},{10,... | collective-permute-start | bytes 1179656 | tf_op jit(solution)/shard_map/ppermute | solution.py:162
  25.7 3.1 %collective-permute-start.5 = (bf16[128,1536]{1,0:T(8,128)(2,1)S(1)}, bf16[128,1536]{1,0:T(8,128)(2,1)S(1)}, u32[]{:S(2)}, u32[]{:S(2)}) collective-permute-start(bf16[128,1536]{1,0:T(8,128)(2,1)S(1)} %pad_maximum_fusion.1), channel_id=1, source_target_pairs={{0,8},{1,9},{2,10},{3,11},{4,12},{5,13},{6,14},{7,15},{8,0},{9,1},... | collective-permute-start | bytes 1179656 | tf_op jit(solution)/shard_map/ppermute | solution.py:162
  30.8 5.1 %collective-permute-start = (bf16[128,1536]{1,0:T(8,128)(2,1)S(1)}, bf16[128,1536]{1,0:T(8,128)(2,1)S(1)}, u32[]{:S(2)}, u32[]{:S(2)}) collective-permute-start(bf16[128,1536]{1,0:T(8,128)(2,1)S(1)} %pad_maximum_fusion.1), channel_id=1, source_target_pairs={{0,4},{1,5},{2,6},{3,7},{4,8},{5,9},{6,10},{7,11},{8,12},{9,13},{1... | collective-permute-start | bytes 1179656 | tf_op jit(solution)/shard_map/ppermute | solution.py:162
  37.7 2.6 %collective-permute-start.6 = (bf16[128,1536]{1,0:T(8,128)(2,1)S(1)}, bf16[128,1536]{1,0:T(8,128)(2,1)S(1)}, u32[]{:S(2)}, u32[]{:S(2)}) collective-permute-start(bf16[128,1536]{1,0:T(8,128)(2,1)S(1)} %collective-permute-done.2), channel_id=1, source_target_pairs={{0,12},{1,13},{2,14},{3,15},{4,0},{5,1},{6,2},{7,3},{8,4},{9,5},{1... | collective-permute-start | bytes 1179656 | tf_op jit(solution)/shard_map/ppermute | solution.py:162
  40.3 4.4 %collective-permute-start.3 = (bf16[128,1536]{1,0:T(8,128)(2,1)S(1)}, bf16[128,1536]{1,0:T(8,128)(2,1)S(1)}, u32[]{:S(2)}, u32[]{:S(2)}) collective-permute-start(bf16[128,1536]{1,0:T(8,128)(2,1)S(1)} %collective-permute-done.2), channel_id=1, source_target_pairs={{0,4},{1,5},{2,6},{3,7},{4,8},{5,9},{6,10},{7,11},{8,12},{9,13},{1... | collective-permute-start | bytes 1179656 | tf_op jit(solution)/shard_map/ppermute | solution.py:162
  44.8 4.4 %collective-permute-start.7 = (bf16[128,1536]{1,0:T(8,128)(2,1)S(1)}, bf16[128,1536]{1,0:T(8,128)(2,1)S(1)}, u32[]{:S(2)}, u32[]{:S(2)}) collective-permute-start(bf16[128,1536]{1,0:T(8,128)(2,1)S(1)} %collective-permute-done.5), channel_id=1, source_target_pairs={{0,2},{1,3},{2,0},{3,1},{4,6},{5,7},{6,4},{7,5},{8,10},{9,11},{10,... | collective-permute-start | bytes 1179656 | tf_op jit(solution)/shard_map/ppermute | solution.py:162
  50.7 5.3 %collective-permute-done.6 = bf16[128,1536]{1,0:T(8,128)(2,1)S(1)} collective-permute-done((bf16[128,1536]{1,0:T(8,128)(2,1)S(1)}, bf16[128,1536]{1,0:T(8,128)(2,1)S(1)}, u32[]{:S(2)}, u32[]{:S(2)}) %collective-permute-start.6) | collective-permute-done | bytes 393248 | tf_op jit(solution)/shard_map/ppermute | solution.py:162
  61.9 2.4 %collective-permute-start.4 = (bf16[512,1536]{1,0:T(8,128)(2,1)S(1)}, bf16[512,1536]{1,0:T(8,128)(2,1)}, u32[]{:S(2)}, u32[]{:S(2)}) collective-permute-start(bf16[512,1536]{1,0:T(8,128)(2,1)S(1)} %pad_maximum_fusion.refs_0_), channel_id=1, source_target_pairs={{0,1},{1,0},{2,3},{3,2},{4,5},{5,4},{6,7},{7,6},{8,9},{9,8},{10,11... | collective-permute-start | bytes 4718600 | tf_op jit(solution)/shard_map/ppermute | solution.py:151
  67.5 10.5 %all-to-all-done = bf16[32,160,128]{2,1,0:T(8,128)(2,1)S(1)} async-done(((bf16[32,160,128]{2,1,0:T(8,128)(2,1)}), bf16[32,160,128]{2,1,0:T(8,128)(2,1)S(1)}, u32[]{:S(2)}, u32[]{:S(2)}) %all-to-all-start) | async-done | bytes 1310752 | tf_op jit(solution)/shard_map/all_to_all | solution.py:141
  78.0 7.4 %shard_map.102 = (bf16[160,32,128]{2,1,0:T(8,128)(2,1)}, bf16[160,1536]{1,0:T(8,128)(2,1)}, bf16[32,160,128]{2,1,0:T(8,128)(2,1)}) custom-call(s32[16]{0:T(128)S(1)} %stack.78.numbers, bf16[160,32,128]{2,1,0:T(8,128)(2,1)S(1)} %bitcast.31, bf16[512,1536]{1,0:T(8,128)(2,1)S(1)} %pad_maximum_fusion.refs_0_, bf16[512,1536]{1,0:T(8,128)(2,1)} %collective-permute-done.4.refs_1_, ...), custom_call_target="tpu_custom_call" | custom-call | tf_op jit(solution)/shard_map/pallas_call | solution.py:44
  85.5 13.2 %all-to-all-start.1 = ((bf16[32,160,128]{2,1,0:T(8,128)(2,1)}), bf16[32,160,128]{2,1,0:T(8,128)(2,1)S(1)}, u32[]{:S(2)}, u32[]{:S(2)}) async-start(bf16[32,160,128]{2,1,0:T(8,128)(2,1)} %bitcast.33), calls=%async_computation.1 | async-start | bytes 2621440 | tf_op jit(solution)/shard_map/all_to_all | solution.py:141
  100.6 2.4 %collective-permute-start.10 = (bf16[160,1536]{1,0:T(8,128)(2,1)S(1)}, bf16[160,1536]{1,0:T(8,128)(2,1)}, u32[]{:S(2)}, u32[]{:S(2)}) collective-permute-start(bf16[160,1536]{1,0:T(8,128)(2,1)S(1)} %copy-done.1), channel_id=1, source_target_pairs={{0,1},{1,0},{2,3},{3,2},{4,5},{5,4},{6,7},{7,6},{8,9},{9,8},{10,11... | collective-permute-start | bytes 1474568 | tf_op jit(solution)/shard_map/ppermute | solution.py:151
  104.7 3.3 %shard_map.104 = (bf16[128,1536]{1,0:T(8,128)(2,1)S(1)}, bf16[128,1536]{1,0:T(8,128)(2,1)S(1)}, bf16[128,1536]{1,0:T(8,128)(2,1)S(1)}, bf16[128,1536]{1,0:T(8,12...) custom-call(s32[8]{0:T(128)S(1)} %stack.79.numbers, ...), custom_call_target="tpu_custom_call" | custom-call | tf_op jit(solution)/shard_map/pallas_call | solution.py:44
  107.9 4.7 %collective-permute-start.13 = (bf16[128,1536]{1,0:T(8,128)(2,1)S(1)}, bf16[128,1536]{1,0:T(8,128)(2,1)S(1)}, u32[]{:S(2)}, u32[]{:S(2)}) collective-permute-start(bf16[128,1536]{1,0:T(8,128)(2,1)S(1)} %get-tuple-element.45), channel_id=1, source_target_pairs={{0,2},{1,3},{2,0},{3,1},{4,6},{5,7},{6,4},{7,5},{8,10},{9,11},{10,... | collective-permute-start | bytes 1179656 | tf_op jit(solution)/shard_map/ppermute | solution.py:162
  114.7 3.7 %collective-permute-start.12 = (bf16[128,1536]{1,0:T(8,128)(2,1)S(1)}, bf16[128,1536]{1,0:T(8,128)(2,1)S(1)}, u32[]{:S(2)}, u32[]{:S(2)}) collective-permute-start(bf16[128,1536]{1,0:T(8,128)(2,1)S(1)} %get-tuple-element.43), channel_id=1, source_target_pairs={{0,12},{1,13},{2,14},{3,15},{4,0},{5,1},{6,2},{7,3},{8,4},{9,5},{1... | collective-permute-start | bytes 1179656 | tf_op jit(solution)/shard_map/ppermute | solution.py:162
  118.4 3.3 %collective-permute-start.15 = (bf16[128,1536]{1,0:T(8,128)(2,1)S(1)}, bf16[128,1536]{1,0:T(8,128)(2,1)S(1)}, u32[]{:S(2)}, u32[]{:S(2)}) collective-permute-start(bf16[128,1536]{1,0:T(8,128)(2,1)S(1)} %get-tuple-element.47), channel_id=1, source_target_pairs={{0,4},{1,5},{2,6},{3,7},{4,8},{5,9},{6,10},{7,11},{8,12},{9,13},{1... | collective-permute-start | bytes 1179656 | tf_op jit(solution)/shard_map/ppermute | solution.py:162
  121.8 2.5 %collective-permute-start.16 = (bf16[128,1536]{1,0:T(8,128)(2,1)S(1)}, bf16[128,1536]{1,0:T(8,128)(2,1)S(1)}, u32[]{:S(2)}, u32[]{:S(2)}) collective-permute-start(bf16[128,1536]{1,0:T(8,128)(2,1)S(1)} %get-tuple-element.48), channel_id=1, source_target_pairs={{0,12},{1,13},{2,14},{3,15},{4,0},{5,1},{6,2},{7,3},{8,4},{9,5},{1... | collective-permute-start | bytes 1179656 | tf_op jit(solution)/shard_map/ppermute | solution.py:162
  124.4 3.2 %collective-permute-start.14 = (bf16[128,1536]{1,0:T(8,128)(2,1)S(1)}, bf16[128,1536]{1,0:T(8,128)(2,1)S(1)}, u32[]{:S(2)}, u32[]{:S(2)}) collective-permute-start(bf16[128,1536]{1,0:T(8,128)(2,1)S(1)} %add_convert_fusion.2), channel_id=1, source_target_pairs={{0,8},{1,9},{2,10},{3,11},{4,12},{5,13},{6,14},{7,15},{8,0},{9,1},... | collective-permute-start | bytes 1179656 | tf_op jit(solution)/shard_map/ppermute | solution.py:162
  127.6 7.3 %collective-permute-done.15 = bf16[128,1536]{1,0:T(8,128)(2,1)S(1)} collective-permute-done((bf16[128,1536]{1,0:T(8,128)(2,1)S(1)}, bf16[128,1536]{1,0:T(8,128)(2,1)S(1)}, u32[]{:S(2)}, u32[]{:S(2)}) %collective-permute-start.15) | collective-permute-done | bytes 393248 | tf_op jit(solution)/shard_map/ppermute | solution.py:162
  134.9 10.7 %collective-permute-done.16 = bf16[128,1536]{1,0:T(8,128)(2,1)S(1)} collective-permute-done((bf16[128,1536]{1,0:T(8,128)(2,1)S(1)}, bf16[128,1536]{1,0:T(8,128)(2,1)S(1)}, u32[]{:S(2)}, u32[]{:S(2)}) %collective-permute-start.16) | collective-permute-done | bytes 393248 | tf_op jit(solution)/shard_map/ppermute | solution.py:162
  145.7 2.7 %collective-permute-start.17 = (bf16[128,1536]{1,0:T(8,128)(2,1)S(1)}, bf16[128,1536]{1,0:T(8,128)(2,1)S(1)}, u32[]{:S(2)}, u32[]{:S(2)}) collective-permute-start(bf16[128,1536]{1,0:T(8,128)(2,1)S(1)} %add_convert_fusion.1), channel_id=1, source_target_pairs={{0,2},{1,3},{2,0},{3,1},{4,6},{5,7},{6,4},{7,5},{8,10},{9,11},{10,... | collective-permute-start | bytes 1179656 | tf_op jit(solution)/shard_map/ppermute | solution.py:162
  148.5 9.8 %collective-permute-done.17 = bf16[128,1536]{1,0:T(8,128)(2,1)S(1)} collective-permute-done((bf16[128,1536]{1,0:T(8,128)(2,1)S(1)}, bf16[128,1536]{1,0:T(8,128)(2,1)S(1)}, u32[]{:S(2)}, u32[]{:S(2)}) %collective-permute-start.17) | collective-permute-done | bytes 393248 | tf_op jit(solution)/shard_map/ppermute | solution.py:162
  (44 shorter events, 22.8 us)
Async XLA Ops:
  3.6 17.4 %copy-start.3 = (bf16[1,128,512]{2,1,0:T(8,128)(2,1)S(1)}, bf16[1,128,512]{2,1,0:T(8,128)(2,1)}, u32[]{:S(2)}) copy-start(bf16[1,128,512]{2,1,0:T(8,128)(2,1)} %param.11) | copy-start | bytes 393220
  3.6 17.4 %copy-start.4 = (bf16[1,128,512]{2,1,0:T(8,128)(2,1)S(1)}, bf16[1,128,512]{2,1,0:T(8,128)(2,1)}, u32[]{:S(2)}) copy-start(bf16[1,128,512]{2,1,0:T(8,128)(2,1)} %param.10) | copy-start | bytes 393220
  3.6 17.4 %copy-start.5 = (bf16[1,128,512]{2,1,0:T(8,128)(2,1)S(1)}, bf16[1,128,512]{2,1,0:T(8,128)(2,1)}, u32[]{:S(2)}) copy-start(bf16[1,128,512]{2,1,0:T(8,128)(2,1)} %param.9) | copy-start | bytes 393220
  3.6 74.4 %all-to-all-start = ((bf16[32,160,128]{2,1,0:T(8,128)(2,1)}), bf16[32,160,128]{2,1,0:T(8,128)(2,1)S(1)}, u32[]{:S(2)}, u32[]{:S(2)}) async-start(bf16[32,160,128]{2,1,0:T(8,128)(2,1)} %bitcast.32), calls=%async_computation | async-start | bytes 2621440 | tf_op jit(solution)/shard_map/all_to_all | solution.py:141
  21.1 16.6 %collective-permute-start.2 = (bf16[128,1536]{1,0:T(8,128)(2,1)S(1)}, bf16[128,1536]{1,0:T(8,128)(2,1)S(1)}, u32[]{:S(2)}, u32[]{:S(2)}) collective-permute-start(bf16[128,1536]{1,0:T(8,128)(2,1)S(1)} %pad_maximum_fusion.1), channel_id=1, source_target_pairs={{0,2},{1,3},{2,0},{3,1},{4,6},{5,7},{6,4},{7,5},{8,10},{9,11},{10,... | collective-permute-start | bytes 1179656 | tf_op jit(solution)/shard_map/ppermute | solution.py:162
  25.7 19.0 %collective-permute-start.5 = (bf16[128,1536]{1,0:T(8,128)(2,1)S(1)}, bf16[128,1536]{1,0:T(8,128)(2,1)S(1)}, u32[]{:S(2)}, u32[]{:S(2)}) collective-permute-start(bf16[128,1536]{1,0:T(8,128)(2,1)S(1)} %pad_maximum_fusion.1), channel_id=1, source_target_pairs={{0,8},{1,9},{2,10},{3,11},{4,12},{5,13},{6,14},{7,15},{8,0},{9,1},... | collective-permute-start | bytes 1179656 | tf_op jit(solution)/shard_map/ppermute | solution.py:162
  28.9 32.9 %collective-permute-start.1 = (bf16[128,1536]{1,0:T(8,128)(2,1)S(1)}, bf16[128,1536]{1,0:T(8,128)(2,1)S(1)}, u32[]{:S(2)}, u32[]{:S(2)}) collective-permute-start(bf16[128,1536]{1,0:T(8,128)(2,1)S(1)} %pad_maximum_fusion.1), channel_id=1, source_target_pairs={{0,12},{1,13},{2,14},{3,15},{4,0},{5,1},{6,2},{7,3},{8,4},{9,5},{1... | collective-permute-start | bytes 1179656 | tf_op jit(solution)/shard_map/ppermute | solution.py:162
  30.8 31.0 %collective-permute-start = (bf16[128,1536]{1,0:T(8,128)(2,1)S(1)}, bf16[128,1536]{1,0:T(8,128)(2,1)S(1)}, u32[]{:S(2)}, u32[]{:S(2)}) collective-permute-start(bf16[128,1536]{1,0:T(8,128)(2,1)S(1)} %pad_maximum_fusion.1), channel_id=1, source_target_pairs={{0,4},{1,5},{2,6},{3,7},{4,8},{5,9},{6,10},{7,11},{8,12},{9,13},{1... | collective-permute-start | bytes 1179656 | tf_op jit(solution)/shard_map/ppermute | solution.py:162
  37.7 18.3 %collective-permute-start.6 = (bf16[128,1536]{1,0:T(8,128)(2,1)S(1)}, bf16[128,1536]{1,0:T(8,128)(2,1)S(1)}, u32[]{:S(2)}, u32[]{:S(2)}) collective-permute-start(bf16[128,1536]{1,0:T(8,128)(2,1)S(1)} %collective-permute-done.2), channel_id=1, source_target_pairs={{0,12},{1,13},{2,14},{3,15},{4,0},{5,1},{6,2},{7,3},{8,4},{9,5},{1... | collective-permute-start | bytes 1179656 | tf_op jit(solution)/shard_map/ppermute | solution.py:162
  40.3 21.5 %collective-permute-start.3 = (bf16[128,1536]{1,0:T(8,128)(2,1)S(1)}, bf16[128,1536]{1,0:T(8,128)(2,1)S(1)}, u32[]{:S(2)}, u32[]{:S(2)}) collective-permute-start(bf16[128,1536]{1,0:T(8,128)(2,1)S(1)} %collective-permute-done.2), channel_id=1, source_target_pairs={{0,4},{1,5},{2,6},{3,7},{4,8},{5,9},{6,10},{7,11},{8,12},{9,13},{1... | collective-permute-start | bytes 1179656 | tf_op jit(solution)/shard_map/ppermute | solution.py:162
  44.8 14.3 %collective-permute-start.7 = (bf16[128,1536]{1,0:T(8,128)(2,1)S(1)}, bf16[128,1536]{1,0:T(8,128)(2,1)S(1)}, u32[]{:S(2)}, u32[]{:S(2)}) collective-permute-start(bf16[128,1536]{1,0:T(8,128)(2,1)S(1)} %collective-permute-done.5), channel_id=1, source_target_pairs={{0,2},{1,3},{2,0},{3,1},{4,6},{5,7},{6,4},{7,5},{8,10},{9,11},{10,... | collective-permute-start | bytes 1179656 | tf_op jit(solution)/shard_map/ppermute | solution.py:162
  59.9 5.6 %collective-permute-start.8 = (bf16[512,1536]{1,0:T(8,128)(2,1)}, bf16[512,1536]{1,0:T(8,128)(2,1)}, u32[]{:S(2)}, u32[]{:S(2)}) collective-permute-start(bf16[512,1536]{1,0:T(8,128)(2,1)} %constant_dynamic-update-slice_fusion.refs_2_), channel_id=1, source_target_pairs={{0,1},{1,0},{2,3},{3,2},{4,5},{5,4},{6,7},{7,6},{8,9},{9,8},{10,11... | collective-permute-start | bytes 4718600 | tf_op jit(solution)/shard_map/ppermute | solution.py:151
  61.9 5.6 %collective-permute-start.4 = (bf16[512,1536]{1,0:T(8,128)(2,1)S(1)}, bf16[512,1536]{1,0:T(8,128)(2,1)}, u32[]{:S(2)}, u32[]{:S(2)}) collective-permute-start(bf16[512,1536]{1,0:T(8,128)(2,1)S(1)} %pad_maximum_fusion.refs_0_), channel_id=1, source_target_pairs={{0,1},{1,0},{2,3},{3,2},{4,5},{5,4},{6,7},{7,6},{8,9},{9,8},{10,11... | collective-permute-start | bytes 4718600 | tf_op jit(solution)/shard_map/ppermute | solution.py:151
  85.5 15.2 %copy-start.1 = (bf16[160,1536]{1,0:T(8,128)(2,1)S(1)}, bf16[160,1536]{1,0:T(8,128)(2,1)}, u32[]{:S(2)}) copy-start(bf16[160,1536]{1,0:T(8,128)(2,1)} %get-tuple-element.40.own_sides) | copy-start | bytes 1474564
  85.5 73.8 %all-to-all-start.1 = ((bf16[32,160,128]{2,1,0:T(8,128)(2,1)}), bf16[32,160,128]{2,1,0:T(8,128)(2,1)S(1)}, u32[]{:S(2)}, u32[]{:S(2)}) async-start(bf16[32,160,128]{2,1,0:T(8,128)(2,1)} %bitcast.33), calls=%async_computation.1 | async-start | bytes 2621440 | tf_op jit(solution)/shard_map/all_to_all | solution.py:141
  98.7 6.0 %collective-permute-start.9 = (bf16[32,160,128]{2,1,0:T(8,128)(2,1)S(1)}, bf16[32,160,128]{2,1,0:T(8,128)(2,1)}, u32[]{:S(2)}, u32[]{:S(2)}) collective-permute-start(bf16[32,160,128]{2,1,0:T(8,128)(2,1)S(1)} %copy-done), channel_id=1, source_target_pairs={{0,1},{1,0},{2,3},{3,2},{4,5},{5,4},{6,7},{7,6},{8,9},{9,8},{10,11... | collective-permute-start | bytes 3932168 | tf_op jit(solution)/shard_map/ppermute | solution.py:151
  100.6 4.0 %collective-permute-start.10 = (bf16[160,1536]{1,0:T(8,128)(2,1)S(1)}, bf16[160,1536]{1,0:T(8,128)(2,1)}, u32[]{:S(2)}, u32[]{:S(2)}) collective-permute-start(bf16[160,1536]{1,0:T(8,128)(2,1)S(1)} %copy-done.1), channel_id=1, source_target_pairs={{0,1},{1,0},{2,3},{3,2},{4,5},{5,4},{6,7},{7,6},{8,9},{9,8},{10,11... | collective-permute-start | bytes 1474568 | tf_op jit(solution)/shard_map/ppermute | solution.py:151
  107.9 16.4 %collective-permute-start.13 = (bf16[128,1536]{1,0:T(8,128)(2,1)S(1)}, bf16[128,1536]{1,0:T(8,128)(2,1)S(1)}, u32[]{:S(2)}, u32[]{:S(2)}) collective-permute-start(bf16[128,1536]{1,0:T(8,128)(2,1)S(1)} %get-tuple-element.45), channel_id=1, source_target_pairs={{0,2},{1,3},{2,0},{3,1},{4,6},{5,7},{6,4},{7,5},{8,10},{9,11},{10,... | collective-permute-start | bytes 1179656 | tf_op jit(solution)/shard_map/ppermute | solution.py:162
  112.6 35.8 %collective-permute-start.11 = (bf16[128,1536]{1,0:T(8,128)(2,1)S(1)}, bf16[128,1536]{1,0:T(8,128)(2,1)S(1)}, u32[]{:S(2)}, u32[]{:S(2)}) collective-permute-start(bf16[128,1536]{1,0:T(8,128)(2,1)S(1)} %get-tuple-element.42), channel_id=1, source_target_pairs={{0,4},{1,5},{2,6},{3,7},{4,8},{5,9},{6,10},{7,11},{8,12},{9,13},{1... | collective-permute-start | bytes 1179656 | tf_op jit(solution)/shard_map/ppermute | solution.py:162
  114.7 33.7 %collective-permute-start.12 = (bf16[128,1536]{1,0:T(8,128)(2,1)S(1)}, bf16[128,1536]{1,0:T(8,128)(2,1)S(1)}, u32[]{:S(2)}, u32[]{:S(2)}) collective-permute-start(bf16[128,1536]{1,0:T(8,128)(2,1)S(1)} %get-tuple-element.43), channel_id=1, source_target_pairs={{0,12},{1,13},{2,14},{3,15},{4,0},{5,1},{6,2},{7,3},{8,4},{9,5},{1... | collective-permute-start | bytes 1179656 | tf_op jit(solution)/shard_map/ppermute | solution.py:162
  118.4 16.4 %collective-permute-start.15 = (bf16[128,1536]{1,0:T(8,128)(2,1)S(1)}, bf16[128,1536]{1,0:T(8,128)(2,1)S(1)}, u32[]{:S(2)}, u32[]{:S(2)}) collective-permute-start(bf16[128,1536]{1,0:T(8,128)(2,1)S(1)} %get-tuple-element.47), channel_id=1, source_target_pairs={{0,4},{1,5},{2,6},{3,7},{4,8},{5,9},{6,10},{7,11},{8,12},{9,13},{1... | collective-permute-start | bytes 1179656 | tf_op jit(solution)/shard_map/ppermute | solution.py:162
  121.8 23.8 %collective-permute-start.16 = (bf16[128,1536]{1,0:T(8,128)(2,1)S(1)}, bf16[128,1536]{1,0:T(8,128)(2,1)S(1)}, u32[]{:S(2)}, u32[]{:S(2)}) collective-permute-start(bf16[128,1536]{1,0:T(8,128)(2,1)S(1)} %get-tuple-element.48), channel_id=1, source_target_pairs={{0,12},{1,13},{2,14},{3,15},{4,0},{5,1},{6,2},{7,3},{8,4},{9,5},{1... | collective-permute-start | bytes 1179656 | tf_op jit(solution)/shard_map/ppermute | solution.py:162
  124.4 24.0 %collective-permute-start.14 = (bf16[128,1536]{1,0:T(8,128)(2,1)S(1)}, bf16[128,1536]{1,0:T(8,128)(2,1)S(1)}, u32[]{:S(2)}, u32[]{:S(2)}) collective-permute-start(bf16[128,1536]{1,0:T(8,128)(2,1)S(1)} %add_convert_fusion.2), channel_id=1, source_target_pairs={{0,8},{1,9},{2,10},{3,11},{4,12},{5,13},{6,14},{7,15},{8,0},{9,1},... | collective-permute-start | bytes 1179656 | tf_op jit(solution)/shard_map/ppermute | solution.py:162
  145.7 12.5 %collective-permute-start.17 = (bf16[128,1536]{1,0:T(8,128)(2,1)S(1)}, bf16[128,1536]{1,0:T(8,128)(2,1)S(1)}, u32[]{:S(2)}, u32[]{:S(2)}) collective-permute-start(bf16[128,1536]{1,0:T(8,128)(2,1)S(1)} %add_convert_fusion.1), channel_id=1, source_target_pairs={{0,2},{1,3},{2,0},{3,1},{4,6},{5,7},{6,4},{7,5},{8,10},{9,11},{10,... | collective-permute-start | bytes 1179656 | tf_op jit(solution)/shard_map/ppermute | solution.py:162
  (2 other events, 14.3 us)

commit v11 on v10

--- a/solution.py
+++ b/solution.py
@@ -329,14 +329,17 @@
     def summed(*arrays):
         return add(*arrays).astype(tokens.dtype)
 
-    two = summed(terms[2, 0], chip_shift(terms[2, 1], 0, 1))
+    crossed, one, three = lax.optimization_barrier(
+        (chip_shift(terms[2, 1], 0, 1), terms[1, 0], terms[3, 0])
+    )
+    two = summed(terms[2, 0], crossed)
     across = summed(
         terms[0, 1], chip_shift(terms[1, 1], 1, 0), chip_shift(terms[3, 1], 3, 0)
     )
     total = add(
         terms[0, 0],
-        chip_shift(terms[1, 0], 1, 0),
-        chip_shift(terms[3, 0], 3, 0),
+        chip_shift(one, 1, 0),
+        chip_shift(three, 3, 0),
         chip_shift(two, 2, 0),
         chip_shift(across, 0, 1),
     )

time: 162 us -> 158 us (0.975)
  the two profiles are of different devices: /device:TPU:24 before, /device:TPU:6 now
where the time goes in v11:
time: 158 us; the launch traced here: 157 us
  starting transfers between devices  89 us (56%)
  waiting for transfers between devices  46.8 us (30%)
  Pallas kernels  15.2 us (10%)
  local copies, waits for them, and re-layouts  4.1 us (3%)
    ppermute x14, starting transfers between devices, chip_shift(): return lax.ppermute(array, 'fsdp', pairs)  49.6 us
    all_to_all x2, starting transfers between devices, exchange(): lax.all_to_all(sent, 'ep', split_axis=0, concat_axis=0, tiled=True, axis_...  30.8 us
    ppermute x14, waiting for transfers between devices, chip_shift(): return lax.ppermute(array, 'fsdp', pairs)  30.3 us
    pallas_call x3, Pallas kernels, vmem_call(): pl.pallas_call(kernel, out_shape=jax.tree.map(lambda s: pltpu.HBM(s.shape...  12.2 us
    all_to_all x2, waiting for transfers between devices, exchange(): lax.all_to_all(sent, 'ep', split_axis=0, concat_axis=0, tiled=True, axis_...  11.9 us
    ppermute x4, starting transfers between devices, core_swap(): lax.ppermute(array, 'fsdp', [(f, f ^ 1) for f in range(2 * Y * X_HI)])  8.65 us
    ppermute x4, waiting for transfers between devices, core_swap(): lax.ppermute(array, 'fsdp', [(f, f ^ 1) for f in range(2 * Y * X_HI)])  4.56 us
  transfers between devices with their start and end apart: 20, of which 12 were waited for; matrix products, arithmetic and copies ran while one was open for 3% of the time, Pallas kernels for 2%

profile of v11, /device:TPU:6, one launch (start us, length us, event | category | flops | bytes accessed | tf_op | source)
XLA Modules:
  0.0 156.8 jit_solution(2305787709626317007)
XLA Ops:
  0.6 2.9 %shard_map.101 = (bf16[160,32,128]{2,1,0:T(8,128)(2,1)}, bf16[160,128]{1,0:T(8,128)(2,1)}) custom-call(s32[1,128]{1,0:T(1,128)} %bitcast.40, bf16[128,2048]{1,0:T(8,128)(2,1)} %tokens.1, bf16[128,2048]{1,0:T(8,128)(2,1)} %cotangent.1), custom_call_target="tpu_custom_call" | custom-call | tf_op jit(solution)/shard_map/pallas_call | solution.py:100
  3.6 17.4 %all-to-all-start = ((bf16[32,160,128]{2,1,0:T(8,128)(2,1)}), bf16[32,160,128]{2,1,0:T(8,128)(2,1)S(1)}, u32[]{:S(2)}, u32[]{:S(2)}) async-start(bf16[32,160,128]{2,1,0:T(8,128)(2,1)} %bitcast.32), calls=%async_computation | async-start | bytes 2621440 | tf_op jit(solution)/shard_map/all_to_all | solution.py:141
  21.1 3.3 %collective-permute-start.2 = (bf16[128,1536]{1,0:T(8,128)(2,1)S(1)}, bf16[128,1536]{1,0:T(8,128)(2,1)S(1)}, u32[]{:S(2)}, u32[]{:S(2)}) collective-permute-start(bf16[128,1536]{1,0:T(8,128)(2,1)S(1)} %pad_maximum_fusion.1), channel_id=1, source_target_pairs={{0,2},{1,3},{2,0},{3,1},{4,6},{5,7},{6,4},{7,5},{8,10},{9,11},{10,... | collective-permute-start | bytes 1179656 | tf_op jit(solution)/shard_map/ppermute | solution.py:162
  24.4 5.1 %collective-permute-start.5 = (bf16[128,1536]{1,0:T(8,128)(2,1)S(1)}, bf16[128,1536]{1,0:T(8,128)(2,1)S(1)}, u32[]{:S(2)}, u32[]{:S(2)}) collective-permute-start(bf16[128,1536]{1,0:T(8,128)(2,1)S(1)} %pad_maximum_fusion.1), channel_id=1, source_target_pairs={{0,8},{1,9},{2,10},{3,11},{4,12},{5,13},{6,14},{7,15},{8,0},{9,1},... | collective-permute-start | bytes 1179656 | tf_op jit(solution)/shard_map/ppermute | solution.py:162
  29.5 3.0 %collective-permute-start.1 = (bf16[128,1536]{1,0:T(8,128)(2,1)S(1)}, bf16[128,1536]{1,0:T(8,128)(2,1)S(1)}, u32[]{:S(2)}, u32[]{:S(2)}) collective-permute-start(bf16[128,1536]{1,0:T(8,128)(2,1)S(1)} %pad_maximum_fusion.1), channel_id=1, source_target_pairs={{0,12},{1,13},{2,14},{3,15},{4,0},{5,1},{6,2},{7,3},{8,4},{9,5},{1... | collective-permute-start | bytes 1179656 | tf_op jit(solution)/shard_map/ppermute | solution.py:162
  32.5 2.9 %collective-permute-start = (bf16[128,1536]{1,0:T(8,128)(2,1)S(1)}, bf16[128,1536]{1,0:T(8,128)(2,1)S(1)}, u32[]{:S(2)}, u32[]{:S(2)}) collective-permute-start(bf16[128,1536]{1,0:T(8,128)(2,1)S(1)} %pad_maximum_fusion.1), channel_id=1, source_target_pairs={{0,4},{1,5},{2,6},{3,7},{4,8},{5,9},{6,10},{7,11},{8,12},{9,13},{1... | collective-permute-start | bytes 1179656 | tf_op jit(solution)/shard_map/ppermute | solution.py:162
  38.1 4.9 %collective-permute-start.6 = (bf16[128,1536]{1,0:T(8,128)(2,1)S(1)}, bf16[128,1536]{1,0:T(8,128)(2,1)S(1)}, u32[]{:S(2)}, u32[]{:S(2)}) collective-permute-start(bf16[128,1536]{1,0:T(8,128)(2,1)S(1)} %collective-permute-done.2), channel_id=1, source_target_pairs={{0,12},{1,13},{2,14},{3,15},{4,0},{5,1},{6,2},{7,3},{8,4},{9,5},{1... | collective-permute-start | bytes 1179656 | tf_op jit(solution)/shard_map/ppermute | solution.py:162
  45.0 3.7 %collective-permute-start.7 = (bf16[128,1536]{1,0:T(8,128)(2,1)S(1)}, bf16[128,1536]{1,0:T(8,128)(2,1)S(1)}, u32[]{:S(2)}, u32[]{:S(2)}) collective-permute-start(bf16[128,1536]{1,0:T(8,128)(2,1)S(1)} %collective-permute-done.5), channel_id=1, source_target_pairs={{0,2},{1,3},{2,0},{3,1},{4,6},{5,7},{6,4},{7,5},{8,10},{9,11},{10,... | collective-permute-start | bytes 1179656 | tf_op jit(solution)/shard_map/ppermute | solution.py:162
  50.2 4.8 %collective-permute-done.6 = bf16[128,1536]{1,0:T(8,128)(2,1)S(1)} collective-permute-done((bf16[128,1536]{1,0:T(8,128)(2,1)S(1)}, bf16[128,1536]{1,0:T(8,128)(2,1)S(1)}, u32[]{:S(2)}, u32[]{:S(2)}) %collective-permute-start.6) | collective-permute-done | bytes 393248 | tf_op jit(solution)/shard_map/ppermute | solution.py:162
  55.8 3.3 %collective-permute-done.7 = bf16[128,1536]{1,0:T(8,128)(2,1)S(1)} collective-permute-done((bf16[128,1536]{1,0:T(8,128)(2,1)S(1)}, bf16[128,1536]{1,0:T(8,128)(2,1)S(1)}, u32[]{:S(2)}, u32[]{:S(2)}) %collective-permute-start.7) | collective-permute-done | bytes 393248 | tf_op jit(solution)/shard_map/ppermute | solution.py:162
  67.6 10.1 %all-to-all-done = bf16[32,160,128]{2,1,0:T(8,128)(2,1)S(1)} async-done(((bf16[32,160,128]{2,1,0:T(8,128)(2,1)}), bf16[32,160,128]{2,1,0:T(8,128)(2,1)S(1)}, u32[]{:S(2)}, u32[]{:S(2)}) %all-to-all-start) | async-done | bytes 1310752 | tf_op jit(solution)/shard_map/all_to_all | solution.py:141
  77.8 7.4 %shard_map.102 = (bf16[160,32,128]{2,1,0:T(8,128)(2,1)}, bf16[160,1536]{1,0:T(8,128)(2,1)}, bf16[32,160,128]{2,1,0:T(8,128)(2,1)}) custom-call(s32[16]{0:T(128)S(1)} %stack.78.numbers, bf16[160,32,128]{2,1,0:T(8,128)(2,1)S(1)} %bitcast.31, bf16[512,1536]{1,0:T(8,128)(2,1)S(1)} %pad_maximum_fusion.refs_0_, bf16[512,1536]{1,0:T(8,128)(2,1)} %collective-permute-done.4.refs_1_, ...), custom_call_target="tpu_custom_call" | custom-call | tf_op jit(solution)/shard_map/pallas_call | solution.py:44
  85.2 13.5 %all-to-all-start.1 = ((bf16[32,160,128]{2,1,0:T(8,128)(2,1)}), bf16[32,160,128]{2,1,0:T(8,128)(2,1)S(1)}, u32[]{:S(2)}, u32[]{:S(2)}) async-start(bf16[32,160,128]{2,1,0:T(8,128)(2,1)} %bitcast.33), calls=%async_computation.1 | async-start | bytes 2621440 | tf_op jit(solution)/shard_map/all_to_all | solution.py:141
  104.6 3.3 %shard_map.104 = (bf16[128,1536]{1,0:T(8,128)(2,1)S(1)}, bf16[128,1536]{1,0:T(8,128)(2,1)S(1)}, bf16[128,1536]{1,0:T(8,128)(2,1)S(1)}, bf16[128,1536]{1,0:T(8,12...) custom-call(s32[8]{0:T(128)S(1)} %stack.79.numbers, ...), custom_call_target="tpu_custom_call" | custom-call | tf_op jit(solution)/shard_map/pallas_call | solution.py:44
  107.9 3.4 %collective-permute-start.11 = (bf16[128,1536]{1,0:T(8,128)(2,1)S(1)}, bf16[128,1536]{1,0:T(8,128)(2,1)S(1)}, u32[]{:S(2)}, u32[]{:S(2)}) collective-permute-start(bf16[128,1536]{1,0:T(8,128)(2,1)S(1)} %get-tuple-element.45), channel_id=1, source_target_pairs={{0,2},{1,3},{2,0},{3,1},{4,6},{5,7},{6,4},{7,5},{8,10},{9,11},{10,... | collective-permute-start | bytes 1179656 | tf_op jit(solution)/shard_map/ppermute | solution.py:162
  111.3 3.5 %collective-permute-start.15 = (bf16[128,1536]{1,0:T(8,128)(2,1)S(1)}, bf16[128,1536]{1,0:T(8,128)(2,1)S(1)}, u32[]{:S(2)}, u32[]{:S(2)}) collective-permute-start(bf16[128,1536]{1,0:T(8,128)(2,1)S(1)} %get-tuple-element.53), channel_id=1, source_target_pairs={{0,4},{1,5},{2,6},{3,7},{4,8},{5,9},{6,10},{7,11},{8,12},{9,13},{1... | collective-permute-start | bytes 1179656 | tf_op jit(solution)/shard_map/ppermute | solution.py:162
  114.7 3.6 %collective-permute-start.16 = (bf16[128,1536]{1,0:T(8,128)(2,1)S(1)}, bf16[128,1536]{1,0:T(8,128)(2,1)S(1)}, u32[]{:S(2)}, u32[]{:S(2)}) collective-permute-start(bf16[128,1536]{1,0:T(8,128)(2,1)S(1)} %get-tuple-element.54), channel_id=1, source_target_pairs={{0,12},{1,13},{2,14},{3,15},{4,0},{5,1},{6,2},{7,3},{8,4},{9,5},{1... | collective-permute-start | bytes 1179656 | tf_op jit(solution)/shard_map/ppermute | solution.py:162
  118.3 6.5 %collective-permute-done.11 = bf16[128,1536]{1,0:T(8,128)(2,1)S(1)} collective-permute-done((bf16[128,1536]{1,0:T(8,128)(2,1)S(1)}, bf16[128,1536]{1,0:T(8,128)(2,1)S(1)}, u32[]{:S(2)}, u32[]{:S(2)}) %collective-permute-start.11) | collective-permute-done | bytes 393248 | tf_op jit(solution)/shard_map/ppermute | solution.py:162
  124.8 3.5 %collective-permute-start.12 = (bf16[128,1536]{1,0:T(8,128)(2,1)S(1)}, bf16[128,1536]{1,0:T(8,128)(2,1)S(1)}, u32[]{:S(2)}, u32[]{:S(2)}) collective-permute-start(bf16[128,1536]{1,0:T(8,128)(2,1)S(1)} %get-tuple-element.48), channel_id=1, source_target_pairs={{0,4},{1,5},{2,6},{3,7},{4,8},{5,9},{6,10},{7,11},{8,12},{9,13},{1... | collective-permute-start | bytes 1179656 | tf_op jit(solution)/shard_map/ppermute | solution.py:162
  128.3 3.6 %collective-permute-start.13 = (bf16[128,1536]{1,0:T(8,128)(2,1)S(1)}, bf16[128,1536]{1,0:T(8,128)(2,1)S(1)}, u32[]{:S(2)}, u32[]{:S(2)}) collective-permute-start(bf16[128,1536]{1,0:T(8,128)(2,1)S(1)} %get-tuple-element.49), channel_id=1, source_target_pairs={{0,12},{1,13},{2,14},{3,15},{4,0},{5,1},{6,2},{7,3},{8,4},{9,5},{1... | collective-permute-start | bytes 1179656 | tf_op jit(solution)/shard_map/ppermute | solution.py:162
  132.0 3.9 %collective-permute-start.14 = (bf16[128,1536]{1,0:T(8,128)(2,1)S(1)}, bf16[128,1536]{1,0:T(8,128)(2,1)S(1)}, u32[]{:S(2)}, u32[]{:S(2)}) collective-permute-start(bf16[128,1536]{1,0:T(8,128)(2,1)S(1)} %add_convert_fusion.2), channel_id=1, source_target_pairs={{0,8},{1,9},{2,10},{3,11},{4,12},{5,13},{6,14},{7,15},{8,0},{9,1},... | collective-permute-start | bytes 1179656 | tf_op jit(solution)/shard_map/ppermute | solution.py:162
  136.0 3.4 %collective-permute-start.17 = (bf16[128,1536]{1,0:T(8,128)(2,1)S(1)}, bf16[128,1536]{1,0:T(8,128)(2,1)S(1)}, u32[]{:S(2)}, u32[]{:S(2)}) collective-permute-start(bf16[128,1536]{1,0:T(8,128)(2,1)S(1)} %add_convert_fusion.1), channel_id=1, source_target_pairs={{0,2},{1,3},{2,0},{3,1},{4,6},{5,7},{6,4},{7,5},{8,10},{9,11},{10,... | collective-permute-start | bytes 1179656 | tf_op jit(solution)/shard_map/ppermute | solution.py:162
  142.2 5.9 %collective-permute-done.14 = bf16[128,1536]{1,0:T(8,128)(2,1)S(1)} collective-permute-done((bf16[128,1536]{1,0:T(8,128)(2,1)S(1)}, bf16[128,1536]{1,0:T(8,128)(2,1)S(1)}, u32[]{:S(2)}, u32[]{:S(2)}) %collective-permute-start.14) | collective-permute-done | bytes 393248 | tf_op jit(solution)/shard_map/ppermute | solution.py:162
  148.1 4.3 %collective-permute-done.17 = bf16[128,1536]{1,0:T(8,128)(2,1)S(1)} collective-permute-done((bf16[128,1536]{1,0:T(8,128)(2,1)S(1)}, bf16[128,1536]{1,0:T(8,128)(2,1)S(1)}, u32[]{:S(2)}, u32[]{:S(2)}) %collective-permute-start.17) | collective-permute-done | bytes 393248 | tf_op jit(solution)/shard_map/ppermute | solution.py:162
  (44 shorter events, 28.7 us)
Async XLA Ops:
  3.6 17.4 %copy-start.3 = (bf16[1,128,512]{2,1,0:T(8,128)(2,1)S(1)}, bf16[1,128,512]{2,1,0:T(8,128)(2,1)}, u32[]{:S(2)}) copy-start(bf16[1,128,512]{2,1,0:T(8,128)(2,1)} %param.11) | copy-start | bytes 393220
  3.6 17.4 %copy-start.4 = (bf16[1,128,512]{2,1,0:T(8,128)(2,1)S(1)}, bf16[1,128,512]{2,1,0:T(8,128)(2,1)}, u32[]{:S(2)}) copy-start(bf16[1,128,512]{2,1,0:T(8,128)(2,1)} %param.10) | copy-start | bytes 393220
  3.6 17.4 %copy-start.5 = (bf16[1,128,512]{2,1,0:T(8,128)(2,1)S(1)}, bf16[1,128,512]{2,1,0:T(8,128)(2,1)}, u32[]{:S(2)}) copy-start(bf16[1,128,512]{2,1,0:T(8,128)(2,1)} %param.9) | copy-start | bytes 393220
  3.6 74.2 %all-to-all-start = ((bf16[32,160,128]{2,1,0:T(8,128)(2,1)}), bf16[32,160,128]{2,1,0:T(8,128)(2,1)S(1)}, u32[]{:S(2)}, u32[]{:S(2)}) async-start(bf16[32,160,128]{2,1,0:T(8,128)(2,1)} %bitcast.32), calls=%async_computation | async-start | bytes 2621440 | tf_op jit(solution)/shard_map/all_to_all | solution.py:141
  21.1 17.1 %collective-permute-start.2 = (bf16[128,1536]{1,0:T(8,128)(2,1)S(1)}, bf16[128,1536]{1,0:T(8,128)(2,1)S(1)}, u32[]{:S(2)}, u32[]{:S(2)}) collective-permute-start(bf16[128,1536]{1,0:T(8,128)(2,1)S(1)} %pad_maximum_fusion.1), channel_id=1, source_target_pairs={{0,2},{1,3},{2,0},{3,1},{4,6},{5,7},{6,4},{7,5},{8,10},{9,11},{10,... | collective-permute-start | bytes 1179656 | tf_op jit(solution)/shard_map/ppermute | solution.py:162
  24.4 20.6 %collective-permute-start.5 = (bf16[128,1536]{1,0:T(8,128)(2,1)S(1)}, bf16[128,1536]{1,0:T(8,128)(2,1)S(1)}, u32[]{:S(2)}, u32[]{:S(2)}) collective-permute-start(bf16[128,1536]{1,0:T(8,128)(2,1)S(1)} %pad_maximum_fusion.1), channel_id=1, source_target_pairs={{0,8},{1,9},{2,10},{3,11},{4,12},{5,13},{6,14},{7,15},{8,0},{9,1},... | collective-permute-start | bytes 1179656 | tf_op jit(solution)/shard_map/ppermute | solution.py:162
  29.5 32.4 %collective-permute-start.1 = (bf16[128,1536]{1,0:T(8,128)(2,1)S(1)}, bf16[128,1536]{1,0:T(8,128)(2,1)S(1)}, u32[]{:S(2)}, u32[]{:S(2)}) collective-permute-start(bf16[128,1536]{1,0:T(8,128)(2,1)S(1)} %pad_maximum_fusion.1), channel_id=1, source_target_pairs={{0,12},{1,13},{2,14},{3,15},{4,0},{5,1},{6,2},{7,3},{8,4},{9,5},{1... | collective-permute-start | bytes 1179656 | tf_op jit(solution)/shard_map/ppermute | solution.py:162
  32.5 29.4 %collective-permute-start = (bf16[128,1536]{1,0:T(8,128)(2,1)S(1)}, bf16[128,1536]{1,0:T(8,128)(2,1)S(1)}, u32[]{:S(2)}, u32[]{:S(2)}) collective-permute-start(bf16[128,1536]{1,0:T(8,128)(2,1)S(1)} %pad_maximum_fusion.1), channel_id=1, source_target_pairs={{0,4},{1,5},{2,6},{3,7},{4,8},{5,9},{6,10},{7,11},{8,12},{9,13},{1... | collective-permute-start | bytes 1179656 | tf_op jit(solution)/shard_map/ppermute | solution.py:162
  38.1 16.9 %collective-permute-start.6 = (bf16[128,1536]{1,0:T(8,128)(2,1)S(1)}, bf16[128,1536]{1,0:T(8,128)(2,1)S(1)}, u32[]{:S(2)}, u32[]{:S(2)}) collective-permute-start(bf16[128,1536]{1,0:T(8,128)(2,1)S(1)} %collective-permute-done.2), channel_id=1, source_target_pairs={{0,12},{1,13},{2,14},{3,15},{4,0},{5,1},{6,2},{7,3},{8,4},{9,5},{1... | collective-permute-start | bytes 1179656 | tf_op jit(solution)/shard_map/ppermute | solution.py:162
  43.1 18.8 %collective-permute-start.3 = (bf16[128,1536]{1,0:T(8,128)(2,1)S(1)}, bf16[128,1536]{1,0:T(8,128)(2,1)S(1)}, u32[]{:S(2)}, u32[]{:S(2)}) collective-permute-start(bf16[128,1536]{1,0:T(8,128)(2,1)S(1)} %collective-permute-done.2), channel_id=1, source_target_pairs={{0,4},{1,5},{2,6},{3,7},{4,8},{5,9},{6,10},{7,11},{8,12},{9,13},{1... | collective-permute-start | bytes 1179656 | tf_op jit(solution)/shard_map/ppermute | solution.py:162
  45.0 14.2 %collective-permute-start.7 = (bf16[128,1536]{1,0:T(8,128)(2,1)S(1)}, bf16[128,1536]{1,0:T(8,128)(2,1)S(1)}, u32[]{:S(2)}, u32[]{:S(2)}) collective-permute-start(bf16[128,1536]{1,0:T(8,128)(2,1)S(1)} %collective-permute-done.5), channel_id=1, source_target_pairs={{0,2},{1,3},{2,0},{3,1},{4,6},{5,7},{6,4},{7,5},{8,10},{9,11},{10,... | collective-permute-start | bytes 1179656 | tf_op jit(solution)/shard_map/ppermute | solution.py:162
  60.0 5.6 %collective-permute-start.8 = (bf16[512,1536]{1,0:T(8,128)(2,1)}, bf16[512,1536]{1,0:T(8,128)(2,1)}, u32[]{:S(2)}, u32[]{:S(2)}) collective-permute-start(bf16[512,1536]{1,0:T(8,128)(2,1)} %constant_dynamic-update-slice_fusion.refs_2_), channel_id=1, source_target_pairs={{0,1},{1,0},{2,3},{3,2},{4,5},{5,4},{6,7},{7,6},{8,9},{9,8},{10,11... | collective-permute-start | bytes 4718600 | tf_op jit(solution)/shard_map/ppermute | solution.py:151
  62.0 5.6 %collective-permute-start.4 = (bf16[512,1536]{1,0:T(8,128)(2,1)S(1)}, bf16[512,1536]{1,0:T(8,128)(2,1)}, u32[]{:S(2)}, u32[]{:S(2)}) collective-permute-start(bf16[512,1536]{1,0:T(8,128)(2,1)S(1)} %pad_maximum_fusion.refs_0_), channel_id=1, source_target_pairs={{0,1},{1,0},{2,3},{3,2},{4,5},{5,4},{6,7},{7,6},{8,9},{9,8},{10,11... | collective-permute-start | bytes 4718600 | tf_op jit(solution)/shard_map/ppermute | solution.py:151
  85.2 15.4 %copy-start.1 = (bf16[160,1536]{1,0:T(8,128)(2,1)S(1)}, bf16[160,1536]{1,0:T(8,128)(2,1)}, u32[]{:S(2)}) copy-start(bf16[160,1536]{1,0:T(8,128)(2,1)} %get-tuple-element.43.own_sides) | copy-start | bytes 1474564
  85.2 70.0 %all-to-all-start.1 = ((bf16[32,160,128]{2,1,0:T(8,128)(2,1)}), bf16[32,160,128]{2,1,0:T(8,128)(2,1)S(1)}, u32[]{:S(2)}, u32[]{:S(2)}) async-start(bf16[32,160,128]{2,1,0:T(8,128)(2,1)} %bitcast.33), calls=%async_computation.1 | async-start | bytes 2621440 | tf_op jit(solution)/shard_map/all_to_all | solution.py:141
  98.7 6.0 %collective-permute-start.9 = (bf16[32,160,128]{2,1,0:T(8,128)(2,1)S(1)}, bf16[32,160,128]{2,1,0:T(8,128)(2,1)}, u32[]{:S(2)}, u32[]{:S(2)}) collective-permute-start(bf16[32,160,128]{2,1,0:T(8,128)(2,1)S(1)} %copy-done), channel_id=1, source_target_pairs={{0,1},{1,0},{2,3},{3,2},{4,5},{5,4},{6,7},{7,6},{8,9},{9,8},{10,11... | collective-permute-start | bytes 3932168 | tf_op jit(solution)/shard_map/ppermute | solution.py:151
  100.6 4.0 %collective-permute-start.10 = (bf16[160,1536]{1,0:T(8,128)(2,1)S(1)}, bf16[160,1536]{1,0:T(8,128)(2,1)}, u32[]{:S(2)}, u32[]{:S(2)}) collective-permute-start(bf16[160,1536]{1,0:T(8,128)(2,1)S(1)} %copy-done.1), channel_id=1, source_target_pairs={{0,1},{1,0},{2,3},{3,2},{4,5},{5,4},{6,7},{7,6},{8,9},{9,8},{10,11... | collective-permute-start | bytes 1474568 | tf_op jit(solution)/shard_map/ppermute | solution.py:151
  107.9 16.9 %collective-permute-start.11 = (bf16[128,1536]{1,0:T(8,128)(2,1)S(1)}, bf16[128,1536]{1,0:T(8,128)(2,1)S(1)}, u32[]{:S(2)}, u32[]{:S(2)}) collective-permute-start(bf16[128,1536]{1,0:T(8,128)(2,1)S(1)} %get-tuple-element.45), channel_id=1, source_target_pairs={{0,2},{1,3},{2,0},{3,1},{4,6},{5,7},{6,4},{7,5},{8,10},{9,11},{10,... | collective-permute-start | bytes 1179656 | tf_op jit(solution)/shard_map/ppermute | solution.py:162
  111.3 24.6 %collective-permute-start.15 = (bf16[128,1536]{1,0:T(8,128)(2,1)S(1)}, bf16[128,1536]{1,0:T(8,128)(2,1)S(1)}, u32[]{:S(2)}, u32[]{:S(2)}) collective-permute-start(bf16[128,1536]{1,0:T(8,128)(2,1)S(1)} %get-tuple-element.53), channel_id=1, source_target_pairs={{0,4},{1,5},{2,6},{3,7},{4,8},{5,9},{6,10},{7,11},{8,12},{9,13},{1... | collective-permute-start | bytes 1179656 | tf_op jit(solution)/shard_map/ppermute | solution.py:162
  114.7 21.1 %collective-permute-start.16 = (bf16[128,1536]{1,0:T(8,128)(2,1)S(1)}, bf16[128,1536]{1,0:T(8,128)(2,1)S(1)}, u32[]{:S(2)}, u32[]{:S(2)}) collective-permute-start(bf16[128,1536]{1,0:T(8,128)(2,1)S(1)} %get-tuple-element.54), channel_id=1, source_target_pairs={{0,12},{1,13},{2,14},{3,15},{4,0},{5,1},{6,2},{7,3},{8,4},{9,5},{1... | collective-permute-start | bytes 1179656 | tf_op jit(solution)/shard_map/ppermute | solution.py:162
  124.8 14.7 %collective-permute-start.12 = (bf16[128,1536]{1,0:T(8,128)(2,1)S(1)}, bf16[128,1536]{1,0:T(8,128)(2,1)S(1)}, u32[]{:S(2)}, u32[]{:S(2)}) collective-permute-start(bf16[128,1536]{1,0:T(8,128)(2,1)S(1)} %get-tuple-element.48), channel_id=1, source_target_pairs={{0,4},{1,5},{2,6},{3,7},{4,8},{5,9},{6,10},{7,11},{8,12},{9,13},{1... | collective-permute-start | bytes 1179656 | tf_op jit(solution)/shard_map/ppermute | solution.py:162
  128.3 13.9 %collective-permute-start.13 = (bf16[128,1536]{1,0:T(8,128)(2,1)S(1)}, bf16[128,1536]{1,0:T(8,128)(2,1)S(1)}, u32[]{:S(2)}, u32[]{:S(2)}) collective-permute-start(bf16[128,1536]{1,0:T(8,128)(2,1)S(1)} %get-tuple-element.49), channel_id=1, source_target_pairs={{0,12},{1,13},{2,14},{3,15},{4,0},{5,1},{6,2},{7,3},{8,4},{9,5},{1... | collective-permute-start | bytes 1179656 | tf_op jit(solution)/shard_map/ppermute | solution.py:162
  132.0 16.2 %collective-permute-start.14 = (bf16[128,1536]{1,0:T(8,128)(2,1)S(1)}, bf16[128,1536]{1,0:T(8,128)(2,1)S(1)}, u32[]{:S(2)}, u32[]{:S(2)}) collective-permute-start(bf16[128,1536]{1,0:T(8,128)(2,1)S(1)} %add_convert_fusion.2), channel_id=1, source_target_pairs={{0,8},{1,9},{2,10},{3,11},{4,12},{5,13},{6,14},{7,15},{8,0},{9,1},... | collective-permute-start | bytes 1179656 | tf_op jit(solution)/shard_map/ppermute | solution.py:162
  136.0 16.4 %collective-permute-start.17 = (bf16[128,1536]{1,0:T(8,128)(2,1)S(1)}, bf16[128,1536]{1,0:T(8,128)(2,1)S(1)}, u32[]{:S(2)}, u32[]{:S(2)}) collective-permute-start(bf16[128,1536]{1,0:T(8,128)(2,1)S(1)} %add_convert_fusion.1), channel_id=1, source_target_pairs={{0,2},{1,3},{2,0},{3,1},{4,6},{5,7},{6,4},{7,5},{8,10},{9,11},{10,... | collective-permute-start | bytes 1179656 | tf_op jit(solution)/shard_map/ppermute | solution.py:162
  (2 other events, 16.2 us)

commit v12 on v10

--- a/solution.py
+++ b/solution.py
@@ -329,17 +329,14 @@
     def summed(*arrays):
         return add(*arrays).astype(tokens.dtype)
 
+    near, far = chip_shift(terms[1, 1], 1, 0), chip_shift(terms[3, 1], 3, 0)
+    one, three = chip_shift(terms[1, 0], 1, 0), chip_shift(terms[3, 0], 3, 0)
     two = summed(terms[2, 0], chip_shift(terms[2, 1], 0, 1))
-    across = summed(
-        terms[0, 1], chip_shift(terms[1, 1], 1, 0), chip_shift(terms[3, 1], 3, 0)
-    )
-    total = add(
-        terms[0, 0],
-        chip_shift(terms[1, 0], 1, 0),
-        chip_shift(terms[3, 0], 3, 0),
-        chip_shift(two, 2, 0),
-        chip_shift(across, 0, 1),
-    )
+    across = summed(terms[0, 1], near, far)
+    partial = add(terms[0, 0], one, three)
+    last = add(chip_shift(two, 2, 0), chip_shift(across, 0, 1))
+    last, partial = lax.optimization_barrier((last, partial))
+    total = last + partial
 
     grads = total.astype(jnp.bfloat16)
     grad_wg = grads[None, :, :hidden_width]

time: 162 us -> 158 us (0.975)
  the two profiles are of different devices: /device:TPU:24 before, /device:TPU:6 now
where the time goes in v12:
time: 158 us; the launch traced here: 157 us
  starting transfers between devices  89.7 us (57%)
  waiting for transfers between devices  46.1 us (29%)
  Pallas kernels  15.2 us (10%)
  local copies, waits for them, and re-layouts  4.1 us (3%)
    ppermute x14, starting transfers between devices, chip_shift(): return lax.ppermute(array, 'fsdp', pairs)  50.2 us
    all_to_all x2, starting transfers between devices, exchange(): lax.all_to_all(sent, 'ep', split_axis=0, concat_axis=0, tiled=True, axis_...  30.8 us
    ppermute x14, waiting for transfers between devices, chip_shift(): return lax.ppermute(array, 'fsdp', pairs)  24.4 us
    all_to_all x2, waiting for transfers between devices, exchange(): lax.all_to_all(sent, 'ep', split_axis=0, concat_axis=0, tiled=True, axis_...  17.1 us
    pallas_call x3, Pallas kernels, vmem_call(): pl.pallas_call(kernel, out_shape=jax.tree.map(lambda s: pltpu.HBM(s.shape...  12.2 us
    ppermute x4, starting transfers between devices, core_swap(): lax.ppermute(array, 'fsdp', [(f, f ^ 1) for f in range(2 * Y * X_HI)])  8.65 us
    ppermute x4, waiting for transfers between devices, core_swap(): lax.ppermute(array, 'fsdp', [(f, f ^ 1) for f in range(2 * Y * X_HI)])  4.56 us
  transfers between devices with their start and end apart: 20, of which 11 were waited for; matrix products, arithmetic and copies ran while one was open for 3% of the time, Pallas kernels for 2%

profile of v12, /device:TPU:6, one launch (start us, length us, event | category | flops | bytes accessed | tf_op | source)
XLA Modules:
  0.0 156.8 jit_solution(1122617424267922653)
XLA Ops:
  0.6 2.9 %shard_map.101 = (bf16[160,32,128]{2,1,0:T(8,128)(2,1)}, bf16[160,128]{1,0:T(8,128)(2,1)}) custom-call(s32[1,128]{1,0:T(1,128)} %bitcast.40, bf16[128,2048]{1,0:T(8,128)(2,1)} %tokens.1, bf16[128,2048]{1,0:T(8,128)(2,1)} %cotangent.1), custom_call_target="tpu_custom_call" | custom-call | tf_op jit(solution)/shard_map/pallas_call | solution.py:100
  3.6 17.4 %all-to-all-start = ((bf16[32,160,128]{2,1,0:T(8,128)(2,1)}), bf16[32,160,128]{2,1,0:T(8,128)(2,1)S(1)}, u32[]{:S(2)}, u32[]{:S(2)}) async-start(bf16[32,160,128]{2,1,0:T(8,128)(2,1)} %bitcast.32), calls=%async_computation | async-start | bytes 2621440 | tf_op jit(solution)/shard_map/all_to_all | solution.py:141
  21.1 3.3 %collective-permute-start.2 = (bf16[128,1536]{1,0:T(8,128)(2,1)S(1)}, bf16[128,1536]{1,0:T(8,128)(2,1)S(1)}, u32[]{:S(2)}, u32[]{:S(2)}) collective-permute-start(bf16[128,1536]{1,0:T(8,128)(2,1)S(1)} %pad_maximum_fusion.1), channel_id=1, source_target_pairs={{0,2},{1,3},{2,0},{3,1},{4,6},{5,7},{6,4},{7,5},{8,10},{9,11},{10,... | collective-permute-start | bytes 1179656 | tf_op jit(solution)/shard_map/ppermute | solution.py:162
  24.4 5.1 %collective-permute-start.5 = (bf16[128,1536]{1,0:T(8,128)(2,1)S(1)}, bf16[128,1536]{1,0:T(8,128)(2,1)S(1)}, u32[]{:S(2)}, u32[]{:S(2)}) collective-permute-start(bf16[128,1536]{1,0:T(8,128)(2,1)S(1)} %pad_maximum_fusion.1), channel_id=1, source_target_pairs={{0,8},{1,9},{2,10},{3,11},{4,12},{5,13},{6,14},{7,15},{8,0},{9,1},... | collective-permute-start | bytes 1179656 | tf_op jit(solution)/shard_map/ppermute | solution.py:162
  29.5 3.0 %collective-permute-start.1 = (bf16[128,1536]{1,0:T(8,128)(2,1)S(1)}, bf16[128,1536]{1,0:T(8,128)(2,1)S(1)}, u32[]{:S(2)}, u32[]{:S(2)}) collective-permute-start(bf16[128,1536]{1,0:T(8,128)(2,1)S(1)} %pad_maximum_fusion.1), channel_id=1, source_target_pairs={{0,12},{1,13},{2,14},{3,15},{4,0},{5,1},{6,2},{7,3},{8,4},{9,5},{1... | collective-permute-start | bytes 1179656 | tf_op jit(solution)/shard_map/ppermute | solution.py:162
  32.5 2.9 %collective-permute-start = (bf16[128,1536]{1,0:T(8,128)(2,1)S(1)}, bf16[128,1536]{1,0:T(8,128)(2,1)S(1)}, u32[]{:S(2)}, u32[]{:S(2)}) collective-permute-start(bf16[128,1536]{1,0:T(8,128)(2,1)S(1)} %pad_maximum_fusion.1), channel_id=1, source_target_pairs={{0,4},{1,5},{2,6},{3,7},{4,8},{5,9},{6,10},{7,11},{8,12},{9,13},{1... | collective-permute-start | bytes 1179656 | tf_op jit(solution)/shard_map/ppermute | solution.py:162
  35.4 2.8 %collective-permute-done.2 = bf16[128,1536]{1,0:T(8,128)(2,1)S(1)} collective-permute-done((bf16[128,1536]{1,0:T(8,128)(2,1)S(1)}, bf16[128,1536]{1,0:T(8,128)(2,1)S(1)}, u32[]{:S(2)}, u32[]{:S(2)}) %collective-permute-start.2) | collective-permute-done | bytes 393248 | tf_op jit(solution)/shard_map/ppermute | solution.py:162
  38.1 4.9 %collective-permute-start.6 = (bf16[128,1536]{1,0:T(8,128)(2,1)S(1)}, bf16[128,1536]{1,0:T(8,128)(2,1)S(1)}, u32[]{:S(2)}, u32[]{:S(2)}) collective-permute-start(bf16[128,1536]{1,0:T(8,128)(2,1)S(1)} %collective-permute-done.2), channel_id=1, source_target_pairs={{0,12},{1,13},{2,14},{3,15},{4,0},{5,1},{6,2},{7,3},{8,4},{9,5},{1... | collective-permute-start | bytes 1179656 | tf_op jit(solution)/shard_map/ppermute | solution.py:162
  45.0 3.7 %collective-permute-start.7 = (bf16[128,1536]{1,0:T(8,128)(2,1)S(1)}, bf16[128,1536]{1,0:T(8,128)(2,1)S(1)}, u32[]{:S(2)}, u32[]{:S(2)}) collective-permute-start(bf16[128,1536]{1,0:T(8,128)(2,1)S(1)} %collective-permute-done.5), channel_id=1, source_target_pairs={{0,2},{1,3},{2,0},{3,1},{4,6},{5,7},{6,4},{7,5},{8,10},{9,11},{10,... | collective-permute-start | bytes 1179656 | tf_op jit(solution)/shard_map/ppermute | solution.py:162
  50.2 4.8 %collective-permute-done.6 = bf16[128,1536]{1,0:T(8,128)(2,1)S(1)} collective-permute-done((bf16[128,1536]{1,0:T(8,128)(2,1)S(1)}, bf16[128,1536]{1,0:T(8,128)(2,1)S(1)}, u32[]{:S(2)}, u32[]{:S(2)}) %collective-permute-start.6) | collective-permute-done | bytes 393248 | tf_op jit(solution)/shard_map/ppermute | solution.py:162
  55.8 3.3 %collective-permute-done.7 = bf16[128,1536]{1,0:T(8,128)(2,1)S(1)} collective-permute-done((bf16[128,1536]{1,0:T(8,128)(2,1)S(1)}, bf16[128,1536]{1,0:T(8,128)(2,1)S(1)}, u32[]{:S(2)}, u32[]{:S(2)}) %collective-permute-start.7) | collective-permute-done | bytes 393248 | tf_op jit(solution)/shard_map/ppermute | solution.py:162
  67.6 10.1 %all-to-all-done = bf16[32,160,128]{2,1,0:T(8,128)(2,1)S(1)} async-done(((bf16[32,160,128]{2,1,0:T(8,128)(2,1)}), bf16[32,160,128]{2,1,0:T(8,128)(2,1)S(1)}, u32[]{:S(2)}, u32[]{:S(2)}) %all-to-all-start) | async-done | bytes 1310752 | tf_op jit(solution)/shard_map/all_to_all | solution.py:141
  77.8 7.4 %shard_map.102 = (bf16[160,32,128]{2,1,0:T(8,128)(2,1)}, bf16[160,1536]{1,0:T(8,128)(2,1)}, bf16[32,160,128]{2,1,0:T(8,128)(2,1)}) custom-call(s32[16]{0:T(128)S(1)} %stack.78.numbers, bf16[160,32,128]{2,1,0:T(8,128)(2,1)S(1)} %bitcast.31, bf16[512,1536]{1,0:T(8,128)(2,1)S(1)} %pad_maximum_fusion.refs_0_, bf16[512,1536]{1,0:T(8,128)(2,1)} %collective-permute-done.4.refs_1_, ...), custom_call_target="tpu_custom_call" | custom-call | tf_op jit(solution)/shard_map/pallas_call | solution.py:44
  85.2 13.5 %all-to-all-start.1 = ((bf16[32,160,128]{2,1,0:T(8,128)(2,1)}), bf16[32,160,128]{2,1,0:T(8,128)(2,1)S(1)}, u32[]{:S(2)}, u32[]{:S(2)}) async-start(bf16[32,160,128]{2,1,0:T(8,128)(2,1)} %bitcast.33), calls=%async_computation.1 | async-start | bytes 2621440 | tf_op jit(solution)/shard_map/all_to_all | solution.py:141
  104.6 3.3 %shard_map.104 = (bf16[128,1536]{1,0:T(8,128)(2,1)S(1)}, bf16[128,1536]{1,0:T(8,128)(2,1)S(1)}, bf16[128,1536]{1,0:T(8,128)(2,1)S(1)}, bf16[128,1536]{1,0:T(8,12...) custom-call(s32[8]{0:T(128)S(1)} %stack.79.numbers, ...), custom_call_target="tpu_custom_call" | custom-call | tf_op jit(solution)/shard_map/pallas_call | solution.py:44
  107.9 3.4 %collective-permute-start.11 = (bf16[128,1536]{1,0:T(8,128)(2,1)S(1)}, bf16[128,1536]{1,0:T(8,128)(2,1)S(1)}, u32[]{:S(2)}, u32[]{:S(2)}) collective-permute-start(bf16[128,1536]{1,0:T(8,128)(2,1)S(1)} %get-tuple-element.44), channel_id=1, source_target_pairs={{0,2},{1,3},{2,0},{3,1},{4,6},{5,7},{6,4},{7,5},{8,10},{9,11},{10,... | collective-permute-start | bytes 1179656 | tf_op jit(solution)/shard_map/ppermute | solution.py:162
  111.3 3.5 %collective-permute-start.13 = (bf16[128,1536]{1,0:T(8,128)(2,1)S(1)}, bf16[128,1536]{1,0:T(8,128)(2,1)S(1)}, u32[]{:S(2)}, u32[]{:S(2)}) collective-permute-start(bf16[128,1536]{1,0:T(8,128)(2,1)S(1)} %get-tuple-element.46), channel_id=1, source_target_pairs={{0,4},{1,5},{2,6},{3,7},{4,8},{5,9},{6,10},{7,11},{8,12},{9,13},{1... | collective-permute-start | bytes 1179656 | tf_op jit(solution)/shard_map/ppermute | solution.py:162
  114.7 3.6 %collective-permute-start.14 = (bf16[128,1536]{1,0:T(8,128)(2,1)S(1)}, bf16[128,1536]{1,0:T(8,128)(2,1)S(1)}, u32[]{:S(2)}, u32[]{:S(2)}) collective-permute-start(bf16[128,1536]{1,0:T(8,128)(2,1)S(1)} %get-tuple-element.47), channel_id=1, source_target_pairs={{0,12},{1,13},{2,14},{3,15},{4,0},{5,1},{6,2},{7,3},{8,4},{9,5},{1... | collective-permute-start | bytes 1179656 | tf_op jit(solution)/shard_map/ppermute | solution.py:162
  120.6 4.8 %collective-permute-start.17 = (bf16[128,1536]{1,0:T(8,128)(2,1)S(1)}, bf16[128,1536]{1,0:T(8,128)(2,1)S(1)}, u32[]{:S(2)}, u32[]{:S(2)}) collective-permute-start(bf16[128,1536]{1,0:T(8,128)(2,1)S(1)} %get-tuple-element.50), channel_id=1, source_target_pairs={{0,12},{1,13},{2,14},{3,15},{4,0},{5,1},{6,2},{7,3},{8,4},{9,5},{1... | collective-permute-start | bytes 1179656 | tf_op jit(solution)/shard_map/ppermute | solution.py:162
  125.5 4.5 %collective-permute-start.12 = (bf16[128,1536]{1,0:T(8,128)(2,1)S(1)}, bf16[128,1536]{1,0:T(8,128)(2,1)S(1)}, u32[]{:S(2)}, u32[]{:S(2)}) collective-permute-start(bf16[128,1536]{1,0:T(8,128)(2,1)S(1)} %add_convert_fusion.2), channel_id=1, source_target_pairs={{0,8},{1,9},{2,10},{3,11},{4,12},{5,13},{6,14},{7,15},{8,0},{9,1},... | collective-permute-start | bytes 1179656 | tf_op jit(solution)/shard_map/ppermute | solution.py:162
  130.2 3.4 %collective-permute-start.15 = (bf16[128,1536]{1,0:T(8,128)(2,1)S(1)}, bf16[128,1536]{1,0:T(8,128)(2,1)S(1)}, u32[]{:S(2)}, u32[]{:S(2)}) collective-permute-start(bf16[128,1536]{1,0:T(8,128)(2,1)S(1)} %add_convert_fusion.1), channel_id=1, source_target_pairs={{0,2},{1,3},{2,0},{3,1},{4,6},{5,7},{6,4},{7,5},{8,10},{9,11},{10,... | collective-permute-start | bytes 1179656 | tf_op jit(solution)/shard_map/ppermute | solution.py:162
  134.0 9.6 %collective-permute-done.17 = bf16[128,1536]{1,0:T(8,128)(2,1)S(1)} collective-permute-done((bf16[128,1536]{1,0:T(8,128)(2,1)S(1)}, bf16[128,1536]{1,0:T(8,128)(2,1)S(1)}, u32[]{:S(2)}, u32[]{:S(2)}) %collective-permute-start.17) | collective-permute-done | bytes 393248 | tf_op jit(solution)/shard_map/ppermute | solution.py:162
  143.7 3.5 %collective-permute-done.15 = bf16[128,1536]{1,0:T(8,128)(2,1)S(1)} collective-permute-done((bf16[128,1536]{1,0:T(8,128)(2,1)S(1)}, bf16[128,1536]{1,0:T(8,128)(2,1)S(1)}, u32[]{:S(2)}, u32[]{:S(2)}) %collective-permute-start.15) | collective-permute-done | bytes 393248 | tf_op jit(solution)/shard_map/ppermute | solution.py:162
  148.2 7.0 %all-to-all-done.1 = bf16[32,160,128]{2,1,0:T(8,128)(2,1)S(1)} async-done(((bf16[32,160,128]{2,1,0:T(8,128)(2,1)}), bf16[32,160,128]{2,1,0:T(8,128)(2,1)S(1)}, u32[]{:S(2)}, u32[]{:S(2)}) %all-to-all-start.1) | async-done | bytes 1310752 | tf_op jit(solution)/shard_map/all_to_all | solution.py:141
  (46 shorter events, 24.1 us)
Async XLA Ops:
  3.6 17.4 %copy-start.3 = (bf16[1,128,512]{2,1,0:T(8,128)(2,1)S(1)}, bf16[1,128,512]{2,1,0:T(8,128)(2,1)}, u32[]{:S(2)}) copy-start(bf16[1,128,512]{2,1,0:T(8,128)(2,1)} %param.11) | copy-start | bytes 393220
  3.6 17.4 %copy-start.4 = (bf16[1,128,512]{2,1,0:T(8,128)(2,1)S(1)}, bf16[1,128,512]{2,1,0:T(8,128)(2,1)}, u32[]{:S(2)}) copy-start(bf16[1,128,512]{2,1,0:T(8,128)(2,1)} %param.10) | copy-start | bytes 393220
  3.6 17.4 %copy-start.5 = (bf16[1,128,512]{2,1,0:T(8,128)(2,1)S(1)}, bf16[1,128,512]{2,1,0:T(8,128)(2,1)}, u32[]{:S(2)}) copy-start(bf16[1,128,512]{2,1,0:T(8,128)(2,1)} %param.9) | copy-start | bytes 393220
  3.6 74.2 %all-to-all-start = ((bf16[32,160,128]{2,1,0:T(8,128)(2,1)}), bf16[32,160,128]{2,1,0:T(8,128)(2,1)S(1)}, u32[]{:S(2)}, u32[]{:S(2)}) async-start(bf16[32,160,128]{2,1,0:T(8,128)(2,1)} %bitcast.32), calls=%async_computation | async-start | bytes 2621440 | tf_op jit(solution)/shard_map/all_to_all | solution.py:141
  21.1 17.1 %collective-permute-start.2 = (bf16[128,1536]{1,0:T(8,128)(2,1)S(1)}, bf16[128,1536]{1,0:T(8,128)(2,1)S(1)}, u32[]{:S(2)}, u32[]{:S(2)}) collective-permute-start(bf16[128,1536]{1,0:T(8,128)(2,1)S(1)} %pad_maximum_fusion.1), channel_id=1, source_target_pairs={{0,2},{1,3},{2,0},{3,1},{4,6},{5,7},{6,4},{7,5},{8,10},{9,11},{10,... | collective-permute-start | bytes 1179656 | tf_op jit(solution)/shard_map/ppermute | solution.py:162
  24.4 20.6 %collective-permute-start.5 = (bf16[128,1536]{1,0:T(8,128)(2,1)S(1)}, bf16[128,1536]{1,0:T(8,128)(2,1)S(1)}, u32[]{:S(2)}, u32[]{:S(2)}) collective-permute-start(bf16[128,1536]{1,0:T(8,128)(2,1)S(1)} %pad_maximum_fusion.1), channel_id=1, source_target_pairs={{0,8},{1,9},{2,10},{3,11},{4,12},{5,13},{6,14},{7,15},{8,0},{9,1},... | collective-permute-start | bytes 1179656 | tf_op jit(solution)/shard_map/ppermute | solution.py:162
  29.5 32.4 %collective-permute-start.1 = (bf16[128,1536]{1,0:T(8,128)(2,1)S(1)}, bf16[128,1536]{1,0:T(8,128)(2,1)S(1)}, u32[]{:S(2)}, u32[]{:S(2)}) collective-permute-start(bf16[128,1536]{1,0:T(8,128)(2,1)S(1)} %pad_maximum_fusion.1), channel_id=1, source_target_pairs={{0,12},{1,13},{2,14},{3,15},{4,0},{5,1},{6,2},{7,3},{8,4},{9,5},{1... | collective-permute-start | bytes 1179656 | tf_op jit(solution)/shard_map/ppermute | solution.py:162
  32.5 29.4 %collective-permute-start = (bf16[128,1536]{1,0:T(8,128)(2,1)S(1)}, bf16[128,1536]{1,0:T(8,128)(2,1)S(1)}, u32[]{:S(2)}, u32[]{:S(2)}) collective-permute-start(bf16[128,1536]{1,0:T(8,128)(2,1)S(1)} %pad_maximum_fusion.1), channel_id=1, source_target_pairs={{0,4},{1,5},{2,6},{3,7},{4,8},{5,9},{6,10},{7,11},{8,12},{9,13},{1... | collective-permute-start | bytes 1179656 | tf_op jit(solution)/shard_map/ppermute | solution.py:162
  38.1 16.9 %collective-permute-start.6 = (bf16[128,1536]{1,0:T(8,128)(2,1)S(1)}, bf16[128,1536]{1,0:T(8,128)(2,1)S(1)}, u32[]{:S(2)}, u32[]{:S(2)}) collective-permute-start(bf16[128,1536]{1,0:T(8,128)(2,1)S(1)} %collective-permute-done.2), channel_id=1, source_target_pairs={{0,12},{1,13},{2,14},{3,15},{4,0},{5,1},{6,2},{7,3},{8,4},{9,5},{1... | collective-permute-start | bytes 1179656 | tf_op jit(solution)/shard_map/ppermute | solution.py:162
  43.1 18.8 %collective-permute-start.3 = (bf16[128,1536]{1,0:T(8,128)(2,1)S(1)}, bf16[128,1536]{1,0:T(8,128)(2,1)S(1)}, u32[]{:S(2)}, u32[]{:S(2)}) collective-permute-start(bf16[128,1536]{1,0:T(8,128)(2,1)S(1)} %collective-permute-done.2), channel_id=1, source_target_pairs={{0,4},{1,5},{2,6},{3,7},{4,8},{5,9},{6,10},{7,11},{8,12},{9,13},{1... | collective-permute-start | bytes 1179656 | tf_op jit(solution)/shard_map/ppermute | solution.py:162
  45.0 14.2 %collective-permute-start.7 = (bf16[128,1536]{1,0:T(8,128)(2,1)S(1)}, bf16[128,1536]{1,0:T(8,128)(2,1)S(1)}, u32[]{:S(2)}, u32[]{:S(2)}) collective-permute-start(bf16[128,1536]{1,0:T(8,128)(2,1)S(1)} %collective-permute-done.5), channel_id=1, source_target_pairs={{0,2},{1,3},{2,0},{3,1},{4,6},{5,7},{6,4},{7,5},{8,10},{9,11},{10,... | collective-permute-start | bytes 1179656 | tf_op jit(solution)/shard_map/ppermute | solution.py:162
  60.0 5.6 %collective-permute-start.8 = (bf16[512,1536]{1,0:T(8,128)(2,1)}, bf16[512,1536]{1,0:T(8,128)(2,1)}, u32[]{:S(2)}, u32[]{:S(2)}) collective-permute-start(bf16[512,1536]{1,0:T(8,128)(2,1)} %constant_dynamic-update-slice_fusion.refs_2_), channel_id=1, source_target_pairs={{0,1},{1,0},{2,3},{3,2},{4,5},{5,4},{6,7},{7,6},{8,9},{9,8},{10,11... | collective-permute-start | bytes 4718600 | tf_op jit(solution)/shard_map/ppermute | solution.py:151
  62.0 5.6 %collective-permute-start.4 = (bf16[512,1536]{1,0:T(8,128)(2,1)S(1)}, bf16[512,1536]{1,0:T(8,128)(2,1)}, u32[]{:S(2)}, u32[]{:S(2)}) collective-permute-start(bf16[512,1536]{1,0:T(8,128)(2,1)S(1)} %pad_maximum_fusion.refs_0_), channel_id=1, source_target_pairs={{0,1},{1,0},{2,3},{3,2},{4,5},{5,4},{6,7},{7,6},{8,9},{9,8},{10,11... | collective-permute-start | bytes 4718600 | tf_op jit(solution)/shard_map/ppermute | solution.py:151
  85.2 15.4 %copy-start.1 = (bf16[160,1536]{1,0:T(8,128)(2,1)S(1)}, bf16[160,1536]{1,0:T(8,128)(2,1)}, u32[]{:S(2)}) copy-start(bf16[160,1536]{1,0:T(8,128)(2,1)} %get-tuple-element.42.own_sides) | copy-start | bytes 1474564
  85.2 70.0 %all-to-all-start.1 = ((bf16[32,160,128]{2,1,0:T(8,128)(2,1)}), bf16[32,160,128]{2,1,0:T(8,128)(2,1)S(1)}, u32[]{:S(2)}, u32[]{:S(2)}) async-start(bf16[32,160,128]{2,1,0:T(8,128)(2,1)} %bitcast.33), calls=%async_computation.1 | async-start | bytes 2621440 | tf_op jit(solution)/shard_map/all_to_all | solution.py:141
  98.7 6.0 %collective-permute-start.9 = (bf16[32,160,128]{2,1,0:T(8,128)(2,1)S(1)}, bf16[32,160,128]{2,1,0:T(8,128)(2,1)}, u32[]{:S(2)}, u32[]{:S(2)}) collective-permute-start(bf16[32,160,128]{2,1,0:T(8,128)(2,1)S(1)} %copy-done), channel_id=1, source_target_pairs={{0,1},{1,0},{2,3},{3,2},{4,5},{5,4},{6,7},{7,6},{8,9},{9,8},{10,11... | collective-permute-start | bytes 3932168 | tf_op jit(solution)/shard_map/ppermute | solution.py:151
  100.6 4.0 %collective-permute-start.10 = (bf16[160,1536]{1,0:T(8,128)(2,1)S(1)}, bf16[160,1536]{1,0:T(8,128)(2,1)}, u32[]{:S(2)}, u32[]{:S(2)}) collective-permute-start(bf16[160,1536]{1,0:T(8,128)(2,1)S(1)} %copy-done.1), channel_id=1, source_target_pairs={{0,1},{1,0},{2,3},{3,2},{4,5},{5,4},{6,7},{7,6},{8,9},{9,8},{10,11... | collective-permute-start | bytes 1474568 | tf_op jit(solution)/shard_map/ppermute | solution.py:151
  107.9 17.5 %collective-permute-start.11 = (bf16[128,1536]{1,0:T(8,128)(2,1)S(1)}, bf16[128,1536]{1,0:T(8,128)(2,1)S(1)}, u32[]{:S(2)}, u32[]{:S(2)}) collective-permute-start(bf16[128,1536]{1,0:T(8,128)(2,1)S(1)} %get-tuple-element.44), channel_id=1, source_target_pairs={{0,2},{1,3},{2,0},{3,1},{4,6},{5,7},{6,4},{7,5},{8,10},{9,11},{10,... | collective-permute-start | bytes 1179656 | tf_op jit(solution)/shard_map/ppermute | solution.py:162
  111.3 18.8 %collective-permute-start.13 = (bf16[128,1536]{1,0:T(8,128)(2,1)S(1)}, bf16[128,1536]{1,0:T(8,128)(2,1)S(1)}, u32[]{:S(2)}, u32[]{:S(2)}) collective-permute-start(bf16[128,1536]{1,0:T(8,128)(2,1)S(1)} %get-tuple-element.46), channel_id=1, source_target_pairs={{0,4},{1,5},{2,6},{3,7},{4,8},{5,9},{6,10},{7,11},{8,12},{9,13},{1... | collective-permute-start | bytes 1179656 | tf_op jit(solution)/shard_map/ppermute | solution.py:162
  114.7 15.3 %collective-permute-start.14 = (bf16[128,1536]{1,0:T(8,128)(2,1)S(1)}, bf16[128,1536]{1,0:T(8,128)(2,1)S(1)}, u32[]{:S(2)}, u32[]{:S(2)}) collective-permute-start(bf16[128,1536]{1,0:T(8,128)(2,1)S(1)} %get-tuple-element.47), channel_id=1, source_target_pairs={{0,12},{1,13},{2,14},{3,15},{4,0},{5,1},{6,2},{7,3},{8,4},{9,5},{1... | collective-permute-start | bytes 1179656 | tf_op jit(solution)/shard_map/ppermute | solution.py:162
  118.3 15.6 %collective-permute-start.16 = (bf16[128,1536]{1,0:T(8,128)(2,1)S(1)}, bf16[128,1536]{1,0:T(8,128)(2,1)S(1)}, u32[]{:S(2)}, u32[]{:S(2)}) collective-permute-start(bf16[128,1536]{1,0:T(8,128)(2,1)S(1)} %get-tuple-element.49), channel_id=1, source_target_pairs={{0,4},{1,5},{2,6},{3,7},{4,8},{5,9},{6,10},{7,11},{8,12},{9,13},{1... | collective-permute-start | bytes 1179656 | tf_op jit(solution)/shard_map/ppermute | solution.py:162
  120.6 23.0 %collective-permute-start.17 = (bf16[128,1536]{1,0:T(8,128)(2,1)S(1)}, bf16[128,1536]{1,0:T(8,128)(2,1)S(1)}, u32[]{:S(2)}, u32[]{:S(2)}) collective-permute-start(bf16[128,1536]{1,0:T(8,128)(2,1)S(1)} %get-tuple-element.50), channel_id=1, source_target_pairs={{0,12},{1,13},{2,14},{3,15},{4,0},{5,1},{6,2},{7,3},{8,4},{9,5},{1... | collective-permute-start | bytes 1179656 | tf_op jit(solution)/shard_map/ppermute | solution.py:162
  125.5 18.2 %collective-permute-start.12 = (bf16[128,1536]{1,0:T(8,128)(2,1)S(1)}, bf16[128,1536]{1,0:T(8,128)(2,1)S(1)}, u32[]{:S(2)}, u32[]{:S(2)}) collective-permute-start(bf16[128,1536]{1,0:T(8,128)(2,1)S(1)} %add_convert_fusion.2), channel_id=1, source_target_pairs={{0,8},{1,9},{2,10},{3,11},{4,12},{5,13},{6,14},{7,15},{8,0},{9,1},... | collective-permute-start | bytes 1179656 | tf_op jit(solution)/shard_map/ppermute | solution.py:162
  130.2 17.1 %collective-permute-start.15 = (bf16[128,1536]{1,0:T(8,128)(2,1)S(1)}, bf16[128,1536]{1,0:T(8,128)(2,1)S(1)}, u32[]{:S(2)}, u32[]{:S(2)}) collective-permute-start(bf16[128,1536]{1,0:T(8,128)(2,1)S(1)} %add_convert_fusion.1), channel_id=1, source_target_pairs={{0,2},{1,3},{2,0},{3,1},{4,6},{5,7},{6,4},{7,5},{8,10},{9,11},{10,... | collective-permute-start | bytes 1179656 | tf_op jit(solution)/shard_map/ppermute | solution.py:162
  (2 other events, 21.3 us)

commit v13 on v12

--- a/solution.py
+++ b/solution.py
@@ -13,7 +13,7 @@
     )
 
 
-PAIR, FIRST = 2, 11
+PAIR, FIRST = 2, 9
 
 
 def slot_matrix(bucket, expert_count, capacity):

time: 158 us -> 161 us (1.019)
  the two profiles are of different devices: /device:TPU:6 before, /device:TPU:1 now
where the time goes in v13:
time: 161 us; the launch traced here: 160 us
  starting transfers between devices  93.4 us (58%)
  waiting for transfers between devices  45.5 us (28%)
  Pallas kernels  15.2 us (9%)
  local copies, waits for them, and re-layouts  4.1 us (3%)
    ppermute x14, starting transfers between devices, chip_shift(): return lax.ppermute(array, 'fsdp', pairs)  49.3 us
    all_to_all x2, starting transfers between devices, exchange(): lax.all_to_all(sent, 'ep', split_axis=0, concat_axis=0, tiled=True, axis_...  32.4 us
    ppermute x14, waiting for transfers between devices, chip_shift(): return lax.ppermute(array, 'fsdp', pairs)  20.9 us
    all_to_all x2, waiting for transfers between devices, exchange(): lax.all_to_all(sent, 'ep', split_axis=0, concat_axis=0, tiled=True, axis_...  19.4 us
    pallas_call x3, Pallas kernels, vmem_call(): pl.pallas_call(kernel, out_shape=jax.tree.map(lambda s: pltpu.HBM(s.shape...  12.2 us
    ppermute x4, starting transfers between devices, core_swap(): lax.ppermute(array, 'fsdp', [(f, f ^ 1) for f in range(2 * Y * X_HI)])  11.6 us
    ppermute x4, waiting for transfers between devices, core_swap(): lax.ppermute(array, 'fsdp', [(f, f ^ 1) for f in range(2 * Y * X_HI)])  5.24 us
  transfers between devices with their start and end apart: 20, of which 12 were waited for; matrix products, arithmetic and copies ran while one was open for 3% of the time, Pallas kernels for 2%

profile of v13, /device:TPU:1, one launch (start us, length us, event | category | flops | bytes accessed | tf_op | source)
XLA Modules:
  0.0 160.0 jit_solution(12400521363861888865)
XLA Ops:
  0.6 2.9 %shard_map.101 = (bf16[160,32,128]{2,1,0:T(8,128)(2,1)}, bf16[160,128]{1,0:T(8,128)(2,1)}) custom-call(s32[1,128]{1,0:T(1,128)} %bitcast.40, bf16[128,2048]{1,0:T(8,128)(2,1)} %tokens.1, bf16[128,2048]{1,0:T(8,128)(2,1)} %cotangent.1), custom_call_target="tpu_custom_call" | custom-call | tf_op jit(solution)/shard_map/pallas_call | solution.py:100
  3.6 19.4 %all-to-all-start = ((bf16[32,160,128]{2,1,0:T(8,128)(2,1)}), bf16[32,160,128]{2,1,0:T(8,128)(2,1)S(1)}, u32[]{:S(2)}, u32[]{:S(2)}) async-start(bf16[32,160,128]{2,1,0:T(8,128)(2,1)} %bitcast.32), calls=%async_computation | async-start | bytes 2621440 | tf_op jit(solution)/shard_map/all_to_all | solution.py:141
  23.1 4.3 %collective-permute-start.2 = (bf16[128,1536]{1,0:T(8,128)(2,1)S(1)}, bf16[128,1536]{1,0:T(8,128)(2,1)S(1)}, u32[]{:S(2)}, u32[]{:S(2)}) collective-permute-start(bf16[128,1536]{1,0:T(8,128)(2,1)S(1)} %pad_maximum_fusion.1), channel_id=1, source_target_pairs={{0,2},{1,3},{2,0},{3,1},{4,6},{5,7},{6,4},{7,5},{8,10},{9,11},{10,... | collective-permute-start | bytes 1179656 | tf_op jit(solution)/shard_map/ppermute | solution.py:162
  27.5 4.8 %collective-permute-start.5 = (bf16[128,1536]{1,0:T(8,128)(2,1)S(1)}, bf16[128,1536]{1,0:T(8,128)(2,1)S(1)}, u32[]{:S(2)}, u32[]{:S(2)}) collective-permute-start(bf16[128,1536]{1,0:T(8,128)(2,1)S(1)} %pad_maximum_fusion.1), channel_id=1, source_target_pairs={{0,8},{1,9},{2,10},{3,11},{4,12},{5,13},{6,14},{7,15},{8,0},{9,1},... | collective-permute-start | bytes 1179656 | tf_op jit(solution)/shard_map/ppermute | solution.py:162
  32.3 2.7 %collective-permute-start.1 = (bf16[128,1536]{1,0:T(8,128)(2,1)S(1)}, bf16[128,1536]{1,0:T(8,128)(2,1)S(1)}, u32[]{:S(2)}, u32[]{:S(2)}) collective-permute-start(bf16[128,1536]{1,0:T(8,128)(2,1)S(1)} %pad_maximum_fusion.1), channel_id=1, source_target_pairs={{0,12},{1,13},{2,14},{3,15},{4,0},{5,1},{6,2},{7,3},{8,4},{9,5},{1... | collective-permute-start | bytes 1179656 | tf_op jit(solution)/shard_map/ppermute | solution.py:162
  35.0 2.6 %collective-permute-start = (bf16[128,1536]{1,0:T(8,128)(2,1)S(1)}, bf16[128,1536]{1,0:T(8,128)(2,1)S(1)}, u32[]{:S(2)}, u32[]{:S(2)}) collective-permute-start(bf16[128,1536]{1,0:T(8,128)(2,1)S(1)} %pad_maximum_fusion.1), channel_id=1, source_target_pairs={{0,4},{1,5},{2,6},{3,7},{4,8},{5,9},{6,10},{7,11},{8,12},{9,13},{1... | collective-permute-start | bytes 1179656 | tf_op jit(solution)/shard_map/ppermute | solution.py:162
  38.9 4.6 %collective-permute-start.6 = (bf16[128,1536]{1,0:T(8,128)(2,1)S(1)}, bf16[128,1536]{1,0:T(8,128)(2,1)S(1)}, u32[]{:S(2)}, u32[]{:S(2)}) collective-permute-start(bf16[128,1536]{1,0:T(8,128)(2,1)S(1)} %collective-permute-done.2), channel_id=1, source_target_pairs={{0,12},{1,13},{2,14},{3,15},{4,0},{5,1},{6,2},{7,3},{8,4},{9,5},{1... | collective-permute-start | bytes 1179656 | tf_op jit(solution)/shard_map/ppermute | solution.py:162
  45.5 3.3 %collective-permute-start.7 = (bf16[128,1536]{1,0:T(8,128)(2,1)S(1)}, bf16[128,1536]{1,0:T(8,128)(2,1)S(1)}, u32[]{:S(2)}, u32[]{:S(2)}) collective-permute-start(bf16[128,1536]{1,0:T(8,128)(2,1)S(1)} %collective-permute-done.5), channel_id=1, source_target_pairs={{0,2},{1,3},{2,0},{3,1},{4,6},{5,7},{6,4},{7,5},{8,10},{9,11},{10,... | collective-permute-start | bytes 1179656 | tf_op jit(solution)/shard_map/ppermute | solution.py:162
  50.4 7.7 %collective-permute-done.6 = bf16[128,1536]{1,0:T(8,128)(2,1)S(1)} collective-permute-done((bf16[128,1536]{1,0:T(8,128)(2,1)S(1)}, bf16[128,1536]{1,0:T(8,128)(2,1)S(1)}, u32[]{:S(2)}, u32[]{:S(2)}) %collective-permute-start.6) | collective-permute-done | bytes 393248 | tf_op jit(solution)/shard_map/ppermute | solution.py:162
  60.3 4.8 %collective-permute-start.8 = (bf16[512,1536]{1,0:T(8,128)(2,1)}, bf16[512,1536]{1,0:T(8,128)(2,1)}, u32[]{:S(2)}, u32[]{:S(2)}) collective-permute-start(bf16[512,1536]{1,0:T(8,128)(2,1)} %constant_dynamic-update-slice_fusion.refs_2_), channel_id=1, source_target_pairs={{0,1},{1,0},{2,3},{3,2},{4,5},{5,4},{6,7},{7,6},{8,9},{9,8},{10,11... | collective-permute-start | bytes 4718600 | tf_op jit(solution)/shard_map/ppermute | solution.py:151
  68.4 2.2 %collective-permute-done.4.refs_1_ = bf16[512,1536]{1,0:T(8,128)(2,1)} collective-permute-done((bf16[512,1536]{1,0:T(8,128)(2,1)S(1)}, bf16[512,1536]{1,0:T(8,128)(2,1)}, u32[]{:S(2)}, u32[]{:S(2)}) %collective-permute-start.4) | collective-permute-done | bytes 1572896 | tf_op jit(solution)/shard_map/ppermute | solution.py:151
  70.6 9.8 %all-to-all-done = bf16[32,160,128]{2,1,0:T(8,128)(2,1)S(1)} async-done(((bf16[32,160,128]{2,1,0:T(8,128)(2,1)}), bf16[32,160,128]{2,1,0:T(8,128)(2,1)S(1)}, u32[]{:S(2)}, u32[]{:S(2)}) %all-to-all-start) | async-done | bytes 1310752 | tf_op jit(solution)/shard_map/all_to_all | solution.py:141
  80.4 7.4 %shard_map.102 = (bf16[160,32,128]{2,1,0:T(8,128)(2,1)}, bf16[160,1536]{1,0:T(8,128)(2,1)}, bf16[32,160,128]{2,1,0:T(8,128)(2,1)}) custom-call(s32[16]{0:T(128)S(1)} %stack.78.numbers, bf16[160,32,128]{2,1,0:T(8,128)(2,1)S(1)} %bitcast.31, bf16[512,1536]{1,0:T(8,128)(2,1)S(1)} %pad_maximum_fusion.refs_0_, bf16[512,1536]{1,0:T(8,128)(2,1)} %collective-permute-done.4.refs_1_, ...), custom_call_target="tpu_custom_call" | custom-call | tf_op jit(solution)/shard_map/pallas_call | solution.py:44
  87.9 13.0 %all-to-all-start.1 = ((bf16[32,160,128]{2,1,0:T(8,128)(2,1)}), bf16[32,160,128]{2,1,0:T(8,128)(2,1)S(1)}, u32[]{:S(2)}, u32[]{:S(2)}) async-start(bf16[32,160,128]{2,1,0:T(8,128)(2,1)} %bitcast.33), calls=%async_computation.1 | async-start | bytes 2621440 | tf_op jit(solution)/shard_map/all_to_all | solution.py:141
  100.9 3.0 %collective-permute-start.9 = (bf16[32,160,128]{2,1,0:T(8,128)(2,1)S(1)}, bf16[32,160,128]{2,1,0:T(8,128)(2,1)}, u32[]{:S(2)}, u32[]{:S(2)}) collective-permute-start(bf16[32,160,128]{2,1,0:T(8,128)(2,1)S(1)} %copy-done), channel_id=1, source_target_pairs={{0,1},{1,0},{2,3},{3,2},{4,5},{5,4},{6,7},{7,6},{8,9},{9,8},{10,11... | collective-permute-start | bytes 3932168 | tf_op jit(solution)/shard_map/ppermute | solution.py:151
  107.8 3.3 %shard_map.104 = (bf16[128,1536]{1,0:T(8,128)(2,1)S(1)}, bf16[128,1536]{1,0:T(8,128)(2,1)S(1)}, bf16[128,1536]{1,0:T(8,128)(2,1)S(1)}, bf16[128,1536]{1,0:T(8,12...) custom-call(s32[8]{0:T(128)S(1)} %stack.79.numbers, ...), custom_call_target="tpu_custom_call" | custom-call | tf_op jit(solution)/shard_map/pallas_call | solution.py:44
  111.1 4.3 %collective-permute-start.11 = (bf16[128,1536]{1,0:T(8,128)(2,1)S(1)}, bf16[128,1536]{1,0:T(8,128)(2,1)S(1)}, u32[]{:S(2)}, u32[]{:S(2)}) collective-permute-start(bf16[128,1536]{1,0:T(8,128)(2,1)S(1)} %get-tuple-element.44), channel_id=1, source_target_pairs={{0,2},{1,3},{2,0},{3,1},{4,6},{5,7},{6,4},{7,5},{8,10},{9,11},{10,... | collective-permute-start | bytes 1179656 | tf_op jit(solution)/shard_map/ppermute | solution.py:162
  115.4 3.2 %collective-permute-start.13 = (bf16[128,1536]{1,0:T(8,128)(2,1)S(1)}, bf16[128,1536]{1,0:T(8,128)(2,1)S(1)}, u32[]{:S(2)}, u32[]{:S(2)}) collective-permute-start(bf16[128,1536]{1,0:T(8,128)(2,1)S(1)} %get-tuple-element.46), channel_id=1, source_target_pairs={{0,4},{1,5},{2,6},{3,7},{4,8},{5,9},{6,10},{7,11},{8,12},{9,13},{1... | collective-permute-start | bytes 1179656 | tf_op jit(solution)/shard_map/ppermute | solution.py:162
  118.6 3.4 %collective-permute-start.14 = (bf16[128,1536]{1,0:T(8,128)(2,1)S(1)}, bf16[128,1536]{1,0:T(8,128)(2,1)S(1)}, u32[]{:S(2)}, u32[]{:S(2)}) collective-permute-start(bf16[128,1536]{1,0:T(8,128)(2,1)S(1)} %get-tuple-element.47), channel_id=1, source_target_pairs={{0,12},{1,13},{2,14},{3,15},{4,0},{5,1},{6,2},{7,3},{8,4},{9,5},{1... | collective-permute-start | bytes 1179656 | tf_op jit(solution)/shard_map/ppermute | solution.py:162
  123.9 4.6 %collective-permute-start.17 = (bf16[128,1536]{1,0:T(8,128)(2,1)S(1)}, bf16[128,1536]{1,0:T(8,128)(2,1)S(1)}, u32[]{:S(2)}, u32[]{:S(2)}) collective-permute-start(bf16[128,1536]{1,0:T(8,128)(2,1)S(1)} %get-tuple-element.50), channel_id=1, source_target_pairs={{0,12},{1,13},{2,14},{3,15},{4,0},{5,1},{6,2},{7,3},{8,4},{9,5},{1... | collective-permute-start | bytes 1179656 | tf_op jit(solution)/shard_map/ppermute | solution.py:162
  128.6 2.9 %collective-permute-start.12 = (bf16[128,1536]{1,0:T(8,128)(2,1)S(1)}, bf16[128,1536]{1,0:T(8,128)(2,1)S(1)}, u32[]{:S(2)}, u32[]{:S(2)}) collective-permute-start(bf16[128,1536]{1,0:T(8,128)(2,1)S(1)} %add_convert_fusion.2), channel_id=1, source_target_pairs={{0,8},{1,9},{2,10},{3,11},{4,12},{5,13},{6,14},{7,15},{8,0},{9,1},... | collective-permute-start | bytes 1179656 | tf_op jit(solution)/shard_map/ppermute | solution.py:162
  131.7 4.7 %collective-permute-start.15 = (bf16[128,1536]{1,0:T(8,128)(2,1)S(1)}, bf16[128,1536]{1,0:T(8,128)(2,1)S(1)}, u32[]{:S(2)}, u32[]{:S(2)}) collective-permute-start(bf16[128,1536]{1,0:T(8,128)(2,1)S(1)} %add_convert_fusion.1), channel_id=1, source_target_pairs={{0,2},{1,3},{2,0},{3,1},{4,6},{5,7},{6,4},{7,5},{8,10},{9,11},{10,... | collective-permute-start | bytes 1179656 | tf_op jit(solution)/shard_map/ppermute | solution.py:162
  139.0 7.9 %collective-permute-done.12 = bf16[128,1536]{1,0:T(8,128)(2,1)S(1)} collective-permute-done((bf16[128,1536]{1,0:T(8,128)(2,1)S(1)}, bf16[128,1536]{1,0:T(8,128)(2,1)S(1)}, u32[]{:S(2)}, u32[]{:S(2)}) %collective-permute-start.12) | collective-permute-done | bytes 393248 | tf_op jit(solution)/shard_map/ppermute | solution.py:162
  148.8 9.6 %all-to-all-done.1 = bf16[32,160,128]{2,1,0:T(8,128)(2,1)S(1)} async-done(((bf16[32,160,128]{2,1,0:T(8,128)(2,1)}), bf16[32,160,128]{2,1,0:T(8,128)(2,1)S(1)}, u32[]{:S(2)}, u32[]{:S(2)}) %all-to-all-start.1) | async-done | bytes 1310752 | tf_op jit(solution)/shard_map/all_to_all | solution.py:141
  (46 shorter events, 22.4 us)
Async XLA Ops:
  3.6 19.5 %copy-start.3 = (bf16[1,128,512]{2,1,0:T(8,128)(2,1)S(1)}, bf16[1,128,512]{2,1,0:T(8,128)(2,1)}, u32[]{:S(2)}) copy-start(bf16[1,128,512]{2,1,0:T(8,128)(2,1)} %param.11) | copy-start | bytes 393220
  3.6 19.5 %copy-start.4 = (bf16[1,128,512]{2,1,0:T(8,128)(2,1)S(1)}, bf16[1,128,512]{2,1,0:T(8,128)(2,1)}, u32[]{:S(2)}) copy-start(bf16[1,128,512]{2,1,0:T(8,128)(2,1)} %param.10) | copy-start | bytes 393220
  3.6 19.5 %copy-start.5 = (bf16[1,128,512]{2,1,0:T(8,128)(2,1)S(1)}, bf16[1,128,512]{2,1,0:T(8,128)(2,1)}, u32[]{:S(2)}) copy-start(bf16[1,128,512]{2,1,0:T(8,128)(2,1)} %param.9) | copy-start | bytes 393220
  3.6 76.8 %all-to-all-start = ((bf16[32,160,128]{2,1,0:T(8,128)(2,1)}), bf16[32,160,128]{2,1,0:T(8,128)(2,1)S(1)}, u32[]{:S(2)}, u32[]{:S(2)}) async-start(bf16[32,160,128]{2,1,0:T(8,128)(2,1)} %bitcast.32), calls=%async_computation | async-start | bytes 2621440 | tf_op jit(solution)/shard_map/all_to_all | solution.py:141
  23.1 15.8 %collective-permute-start.2 = (bf16[128,1536]{1,0:T(8,128)(2,1)S(1)}, bf16[128,1536]{1,0:T(8,128)(2,1)S(1)}, u32[]{:S(2)}, u32[]{:S(2)}) collective-permute-start(bf16[128,1536]{1,0:T(8,128)(2,1)S(1)} %pad_maximum_fusion.1), channel_id=1, source_target_pairs={{0,2},{1,3},{2,0},{3,1},{4,6},{5,7},{6,4},{7,5},{8,10},{9,11},{10,... | collective-permute-start | bytes 1179656 | tf_op jit(solution)/shard_map/ppermute | solution.py:162
  27.5 18.0 %collective-permute-start.5 = (bf16[128,1536]{1,0:T(8,128)(2,1)S(1)}, bf16[128,1536]{1,0:T(8,128)(2,1)S(1)}, u32[]{:S(2)}, u32[]{:S(2)}) collective-permute-start(bf16[128,1536]{1,0:T(8,128)(2,1)S(1)} %pad_maximum_fusion.1), channel_id=1, source_target_pairs={{0,8},{1,9},{2,10},{3,11},{4,12},{5,13},{6,14},{7,15},{8,0},{9,1},... | collective-permute-start | bytes 1179656 | tf_op jit(solution)/shard_map/ppermute | solution.py:162
  32.3 32.7 %collective-permute-start.1 = (bf16[128,1536]{1,0:T(8,128)(2,1)S(1)}, bf16[128,1536]{1,0:T(8,128)(2,1)S(1)}, u32[]{:S(2)}, u32[]{:S(2)}) collective-permute-start(bf16[128,1536]{1,0:T(8,128)(2,1)S(1)} %pad_maximum_fusion.1), channel_id=1, source_target_pairs={{0,12},{1,13},{2,14},{3,15},{4,0},{5,1},{6,2},{7,3},{8,4},{9,5},{1... | collective-permute-start | bytes 1179656 | tf_op jit(solution)/shard_map/ppermute | solution.py:162
  35.0 30.1 %collective-permute-start = (bf16[128,1536]{1,0:T(8,128)(2,1)S(1)}, bf16[128,1536]{1,0:T(8,128)(2,1)S(1)}, u32[]{:S(2)}, u32[]{:S(2)}) collective-permute-start(bf16[128,1536]{1,0:T(8,128)(2,1)S(1)} %pad_maximum_fusion.1), channel_id=1, source_target_pairs={{0,4},{1,5},{2,6},{3,7},{4,8},{5,9},{6,10},{7,11},{8,12},{9,13},{1... | collective-permute-start | bytes 1179656 | tf_op jit(solution)/shard_map/ppermute | solution.py:162
  38.9 19.2 %collective-permute-start.6 = (bf16[128,1536]{1,0:T(8,128)(2,1)S(1)}, bf16[128,1536]{1,0:T(8,128)(2,1)S(1)}, u32[]{:S(2)}, u32[]{:S(2)}) collective-permute-start(bf16[128,1536]{1,0:T(8,128)(2,1)S(1)} %collective-permute-done.2), channel_id=1, source_target_pairs={{0,12},{1,13},{2,14},{3,15},{4,0},{5,1},{6,2},{7,3},{8,4},{9,5},{1... | collective-permute-start | bytes 1179656 | tf_op jit(solution)/shard_map/ppermute | solution.py:162
  43.6 21.5 %collective-permute-start.3 = (bf16[128,1536]{1,0:T(8,128)(2,1)S(1)}, bf16[128,1536]{1,0:T(8,128)(2,1)S(1)}, u32[]{:S(2)}, u32[]{:S(2)}) collective-permute-start(bf16[128,1536]{1,0:T(8,128)(2,1)S(1)} %collective-permute-done.2), channel_id=1, source_target_pairs={{0,4},{1,5},{2,6},{3,7},{4,8},{5,9},{6,10},{7,11},{8,12},{9,13},{1... | collective-permute-start | bytes 1179656 | tf_op jit(solution)/shard_map/ppermute | solution.py:162
  45.5 13.9 %collective-permute-start.7 = (bf16[128,1536]{1,0:T(8,128)(2,1)S(1)}, bf16[128,1536]{1,0:T(8,128)(2,1)S(1)}, u32[]{:S(2)}, u32[]{:S(2)}) collective-permute-start(bf16[128,1536]{1,0:T(8,128)(2,1)S(1)} %collective-permute-done.5), channel_id=1, source_target_pairs={{0,2},{1,3},{2,0},{3,1},{4,6},{5,7},{6,4},{7,5},{8,10},{9,11},{10,... | collective-permute-start | bytes 1179656 | tf_op jit(solution)/shard_map/ppermute | solution.py:162
  60.3 8.2 %collective-permute-start.8 = (bf16[512,1536]{1,0:T(8,128)(2,1)}, bf16[512,1536]{1,0:T(8,128)(2,1)}, u32[]{:S(2)}, u32[]{:S(2)}) collective-permute-start(bf16[512,1536]{1,0:T(8,128)(2,1)} %constant_dynamic-update-slice_fusion.refs_2_), channel_id=1, source_target_pairs={{0,1},{1,0},{2,3},{3,2},{4,5},{5,4},{6,7},{7,6},{8,9},{9,8},{10,11... | collective-permute-start | bytes 4718600 | tf_op jit(solution)/shard_map/ppermute | solution.py:151
  65.2 5.4 %collective-permute-start.4 = (bf16[512,1536]{1,0:T(8,128)(2,1)S(1)}, bf16[512,1536]{1,0:T(8,128)(2,1)}, u32[]{:S(2)}, u32[]{:S(2)}) collective-permute-start(bf16[512,1536]{1,0:T(8,128)(2,1)S(1)} %pad_maximum_fusion.refs_0_), channel_id=1, source_target_pairs={{0,1},{1,0},{2,3},{3,2},{4,5},{5,4},{6,7},{7,6},{8,9},{9,8},{10,11... | collective-permute-start | bytes 4718600 | tf_op jit(solution)/shard_map/ppermute | solution.py:151
  87.9 16.0 %copy-start.1 = (bf16[160,1536]{1,0:T(8,128)(2,1)S(1)}, bf16[160,1536]{1,0:T(8,128)(2,1)}, u32[]{:S(2)}) copy-start(bf16[160,1536]{1,0:T(8,128)(2,1)} %get-tuple-element.42.own_sides) | copy-start | bytes 1474564
  87.9 70.5 %all-to-all-start.1 = ((bf16[32,160,128]{2,1,0:T(8,128)(2,1)}), bf16[32,160,128]{2,1,0:T(8,128)(2,1)S(1)}, u32[]{:S(2)}, u32[]{:S(2)}) async-start(bf16[32,160,128]{2,1,0:T(8,128)(2,1)} %bitcast.33), calls=%async_computation.1 | async-start | bytes 2621440 | tf_op jit(solution)/shard_map/all_to_all | solution.py:141
  100.9 6.9 %collective-permute-start.9 = (bf16[32,160,128]{2,1,0:T(8,128)(2,1)S(1)}, bf16[32,160,128]{2,1,0:T(8,128)(2,1)}, u32[]{:S(2)}, u32[]{:S(2)}) collective-permute-start(bf16[32,160,128]{2,1,0:T(8,128)(2,1)S(1)} %copy-done), channel_id=1, source_target_pairs={{0,1},{1,0},{2,3},{3,2},{4,5},{5,4},{6,7},{7,6},{8,9},{9,8},{10,11... | collective-permute-start | bytes 3932168 | tf_op jit(solution)/shard_map/ppermute | solution.py:151
  103.9 3.9 %collective-permute-start.10 = (bf16[160,1536]{1,0:T(8,128)(2,1)S(1)}, bf16[160,1536]{1,0:T(8,128)(2,1)}, u32[]{:S(2)}, u32[]{:S(2)}) collective-permute-start(bf16[160,1536]{1,0:T(8,128)(2,1)S(1)} %copy-done.1), channel_id=1, source_target_pairs={{0,1},{1,0},{2,3},{3,2},{4,5},{5,4},{6,7},{7,6},{8,9},{9,8},{10,11... | collective-permute-start | bytes 1474568 | tf_op jit(solution)/shard_map/ppermute | solution.py:151
  111.1 17.4 %collective-permute-start.11 = (bf16[128,1536]{1,0:T(8,128)(2,1)S(1)}, bf16[128,1536]{1,0:T(8,128)(2,1)S(1)}, u32[]{:S(2)}, u32[]{:S(2)}) collective-permute-start(bf16[128,1536]{1,0:T(8,128)(2,1)S(1)} %get-tuple-element.44), channel_id=1, source_target_pairs={{0,2},{1,3},{2,0},{3,1},{4,6},{5,7},{6,4},{7,5},{8,10},{9,11},{10,... | collective-permute-start | bytes 1179656 | tf_op jit(solution)/shard_map/ppermute | solution.py:162
  115.4 16.1 %collective-permute-start.13 = (bf16[128,1536]{1,0:T(8,128)(2,1)S(1)}, bf16[128,1536]{1,0:T(8,128)(2,1)S(1)}, u32[]{:S(2)}, u32[]{:S(2)}) collective-permute-start(bf16[128,1536]{1,0:T(8,128)(2,1)S(1)} %get-tuple-element.46), channel_id=1, source_target_pairs={{0,4},{1,5},{2,6},{3,7},{4,8},{5,9},{6,10},{7,11},{8,12},{9,13},{1... | collective-permute-start | bytes 1179656 | tf_op jit(solution)/shard_map/ppermute | solution.py:162
  118.6 12.9 %collective-permute-start.14 = (bf16[128,1536]{1,0:T(8,128)(2,1)S(1)}, bf16[128,1536]{1,0:T(8,128)(2,1)S(1)}, u32[]{:S(2)}, u32[]{:S(2)}) collective-permute-start(bf16[128,1536]{1,0:T(8,128)(2,1)S(1)} %get-tuple-element.47), channel_id=1, source_target_pairs={{0,12},{1,13},{2,14},{3,15},{4,0},{5,1},{6,2},{7,3},{8,4},{9,5},{1... | collective-permute-start | bytes 1179656 | tf_op jit(solution)/shard_map/ppermute | solution.py:162
  122.0 15.4 %collective-permute-start.16 = (bf16[128,1536]{1,0:T(8,128)(2,1)S(1)}, bf16[128,1536]{1,0:T(8,128)(2,1)S(1)}, u32[]{:S(2)}, u32[]{:S(2)}) collective-permute-start(bf16[128,1536]{1,0:T(8,128)(2,1)S(1)} %get-tuple-element.49), channel_id=1, source_target_pairs={{0,4},{1,5},{2,6},{3,7},{4,8},{5,9},{6,10},{7,11},{8,12},{9,13},{1... | collective-permute-start | bytes 1179656 | tf_op jit(solution)/shard_map/ppermute | solution.py:162
  123.9 15.0 %collective-permute-start.17 = (bf16[128,1536]{1,0:T(8,128)(2,1)S(1)}, bf16[128,1536]{1,0:T(8,128)(2,1)S(1)}, u32[]{:S(2)}, u32[]{:S(2)}) collective-permute-start(bf16[128,1536]{1,0:T(8,128)(2,1)S(1)} %get-tuple-element.50), channel_id=1, source_target_pairs={{0,12},{1,13},{2,14},{3,15},{4,0},{5,1},{6,2},{7,3},{8,4},{9,5},{1... | collective-permute-start | bytes 1179656 | tf_op jit(solution)/shard_map/ppermute | solution.py:162
  128.6 18.2 %collective-permute-start.12 = (bf16[128,1536]{1,0:T(8,128)(2,1)S(1)}, bf16[128,1536]{1,0:T(8,128)(2,1)S(1)}, u32[]{:S(2)}, u32[]{:S(2)}) collective-permute-start(bf16[128,1536]{1,0:T(8,128)(2,1)S(1)} %add_convert_fusion.2), channel_id=1, source_target_pairs={{0,8},{1,9},{2,10},{3,11},{4,12},{5,13},{6,14},{7,15},{8,0},{9,1},... | collective-permute-start | bytes 1179656 | tf_op jit(solution)/shard_map/ppermute | solution.py:162
  131.7 16.1 %collective-permute-start.15 = (bf16[128,1536]{1,0:T(8,128)(2,1)S(1)}, bf16[128,1536]{1,0:T(8,128)(2,1)S(1)}, u32[]{:S(2)}, u32[]{:S(2)}) collective-permute-start(bf16[128,1536]{1,0:T(8,128)(2,1)S(1)} %add_convert_fusion.1), channel_id=1, source_target_pairs={{0,2},{1,3},{2,0},{3,1},{4,6},{5,7},{6,4},{7,5},{8,10},{9,11},{10,... | collective-permute-start | bytes 1179656 | tf_op jit(solution)/shard_map/ppermute | solution.py:162
  (2 other events, 23.5 us)
